TPU v7x, 32 devices: a whole 2x2x4 slice. The times are simulated.
32 devices in a mesh: beam: 16 (over z, x, core), head: 2 (over y).
Axes of the slice: x: 2, y: 2, z: 4, core: 2. Of those that a mesh axis runs over, the one named last changes fastest.
Arguments:
- queries: bfloat16 [64, 8192], P('beam', 'head')
- new_keys: bfloat16 [64, 1024], P('beam', 'head')
- new_values: bfloat16 [64, 1024], P('beam', 'head'), may hold values from -6 to 6
- prompt_keys: bfloat16 [4, 4096, 1024], P(None, 'beam', 'head')
- prompt_values: bfloat16 [4, 4096, 1024], P(None, 'beam', 'head'), may hold values from -6 to 6
- private_keys: bfloat16 [64, 512, 1024], P('beam', None, 'head'), may hold values from -16 to 16
- private_values: bfloat16 [64, 512, 1024], P('beam', None, 'head'), may hold values from -6 to 6
- parents: int32 [64], P('beam'), may hold values from 0 to 63, as said below
- block_counts: int32 [64], P('beam'), may hold values from 1 to 4
- out_weight: bfloat16 [8192, 8192], P('head', 'beam'), may hold values from -0.0625 to 0.0625
Outputs:
- mixed: bfloat16 [64, 8192], P('head', 'beam')
Inputs may be any that keep to these rules, and one draw needn't show every extreme that they name: Every beam's parent belongs to the same request: parents[b] // 16 == b // 16.
All inputs are finite; a program needn't handle non-finite values.
Results may differ from a plain program's by a relative error of at most 0.0049.
Values may be sent and summed in bfloat16 or wider, within the bound.
No kernel may reach another device: no remote copies, remote signals or barrier semaphores. Data moves between devices by JAX's collectives and lax.ppermute only.
A program may use at most 128 MiB of HBM per device.

v0:
```python
import math

import jax
import jax.numpy as jnp
from jax import lax
from jax.sharding import PartitionSpec as P

HD = 128
QPK = 8
BEAM_WIDTH = 16
BLOCK_LEN = 128


masked_score = -1e30


def shifted(x, axis, by):
    length = lax.axis_size(axis)
    pairs = [(i, i + by) for i in range(length) if 0 <= i + by < length]
    return lax.ppermute(x, axis, pairs)


def suffix_part(query_head_count, cache_keys, cache_values, counts):
    beams = cache_keys.shape[0]
    length = cache_keys.shape[1]
    heads = query_head_count.shape[1]
    key_heads = cache_keys.reshape(beams, length, heads, HD)
    value_heads = cache_values.reshape(beams, length, heads, HD)
    scores = jnp.einsum(
        "bkqd,bpkd->bkqp", query_head_count, key_heads, preferred_element_type=jnp.float32
    ) * (1.0 / math.sqrt(HD))
    allowed = lax.broadcasted_iota(jnp.int32, (beams, length), 1) < (counts * BLOCK_LEN)[:, None]
    scores = jnp.where(allowed[:, None, None, :], scores, masked_score)
    highest = jnp.max(scores, axis=-1)
    weights = jnp.exp(scores - highest[..., None])
    totals = jnp.sum(weights, axis=-1)
    summed = jnp.einsum(
        "bkqp,bpkd->bkqd",
        weights.astype(jnp.bfloat16),
        value_heads,
        preferred_element_type=jnp.float32,
    )
    return (summed, highest, totals)


def per_device(
    queries,
    new_keys,
    new_values,
    prompt_keys,
    prompt_values,
    private_keys,
    private_values,
    parents,
    block_counts,
    out_weight,
):
    local_beams = queries.shape[0]
    local_heads = new_keys.shape[1] // HD
    token_position = lax.axis_index("beam")
    group = BEAM_WIDTH // local_beams
    logit_scale = 1.0 / math.sqrt(HD)
    query_head_count = queries.reshape(local_beams, local_heads, QPK, HD)
    everyone = lax.all_gather(queries, "beam", axis=0, tiled=True)
    requests = prompt_keys.shape[0]
    prompt_len = prompt_keys.shape[1]
    all_beams = requests * BEAM_WIDTH
    query_groups = everyone.reshape(requests, BEAM_WIDTH, local_heads, QPK, HD)
    prompt_heads = prompt_keys.reshape(requests, prompt_len, local_heads, HD)
    prompt_vals = prompt_values.reshape(requests, prompt_len, local_heads, HD)
    scores = (
        jnp.einsum(
            "rbkqd,rtkd->rbkqt", query_groups, prompt_heads, preferred_element_type=jnp.float32
        )
        * logit_scale
    )
    local_max = jnp.max(scores, axis=-1)
    prompt_max = lax.pmax(local_max, "beam")
    weights = jnp.exp(scores - prompt_max[..., None])
    totals = jnp.sum(weights, axis=-1)
    summed = jnp.einsum(
        "rbkqt,rtkd->rbkqd",
        weights.astype(jnp.bfloat16),
        prompt_vals,
        preferred_element_type=jnp.float32,
    )
    prompt_num, prompt_denominator = (
        lax.psum_scatter(summed.reshape(all_beams, -1), "beam", scatter_dimension=0, tiled=True),
        lax.psum_scatter(totals.reshape(all_beams, -1), "beam", scatter_dimension=0, tiled=True),
    )
    prompt_num = prompt_num.reshape(local_beams, local_heads, QPK, HD)
    prompt_denominator = prompt_denominator.reshape(local_beams, local_heads, QPK)
    own_max = lax.dynamic_slice_in_dim(
        prompt_max.reshape(all_beams, local_heads, QPK),
        token_position * local_beams,
        local_beams,
        0,
    )
    holder = parents // local_beams - token_position
    moved_keys = private_keys
    moved_values = private_values
    shifted_count_totals = block_counts
    for offset in range(1 - group, group):
        chosen = holder == offset
        if offset == 0:
            source = (private_keys, private_values, block_counts)
        else:
            arrived = shifted(
                (private_keys, private_values, block_counts.astype(jnp.bfloat16)), "beam", -offset
            )
            source = (arrived[0], arrived[1], arrived[2].astype(jnp.int32))
        picked_rows = jnp.clip(
            parents - (token_position + offset) * local_beams, 0, local_beams - 1
        )
        moved_keys = jnp.where(
            chosen[:, None, None], jnp.take(source[0], picked_rows, axis=0), moved_keys
        )
        moved_values = jnp.where(
            chosen[:, None, None], jnp.take(source[1], picked_rows, axis=0), moved_values
        )
        shifted_count_totals = jnp.where(
            chosen, jnp.take(source[2], picked_rows), shifted_count_totals
        )
    suffix_num, suffix_max, suffix_den = suffix_part(
        query_head_count, moved_keys, moved_values, shifted_count_totals
    )
    fresh_head_rows = new_keys.reshape(local_beams, local_heads, HD)
    beam_self_logit = (
        jnp.einsum(
            "sxjr,sxr->sxj", query_head_count, fresh_head_rows, preferred_element_type=jnp.float32
        )
        * logit_scale
    )
    overall = jnp.maximum(jnp.maximum(own_max, suffix_max), beam_self_logit)
    first = jnp.exp(own_max - overall)
    second = jnp.exp(suffix_max - overall)
    third = jnp.exp(beam_self_logit - overall)
    own_values = new_values.reshape(local_beams, local_heads, 1, HD).astype(jnp.float32)
    numer = (
        first[..., None] * prompt_num
        + second[..., None] * suffix_num
        + third[..., None] * own_values
    )
    denom = first * prompt_denominator + second * suffix_den + third
    attended = (numer / denom[..., None]).astype(jnp.bfloat16).reshape(local_beams, -1)
    products = jnp.dot(
        lax.all_gather(attended, "beam", axis=0, tiled=True),
        out_weight,
        preferred_element_type=jnp.float32,
    )
    return lax.psum_scatter(products, "head", scatter_dimension=0, tiled=True).astype(jnp.bfloat16)


def solution(mesh):
    placed = (
        P("beam", "head"),
        P("beam", "head"),
        P("beam", "head"),
        P(None, "beam", "head"),
        P(None, "beam", "head"),
        P("beam", None, "head"),
        P("beam", None, "head"),
        P("beam"),
        P("beam"),
        P("head", "beam"),
    )
    return jax.shard_map(
        per_device, mesh=mesh, in_specs=placed, out_specs=P("head", "beam"), check_vma=False
    )
```

profile of v0, /device:TPU:0, one launch (start us, length us, event | category | flops | bytes accessed | tf_op | source)
XLA Modules:
  0.0 625.7 jit_solution(2290805222598437105)
XLA Ops:
  6.5 5.8 collective-permute-start.11
  12.3 4.8 collective-permute-start.10
  17.8 1.3 collective-permute-start.2
  19.1 1.3 collective-permute-start.1
  20.4 1.3 collective-permute-start
  21.7 5.6 collective-permute-start.5
  27.3 4.1 collective-permute-start.4
  31.4 1.6 collective-permute-start.3
  33.0 46.8 %collective-permute-done.5 = bf16[4]{0:T(256)(128)(2,1)S(1)} collective-permute-done((bf16[4]{0:T(256)(128)(2,1)S(1)}, bf16[4]{0:T(256)(128)(2,1)S(1)}, u32[]{:S(2)}, u32[]{:S(2)}) %collective-permute-start.5) | collective-permute-done | bytes 40 | tf_op jit(solution)/shard_map/ppermute | solution.py:20
  79.8 2.7 collective-permute-start.9
  82.5 1.3 collective-permute-start.8
  83.8 1.3 collective-permute-start.7
  85.1 1.3 collective-permute-start.6
  86.4 151.8 %all-gather = bf16[16,4,4096]{2,1,0:T(4,128)(2,1)S(1)} all-gather(bf16[1,4,4096]{2,1,0:T(4,128)(2,1)} %bitcast.84), channel_id=1, replica_groups=mesh['beam'=16,'head'=2] {'beam'}, dimensions={0}, use_global_device_ids=true | all-gather | bytes 557056 | tf_op jit(solution)/shard_map/all_gather | solution.py:64
  238.2 1.3 reshape.88
  239.8 2.6 collective-permute-start.17
  242.4 1.6 bitcast_reduce_fusion
  244.0 1.3 reshape.93
  245.4 84.6 %pmax.7 = f32[4,16,4,8]{1,3,2,0:T(8,128)S(1)} all-reduce(f32[4,16,4,8]{1,3,2,0:T(8,128)S(1)} %get-tuple-element.50), channel_id=1, replica_groups=mesh['beam'=16,'head'=2] {'beam'}, use_global_device_ids=true, to_apply=%region_1.0 | all-reduce | flops 2048 | bytes 16384 | tf_op jit(solution)/shard_map/pmax | solution.py:78
  329.9 0.7 fusion.21
  330.7 2.6 collective-permute-start.16
  333.4 2.6 collective-permute-start.15
  336.0 1.3 collective-permute-start.14
  337.3 1.3 collective-permute-start.13
  339.3 1.2 reshape.94
  341.3 2.1 gather_fusion.10
  343.5 3.6 gather_fusion.17
  348.5 171.2 %all-reduce.1 = f32[64,32]{0,1:T(8,128)S(1)} all-reduce(f32[64,32]{0,1:T(8,128)S(1)} %reshape.97), channel_id=3, replica_groups=mesh['beam'=16,'head'=2] {'beam'}, use_global_device_ids=true, to_apply=%region_5.8.clone | all-reduce | flops 2048 | bytes 16384
  524.1 1.3 collective-permute-start.12
  525.5 0.9 dynamic-slice_bitcast_fusion
  526.4 3.6 gather_fusion.13
  530.0 3.6 gather_fusion.12
  533.7 3.6 gather_fusion.11
  537.3 3.7 gather_fusion.9
  540.9 3.6 gather_fusion.8
  544.6 3.6 gather_fusion.7
  548.1 3.6 gather_fusion.20
  551.8 3.6 gather_fusion.19
  555.3 3.6 gather_fusion.18
  558.9 3.6 gather_fusion.16
  562.6 3.6 gather_fusion.15
  566.2 7.5 %fusion.69 = (f32[4,4,8]{2,1,0:T(4,128)S(1)}, f32[4,4,8,512]{3,2,1,0:T(8,128)S(1)}) fusion(bf16[1,4,32,128]{3,1,2,0:T(4,128)(2,1)S(1)} %bitcast.86, pred[4,512]{1,0:T(4,128)(4,1)S(1)} %iota_compare_fusion, bf16[4,512,512]{2,1,0:T(8,128)(2,1)S(1)} %copy-done.1, bf16[4,512,512]{2,1,0:T(8,128)(2,1)} %gather_fusion.13, ...), kind=kOutput, calls=%fused_computation.121 | convolution fusion | flops 31653760 | bytes 17074744 | tf_op jit(solution)/shard_map/bkqd,bpkd->bkqp/dot_general | solution.py:29
  573.9 3.8 gather_fusion.14
  577.7 7.2 %fusion.44 = bf16[4,4,8,128]{3,2,1,0:T(8,128)(2,1)S(1)} fusion(f32[4,4,8,512]{3,2,1,0:T(8,128)S(1)} %get-tuple-element.49, f32[4,4,8]{2,1,0:T(4,128)S(1)} %get-tuple-element.48, f32[1,4,32,128]{3,1,2,0:T(4,128)S(1)} %dynamic-slice_bitcast_fusion, f32[4,4,8]{2,1,0:T(4,128)S(1)} %get-tuple-element.6, f32[4,4,128]{2,1,0:T(4,128)S(1)} %reshape.100, ...), kind=kOutput, calls=%fused_computation.56 | convolution fusion | flops 31703040 | bytes 17148472 | tf_op jit(solution)/shard_map/bkqp,bpkd->bkqd/dot_general | solution.py:37
  584.9 18.9 %all-gather.1 = bf16[16,4,4096]{2,1,0:T(4,128)(2,1)S(1)} all-gather(bf16[1,4,4096]{2,1,0:T(4,128)(2,1)S(1)} %reshape.292), channel_id=1, replica_groups=mesh['beam'=16,'head'=2] {'beam'}, dimensions={0}, use_global_device_ids=true | all-gather | bytes 557056 | tf_op jit(solution)/shard_map/all_gather | solution.py:147
  604.0 3.7 fusion.70
  607.7 9.7 %reduce-scatter.3.cloned.1.call-done = f32[32,512]{1,0:T(8,128)} async-done(((f32[64,512]{1,0:T(8,128)}), f32[32,512]{1,0:T(8,128)}) %reduce-scatter.3.cloned.1.call-update) | async-done | bytes 65552 | tf_op jit(solution)/shard_map/reduce_scatter | solution.py:151
  617.4 1.5 convert_element_type.61
  (78 shorter events, 7.9 us)
Async XLA Ops:
  6.5 233.0 %copy-start.3 = (bf16[4,256,512]{2,1,0:T(8,128)(2,1)S(1)}, bf16[4,256,512]{2,1,0:T(8,128)(2,1)}, u32[]{:S(2)}) copy-start(bf16[4,256,512]{2,1,0:T(8,128)(2,1)} %param.17) | copy-start | bytes 3145732
  6.5 518.9 %all-reduce.4.cloned.1.call-start = ((), (), s32[]{:S(2)}) async-start(), calls=%async_computation.2 | async-start | bytes 2097152
  6.5 78.5 %collective-permute-start.11 = (bf16[4,512,512]{2,1,0:T(8,128)(2,1)}, bf16[4,512,512]{2,1,0:T(8,128)(2,1)}, u32[]{:S(2)}, u32[]{:S(2)}) collective-permute-start(bf16[4,512,512]{2,1,0:T(8,128)(2,1)} %param.19), channel_id=1, source_target_pairs={{0,6},{2,8},{4,10},{6,12},{8,14},{10,16},{12,18},{14,20},{16,22},{... | collective-permute-start | bytes 6291464 | tf_op jit(solution)/shard_map/ppermute | solution.py:20
  12.3 227.5 %collective-permute-start.10 = (bf16[4,512,512]{2,1,0:T(8,128)(2,1)}, bf16[4,512,512]{2,1,0:T(8,128)(2,1)}, u32[]{:S(2)}, u32[]{:S(2)}) collective-permute-start(bf16[4,512,512]{2,1,0:T(8,128)(2,1)} %param.19), channel_id=1, source_target_pairs={{0,4},{2,6},{4,8},{6,10},{8,12},{10,14},{12,16},{14,18},{16,20},{1... | collective-permute-start | bytes 6291464 | tf_op jit(solution)/shard_map/ppermute | solution.py:20
  17.8 3.9 collective-permute-start.2
  19.1 8.2 %collective-permute-start.1 = (bf16[4]{0:T(256)(128)(2,1)S(1)}, bf16[4]{0:T(256)(128)(2,1)S(1)}, u32[]{:S(2)}, u32[]{:S(2)}) collective-permute-start(bf16[4]{0:T(256)(128)(2,1)S(1)} %convert_element_type.49), channel_id=1, source_target_pairs={{4,0},{6,2},{8,4},{10,6},{12,8},{14,10},{16,12},{18,14},{20,16},{2... | collective-permute-start | bytes 32 | tf_op jit(solution)/shard_map/ppermute | solution.py:20
  20.4 11.1 %collective-permute-start = (bf16[4]{0:T(256)(128)(2,1)S(1)}, bf16[4]{0:T(256)(128)(2,1)S(1)}, u32[]{:S(2)}, u32[]{:S(2)}) collective-permute-start(bf16[4]{0:T(256)(128)(2,1)S(1)} %convert_element_type.49), channel_id=1, source_target_pairs={{6,0},{8,2},{10,4},{12,6},{14,8},{16,10},{18,12},{20,14},{22,16},{... | collective-permute-start | bytes 32 | tf_op jit(solution)/shard_map/ppermute | solution.py:20
  21.7 58.1 %collective-permute-start.5 = (bf16[4]{0:T(256)(128)(2,1)S(1)}, bf16[4]{0:T(256)(128)(2,1)S(1)}, u32[]{:S(2)}, u32[]{:S(2)}) collective-permute-start(bf16[4]{0:T(256)(128)(2,1)S(1)} %convert_element_type.49), channel_id=1, source_target_pairs={{0,6},{2,8},{4,10},{6,12},{8,14},{10,16},{12,18},{14,20},{16,22},{... | collective-permute-start | bytes 32 | tf_op jit(solution)/shard_map/ppermute | solution.py:20
  27.3 55.1 %collective-permute-start.4 = (bf16[4]{0:T(256)(128)(2,1)S(1)}, bf16[4]{0:T(256)(128)(2,1)S(1)}, u32[]{:S(2)}, u32[]{:S(2)}) collective-permute-start(bf16[4]{0:T(256)(128)(2,1)S(1)} %convert_element_type.49), channel_id=1, source_target_pairs={{0,4},{2,6},{4,8},{6,10},{8,12},{10,14},{12,16},{14,18},{16,20},{1... | collective-permute-start | bytes 32 | tf_op jit(solution)/shard_map/ppermute | solution.py:20
  31.4 52.3 %collective-permute-start.3 = (bf16[4]{0:T(256)(128)(2,1)S(1)}, bf16[4]{0:T(256)(128)(2,1)S(1)}, u32[]{:S(2)}, u32[]{:S(2)}) collective-permute-start(bf16[4]{0:T(256)(128)(2,1)S(1)} %convert_element_type.49), channel_id=1, source_target_pairs={{0,2},{2,4},{4,6},{6,8},{8,10},{10,12},{12,14},{14,16},{16,18},{18... | collective-permute-start | bytes 32 | tf_op jit(solution)/shard_map/ppermute | solution.py:20
  79.8 250.9 %collective-permute-start.9 = (bf16[4,512,512]{2,1,0:T(8,128)(2,1)}, bf16[4,512,512]{2,1,0:T(8,128)(2,1)}, u32[]{:S(2)}, u32[]{:S(2)}) collective-permute-start(bf16[4,512,512]{2,1,0:T(8,128)(2,1)} %param.19), channel_id=1, source_target_pairs={{0,2},{2,4},{4,6},{6,8},{8,10},{10,12},{12,14},{14,16},{16,18},{18... | collective-permute-start | bytes 6291464 | tf_op jit(solution)/shard_map/ppermute | solution.py:20
  82.5 250.9 %collective-permute-start.8 = (bf16[4,512,512]{2,1,0:T(8,128)(2,1)}, bf16[4,512,512]{2,1,0:T(8,128)(2,1)}, u32[]{:S(2)}, u32[]{:S(2)}) collective-permute-start(bf16[4,512,512]{2,1,0:T(8,128)(2,1)} %param.19), channel_id=1, source_target_pairs={{2,0},{4,2},{6,4},{8,6},{10,8},{12,10},{14,12},{16,14},{18,16},{20... | collective-permute-start | bytes 6291464 | tf_op jit(solution)/shard_map/ppermute | solution.py:20
  83.8 252.2 %collective-permute-start.7 = (bf16[4,512,512]{2,1,0:T(8,128)(2,1)}, bf16[4,512,512]{2,1,0:T(8,128)(2,1)}, u32[]{:S(2)}, u32[]{:S(2)}) collective-permute-start(bf16[4,512,512]{2,1,0:T(8,128)(2,1)} %param.19), channel_id=1, source_target_pairs={{4,0},{6,2},{8,4},{10,6},{12,8},{14,10},{16,12},{18,14},{20,16},{2... | collective-permute-start | bytes 6291464 | tf_op jit(solution)/shard_map/ppermute | solution.py:20
  85.1 252.2 %collective-permute-start.6 = (bf16[4,512,512]{2,1,0:T(8,128)(2,1)}, bf16[4,512,512]{2,1,0:T(8,128)(2,1)}, u32[]{:S(2)}, u32[]{:S(2)}) collective-permute-start(bf16[4,512,512]{2,1,0:T(8,128)(2,1)} %param.19), channel_id=1, source_target_pairs={{6,0},{8,2},{10,4},{12,6},{14,8},{16,10},{18,12},{20,14},{22,16},{... | collective-permute-start | bytes 6291464 | tf_op jit(solution)/shard_map/ppermute | solution.py:20
  239.8 284.3 %collective-permute-start.17 = (bf16[4,512,512]{2,1,0:T(8,128)(2,1)}, bf16[4,512,512]{2,1,0:T(8,128)(2,1)}, u32[]{:S(2)}, u32[]{:S(2)}) collective-permute-start(bf16[4,512,512]{2,1,0:T(8,128)(2,1)} %param.20), channel_id=1, source_target_pairs={{0,6},{2,8},{4,10},{6,12},{8,14},{10,16},{12,18},{14,20},{16,22},{... | collective-permute-start | bytes 6291464 | tf_op jit(solution)/shard_map/ppermute | solution.py:20
  330.7 221.1 %collective-permute-start.16 = (bf16[4,512,512]{2,1,0:T(8,128)(2,1)}, bf16[4,512,512]{2,1,0:T(8,128)(2,1)}, u32[]{:S(2)}, u32[]{:S(2)}) collective-permute-start(bf16[4,512,512]{2,1,0:T(8,128)(2,1)} %param.20), channel_id=1, source_target_pairs={{0,4},{2,6},{4,8},{6,10},{8,12},{10,14},{12,16},{14,18},{16,20},{1... | collective-permute-start | bytes 6291464 | tf_op jit(solution)/shard_map/ppermute | solution.py:20
  333.4 222.0 %collective-permute-start.15 = (bf16[4,512,512]{2,1,0:T(8,128)(2,1)}, bf16[4,512,512]{2,1,0:T(8,128)(2,1)}, u32[]{:S(2)}, u32[]{:S(2)}) collective-permute-start(bf16[4,512,512]{2,1,0:T(8,128)(2,1)} %param.20), channel_id=1, source_target_pairs={{0,2},{2,4},{4,6},{6,8},{8,10},{10,12},{12,14},{14,16},{16,18},{18... | collective-permute-start | bytes 6291464 | tf_op jit(solution)/shard_map/ppermute | solution.py:20
  336.0 223.0 %collective-permute-start.14 = (bf16[4,512,512]{2,1,0:T(8,128)(2,1)}, bf16[4,512,512]{2,1,0:T(8,128)(2,1)}, u32[]{:S(2)}, u32[]{:S(2)}) collective-permute-start(bf16[4,512,512]{2,1,0:T(8,128)(2,1)} %param.20), channel_id=1, source_target_pairs={{2,0},{4,2},{6,4},{8,6},{10,8},{12,10},{14,12},{16,14},{18,16},{20... | collective-permute-start | bytes 6291464 | tf_op jit(solution)/shard_map/ppermute | solution.py:20
  337.3 225.3 %collective-permute-start.13 = (bf16[4,512,512]{2,1,0:T(8,128)(2,1)}, bf16[4,512,512]{2,1,0:T(8,128)(2,1)}, u32[]{:S(2)}, u32[]{:S(2)}) collective-permute-start(bf16[4,512,512]{2,1,0:T(8,128)(2,1)} %param.20), channel_id=1, source_target_pairs={{4,0},{6,2},{8,4},{10,6},{12,8},{14,10},{16,12},{18,14},{20,16},{2... | collective-permute-start | bytes 6291464 | tf_op jit(solution)/shard_map/ppermute | solution.py:20
  339.2 1.4 copy-start.7
  339.2 1.4 copy-start
  339.2 2.0 copy-start.1
  340.5 276.8 %reduce-scatter.3.cloned.1.call-start = ((), (), s32[]{:S(2)}) async-start(), calls=%async_computation.1 | async-start | bytes 196608 | tf_op jit(solution)/shard_map/reduce_scatter | solution.py:151
  343.5 3.8 copy-start.8
  343.5 176.5 %copy-start.5 = (bf16[4,512]{1,0:T(4,128)(2,1)S(1)}, bf16[4,512]{1,0:T(4,128)(2,1)}, u32[]{:S(2)}) copy-start(bf16[4,512]{1,0:T(4,128)(2,1)} %param.15) | copy-start | bytes 12292
  343.5 176.5 %copy-start.6 = (bf16[4,512]{1,0:T(4,128)(2,1)S(1)}, bf16[4,512]{1,0:T(4,128)(2,1)}, u32[]{:S(2)}) copy-start(bf16[4,512]{1,0:T(4,128)(2,1)} %param.16) | copy-start | bytes 12292
  343.5 176.5 %copy-start.4 = (bf16[4,4096]{1,0:T(4,128)(2,1)S(1)}, bf16[4,4096]{1,0:T(4,128)(2,1)}, u32[]{:S(2)}) copy-start(bf16[4,4096]{1,0:T(4,128)(2,1)} %param.14) | copy-start | bytes 98308
  524.1 49.8 %collective-permute-start.12 = (bf16[4,512,512]{2,1,0:T(8,128)(2,1)}, bf16[4,512,512]{2,1,0:T(8,128)(2,1)}, u32[]{:S(2)}, u32[]{:S(2)}) collective-permute-start(bf16[4,512,512]{2,1,0:T(8,128)(2,1)} %param.20), channel_id=1, source_target_pairs={{6,0},{8,2},{10,4},{12,6},{14,8},{16,10},{18,12},{20,14},{22,16},{... | collective-permute-start | bytes 6291464 | tf_op jit(solution)/shard_map/ppermute | solution.py:20
  573.9 3.8 copy-start.2
Sparse Core Ops, SparseCore 0:
  340.6 144.7 all-reduce.3
  607.8 9.5 reduce-scatter.2
where the time goes:
time: 627 us; the launch traced here: 626 us
  blocking collectives  427 us (68%)
  local copies, waits for them, and re-layouts  60.2 us (10%)
  waiting for transfers between devices  56.5 us (9%)
  starting transfers between devices  44 us (7%)
  matrix products  20.6 us (3%)
  between operations  14.5 us (2%)
    unnamed x1, blocking collectives  171 us
    all_gather x1, blocking collectives, per_device(): everyone = lax.all_gather(queries, 'beam', axis=0, tiled=True)  152 us
    pmax x1, blocking collectives, per_device(): prompt_max = lax.pmax(local_max, 'beam')  84.6 us
    ppermute x18, waiting for transfers between devices, shifted(): return lax.ppermute(x, axis, pairs)  46.8 us
    ppermute x18, starting transfers between devices, shifted(): return lax.ppermute(x, axis, pairs)  44 us
    gather x7, local copies, waits for them, and re-layouts, per_device(): jnp.take(source[1], picked_rows, axis=0)  25.4 us
    gather x7, local copies, waits for them, and re-layouts, per_device(): jnp.take(source[0], picked_rows, axis=0)  23.8 us
    all_gather x1, blocking collectives, per_device(): lax.all_gather(attended, 'beam', axis=0, tiled=True)  18.9 us
  transfers between devices with their start and end apart: 20, of which 2 were waited for; matrix products, arithmetic and copies ran while one was open for 11% of the time, Pallas kernels for 0%

commit v1 on v0

v1 whole, which is shorter than its diff:
```python
import functools
import math

import jax
import jax.numpy as jnp
from jax import lax
from jax.experimental import pallas as pl
from jax.experimental.pallas import tpu as pltpu
from jax.sharding import PartitionSpec as P

HD = 128
QPK = 8
BEAM_WIDTH = 16
BLOCK_LEN = 128
STATS = 128
SCALE = 1.0 / math.sqrt(HD)
LOG2E = math.log2(math.e)

masked_score = -1e30
f32, bf16 = jnp.float32, jnp.bfloat16


def dot(a, b, ca, cb):
    return lax.dot_general(a, b, (((ca,), (cb,)), ((), ())), preferred_element_type=f32)


def soft(scores):
    top = jnp.max(scores, axis=1, keepdims=True)
    weights = jnp.exp2((scores - top) * (SCALE * LOG2E))
    return weights, top * SCALE, jnp.sum(weights, axis=1, keepdims=True)


def prep_kernel(q_hbm, nk_hbm, par_hbm, q_ref, own_ref, tail_ref, nk_ref, par_ref, sems):
    copies = [
        pltpu.make_async_copy(src, dst, sems.at[n])
        for n, (src, dst) in enumerate(((q_hbm, q_ref), (nk_hbm, nk_ref), (par_hbm, par_ref)))
    ]
    for x in copies:
        x.start()
    for x in copies:
        x.wait()
    beams = q_ref.shape[0]
    row = lax.broadcasted_iota(jnp.int32, (beams, STATS), 0)
    parent = jnp.zeros(row.shape, jnp.int32)
    for b in range(beams):
        parent = jnp.where(row == b, par_ref[b], parent)
    tail_ref[...] = parent.astype(f32).astype(bf16)
    lane = lax.broadcasted_iota(jnp.int32, (beams, STATS), 1)
    own = jnp.zeros((beams, STATS), f32)
    for h in range(q_ref.shape[1] // HD):
        k = h // QPK
        key = nk_ref[:, k * HD : (k + 1) * HD].astype(f32)
        s = jnp.sum(q_ref[:, h * HD : (h + 1) * HD].astype(f32) * key, axis=1, keepdims=True)
        own = jnp.where(lane == h, s * SCALE, own)
    own_ref[...] = own


def line_kernel(tail_ref, *refs):
    *pieces, out_ref = refs
    width = pieces[0].shape[1]
    out_ref[:, :width] = jnp.concatenate([x[...] for x in pieces], axis=0)
    out_ref[:, width:] = jnp.concatenate([tail_ref[...]] * len(pieces), axis=0)


def load_kernel(
    cnt_hbm, pk_hbm, pv_hbm, ck_hbm, cv_hbm,
    pk_ref, pv_ref, ck_ref, cv_ref, lim_ref, cnt_ref, cnt_sem, prompt_sems, old_sems,
):
    heads, pairs, _, _ = pk_ref.shape
    olds = ck_hbm.shape[0]
    requests = 2 * pairs
    mine = lax.axis_index("beam") // (BEAM_WIDTH // olds)
    copies = [pltpu.make_async_copy(cnt_hbm, cnt_ref, cnt_sem.at[0])]
    for k in range(heads):
        cols = pl.ds(k * HD, HD)
        for n, (src, dst) in enumerate(((pk_hbm, pk_ref), (pv_hbm, pv_ref))):
            for t in range(requests):
                copies.append(
                    pltpu.make_async_copy(
                        src.at[lax.rem(mine - t + requests, requests), :, cols],
                        dst.at[k, t // 2, :, pl.ds(t % 2 * HD, HD)],
                        prompt_sems.at[n, k, t],
                    )
                )
        for n, (src, dst) in enumerate(((ck_hbm, ck_ref), (cv_hbm, cv_ref))):
            for o in range(olds):
                copies.append(
                    pltpu.make_async_copy(
                        src.at[o, :, cols], dst.at[k, :, pl.ds(o * HD, HD)], old_sems.at[n, k, o]
                    )
                )
    for x in copies:
        x.start()
    for x in copies:
        x.wait()
    lane = lax.broadcasted_iota(jnp.int32, lim_ref.shape, 1)
    limit = jnp.zeros(lim_ref.shape, jnp.int32)
    for o in range(olds):
        limit = jnp.where(lane == o, cnt_ref[o] * BLOCK_LEN, limit)
    lim_ref[...] = limit


def attend_kernel(
    q_ref, pk_ref, pv_ref, ck_ref, cv_ref, lim_ref, out_ref, s_ref, p_ref, cs_ref, cp_ref
):
    count = q_ref.shape[0]
    pieces = [q_ref.at[r] for r in range(count)]
    outs = [out_ref.at[r] for r in range(count)]
    heads, pairs, length, _ = pk_ref.shape
    requests = 2 * pairs
    _, span, olds = ck_ref.shape
    olds = olds // HD
    total = q_ref.shape[2]
    beams = q_ref.shape[1] // requests
    block = count * beams
    stride = heads * QPK
    rows = QPK * block
    me = lax.axis_index("beam")

    parent = jnp.concatenate([x[:, total - STATS :].astype(f32)[:beams] for x in pieces], axis=0)
    parent = jnp.concatenate([parent] * QPK, axis=0).astype(jnp.int32) - me * olds
    column = parent[:, :1]
    local = (column >= 0) & (column < olds)
    limit = jnp.zeros((rows, 1), jnp.int32)
    for o in range(olds):
        limit = jnp.where(column == o, lim_ref[0:1, o : o + 1], limit)
    stats = [jnp.zeros((block, STATS), f32) for _ in range(requests)]
    lane = lax.broadcasted_iota(jnp.int32, (block, STATS), 1) % stride
    blank = jnp.zeros((rows, HD), bf16)
    kept = {}

    def scores(k):
        slot = k % 2
        tiles = [
            x[:, (k * QPK + i) * HD : (k * QPK + i + 1) * HD] for i in range(QPK) for x in pieces
        ]
        q = [
            jnp.concatenate([x[t * beams : (t + 1) * beams] for x in tiles], axis=0)
            for t in range(requests)
        ]
        for u in range(pairs):
            both = jnp.concatenate(
                [
                    jnp.concatenate([q[2 * u], blank], axis=1),
                    jnp.concatenate([blank, q[2 * u + 1]], axis=1),
                ],
                axis=0,
            )
            s_ref[slot, 2 * u * rows : 2 * (u + 1) * rows] = dot(both, pk_ref[k, u], 1, 1)
        chosen = jnp.concatenate([jnp.where(parent == o, q[0], blank) for o in range(olds)], axis=1)
        cs_ref[slot] = dot(chosen, ck_ref[k], 1, 1)

    def weigh(k):
        slot = k % 2
        p, top, den = soft(s_ref[slot])
        p_ref[slot] = p.astype(bf16)
        place = lax.broadcasted_iota(jnp.int32, (rows, span), 1)
        c, ctop, cden = soft(jnp.where(place < limit, cs_ref[slot], masked_score))
        cp_ref[slot] = c.astype(bf16)
        kept[k] = (top, den, ctop, cden)

    def values(k):
        slot = k % 2
        tops, dens, ctop, cden = kept.pop(k)
        nums = []
        for u in range(pairs):
            both = dot(p_ref[slot, 2 * u * rows : 2 * (u + 1) * rows], pv_ref[k, u], 1, 0)
            nums += [both[:rows, :HD], both[rows:, HD:]]
        every = dot(cp_ref[slot], cv_ref[k], 1, 0)
        cnum = every[:, :HD]
        for o in range(1, olds):
            cnum = jnp.where(parent == o, every[:, o * HD : (o + 1) * HD], cnum)
        done = []
        for t in range(requests):
            part = slice(t * rows, (t + 1) * rows)
            num, top, den = nums[t], tops[part], dens[part]
            if t == 0:
                both = jnp.where(local, jnp.maximum(top, ctop), top)
                a = jnp.exp(top - both)
                e = jnp.where(local, jnp.exp(jnp.where(local, ctop, both) - both), 0.0)
                num = a * num + e * cnum
                den = a * den + e * cden
                top = both
            done.append(num * (1.0 / den))
            lse = top + jnp.log(den)
            for i in range(QPK):
                stats[t] = jnp.where(
                    lane == k * QPK + i,
                    jnp.broadcast_to(
                        lse[i * block : (i + 1) * block], (block, STATS)
                    ),
                    stats[t],
                )
        for i in range(QPK):
            cols = slice((k * QPK + i) * HD, (k * QPK + i + 1) * HD)
            for r, out in enumerate(outs):
                first = i * block + r * beams
                out[:, cols] = jnp.concatenate(
                    [x[first : first + beams] for x in done], axis=0
                ).astype(bf16)

    for step in range(heads + 2):
        if step < heads:
            scores(step)
        if 0 <= step - 1 < heads:
            weigh(step - 1)
        if 0 <= step - 2:
            values(step - 2)
    for r, out in enumerate(outs):
        out[:, total - STATS :] = pack_stats(
            jnp.concatenate([x[r * beams : (r + 1) * beams] for x in stats], axis=0), stride
        )


def pack_stats(x, stride):
    hi = x.astype(bf16).astype(f32)
    mid = (x - hi).astype(bf16).astype(f32)
    which = lax.broadcasted_iota(jnp.int32, x.shape, 1) // stride
    return jnp.where(which == 0, hi, jnp.where(which == 1, mid, x - hi - mid)).astype(bf16)


def read_stats(x, stride):
    x = x.astype(f32)
    return x + pltpu.roll(x, STATS - stride, 1) + pltpu.roll(x, STATS - 2 * stride, 1)


def merge(a, b, out):
    total = a.shape[-1]
    count = (total - STATS) // HD
    la, lb = read_stats(a[:, total - STATS :], count), read_stats(b[:, total - STATS :], count)
    top = jnp.maximum(la, lb)
    wa, wb = jnp.exp(la - top), jnp.exp(lb - top)
    den = wa + wb
    wa = wa * (1.0 / den)
    wb = wb * (1.0 / den)
    for h in range(count):
        cols = slice(h * HD, (h + 1) * HD)
        out[:, cols] = (
            wa[:, h : h + 1] * a[:, cols].astype(f32) + wb[:, h : h + 1] * b[:, cols].astype(f32)
        ).astype(bf16)
    lse = top + jnp.log(den)
    lane = lax.broadcasted_iota(jnp.int32, lse.shape, 1)
    again = jnp.where(
        lane < count,
        lse,
        jnp.where(lane < 2 * count, pltpu.roll(lse, count, 1), pltpu.roll(lse, 2 * count, 1)),
    )
    out[:, total - STATS :] = pack_stats(again, count)


def core_kernel(kept0, kept2, came_ref, keep_ref, send_ref):
    merge(kept0.at[0], came_ref.at[0], keep_ref)
    merge(kept2.at[0], came_ref.at[1], send_ref)


def plane_kernel(kept_ref, came_ref, *refs):
    *outs, whole_ref = refs
    merge(kept_ref, came_ref, whole_ref)
    beams = outs[0].shape[0]
    for t, out in enumerate(outs):
        out[...] = whole_ref[t * beams : (t + 1) * beams]


def finish_kernel(own_ref, nv_ref, *refs):
    *parts, out_ref = refs
    beams, total = parts[0].shape
    heads = nv_ref.shape[1] // HD
    stride = heads * QPK
    own = own_ref[...]
    lses = [read_stats(x[:, total - STATS :], stride) for x in parts]
    top = functools.reduce(jnp.maximum, lses, own)
    ws = [jnp.exp(x - top) for x in lses]
    w_own = jnp.exp(own - top)
    inv = 1.0 / functools.reduce(jnp.add, ws, w_own)
    ws = [w * inv for w in ws]
    w_own = w_own * inv
    for k in range(heads):
        value = nv_ref[:, k * HD : (k + 1) * HD].astype(f32)
        for i in range(QPK):
            h = k * QPK + i
            acc = w_own[:, h : h + 1] * value
            for w, x in zip(ws, parts):
                acc = acc + w[:, h : h + 1] * x[:, h * HD : (h + 1) * HD].astype(f32)
            out_ref[:, h * HD : (h + 1) * HD] = acc.astype(bf16)


def project_kernel(near_ref, far_ref, w_ref, keep_ref, send_ref, rows_ref):
    pieces = (near_ref.at[0], far_ref.at[0], near_ref.at[1], far_ref.at[1])
    group = len(pieces)
    _, requests, beams, width = near_ref.shape
    me, side = lax.axis_index("beam"), lax.axis_index("head")
    mine, spot = me // group, me % group
    for r, x in enumerate(pieces):
        for t in range(requests):
            rows_ref[lax.rem(mine - t + requests, requests), spot ^ r] = x[t]
    a = jnp.concatenate(
        [rows_ref[z, j] for z in range(requests) for j in range(group)], axis=0
    )
    out = jnp.dot(a, w_ref[...], preferred_element_type=f32)
    half = requests * BEAM_WIDTH // 2

    @pl.when(side == 0)
    def _():
        keep_ref[...] = out[:half]
        send_ref[...] = out[half:]

    @pl.when(side != 0)
    def _():
        keep_ref[...] = out[half:]
        send_ref[...] = out[:half]


def whole_blocks(n, smem=(), far=()):
    places = [pltpu.SMEM if i in smem else pltpu.HBM if i in far else pltpu.VMEM for i in range(n)]
    return [pl.BlockSpec(memory_space=place) for place in places]


def call(kernel, name, out_shape, *args, smem=(), far=(), scratch=(), vmem=8, cost=None):
    many = isinstance(out_shape, tuple)
    return pl.pallas_call(
        kernel,
        out_shape=out_shape,
        in_specs=whole_blocks(len(args), smem, far),
        out_specs=tuple(whole_blocks(len(out_shape))) if many else whole_blocks(1)[0],
        scratch_shapes=list(scratch),
        compiler_params=pltpu.CompilerParams(vmem_limit_bytes=vmem * 1024 * 1024),
        cost_estimate=cost and pl.CostEstimate(flops=cost, bytes_accessed=cost, transcendentals=0),
        name=name,
    )(*(pltpu.with_memory_space_constraint(x, pltpu.HBM) if i in far else x for i, x in enumerate(args)))


def per_device(
    queries,
    new_keys,
    new_values,
    prompt_keys,
    prompt_values,
    private_keys,
    private_values,
    parents,
    block_counts,
    out_weight,
):
    beams, width = queries.shape
    group = BEAM_WIDTH // beams
    assert group == 4
    devices = lax.axis_size("beam")
    requests = prompt_keys.shape[0]
    sides = lax.axis_size("head")
    total = width + STATS

    def swap(x, with_bit):
        return lax.ppermute(x, "beam", [(i, i ^ with_bit) for i in range(devices)])

    def shift(x, by):
        return lax.ppermute(
            x, "beam", [(i, (i + by * group) % devices) for i in range(devices)]
        )

    rows = requests * beams
    heads = width // (QPK * HD)
    length, span = prompt_keys.shape[1], private_keys.shape[1]
    line = jax.ShapeDtypeStruct((rows, total), bf16)
    asked, own, parent_tail = call(
        prep_kernel,
        "prep",
        (
            jax.ShapeDtypeStruct((beams, width), bf16),
            jax.ShapeDtypeStruct((beams, STATS), f32),
            jax.ShapeDtypeStruct((beams, STATS), bf16),
        ),
        queries,
        new_keys,
        parents,
        far=(0, 1, 2),
        scratch=[
            pltpu.VMEM(new_keys.shape, bf16),
            pltpu.SMEM((beams,), jnp.int32),
            pltpu.SemaphoreType.DMA((3,)),
        ],
    )
    came = [shift(queries, t) for t in range(1, requests)]
    prompt = jax.ShapeDtypeStruct((heads, requests // 2, length, 2 * HD), bf16)
    private = jax.ShapeDtypeStruct((heads, span, beams * HD), bf16)
    caches = call(
        load_kernel,
        "load",
        (prompt, prompt, private, private, jax.ShapeDtypeStruct((8, STATS), jnp.int32)),
        block_counts,
        prompt_keys,
        prompt_values,
        private_keys,
        private_values,
        far=(0, 1, 2, 3, 4),
        scratch=[
            pltpu.SMEM((beams,), jnp.int32),
            pltpu.SemaphoreType.DMA((1,)),
            pltpu.SemaphoreType.DMA((2, heads, requests)),
            pltpu.SemaphoreType.DMA((2, heads, beams)),
        ],
        vmem=10,
        cost=12 * 2**20,
    )
    *came, _ = lax.optimization_barrier((*came, caches[-1]))
    asked = call(line_kernel, "line", line, parent_tail, asked, *came)

    def attend(asked, name):
        many = asked.shape[0] * beams * QPK
        return call(
            attend_kernel,
            name,
            jax.ShapeDtypeStruct(asked.shape, bf16),
            asked,
            *caches,
            scratch=[
                pltpu.VMEM((2, requests * many, length), f32),
                pltpu.VMEM((2, requests * many, length), bf16),
                pltpu.VMEM((2, many, span), f32),
                pltpu.VMEM((2, many, span), bf16),
            ],
            vmem=24,
        )

    other = swap(asked, 2)
    keep0 = attend(asked[None], "attend_own")
    other, keep0 = lax.optimization_barrier((other, keep0))
    far = swap(jnp.stack([asked, other]), 1)
    keep2 = attend(other[None], "attend_side")
    far, keep2 = lax.optimization_barrier((far, keep2))
    send = attend(far, "attend_far")
    keep, send = call(
        core_kernel, "core_merge", (line, line), keep0, keep2, swap(send, 1)
    )
    piece = jax.ShapeDtypeStruct((beams, total), bf16)
    parts = call(
        plane_kernel,
        "plane_merge",
        (piece,) * requests,
        keep,
        swap(send, 2),
        scratch=[pltpu.VMEM((rows, total), bf16)],
    )
    parts = [shift(x, -t) if t else x for t, x in enumerate(parts)]
    attended = call(
        finish_kernel,
        "finish",
        jax.ShapeDtypeStruct((beams, width), bf16),
        own,
        new_values,
        *parts,
    )
    if sides == 2:
        near = jnp.stack([shift(attended, t) if t else attended for t in range(requests)])
        near = jnp.stack([near, swap(near, 2)])
        shape = jax.ShapeDtypeStruct(
            (requests * BEAM_WIDTH // 2, out_weight.shape[1]), f32
        )
        keep, send = call(
            project_kernel,
            "project",
            (shape, shape),
            near,
            swap(near, 1),
            out_weight,
            scratch=[pltpu.VMEM((requests, group, beams, width), bf16)],
            vmem=16,
        )
        return (keep + lax.ppermute(send, "head", [(0, 1), (1, 0)])).astype(bf16)
    rows = lax.all_gather(attended, "beam", axis=0, tiled=True)
    products = jnp.dot(rows, out_weight, preferred_element_type=f32)
    return lax.psum_scatter(products, "head", scatter_dimension=0, tiled=True).astype(bf16)


def solution(mesh):
    placed = (
        P("beam", "head"),
        P("beam", "head"),
        P("beam", "head"),
        P(None, "beam", "head"),
        P(None, "beam", "head"),
        P("beam", None, "head"),
        P("beam", None, "head"),
        P("beam"),
        P("beam"),
        P("head", "beam"),
    )
    return jax.shard_map(
        per_device, mesh=mesh, in_specs=placed, out_specs=P("head", "beam"), check_vma=False
    )
```

time: 627 us -> 57.1 us (0.09)
  blocking collectives: 427 us -> 0 us
  local copies, waits for them, and re-layouts: 60.2 us -> 0.01 us
  waiting for transfers between devices: 56.5 us -> 24.5 us
  starting transfers between devices: 44 us -> 19.1 us
  matrix products: 20.6 us -> 0 us
  between operations: 14.5 us -> 0.17 us
  Pallas kernels: 0 us -> 12.1 us
    unnamed x1 -> x0, blocking collectives: 171 us -> none
    all_gather x2 -> x0, blocking collectives: 171 us -> none  [the longest x1 152 us: per_device(): everyone = lax.all_gather(queries, 'beam', axis=0, tiled=True)]
    pmax x1 -> x0, blocking collectives: 84.6 us -> none  [per_device(): prompt_max = lax.pmax(local_max, 'beam')]
    gather x21 -> x0, local copies, waits for them, and re-layouts: 53.7 us -> none  [the longest x7 25.4 us: per_device(): jnp.take(source[1], picked_rows, axis=0)]
    ppermute x18 -> x16, starting transfers between devices: 44 us -> 19.1 us  [the longest x9 12.1 us: shift(): lax.ppermute(x, 'beam', [(i, (i + by * group) % devices) for i in range(d...]
    ppermute x18 -> x16, waiting for transfers between devices: 46.8 us -> 24.5 us  [the longest x6 12.3 us: swap(): return lax.ppermute(x, 'beam', [(i, i ^ with_bit) for i in range(devices)])]
    dot_general x6 -> x0, matrix products: 20.6 us -> none  [the longest x1 7.46 us: suffix_part(): jnp.einsum('bkqd,bpkd->bkqp', query_head_count, key_heads, preferred_elem...]
    pallas_call x0 -> x10, Pallas kernels: none -> 12.1 us  [call(): pl.pallas_call(kernel, out_shape=out_shape, in_specs=whole_blocks(len(arg...]
  transfers between devices with their start and end apart: 20 -> 16, of which waited for: 2 -> 11; matrix products, arithmetic and copies ran while one was open for 11% -> 0% of each run, Pallas kernels for 0% -> 14%
where the time goes in v1:
time: 57.1 us; the launch traced here: 56.9 us
  waiting for transfers between devices  24.5 us (43%)
  starting transfers between devices  19.1 us (33%)
  Pallas kernels  12.1 us (21%)
  other arithmetic  1.07 us (2%)
    ppermute x6, waiting for transfers between devices, swap(): return lax.ppermute(x, 'beam', [(i, i ^ with_bit) for i in range(devices)])  12.3 us
    ppermute x9, starting transfers between devices, shift(): lax.ppermute(x, 'beam', [(i, (i + by * group) % devices) for i in range(d...  12.1 us
    pallas_call x10, Pallas kernels, call(): pl.pallas_call(kernel, out_shape=out_shape, in_specs=whole_blocks(len(arg...  12.1 us
    ppermute x9, waiting for transfers between devices, shift(): lax.ppermute(x, 'beam', [(i, (i + by * group) % devices) for i in range(d...  9.46 us
    ppermute x6, starting transfers between devices, swap(): return lax.ppermute(x, 'beam', [(i, i ^ with_bit) for i in range(devices)])  5.38 us
    ppermute x1, waiting for transfers between devices, per_device(): return (keep + lax.ppermute(send, 'head', [(0, 1), (1, 0)])).astype(bf16)  2.74 us
    ppermute x1, starting transfers between devices, per_device(): return (keep + lax.ppermute(send, 'head', [(0, 1), (1, 0)])).astype(bf16)  1.59 us
  transfers between devices with their start and end apart: 16, of which 11 were waited for; matrix products, arithmetic and copies ran while one was open for 0% of the time, Pallas kernels for 14%

profile of v1, /device:TPU:0, one launch (start us, length us, event | category | flops | bytes accessed | tf_op | source)
XLA Modules:
  0.0 56.9 jit_solution(8248339072991909003)
XLA Ops:
  0.0 3.0 %collective-permute-start = (bf16[4,4096]{1,0:T(4,128)(2,1)}, bf16[4,4096]{1,0:T(4,128)(2,1)S(1)}, u32[]{:S(2)}, u32[]{:S(2)}) collective-permute-start(bf16[4,4096]{1,0:T(4,128)(2,1)} %q_hbm.1), channel_id=1, source_target_pairs={{0,8},{2,10},{4,12},{6,14},{8,16},{10,18},{12,20},{14,22},{16,24},... | collective-permute-start | bytes 98312 | tf_op jit(solution)/shard_map/ppermute | solution.py:356
  3.0 2.0 %collective-permute-start.2 = (bf16[4,4096]{1,0:T(4,128)(2,1)}, bf16[4,4096]{1,0:T(4,128)(2,1)S(1)}, u32[]{:S(2)}, u32[]{:S(2)}) collective-permute-start(bf16[4,4096]{1,0:T(4,128)(2,1)} %q_hbm.1), channel_id=1, source_target_pairs={{0,24},{2,26},{4,28},{6,30},{8,0},{10,2},{12,4},{14,6},{16,8},{18,... | collective-permute-start | bytes 98312 | tf_op jit(solution)/shard_map/ppermute | solution.py:356
  5.1 1.0 %collective-permute-start.1 = (bf16[4,4096]{1,0:T(4,128)(2,1)}, bf16[4,4096]{1,0:T(4,128)(2,1)S(1)}, u32[]{:S(2)}, u32[]{:S(2)}) collective-permute-start(bf16[4,4096]{1,0:T(4,128)(2,1)} %q_hbm.1), channel_id=1, source_target_pairs={{0,16},{2,18},{4,20},{6,22},{8,24},{10,26},{12,28},{14,30},{16,0},... | collective-permute-start | bytes 98312 | tf_op jit(solution)/shard_map/ppermute | solution.py:356
  6.1 0.9 %prep.1 = (bf16[4,4096]{1,0:T(4,128)(2,1)S(1)}, f32[4,128]{1,0:T(4,128)S(1)}, bf16[4,128]{1,0:T(4,128)(2,1)S(1)}) custom-call(bf16[4,4096]{1,0:T(4,128)(2,1)} %q_hbm.1, bf16[4,512]{1,0:T(4,128)(2,1)} %nk_hbm.1, s32[4]{0:T(128)} %par_hbm.1), custom_call_target="tpu_custom_call" | custom-call | tf_op jit(solution)/shard_map/prep/pallas_call | solution.py:320
  7.0 3.6 %load.1 = (bf16[4,2,256,256]{3,2,1,0:T(8,128)(2,1)S(1)}, bf16[4,2,256,256]{3,2,1,0:T(8,128)(2,1)S(1)}, bf16[4,512,512]{2,1,0:T(8,128)(2,1)S(1)}, bf16[4,512,512]{2,1,0:T(8,128)(2,1)S(1)}, s32[8,128]{1,0:T(8,128)S(1)}) custom-call(s32[4]{0:T(128)} %cnt_hbm.1, bf16[4,256,512]{2,1,0:T(8,128)(2,1)} %pk_hbm.1, bf16[4,256,512]{2,1,0:T(8,128)(2,1)} %pv_hbm.1, ...), custom_call_target="tpu_custom_call" | custom-call | flops 12582912 | bytes 12582912 | tf_op jit(solution)/shard_map/load/pallas_call | solution.py:320
  10.7 0.0 collective-permute-done.refs_1_
  10.7 0.0 collective-permute-done.2.refs_3_
  10.7 0.0 collective-permute-done.1.refs_2_
  10.7 1.6 %collective-permute-start.3 = (bf16[16,4224]{1,0:T(8,128)(2,1)S(1)}, bf16[16,4224]{1,0:T(8,128)(2,1)S(1)}, u32[]{:S(2)}, u32[]{:S(2)}) collective-permute-start(bf16[16,4224]{1,0:T(8,128)(2,1)S(1)} %line.1), channel_id=1, source_target_pairs={{0,4},{2,6},{4,0},{6,2},{8,12},{10,14},{12,8},{14,10},{16,20},{18,... | collective-permute-start | bytes 405512 | tf_op jit(solution)/shard_map/ppermute | solution.py:353
  12.3 1.6 %attend_own.1.kept0 = bf16[1,16,4224]{2,1,0:T(8,128)(2,1)S(1)} custom-call(bf16[1,16,4224]{2,1,0:T(8,128)(2,1)S(1)} %bitcast.9, bf16[4,2,256,256]{3,2,1,0:T(8,128)(2,1)S(1)} %get-tuple-element.35.pk_ref, bf16[4,2,256,256]{3,2,1,0:T(8,128)(2,1)S(1)} %get-tuple-element.36.pv_ref, bf16[4,512,512]{2,1,0:T(8,128)(2,1)S(1)} %get-tuple-element.37.ck_ref, ...), custom_call_target="tpu_custom_call" | custom-call | tf_op jit(solution)/shard_map/attend_own/pallas_call | solution.py:320
  13.9 1.9 %collective-permute-done.3 = bf16[16,4224]{1,0:T(8,128)(2,1)S(1)} collective-permute-done((bf16[16,4224]{1,0:T(8,128)(2,1)S(1)}, bf16[16,4224]{1,0:T(8,128)(2,1)S(1)}, u32[]{:S(2)}, u32[]{:S(2)}) %collective-permute-start.3) | collective-permute-done | bytes 135200 | tf_op jit(solution)/shard_map/ppermute | solution.py:353
  15.9 0.1 collective-permute-start.4
  15.9 1.6 %attend_side.1.kept2 = bf16[1,16,4224]{2,1,0:T(8,128)(2,1)S(1)} custom-call(bf16[1,16,4224]{2,1,0:T(8,128)(2,1)S(1)} %bitcast.12, bf16[4,2,256,256]{3,2,1,0:T(8,128)(2,1)S(1)} %get-tuple-element.35.pk_ref, bf16[4,2,256,256]{3,2,1,0:T(8,128)(2,1)S(1)} %get-tuple-element.36.pv_ref, bf16[4,512,512]{2,1,0:T(8,128)(2,1)S(1)} %get-tuple-element.37.ck_ref, ...), custom_call_target="tpu_custom_call" | custom-call | tf_op jit(solution)/shard_map/attend_side/pallas_call | solution.py:320
  17.6 0.0 copy-start.1
  17.6 0.0 collective-permute-done.4.q_ref
  17.6 0.0 copy-start
  17.6 1.9 %attend_far.1 = bf16[2,16,4224]{2,1,0:T(8,128)(2,1)S(1)} custom-call(bf16[2,16,4224]{2,1,0:T(8,128)(2,1)S(1)} %collective-permute-done.4.q_ref, bf16[4,2,256,256]{3,2,1,0:T(8,128)(2,1)S(1)} %get-tuple-element.35.pk_ref, bf16[4,2,256,256]{3,2,1,0:T(8,128)(2,1)S(1)} %get-tuple-element.36.pv_ref, bf16[4,512,512]{2,1,0:T(8,128)(2,1)S(1)} %get-tuple-element.37.ck_ref, ...), custom_call_target="tpu_custom_call" | custom-call | tf_op jit(solution)/shard_map/attend_far/pallas_call | solution.py:320
  19.5 0.6 collective-permute-start.5
  20.1 1.2 %collective-permute-done.5.came_ref = bf16[2,16,4224]{2,1,0:T(8,128)(2,1)S(1)} collective-permute-done((bf16[2,16,4224]{2,1,0:T(8,128)(2,1)S(1)}, bf16[2,16,4224]{2,1,0:T(8,128)(2,1)S(1)}, u32[]{:S(2)}, u32[]{:S(2)}) %collective-permute-start.5) | collective-permute-done | bytes 270368 | tf_op jit(solution)/shard_map/ppermute | solution.py:353
  21.3 0.7 %core_merge.1 = (bf16[16,4224]{1,0:T(8,128)(2,1)S(1)}, bf16[16,4224]{1,0:T(8,128)(2,1)S(1)}) custom-call(bf16[1,16,4224]{2,1,0:T(8,128)(2,1)S(1)} %attend_own.1.kept0, bf16[1,16,4224]{2,1,0:T(8,128)(2,1)S(1)} %attend_side.1.kept2, bf16[2,16,4224]{2,1,0:T(8,128)(2,1)S(1)} %collective-permute-done.5.came_ref), custom_call_target="tpu_custom_call" | custom-call | tf_op jit(solution)/shard_map/core_merge/pallas_call | solution.py:320
  21.9 1.6 %collective-permute-start.6 = (bf16[16,4224]{1,0:T(8,128)(2,1)S(1)}, bf16[16,4224]{1,0:T(8,128)(2,1)S(1)}, u32[]{:S(2)}, u32[]{:S(2)}) collective-permute-start(bf16[16,4224]{1,0:T(8,128)(2,1)S(1)} %get-tuple-element.44), channel_id=1, source_target_pairs={{0,4},{2,6},{4,0},{6,2},{8,12},{10,14},{12,8},{14,10},{16,20},{18,... | collective-permute-start | bytes 405512 | tf_op jit(solution)/shard_map/ppermute | solution.py:353
  23.5 4.4 %collective-permute-done.6.came_ref = bf16[16,4224]{1,0:T(8,128)(2,1)S(1)} collective-permute-done((bf16[16,4224]{1,0:T(8,128)(2,1)S(1)}, bf16[16,4224]{1,0:T(8,128)(2,1)S(1)}, u32[]{:S(2)}, u32[]{:S(2)}) %collective-permute-start.6) | collective-permute-done | bytes 135200 | tf_op jit(solution)/shard_map/ppermute | solution.py:353
  27.8 0.4 plane_merge.1
  28.2 1.7 %collective-permute-start.7 = (bf16[4,4224]{1,0:T(4,128)(2,1)S(1)}, bf16[4,4224]{1,0:T(4,128)(2,1)S(1)}, u32[]{:S(2)}, u32[]{:S(2)}) collective-permute-start(bf16[4,4224]{1,0:T(4,128)(2,1)S(1)} %get-tuple-element.46), channel_id=1, source_target_pairs={{0,24},{2,26},{4,28},{6,30},{8,0},{10,2},{12,4},{14,6},{16,8},{18,... | collective-permute-start | bytes 101384 | tf_op jit(solution)/shard_map/ppermute | solution.py:356
  29.9 1.4 %collective-permute-start.8 = (bf16[4,4224]{1,0:T(4,128)(2,1)S(1)}, bf16[4,4224]{1,0:T(4,128)(2,1)S(1)}, u32[]{:S(2)}, u32[]{:S(2)}) collective-permute-start(bf16[4,4224]{1,0:T(4,128)(2,1)S(1)} %get-tuple-element.47), channel_id=1, source_target_pairs={{0,16},{2,18},{4,20},{6,22},{8,24},{10,26},{12,28},{14,30},{16,0},... | collective-permute-start | bytes 101384 | tf_op jit(solution)/shard_map/ppermute | solution.py:356
  31.3 0.9 %collective-permute-start.9 = (bf16[4,4224]{1,0:T(4,128)(2,1)S(1)}, bf16[4,4224]{1,0:T(4,128)(2,1)S(1)}, u32[]{:S(2)}, u32[]{:S(2)}) collective-permute-start(bf16[4,4224]{1,0:T(4,128)(2,1)S(1)} %get-tuple-element.48), channel_id=1, source_target_pairs={{0,8},{2,10},{4,12},{6,14},{8,16},{10,18},{12,20},{14,22},{16,24},... | collective-permute-start | bytes 101384 | tf_op jit(solution)/shard_map/ppermute | solution.py:356
  32.2 0.0 collective-permute-done.7.refs_1_
  32.2 3.1 %collective-permute-done.8.refs_2_ = bf16[4,4224]{1,0:T(4,128)(2,1)S(1)} collective-permute-done((bf16[4,4224]{1,0:T(4,128)(2,1)S(1)}, bf16[4,4224]{1,0:T(4,128)(2,1)S(1)}, u32[]{:S(2)}, u32[]{:S(2)}) %collective-permute-start.8) | collective-permute-done | bytes 33824 | tf_op jit(solution)/shard_map/ppermute | solution.py:356
  35.3 1.8 %collective-permute-done.9.refs_3_ = bf16[4,4224]{1,0:T(4,128)(2,1)S(1)} collective-permute-done((bf16[4,4224]{1,0:T(4,128)(2,1)S(1)}, bf16[4,4224]{1,0:T(4,128)(2,1)S(1)}, u32[]{:S(2)}, u32[]{:S(2)}) %collective-permute-start.9) | collective-permute-done | bytes 33824 | tf_op jit(solution)/shard_map/ppermute | solution.py:356
  37.1 0.0 copy-done.1
  37.1 0.4 finish.1
  37.5 0.1 collective-permute-start.12
  37.5 0.5 collective-permute-start.11
  38.1 1.5 %collective-permute-start.10 = (bf16[4,4096]{1,0:T(4,128)(2,1)S(1)}, bf16[4,4096]{1,0:T(4,128)(2,1)S(1)}, u32[]{:S(2)}, u32[]{:S(2)}) collective-permute-start(bf16[4,4096]{1,0:T(4,128)(2,1)S(1)} %finish.1), channel_id=1, source_target_pairs={{0,8},{2,10},{4,12},{6,14},{8,16},{10,18},{12,20},{14,22},{16,24},... | collective-permute-start | bytes 98312 | tf_op jit(solution)/shard_map/ppermute | solution.py:356
  39.5 1.9 %collective-permute-done.12 = bf16[4,4096]{1,0:T(4,128)(2,1)S(1)} collective-permute-done((bf16[4,4096]{1,0:T(4,128)(2,1)S(1)}, bf16[4,4096]{1,0:T(4,128)(2,1)S(1)}, u32[]{:S(2)}, u32[]{:S(2)}) %collective-permute-start.12) | collective-permute-done | bytes 32800 | tf_op jit(solution)/shard_map/ppermute | solution.py:356
  41.4 1.0 %collective-permute-done.11 = bf16[4,4096]{1,0:T(4,128)(2,1)S(1)} collective-permute-done((bf16[4,4096]{1,0:T(4,128)(2,1)S(1)}, bf16[4,4096]{1,0:T(4,128)(2,1)S(1)}, u32[]{:S(2)}, u32[]{:S(2)}) %collective-permute-start.11) | collective-permute-done | bytes 32800 | tf_op jit(solution)/shard_map/ppermute | solution.py:356
  42.4 1.7 %collective-permute-done.10 = bf16[4,4096]{1,0:T(4,128)(2,1)S(1)} collective-permute-done((bf16[4,4096]{1,0:T(4,128)(2,1)S(1)}, bf16[4,4096]{1,0:T(4,128)(2,1)S(1)}, u32[]{:S(2)}, u32[]{:S(2)}) %collective-permute-start.10) | collective-permute-done | bytes 32800 | tf_op jit(solution)/shard_map/ppermute | solution.py:356
  44.1 0.1 pad_maximum_fusion.2
  44.3 1.6 %collective-permute-start.13 = (bf16[4,4,4096]{2,1,0:T(4,128)(2,1)S(1)}, bf16[4,4,4096]{2,1,0:T(4,128)(2,1)S(1)}, u32[]{:S(2)}, u32[]{:S(2)}) collective-permute-start(bf16[4,4,4096]{2,1,0:T(4,128)(2,1)S(1)} %pad_maximum_fusion.2), channel_id=1, source_target_pairs={{0,4},{2,6},{4,0},{6,2},{8,12},{10,14},{12,8},{14,10},{16,20},{18,... | collective-permute-start | bytes 393224 | tf_op jit(solution)/shard_map/ppermute | solution.py:353
  45.8 0.1 fusion
  45.9 3.4 %collective-permute-done.13 = bf16[4,4,4096]{2,1,0:T(4,128)(2,1)S(1)} collective-permute-done((bf16[4,4,4096]{2,1,0:T(4,128)(2,1)S(1)}, bf16[4,4,4096]{2,1,0:T(4,128)(2,1)S(1)}, u32[]{:S(2)}, u32[]{:S(2)}) %collective-permute-start.13) | collective-permute-done | bytes 131104 | tf_op jit(solution)/shard_map/ppermute | solution.py:353
  49.3 0.2 pad_maximum_fusion.1.near_ref
  49.5 0.1 collective-permute-start.14
  49.6 1.5 %collective-permute-done.14.far_ref = bf16[2,4,4,4096]{3,2,1,0:T(4,128)(2,1)S(1)} collective-permute-done((bf16[2,4,4,4096]{3,2,1,0:T(4,128)(2,1)S(1)}, bf16[2,4,4,4096]{3,2,1,0:T(4,128)(2,1)S(1)}, u32[]{:S(2)}, u32[]{:S(2)}) %collective-permute-start.14) | collective-permute-done | bytes 262176 | tf_op jit(solution)/shard_map/ppermute | solution.py:353
  51.1 0.9 %project.1 = (f32[32,512]{1,0:T(8,128)S(1)}, f32[32,512]{1,0:T(8,128)S(1)}) custom-call(bf16[2,4,4,4096]{3,2,1,0:T(4,128)(2,1)S(1)} %pad_maximum_fusion.1.near_ref, bf16[2,4,4,4096]{3,2,1,0:T(4,128)(2,1)S(1)} %collective-permute-done.14.far_ref, bf16[4096,512]{1,0:T(8,128)(2,1)S(1)} %copy-done), custom_call_target="tpu_custom_call" | custom-call | tf_op jit(solution)/shard_map/project/pallas_call | solution.py:320
  52.0 1.6 %collective-permute-start.15 = (f32[32,512]{1,0:T(8,128)S(1)}, f32[32,512]{1,0:T(8,128)S(1)}, u32[]{:S(2)}, u32[]{:S(2)}) collective-permute-start(f32[32,512]{1,0:T(8,128)S(1)} %get-tuple-element.50), channel_id=1, source_target_pairs={{0,1},{1,0},{2,3},{3,2},{4,5},{5,4},{6,7},{7,6},{8,9},{9,8},{10,11... | collective-permute-start | bytes 196616 | tf_op jit(solution)/shard_map/ppermute | solution.py:468
  53.6 2.7 %collective-permute-done.15 = f32[32,512]{1,0:T(8,128)S(1)} collective-permute-done((f32[32,512]{1,0:T(8,128)S(1)}, f32[32,512]{1,0:T(8,128)S(1)}, u32[]{:S(2)}, u32[]{:S(2)}) %collective-permute-start.15) | collective-permute-done | bytes 65568 | tf_op jit(solution)/shard_map/ppermute | solution.py:468
  56.3 0.6 %add_convert_fusion = bf16[32,512]{1,0:T(8,128)(2,1)} fusion(f32[32,512]{1,0:T(8,128)S(1)} %get-tuple-element.49, f32[32,512]{1,0:T(8,128)S(1)} %collective-permute-done.15), kind=kLoop, calls=%fused_computation.3 | loop fusion | flops 32768 | bytes 163840 | tf_op jit(solution)/shard_map/convert_element_type | solution.py:468
  (3 shorter events, 0.1 us)
Async XLA Ops:
  0.0 10.7 %collective-permute-start = (bf16[4,4096]{1,0:T(4,128)(2,1)}, bf16[4,4096]{1,0:T(4,128)(2,1)S(1)}, u32[]{:S(2)}, u32[]{:S(2)}) collective-permute-start(bf16[4,4096]{1,0:T(4,128)(2,1)} %q_hbm.1), channel_id=1, source_target_pairs={{0,8},{2,10},{4,12},{6,14},{8,16},{10,18},{12,20},{14,22},{16,24},... | collective-permute-start | bytes 98312 | tf_op jit(solution)/shard_map/ppermute | solution.py:356
  3.0 7.7 %collective-permute-start.2 = (bf16[4,4096]{1,0:T(4,128)(2,1)}, bf16[4,4096]{1,0:T(4,128)(2,1)S(1)}, u32[]{:S(2)}, u32[]{:S(2)}) collective-permute-start(bf16[4,4096]{1,0:T(4,128)(2,1)} %q_hbm.1), channel_id=1, source_target_pairs={{0,24},{2,26},{4,28},{6,30},{8,0},{10,2},{12,4},{14,6},{16,8},{18,... | collective-permute-start | bytes 98312 | tf_op jit(solution)/shard_map/ppermute | solution.py:356
  5.1 5.6 %collective-permute-start.1 = (bf16[4,4096]{1,0:T(4,128)(2,1)}, bf16[4,4096]{1,0:T(4,128)(2,1)S(1)}, u32[]{:S(2)}, u32[]{:S(2)}) collective-permute-start(bf16[4,4096]{1,0:T(4,128)(2,1)} %q_hbm.1), channel_id=1, source_target_pairs={{0,16},{2,18},{4,20},{6,22},{8,24},{10,26},{12,28},{14,30},{16,0},... | collective-permute-start | bytes 98312 | tf_op jit(solution)/shard_map/ppermute | solution.py:356
  10.7 5.1 %collective-permute-start.3 = (bf16[16,4224]{1,0:T(8,128)(2,1)S(1)}, bf16[16,4224]{1,0:T(8,128)(2,1)S(1)}, u32[]{:S(2)}, u32[]{:S(2)}) collective-permute-start(bf16[16,4224]{1,0:T(8,128)(2,1)S(1)} %line.1), channel_id=1, source_target_pairs={{0,4},{2,6},{4,0},{6,2},{8,12},{10,14},{12,8},{14,10},{16,20},{18,... | collective-permute-start | bytes 405512 | tf_op jit(solution)/shard_map/ppermute | solution.py:353
  15.9 1.7 %collective-permute-start.4 = (bf16[2,16,4224]{2,1,0:T(8,128)(2,1)S(1)}, bf16[2,16,4224]{2,1,0:T(8,128)(2,1)S(1)}, u32[]{:S(2)}, u32[]{:S(2)}) collective-permute-start(bf16[2,16,4224]{2,1,0:T(8,128)(2,1)S(1)} %pad_maximum_fusion), channel_id=1, source_target_pairs={{0,2},{2,0},{4,6},{6,4},{8,10},{10,8},{12,14},{14,12},{16,18},{18,... | collective-permute-start | bytes 811016 | tf_op jit(solution)/shard_map/ppermute | solution.py:353
  17.6 19.5 %copy-start.1 = (bf16[4,512]{1,0:T(4,128)(2,1)S(1)}, bf16[4,512]{1,0:T(4,128)(2,1)}, u32[]{:S(2)}) copy-start(bf16[4,512]{1,0:T(4,128)(2,1)} %nv_ref.1) | copy-start | bytes 12292
  17.6 33.5 %copy-start = (bf16[4096,512]{1,0:T(8,128)(2,1)S(1)}, bf16[4096,512]{1,0:T(8,128)(2,1)}, u32[]{:S(2)}) copy-start(bf16[4096,512]{1,0:T(8,128)(2,1)} %w_ref.1) | copy-start | bytes 12582916
  19.5 1.7 %collective-permute-start.5 = (bf16[2,16,4224]{2,1,0:T(8,128)(2,1)S(1)}, bf16[2,16,4224]{2,1,0:T(8,128)(2,1)S(1)}, u32[]{:S(2)}, u32[]{:S(2)}) collective-permute-start(bf16[2,16,4224]{2,1,0:T(8,128)(2,1)S(1)} %attend_far.1), channel_id=1, source_target_pairs={{0,2},{2,0},{4,6},{6,4},{8,10},{10,8},{12,14},{14,12},{16,18},{18,... | collective-permute-start | bytes 811016 | tf_op jit(solution)/shard_map/ppermute | solution.py:353
  21.9 5.9 %collective-permute-start.6 = (bf16[16,4224]{1,0:T(8,128)(2,1)S(1)}, bf16[16,4224]{1,0:T(8,128)(2,1)S(1)}, u32[]{:S(2)}, u32[]{:S(2)}) collective-permute-start(bf16[16,4224]{1,0:T(8,128)(2,1)S(1)} %get-tuple-element.44), channel_id=1, source_target_pairs={{0,4},{2,6},{4,0},{6,2},{8,12},{10,14},{12,8},{14,10},{16,20},{18,... | collective-permute-start | bytes 405512 | tf_op jit(solution)/shard_map/ppermute | solution.py:353
  28.2 4.0 %collective-permute-start.7 = (bf16[4,4224]{1,0:T(4,128)(2,1)S(1)}, bf16[4,4224]{1,0:T(4,128)(2,1)S(1)}, u32[]{:S(2)}, u32[]{:S(2)}) collective-permute-start(bf16[4,4224]{1,0:T(4,128)(2,1)S(1)} %get-tuple-element.46), channel_id=1, source_target_pairs={{0,24},{2,26},{4,28},{6,30},{8,0},{10,2},{12,4},{14,6},{16,8},{18,... | collective-permute-start | bytes 101384 | tf_op jit(solution)/shard_map/ppermute | solution.py:356
  29.9 5.4 %collective-permute-start.8 = (bf16[4,4224]{1,0:T(4,128)(2,1)S(1)}, bf16[4,4224]{1,0:T(4,128)(2,1)S(1)}, u32[]{:S(2)}, u32[]{:S(2)}) collective-permute-start(bf16[4,4224]{1,0:T(4,128)(2,1)S(1)} %get-tuple-element.47), channel_id=1, source_target_pairs={{0,16},{2,18},{4,20},{6,22},{8,24},{10,26},{12,28},{14,30},{16,0},... | collective-permute-start | bytes 101384 | tf_op jit(solution)/shard_map/ppermute | solution.py:356
  31.3 5.8 %collective-permute-start.9 = (bf16[4,4224]{1,0:T(4,128)(2,1)S(1)}, bf16[4,4224]{1,0:T(4,128)(2,1)S(1)}, u32[]{:S(2)}, u32[]{:S(2)}) collective-permute-start(bf16[4,4224]{1,0:T(4,128)(2,1)S(1)} %get-tuple-element.48), channel_id=1, source_target_pairs={{0,8},{2,10},{4,12},{6,14},{8,16},{10,18},{12,20},{14,22},{16,24},... | collective-permute-start | bytes 101384 | tf_op jit(solution)/shard_map/ppermute | solution.py:356
  37.5 4.0 %collective-permute-start.12 = (bf16[4,4096]{1,0:T(4,128)(2,1)S(1)}, bf16[4,4096]{1,0:T(4,128)(2,1)S(1)}, u32[]{:S(2)}, u32[]{:S(2)}) collective-permute-start(bf16[4,4096]{1,0:T(4,128)(2,1)S(1)} %finish.1), channel_id=1, source_target_pairs={{0,24},{2,26},{4,28},{6,30},{8,0},{10,2},{12,4},{14,6},{16,8},{18,... | collective-permute-start | bytes 98312 | tf_op jit(solution)/shard_map/ppermute | solution.py:356
  37.5 4.9 %collective-permute-start.11 = (bf16[4,4096]{1,0:T(4,128)(2,1)S(1)}, bf16[4,4096]{1,0:T(4,128)(2,1)S(1)}, u32[]{:S(2)}, u32[]{:S(2)}) collective-permute-start(bf16[4,4096]{1,0:T(4,128)(2,1)S(1)} %finish.1), channel_id=1, source_target_pairs={{0,16},{2,18},{4,20},{6,22},{8,24},{10,26},{12,28},{14,30},{16,0},... | collective-permute-start | bytes 98312 | tf_op jit(solution)/shard_map/ppermute | solution.py:356
  38.1 6.1 %collective-permute-start.10 = (bf16[4,4096]{1,0:T(4,128)(2,1)S(1)}, bf16[4,4096]{1,0:T(4,128)(2,1)S(1)}, u32[]{:S(2)}, u32[]{:S(2)}) collective-permute-start(bf16[4,4096]{1,0:T(4,128)(2,1)S(1)} %finish.1), channel_id=1, source_target_pairs={{0,8},{2,10},{4,12},{6,14},{8,16},{10,18},{12,20},{14,22},{16,24},... | collective-permute-start | bytes 98312 | tf_op jit(solution)/shard_map/ppermute | solution.py:356
  44.3 5.0 %collective-permute-start.13 = (bf16[4,4,4096]{2,1,0:T(4,128)(2,1)S(1)}, bf16[4,4,4096]{2,1,0:T(4,128)(2,1)S(1)}, u32[]{:S(2)}, u32[]{:S(2)}) collective-permute-start(bf16[4,4,4096]{2,1,0:T(4,128)(2,1)S(1)} %pad_maximum_fusion.2), channel_id=1, source_target_pairs={{0,4},{2,6},{4,0},{6,2},{8,12},{10,14},{12,8},{14,10},{16,20},{18,... | collective-permute-start | bytes 393224 | tf_op jit(solution)/shard_map/ppermute | solution.py:353
  49.5 1.6 %collective-permute-start.14 = (bf16[2,4,4,4096]{3,2,1,0:T(4,128)(2,1)S(1)}, bf16[2,4,4,4096]{3,2,1,0:T(4,128)(2,1)S(1)}, u32[]{:S(2)}, u32[]{:S(2)}) collective-permute-start(bf16[2,4,4,4096]{3,2,1,0:T(4,128)(2,1)S(1)} %pad_maximum_fusion.1.near_ref), channel_id=1, source_target_pairs={{0,2},{2,0},{4,6},{6,4},{8,10},{10,8},{12,14},{14,12},{16,18},{18,... | collective-permute-start | bytes 786440 | tf_op jit(solution)/shard_map/ppermute | solution.py:353
  52.0 4.3 %collective-permute-start.15 = (f32[32,512]{1,0:T(8,128)S(1)}, f32[32,512]{1,0:T(8,128)S(1)}, u32[]{:S(2)}, u32[]{:S(2)}) collective-permute-start(f32[32,512]{1,0:T(8,128)S(1)} %get-tuple-element.50), channel_id=1, source_target_pairs={{0,1},{1,0},{2,3},{3,2},{4,5},{5,4},{6,7},{7,6},{8,9},{9,8},{10,11... | collective-permute-start | bytes 196616 | tf_op jit(solution)/shard_map/ppermute | solution.py:468

commit v2 on v1

v2 whole, which is shorter than its diff:
```python
import functools
import math

import jax
import jax.numpy as jnp
from jax import lax
from jax.experimental import pallas as pl
from jax.experimental.pallas import tpu as pltpu
from jax.sharding import PartitionSpec as P

HD = 128
QPK = 8
BEAM_WIDTH = 16
BLOCK_LEN = 128
STATS = 128
SCALE = 1.0 / math.sqrt(HD)
LOG2E = math.log2(math.e)

masked_score = -1e30
f32, bf16 = jnp.float32, jnp.bfloat16


def dot(a, b, ca, cb):
    return lax.dot_general(a, b, (((ca,), (cb,)), ((), ())), preferred_element_type=f32)


def soft(scores):
    top = jnp.max(scores, axis=1, keepdims=True)
    weights = jnp.exp2((scores - top) * (SCALE * LOG2E))
    return weights, top * SCALE, jnp.sum(weights, axis=1, keepdims=True)


def line_order(requests):
    return [requests - 1, 0, *range(1, requests - 1)]


def line_kernel(tail_ref, *refs):
    *pieces, out_ref = refs
    width = pieces[0].shape[1]
    for n, x in enumerate(pieces):
        out_ref[n, :, :width] = x[...]
        out_ref[n, :, width:] = tail_ref[...]


def load_private_kernel(
    q_hbm, par_hbm, cnt_hbm, ck_hbm, cv_hbm,
    q_ref, tail_ref, lim_ref, ck_ref, cv_ref, par_ref, cnt_ref, sems, old_sems,
):
    copies = [
        pltpu.make_async_copy(src, dst, sems.at[n])
        for n, (src, dst) in enumerate(((q_hbm, q_ref), (par_hbm, par_ref), (cnt_hbm, cnt_ref)))
    ] + [
        pltpu.make_async_copy(src.at[o], dst.at[o], old_sems.at[n, o])
        for n, (src, dst) in enumerate(((ck_hbm, ck_ref), (cv_hbm, cv_ref)))
        for o in range(ck_ref.shape[0])
    ]
    for x in copies:
        x.start()
    for x in copies[:3]:
        x.wait()
    row = lax.broadcasted_iota(jnp.int32, tail_ref.shape, 0)
    parent = jnp.zeros(row.shape, jnp.int32)
    for b in range(tail_ref.shape[0]):
        parent = jnp.where(row == b, par_ref[b], parent)
    tail_ref[...] = parent.astype(f32).astype(bf16)
    lane = lax.broadcasted_iota(jnp.int32, lim_ref.shape, 1)
    limit = jnp.zeros(lim_ref.shape, jnp.int32)
    for o in range(ck_ref.shape[0]):
        limit = jnp.where(lane == o, cnt_ref[o] * BLOCK_LEN, limit)
    lim_ref[...] = limit
    for x in copies[3:]:
        x.wait()


def load_prompt_kernel(group, pk_hbm, pv_hbm, pk_ref, pv_ref, sems):
    mine = lax.axis_index("beam") // group
    copies = [
        pltpu.make_async_copy(src.at[mine ^ t], dst.at[at], sems.at[n, at])
        for n, (src, dst) in enumerate(((pk_hbm, pk_ref), (pv_hbm, pv_ref)))
        for at, t in enumerate(line_order(pk_ref.shape[0]))
    ]
    for x in copies:
        x.start()
    for x in copies:
        x.wait()


def attend_kernel(qa_ref, qb_ref, pk_ref, pv_ref, lim_ref, ck_ref, cv_ref, *refs):
    *outs, s_ref, p_ref, cs_ref, cp_ref = refs
    count, half, beams, total = qa_ref.shape
    requests, length, width = pk_ref.shape
    pairs = requests // 2
    heads = width // HD
    olds, span, _ = ck_ref.shape
    block = count * beams
    stride = heads * QPK
    rows = QPK * block
    own_at = line_order(requests).index(0)
    pieces = [
        [qa_ref.at[r, n] for n in range(half)] + [qb_ref.at[r, n] for n in range(half)]
        for r in range(count)
    ]

    def beside(ref, k, places):
        return jnp.concatenate([ref[at, :, k * HD : (k + 1) * HD] for at in places], axis=1)

    me = lax.axis_index("beam")

    parent = jnp.concatenate([x[own_at][:, total - STATS :].astype(f32) for x in pieces], axis=0)
    parent = jnp.concatenate([parent] * QPK, axis=0).astype(jnp.int32) - me * olds
    column = parent[:, :1]
    local = (column >= 0) & (column < olds)
    limit = jnp.zeros((rows, 1), jnp.int32)
    for o in range(olds):
        limit = jnp.where(column == o, lim_ref[0:1, o : o + 1], limit)
    stats = [jnp.zeros((block, STATS), f32) for _ in range(requests)]
    lane = lax.broadcasted_iota(jnp.int32, (block, STATS), 1) % stride
    blank = jnp.zeros((rows, HD), bf16)
    kept = {}

    def scores(k):
        q = [
            jnp.concatenate(
                [
                    x[t][:, (k * QPK + i) * HD : (k * QPK + i + 1) * HD]
                    for i in range(QPK)
                    for x in pieces
                ],
                axis=0,
            )
            for t in range(requests)
        ]
        for u in range(pairs):
            both = jnp.concatenate(
                [
                    jnp.concatenate([q[2 * u], blank], axis=1),
                    jnp.concatenate([blank, q[2 * u + 1]], axis=1),
                ],
                axis=0,
            )
            s_ref[k, 2 * u * rows : 2 * (u + 1) * rows] = dot(
                both, beside(pk_ref, k, (2 * u, 2 * u + 1)), 1, 1
            )
        chosen = jnp.concatenate([jnp.where(parent == o, q[own_at], blank) for o in range(olds)], axis=1)
        cs_ref[k] = dot(chosen, beside(ck_ref, k, range(olds)), 1, 1)

    def weigh(k):
        p, top, den = soft(s_ref[k])
        p_ref[k] = p.astype(bf16)
        place = lax.broadcasted_iota(jnp.int32, (rows, span), 1)
        c, ctop, cden = soft(jnp.where(place < limit, cs_ref[k], masked_score))
        cp_ref[k] = c.astype(bf16)
        kept[k] = (top, den, ctop, cden)

    def values(k):
        tops, dens, ctop, cden = kept.pop(k)
        nums = []
        for u in range(pairs):
            both = dot(
                p_ref[k, 2 * u * rows : 2 * (u + 1) * rows],
                beside(pv_ref, k, (2 * u, 2 * u + 1)),
                1,
                0,
            )
            nums += [both[:rows, :HD], both[rows:, HD:]]
        every = dot(cp_ref[k], beside(cv_ref, k, range(olds)), 1, 0)
        cnum = every[:, :HD]
        for o in range(1, olds):
            cnum = jnp.where(parent == o, every[:, o * HD : (o + 1) * HD], cnum)
        done = []
        for t in range(requests):
            part = slice(t * rows, (t + 1) * rows)
            num, top, den = nums[t], tops[part], dens[part]
            if t == own_at:
                both = jnp.where(local, jnp.maximum(top, ctop), top)
                a = jnp.exp(top - both)
                e = jnp.where(local, jnp.exp(jnp.where(local, ctop, both) - both), 0.0)
                num = a * num + e * cnum
                den = a * den + e * cden
                top = both
            done.append(num * (1.0 / den))
            lse = top + jnp.log(den)
            for i in range(QPK):
                stats[t] = jnp.where(
                    lane == k * QPK + i,
                    jnp.broadcast_to(
                        lse[i * block : (i + 1) * block], (block, STATS)
                    ),
                    stats[t],
                )
        for i in range(QPK):
            cols = slice((k * QPK + i) * HD, (k * QPK + i + 1) * HD)
            for r, out in enumerate(outs):
                first = i * block + r * beams
                out[:, cols] = jnp.concatenate(
                    [x[first : first + beams] for x in done], axis=0
                ).astype(bf16)

    for stage in (scores, weigh, values):
        for k in range(heads):
            stage(k)
    for r, out in enumerate(outs):
        out[:, total - STATS :] = pack_stats(
            jnp.concatenate([x[r * beams : (r + 1) * beams] for x in stats], axis=0), stride
        )


def pack_stats(x, stride):
    hi = x.astype(bf16).astype(f32)
    mid = (x - hi).astype(bf16).astype(f32)
    which = lax.broadcasted_iota(jnp.int32, x.shape, 1) // stride
    return jnp.where(which == 0, hi, jnp.where(which == 1, mid, x - hi - mid)).astype(bf16)


def read_stats(x, stride):
    x = x.astype(f32)
    return x + pltpu.roll(x, STATS - stride, 1) + pltpu.roll(x, STATS - 2 * stride, 1)


def merge(a, b, outs):
    total = a.shape[1]
    count = (total - STATS) // HD
    size = a.shape[0] // len(outs)

    def store(cols, value):
        for n, out in enumerate(outs):
            out[:, cols] = value[n * size : (n + 1) * size]

    la, lb = read_stats(a[:, total - STATS :], count), read_stats(b[:, total - STATS :], count)
    top = jnp.maximum(la, lb)
    wa, wb = jnp.exp(la - top), jnp.exp(lb - top)
    den = wa + wb
    wa = wa * (1.0 / den)
    wb = wb * (1.0 / den)
    for h in range(count):
        cols = slice(h * HD, (h + 1) * HD)
        store(
            cols,
            (
                wa[:, h : h + 1] * a[:, cols].astype(f32)
                + wb[:, h : h + 1] * b[:, cols].astype(f32)
            ).astype(bf16),
        )
    lse = top + jnp.log(den)
    lane = lax.broadcasted_iota(jnp.int32, lse.shape, 1)
    again = jnp.where(
        lane < count,
        lse,
        jnp.where(lane < 2 * count, pltpu.roll(lse, count, 1), pltpu.roll(lse, 2 * count, 1)),
    )
    store(slice(total - STATS, total), pack_stats(again, count))


def core_kernel(kept_ref, came_ref, a_ref, b_ref):
    half = a_ref.shape[0]
    outs = {2 * half - 1 - n: ref.at[n % half] for n, ref in enumerate([a_ref] * half + [b_ref] * half)}
    merge(kept_ref, came_ref, [outs[t] for t in line_order(2 * half)])


def plane_kernel(kept_ref, came_ref, *outs):
    kept, came = (
        jnp.concatenate([x[n] for n in range(len(outs))], axis=0) for x in (kept_ref, came_ref)
    )
    merge(kept, came, outs)


def finish_kernel(q_ref, nk_ref, nv_ref, *refs):
    *parts, out_ref = refs
    beams, total = parts[0].shape
    heads = nv_ref.shape[1] // HD
    stride = heads * QPK
    lane = lax.broadcasted_iota(jnp.int32, (beams, STATS), 1)
    own = jnp.zeros((beams, STATS), f32)
    for h in range(stride):
        key = nk_ref[:, h // QPK * HD : (h // QPK + 1) * HD].astype(f32)
        s = jnp.sum(q_ref[:, h * HD : (h + 1) * HD].astype(f32) * key, axis=1, keepdims=True)
        own = jnp.where(lane == h, s * SCALE, own)
    lses = [read_stats(x[:, total - STATS :], stride) for x in parts]
    top = functools.reduce(jnp.maximum, lses, own)
    ws = [jnp.exp(x - top) for x in lses]
    w_own = jnp.exp(own - top)
    inv = 1.0 / functools.reduce(jnp.add, ws, w_own)
    ws = [w * inv for w in ws]
    w_own = w_own * inv
    for k in range(heads):
        value = nv_ref[:, k * HD : (k + 1) * HD].astype(f32)
        for i in range(QPK):
            h = k * QPK + i
            acc = w_own[:, h : h + 1] * value
            for w, x in zip(ws, parts):
                acc = acc + w[:, h : h + 1] * x[:, h * HD : (h + 1) * HD].astype(f32)
            out_ref[:, h * HD : (h + 1) * HD] = acc.astype(bf16)


def project_kernel(near_a, far_a, near_b, far_b, w_ref, keep_ref, send_ref, rows_ref):
    requests, group = rows_ref.shape[:2]
    me, side = lax.axis_index("beam"), lax.axis_index("head")
    mine, spot = me // group, me % group
    order = [0, requests - 1] + list(range(1, requests - 1))
    for first, refs in ((0, (near_a, far_a)), (requests // 2, (near_b, far_b))):
        for core, ref in enumerate(refs):
            for x in range(2):
                for n in range(requests // 2):
                    rows_ref[mine ^ order[first + n], spot ^ (2 * x + core)] = ref[x, n]
    a = jnp.concatenate(
        [rows_ref[z, j] for z in range(requests) for j in range(group)], axis=0
    )
    out = jnp.dot(a, w_ref[...], preferred_element_type=f32)
    half = requests * BEAM_WIDTH // 2

    @pl.when(side == 0)
    def _():
        keep_ref[...] = out[:half]
        send_ref[...] = out[half:].astype(bf16)

    @pl.when(side != 0)
    def _():
        keep_ref[...] = out[half:]
        send_ref[...] = out[:half].astype(bf16)


def whole_blocks(n, smem=(), far=()):
    places = [pltpu.SMEM if i in smem else pltpu.HBM if i in far else pltpu.VMEM for i in range(n)]
    return [pl.BlockSpec(memory_space=place) for place in places]


def call(kernel, name, out_shape, *args, smem=(), far=(), scratch=(), vmem=8, cost=None):
    many = isinstance(out_shape, tuple)
    return pl.pallas_call(
        kernel,
        out_shape=out_shape,
        in_specs=whole_blocks(len(args), smem, far),
        out_specs=tuple(whole_blocks(len(out_shape))) if many else whole_blocks(1)[0],
        scratch_shapes=list(scratch),
        compiler_params=pltpu.CompilerParams(vmem_limit_bytes=vmem * 1024 * 1024),
        cost_estimate=cost and pl.CostEstimate(flops=cost, bytes_accessed=cost, transcendentals=0),
        name=name,
    )(*(pltpu.with_memory_space_constraint(x, pltpu.HBM) if i in far else x for i, x in enumerate(args)))


def per_device(
    queries,
    new_keys,
    new_values,
    prompt_keys,
    prompt_values,
    private_keys,
    private_values,
    parents,
    block_counts,
    out_weight,
):
    beams, width = queries.shape
    group = BEAM_WIDTH // beams
    assert group == 4
    devices = lax.axis_size("beam")
    requests = prompt_keys.shape[0]
    sides = lax.axis_size("head")
    total = width + STATS

    def swap(x, with_bit):
        return lax.ppermute(x, "beam", [(i, i ^ with_bit) for i in range(devices)])

    rows = requests * beams
    heads = width // (QPK * HD)
    length, span = prompt_keys.shape[1], private_keys.shape[1]
    line = jax.ShapeDtypeStruct((rows, total), bf16)
    order = line_order(requests)
    middle = requests // 2
    came = {t: swap(queries, t * group) for t in [requests - 1, *range(1, requests - 1)]}
    prompt = jax.ShapeDtypeStruct(prompt_keys.shape, bf16)
    private = jax.ShapeDtypeStruct(private_keys.shape, bf16)
    own, parent_tail, *olds = call(
        load_private_kernel,
        "load_private",
        (
            jax.ShapeDtypeStruct((beams, width), bf16),
            jax.ShapeDtypeStruct((beams, STATS), bf16),
            jax.ShapeDtypeStruct((8, STATS), jnp.int32),
            private,
            private,
        ),
        queries,
        parents,
        block_counts,
        private_keys,
        private_values,
        far=(0, 1, 2, 3, 4),
        scratch=[
            pltpu.SMEM((beams,), jnp.int32),
            pltpu.SMEM((beams,), jnp.int32),
            pltpu.SemaphoreType.DMA((3,)),
            pltpu.SemaphoreType.DMA((2, beams)),
        ],
        vmem=10,
        cost=8 * 2**20,
    )
    came[requests - 1], parent_tail = lax.optimization_barrier((came[requests - 1], parent_tail))
    came[0] = own
    asked_a = call(
        line_kernel,
        "line",
        jax.ShapeDtypeStruct((middle, beams, total), bf16),
        parent_tail,
        *(came[t] for t in order[:middle]),
    )
    asked_b = jnp.stack([came[t] for t in order[middle:]])
    prompt_keys, prompt_values, _ = lax.optimization_barrier((prompt_keys, prompt_values, asked_b))
    prompts = call(
        functools.partial(load_prompt_kernel, group),
        "load_prompt",
        (prompt, prompt),
        prompt_keys,
        prompt_values,
        far=(0, 1),
        scratch=[pltpu.SemaphoreType.DMA((2, requests))],
        vmem=10,
        cost=4 * 2**20,
    )
    caches = (*prompts, *olds)

    def attend(asked_a, asked_b, name):
        many = asked_a.shape[0] * beams * QPK
        return call(
            attend_kernel,
            name,
            (line,) * asked_a.shape[0],
            asked_a,
            asked_b,
            *caches,
            scratch=[
                pltpu.VMEM((heads, requests * many, length), f32),
                pltpu.VMEM((heads, requests * many, length), bf16),
                pltpu.VMEM((heads, many, span), f32),
                pltpu.VMEM((heads, many, span), bf16),
            ],
            vmem=24,
        )

    other_a, other_b = swap(asked_a, 2), swap(asked_b, 2)
    (keep0,) = attend(asked_a[None], asked_b[None], "attend_own")
    other_a, other_b, keep0 = lax.optimization_barrier((other_a, other_b, keep0))
    far_a = swap(jnp.stack([asked_a, other_a]), 1)
    far_b = swap(jnp.stack([asked_b, other_b]), 1)
    (keep2,) = attend(other_a[None], other_b[None], "attend_side")
    far_a, far_b, keep2 = lax.optimization_barrier((far_a, far_b, keep2))
    far_own, far_side = attend(far_a, far_b, "attend_far")
    half = jax.ShapeDtypeStruct((requests // 2, beams, total), bf16)
    send_a, send_b = call(core_kernel, "side_merge", (half, half), keep2, swap(far_side, 1))
    keep_a, keep_b = call(core_kernel, "own_merge", (half, half), keep0, swap(far_own, 1))
    piece = jax.ShapeDtypeStruct((beams, total), bf16)
    parts = []
    for keep, send in ((keep_a, send_a), (keep_b, send_b)):
        parts += call(
            plane_kernel, "plane_merge", (piece,) * (requests // 2), keep, swap(send, 2)
        )
    parts = [
        swap(x, t * group) if t else x for t, x in zip(range(requests - 1, -1, -1), parts)
    ]
    attended = call(
        finish_kernel,
        "finish",
        jax.ShapeDtypeStruct((beams, width), bf16),
        own,
        new_keys,
        new_values,
        *parts,
    )
    if sides == 2:
        line = [attended] + [
            swap(attended, t * group) for t in [requests - 1, *range(1, requests - 1)]
        ]
        halves = []
        for pieces in (line[: requests // 2], line[requests // 2 :]):
            near = jnp.stack(pieces)
            near = jnp.stack([near, swap(near, 2)])
            halves += [near, swap(near, 1)]
        shape = (requests * BEAM_WIDTH // 2, out_weight.shape[1])
        keep, send = call(
            project_kernel,
            "project",
            (jax.ShapeDtypeStruct(shape, f32), jax.ShapeDtypeStruct(shape, bf16)),
            *halves,
            out_weight,
            scratch=[pltpu.VMEM((requests, group, beams, width), bf16)],
            vmem=16,
        )
        came = lax.ppermute(send, "head", [(0, 1), (1, 0)])
        return (keep + came.astype(f32)).astype(bf16)
    rows = lax.all_gather(attended, "beam", axis=0, tiled=True)
    products = jnp.dot(rows, out_weight, preferred_element_type=f32)
    return lax.psum_scatter(products, "head", scatter_dimension=0, tiled=True).astype(bf16)


def solution(mesh):
    placed = (
        P("beam", "head"),
        P("beam", "head"),
        P("beam", "head"),
        P(None, "beam", "head"),
        P(None, "beam", "head"),
        P("beam", None, "head"),
        P("beam", None, "head"),
        P("beam"),
        P("beam"),
        P("head", "beam"),
    )
    return jax.shard_map(
        per_device, mesh=mesh, in_specs=placed, out_specs=P("head", "beam"), check_vma=False
    )
```

time: 57.1 us -> 53.3 us (0.933)
  waiting for transfers between devices: 24.5 us -> 14.7 us
  starting transfers between devices: 19.1 us -> 25.1 us
    ppermute x6 -> x21, starting transfers between devices: 5.38 us -> 23.5 us  [swap(): return lax.ppermute(x, 'beam', [(i, i ^ with_bit) for i in range(devices)])]
    ppermute x10 -> x1, starting transfers between devices: 13.7 us -> 1.59 us  [per_device(): came = lax.ppermute(send, 'head', [(0, 1), (1, 0)])]
    ppermute x10 -> x1, waiting for transfers between devices: 12.2 us -> 2.39 us  [per_device(): came = lax.ppermute(send, 'head', [(0, 1), (1, 0)])]
    pallas_call x10 -> x12, Pallas kernels: 12.1 us -> 11.9 us  [call(): pl.pallas_call(kernel, out_shape=out_shape, in_specs=whole_blocks(len(arg...]
    ppermute x6 -> x21, waiting for transfers between devices: 12.3 us -> 12.3 us  [swap(): return lax.ppermute(x, 'beam', [(i, i ^ with_bit) for i in range(devices)])]
  transfers between devices with their start and end apart: 16 -> 22, of which waited for: 11 -> 11; matrix products, arithmetic and copies ran while one was open for 0% -> 1% of each run, Pallas kernels for 14% -> 16%
where the time goes in v2:
time: 53.3 us; the launch traced here: 53.1 us
  starting transfers between devices  25.1 us (47%)
  waiting for transfers between devices  14.7 us (28%)
  Pallas kernels  11.9 us (22%)
  other arithmetic  1.16 us (2%)
    ppermute x21, starting transfers between devices, swap(): return lax.ppermute(x, 'beam', [(i, i ^ with_bit) for i in range(devices)])  23.5 us
    ppermute x21, waiting for transfers between devices, swap(): return lax.ppermute(x, 'beam', [(i, i ^ with_bit) for i in range(devices)])  12.3 us
    pallas_call x12, Pallas kernels, call(): pl.pallas_call(kernel, out_shape=out_shape, in_specs=whole_blocks(len(arg...  11.9 us
    ppermute x1, waiting for transfers between devices, per_device(): came = lax.ppermute(send, 'head', [(0, 1), (1, 0)])  2.39 us
    ppermute x1, starting transfers between devices, per_device(): came = lax.ppermute(send, 'head', [(0, 1), (1, 0)])  1.59 us
  transfers between devices with their start and end apart: 22, of which 11 were waited for; matrix products, arithmetic and copies ran while one was open for 1% of the time, Pallas kernels for 16%

profile of v2, /device:TPU:0, one launch (start us, length us, event | category | flops | bytes accessed | tf_op | source)
XLA Modules:
  0.0 53.1 jit_solution(6771760208218155825)
XLA Ops:
  0.0 5.0 %collective-permute-start = (bf16[4,4096]{1,0:T(4,128)(2,1)}, bf16[4,4096]{1,0:T(4,128)(2,1)S(1)}, u32[]{:S(2)}, u32[]{:S(2)}) collective-permute-start(bf16[4,4096]{1,0:T(4,128)(2,1)} %q_hbm.1), channel_id=1, source_target_pairs={{0,24},{2,26},{4,28},{6,30},{8,16},{10,18},{12,20},{14,22},{16,8},... | collective-permute-start | bytes 98312 | tf_op jit(solution)/shard_map/ppermute | solution.py:362
  5.1 0.6 %collective-permute-start.2 = (bf16[4,4096]{1,0:T(4,128)(2,1)}, bf16[4,4096]{1,0:T(4,128)(2,1)S(1)}, u32[]{:S(2)}, u32[]{:S(2)}) collective-permute-start(bf16[4,4096]{1,0:T(4,128)(2,1)} %q_hbm.1), channel_id=1, source_target_pairs={{0,8},{2,10},{4,12},{6,14},{8,0},{10,2},{12,4},{14,6},{16,24},{18,... | collective-permute-start | bytes 98312 | tf_op jit(solution)/shard_map/ppermute | solution.py:362
  5.6 2.3 %load_private.1 = (bf16[4,4096]{1,0:T(4,128)(2,1)S(1)}, bf16[4,128]{1,0:T(4,128)(2,1)S(1)}, s32[8,128]{1,0:T(8,128)S(1)}, bf16[4,512,512]{2,1,0:T(8,128)(2,1)S(1)}, bf16[4,512,512]{2,1,0:T(8,128)(2,1)S(1)}) custom-call(bf16[4,4096]{1,0:T(4,128)(2,1)} %q_hbm.1, s32[4]{0:T(128)} %par_hbm.1, s32[4]{0:T(128)} %cnt_hbm.1, bf16[4,512,512]{2,1,0:T(8,128)(2,1)} %ck_hbm.1, ...), custom_call_target="tpu_custom_call" | custom-call | flops 8388608 | bytes 8388608 | tf_op jit(solution)/shard_map/load_private/pallas_call | solution.py:329
  7.9 1.8 %collective-permute-start.1 = (bf16[2,4,4224]{2,1,0:T(4,128)(2,1)S(1)}, bf16[2,4,4224]{2,1,0:T(4,128)(2,1)S(1)}, u32[]{:S(2)}, u32[]{:S(2)}) collective-permute-start(bf16[2,4,4224]{2,1,0:T(4,128)(2,1)S(1)} %line.1), channel_id=1, source_target_pairs={{0,4},{2,6},{4,0},{6,2},{8,12},{10,14},{12,8},{14,10},{16,20},{18,... | collective-permute-start | bytes 202760 | tf_op jit(solution)/shard_map/ppermute | solution.py:362
  9.7 0.4 collective-permute-done.3
  10.1 0.1 fusion.2
  10.1 1.6 %collective-permute-start.4 = (bf16[2,4,4096]{2,1,0:T(4,128)(2,1)S(1)}, bf16[2,4,4096]{2,1,0:T(4,128)(2,1)S(1)}, u32[]{:S(2)}, u32[]{:S(2)}) collective-permute-start(bf16[2,4,4096]{2,1,0:T(4,128)(2,1)S(1)} %get-tuple-element.68), channel_id=1, source_target_pairs={{0,4},{2,6},{4,0},{6,2},{8,12},{10,14},{12,8},{14,10},{16,20},{18,... | collective-permute-start | bytes 196616 | tf_op jit(solution)/shard_map/ppermute | solution.py:362
  11.7 1.6 %load_prompt.1 = (bf16[4,256,512]{2,1,0:T(8,128)(2,1)S(1)}, bf16[4,256,512]{2,1,0:T(8,128)(2,1)S(1)}) custom-call(bf16[4,256,512]{2,1,0:T(8,128)(2,1)} %pk_hbm, bf16[4,256,512]{2,1,0:T(8,128)(2,1)} %pv_hbm), custom_call_target="tpu_custom_call" | custom-call | flops 4194304 | bytes 4194304 | tf_op jit(solution)/shard_map/load_prompt/pallas_call | solution.py:329
  13.3 1.7 %attend_own.1.kept_ref = bf16[16,4224]{1,0:T(8,128)(2,1)S(1)} custom-call(bf16[1,2,4,4224]{3,2,1,0:T(4,128)(2,1)S(1)} %bitcast.17, bf16[1,2,4,4096]{3,2,1,0:T(4,128)(2,1)S(1)} %get-tuple-element.67.qb_ref, bf16[4,256,512]{2,1,0:T(8,128)(2,1)S(1)} %get-tuple-element.40.pk_ref, bf16[4,256,512]{2,1,0:T(8,128)(2,1)S(1)} %get-tuple-element.41.pv_ref, ...), custom_call_target="tpu_custom_call" | custom-call | tf_op jit(solution)/shard_map/attend_own/pallas_call | solution.py:329
  15.0 0.1 pad_maximum_fusion
  15.1 0.1 collective-permute-start.5
  15.2 0.1 pad_maximum_fusion.1
  15.3 0.6 %collective-permute-start.6 = (bf16[2,2,4,4096]{3,2,1,0:T(4,128)(2,1)S(1)}, bf16[2,2,4,4096]{3,2,1,0:T(4,128)(2,1)S(1)}, u32[]{:S(2)}, u32[]{:S(2)}) collective-permute-start(bf16[2,2,4,4096]{3,2,1,0:T(4,128)(2,1)S(1)} %pad_maximum_fusion.1), channel_id=1, source_target_pairs={{0,2},{2,0},{4,6},{6,4},{8,10},{10,8},{12,14},{14,12},{16,18},{18,... | collective-permute-start | bytes 393224 | tf_op jit(solution)/shard_map/ppermute | solution.py:362
  15.9 1.7 %attend_side.1.kept_ref = bf16[16,4224]{1,0:T(8,128)(2,1)S(1)} custom-call(bf16[1,2,4,4224]{3,2,1,0:T(4,128)(2,1)S(1)} %bitcast.20, bf16[1,2,4,4096]{3,2,1,0:T(4,128)(2,1)S(1)} %bitcast.22, bf16[4,256,512]{2,1,0:T(8,128)(2,1)S(1)} %get-tuple-element.40.pk_ref, bf16[4,256,512]{2,1,0:T(8,128)(2,1)S(1)} %get-tuple-element.41.pv_ref, ...), custom_call_target="tpu_custom_call" | custom-call | tf_op jit(solution)/shard_map/attend_side/pallas_call | solution.py:329
  17.7 2.0 %attend_far.1 = (bf16[16,4224]{1,0:T(8,128)(2,1)S(1)}, bf16[16,4224]{1,0:T(8,128)(2,1)S(1)}) custom-call(bf16[2,2,4,4224]{3,2,1,0:T(4,128)(2,1)S(1)} %collective-permute-done.5.qa_ref, bf16[2,2,4,4096]{3,2,1,0:T(4,128)(2,1)S(1)} %collective-permute-done.6.qb_ref, bf16[4,256,512]{2,1,0:T(8,128)(2,1)S(1)} %get-tuple-element.40.pk_ref, ...), custom_call_target="tpu_custom_call" | custom-call | tf_op jit(solution)/shard_map/attend_far/pallas_call | solution.py:329
  19.7 0.1 collective-permute-start.8
  19.8 0.5 collective-permute-start.7
  20.3 0.8 %collective-permute-done.8.came_ref = bf16[16,4224]{1,0:T(8,128)(2,1)S(1)} collective-permute-done((bf16[16,4224]{1,0:T(8,128)(2,1)S(1)}, bf16[16,4224]{1,0:T(8,128)(2,1)S(1)}, u32[]{:S(2)}, u32[]{:S(2)}) %collective-permute-start.8) | collective-permute-done | bytes 135200 | tf_op jit(solution)/shard_map/ppermute | solution.py:362
  21.1 0.4 side_merge.1
  21.5 1.0 %collective-permute-start.9 = (bf16[2,4,4224]{2,1,0:T(4,128)(2,1)S(1)}, bf16[2,4,4224]{2,1,0:T(4,128)(2,1)S(1)}, u32[]{:S(2)}, u32[]{:S(2)}) collective-permute-start(bf16[2,4,4224]{2,1,0:T(4,128)(2,1)S(1)} %get-tuple-element.54), channel_id=1, source_target_pairs={{0,4},{2,6},{4,0},{6,2},{8,12},{10,14},{12,8},{14,10},{16,20},{18,... | collective-permute-start | bytes 202760 | tf_op jit(solution)/shard_map/ppermute | solution.py:362
  22.5 1.1 %collective-permute-start.12 = (bf16[2,4,4224]{2,1,0:T(4,128)(2,1)S(1)}, bf16[2,4,4224]{2,1,0:T(4,128)(2,1)S(1)}, u32[]{:S(2)}, u32[]{:S(2)}) collective-permute-start(bf16[2,4,4224]{2,1,0:T(4,128)(2,1)S(1)} %get-tuple-element.58), channel_id=1, source_target_pairs={{0,4},{2,6},{4,0},{6,2},{8,12},{10,14},{12,8},{14,10},{16,20},{18,... | collective-permute-start | bytes 202760 | tf_op jit(solution)/shard_map/ppermute | solution.py:362
  23.6 0.4 own_merge.1
  23.9 2.5 %collective-permute-done.9.came_ref = bf16[2,4,4224]{2,1,0:T(4,128)(2,1)S(1)} collective-permute-done((bf16[2,4,4224]{2,1,0:T(4,128)(2,1)S(1)}, bf16[2,4,4224]{2,1,0:T(4,128)(2,1)S(1)}, u32[]{:S(2)}, u32[]{:S(2)}) %collective-permute-start.9) | collective-permute-done | bytes 67616 | tf_op jit(solution)/shard_map/ppermute | solution.py:362
  26.5 0.3 plane_merge.2
  26.7 2.8 %collective-permute-start.10 = (bf16[4,4224]{1,0:T(4,128)(2,1)S(1)}, bf16[4,4224]{1,0:T(4,128)(2,1)S(1)}, u32[]{:S(2)}, u32[]{:S(2)}) collective-permute-start(bf16[4,4224]{1,0:T(4,128)(2,1)S(1)} %get-tuple-element.55), channel_id=1, source_target_pairs={{0,24},{2,26},{4,28},{6,30},{8,16},{10,18},{12,20},{14,22},{16,8},... | collective-permute-start | bytes 101384 | tf_op jit(solution)/shard_map/ppermute | solution.py:362
  29.5 0.3 plane_merge.3
  29.8 1.7 %collective-permute-start.13 = (bf16[4,4224]{1,0:T(4,128)(2,1)S(1)}, bf16[4,4224]{1,0:T(4,128)(2,1)S(1)}, u32[]{:S(2)}, u32[]{:S(2)}) collective-permute-start(bf16[4,4224]{1,0:T(4,128)(2,1)S(1)} %get-tuple-element.59), channel_id=1, source_target_pairs={{0,8},{2,10},{4,12},{6,14},{8,0},{10,2},{12,4},{14,6},{16,24},{18,... | collective-permute-start | bytes 101384 | tf_op jit(solution)/shard_map/ppermute | solution.py:362
  31.5 1.0 %collective-permute-done.10.refs_0_ = bf16[4,4224]{1,0:T(4,128)(2,1)S(1)} collective-permute-done((bf16[4,4224]{1,0:T(4,128)(2,1)S(1)}, bf16[4,4224]{1,0:T(4,128)(2,1)S(1)}, u32[]{:S(2)}, u32[]{:S(2)}) %collective-permute-start.10) | collective-permute-done | bytes 33824 | tf_op jit(solution)/shard_map/ppermute | solution.py:362
  32.5 1.8 %collective-permute-done.11.refs_1_ = bf16[4,4224]{1,0:T(4,128)(2,1)S(1)} collective-permute-done((bf16[4,4224]{1,0:T(4,128)(2,1)S(1)}, bf16[4,4224]{1,0:T(4,128)(2,1)S(1)}, u32[]{:S(2)}, u32[]{:S(2)}) %collective-permute-start.11) | collective-permute-done | bytes 33824 | tf_op jit(solution)/shard_map/ppermute | solution.py:362
  34.4 0.5 finish.1
  34.9 2.0 %collective-permute-start.14 = (bf16[4,4096]{1,0:T(4,128)(2,1)S(1)}, bf16[4,4096]{1,0:T(4,128)(2,1)S(1)}, u32[]{:S(2)}, u32[]{:S(2)}) collective-permute-start(bf16[4,4096]{1,0:T(4,128)(2,1)S(1)} %finish.1), channel_id=1, source_target_pairs={{0,24},{2,26},{4,28},{6,30},{8,16},{10,18},{12,20},{14,22},{16,8},... | collective-permute-start | bytes 98312 | tf_op jit(solution)/shard_map/ppermute | solution.py:362
  36.9 0.6 %collective-permute-start.18 = (bf16[4,4096]{1,0:T(4,128)(2,1)S(1)}, bf16[4,4096]{1,0:T(4,128)(2,1)S(1)}, u32[]{:S(2)}, u32[]{:S(2)}) collective-permute-start(bf16[4,4096]{1,0:T(4,128)(2,1)S(1)} %finish.1), channel_id=1, source_target_pairs={{0,16},{2,18},{4,20},{6,22},{8,24},{10,26},{12,28},{14,30},{16,0},... | collective-permute-start | bytes 98312 | tf_op jit(solution)/shard_map/ppermute | solution.py:362
  37.5 1.8 %collective-permute-start.17 = (bf16[4,4096]{1,0:T(4,128)(2,1)S(1)}, bf16[4,4096]{1,0:T(4,128)(2,1)S(1)}, u32[]{:S(2)}, u32[]{:S(2)}) collective-permute-start(bf16[4,4096]{1,0:T(4,128)(2,1)S(1)} %finish.1), channel_id=1, source_target_pairs={{0,8},{2,10},{4,12},{6,14},{8,0},{10,2},{12,4},{14,6},{16,24},{18,... | collective-permute-start | bytes 98312 | tf_op jit(solution)/shard_map/ppermute | solution.py:362
  39.3 1.3 %collective-permute-done.14 = bf16[4,4096]{1,0:T(4,128)(2,1)S(1)} collective-permute-done((bf16[4,4096]{1,0:T(4,128)(2,1)S(1)}, bf16[4,4096]{1,0:T(4,128)(2,1)S(1)}, u32[]{:S(2)}, u32[]{:S(2)}) %collective-permute-start.14) | collective-permute-done | bytes 32800 | tf_op jit(solution)/shard_map/ppermute | solution.py:362
  40.7 1.1 %collective-permute-start.15 = (bf16[2,4,4096]{2,1,0:T(4,128)(2,1)S(1)}, bf16[2,4,4096]{2,1,0:T(4,128)(2,1)S(1)}, u32[]{:S(2)}, u32[]{:S(2)}) collective-permute-start(bf16[2,4,4096]{2,1,0:T(4,128)(2,1)S(1)} %get-tuple-element.66), channel_id=1, source_target_pairs={{0,4},{2,6},{4,0},{6,2},{8,12},{10,14},{12,8},{14,10},{16,20},{18,... | collective-permute-start | bytes 196616 | tf_op jit(solution)/shard_map/ppermute | solution.py:362
  41.8 1.1 %collective-permute-start.19 = (bf16[2,4,4096]{2,1,0:T(4,128)(2,1)S(1)}, bf16[2,4,4096]{2,1,0:T(4,128)(2,1)S(1)}, u32[]{:S(2)}, u32[]{:S(2)}) collective-permute-start(bf16[2,4,4096]{2,1,0:T(4,128)(2,1)S(1)} %get-tuple-element.64), channel_id=1, source_target_pairs={{0,4},{2,6},{4,0},{6,2},{8,12},{10,14},{12,8},{14,10},{16,20},{18,... | collective-permute-start | bytes 196616 | tf_op jit(solution)/shard_map/ppermute | solution.py:362
  42.9 2.1 %collective-permute-done.15 = bf16[2,4,4096]{2,1,0:T(4,128)(2,1)S(1)} collective-permute-done((bf16[2,4,4096]{2,1,0:T(4,128)(2,1)S(1)}, bf16[2,4,4096]{2,1,0:T(4,128)(2,1)S(1)}, u32[]{:S(2)}, u32[]{:S(2)}) %collective-permute-start.15) | collective-permute-done | bytes 65568 | tf_op jit(solution)/shard_map/ppermute | solution.py:362
  45.0 0.1 pad_maximum_fusion.2.near_a
  45.1 0.1 collective-permute-start.16
  45.2 1.0 %collective-permute-done.19 = bf16[2,4,4096]{2,1,0:T(4,128)(2,1)S(1)} collective-permute-done((bf16[2,4,4096]{2,1,0:T(4,128)(2,1)S(1)}, bf16[2,4,4096]{2,1,0:T(4,128)(2,1)S(1)}, u32[]{:S(2)}, u32[]{:S(2)}) %collective-permute-start.19) | collective-permute-done | bytes 65568 | tf_op jit(solution)/shard_map/ppermute | solution.py:362
  46.2 0.1 pad_maximum_fusion.3.near_b
  46.2 0.1 collective-permute-start.20
  46.3 0.2 collective-permute-done.16.far_a
  46.5 1.1 %collective-permute-done.20.far_b = bf16[2,2,4,4096]{3,2,1,0:T(4,128)(2,1)S(1)} collective-permute-done((bf16[2,2,4,4096]{3,2,1,0:T(4,128)(2,1)S(1)}, bf16[2,2,4,4096]{3,2,1,0:T(4,128)(2,1)S(1)}, u32[]{:S(2)}, u32[]{:S(2)}) %collective-permute-start.20) | collective-permute-done | bytes 131104 | tf_op jit(solution)/shard_map/ppermute | solution.py:362
  47.7 0.9 %project.1 = (f32[32,512]{1,0:T(8,128)S(1)}, bf16[32,512]{1,0:T(8,128)(2,1)S(1)}) custom-call(bf16[2,2,4,4096]{3,2,1,0:T(4,128)(2,1)S(1)} %pad_maximum_fusion.2.near_a, bf16[2,2,4,4096]{3,2,1,0:T(4,128)(2,1)S(1)} %collective-permute-done.16.far_a, bf16[2,2,4,4096]{3,2,1,0:T(4,128)(2,1)S(1)} %pad_maximum_fusion.3.near_b, ...), custom_call_target="tpu_custom_call" | custom-call | tf_op jit(solution)/shard_map/project/pallas_call | solution.py:329
  48.5 1.6 %collective-permute-start.21 = (bf16[32,512]{1,0:T(8,128)(2,1)S(1)}, bf16[32,512]{1,0:T(8,128)(2,1)S(1)}, u32[]{:S(2)}, u32[]{:S(2)}) collective-permute-start(bf16[32,512]{1,0:T(8,128)(2,1)S(1)} %get-tuple-element.62), channel_id=1, source_target_pairs={{0,1},{1,0},{2,3},{3,2},{4,5},{5,4},{6,7},{7,6},{8,9},{9,8},{10,11... | collective-permute-start | bytes 98312 | tf_op jit(solution)/shard_map/ppermute | solution.py:488
  50.1 2.4 %collective-permute-done.21 = bf16[32,512]{1,0:T(8,128)(2,1)S(1)} collective-permute-done((bf16[32,512]{1,0:T(8,128)(2,1)S(1)}, bf16[32,512]{1,0:T(8,128)(2,1)S(1)}, u32[]{:S(2)}, u32[]{:S(2)}) %collective-permute-start.21) | collective-permute-done | bytes 32800 | tf_op jit(solution)/shard_map/ppermute | solution.py:488
  52.5 0.6 %add_convert_fusion = bf16[32,512]{1,0:T(8,128)(2,1)} fusion(f32[32,512]{1,0:T(8,128)S(1)} %get-tuple-element.61, bf16[32,512]{1,0:T(8,128)(2,1)S(1)} %collective-permute-done.21), kind=kLoop, calls=%fused_computation.7 | loop fusion | flops 49152 | bytes 131072 | tf_op jit(solution)/shard_map/convert_element_type | solution.py:489
  (22 shorter events, 0.2 us)
Async XLA Ops:
  0.0 7.9 %collective-permute-start = (bf16[4,4096]{1,0:T(4,128)(2,1)}, bf16[4,4096]{1,0:T(4,128)(2,1)S(1)}, u32[]{:S(2)}, u32[]{:S(2)}) collective-permute-start(bf16[4,4096]{1,0:T(4,128)(2,1)} %q_hbm.1), channel_id=1, source_target_pairs={{0,24},{2,26},{4,28},{6,30},{8,16},{10,18},{12,20},{14,22},{16,8},... | collective-permute-start | bytes 98312 | tf_op jit(solution)/shard_map/ppermute | solution.py:362
  5.0 5.0 %collective-permute-start.3 = (bf16[4,4096]{1,0:T(4,128)(2,1)}, bf16[4,4096]{1,0:T(4,128)(2,1)S(1)}, u32[]{:S(2)}, u32[]{:S(2)}) collective-permute-start(bf16[4,4096]{1,0:T(4,128)(2,1)} %q_hbm.1), channel_id=1, source_target_pairs={{0,16},{2,18},{4,20},{6,22},{8,24},{10,26},{12,28},{14,30},{16,0},... | collective-permute-start | bytes 98312 | tf_op jit(solution)/shard_map/ppermute | solution.py:362
  5.1 5.0 %collective-permute-start.2 = (bf16[4,4096]{1,0:T(4,128)(2,1)}, bf16[4,4096]{1,0:T(4,128)(2,1)S(1)}, u32[]{:S(2)}, u32[]{:S(2)}) collective-permute-start(bf16[4,4096]{1,0:T(4,128)(2,1)} %q_hbm.1), channel_id=1, source_target_pairs={{0,8},{2,10},{4,12},{6,14},{8,0},{10,2},{12,4},{14,6},{16,24},{18,... | collective-permute-start | bytes 98312 | tf_op jit(solution)/shard_map/ppermute | solution.py:362
  7.9 7.1 %collective-permute-start.1 = (bf16[2,4,4224]{2,1,0:T(4,128)(2,1)S(1)}, bf16[2,4,4224]{2,1,0:T(4,128)(2,1)S(1)}, u32[]{:S(2)}, u32[]{:S(2)}) collective-permute-start(bf16[2,4,4224]{2,1,0:T(4,128)(2,1)S(1)} %line.1), channel_id=1, source_target_pairs={{0,4},{2,6},{4,0},{6,2},{8,12},{10,14},{12,8},{14,10},{16,20},{18,... | collective-permute-start | bytes 202760 | tf_op jit(solution)/shard_map/ppermute | solution.py:362
  10.1 4.9 %collective-permute-start.4 = (bf16[2,4,4096]{2,1,0:T(4,128)(2,1)S(1)}, bf16[2,4,4096]{2,1,0:T(4,128)(2,1)S(1)}, u32[]{:S(2)}, u32[]{:S(2)}) collective-permute-start(bf16[2,4,4096]{2,1,0:T(4,128)(2,1)S(1)} %get-tuple-element.68), channel_id=1, source_target_pairs={{0,4},{2,6},{4,0},{6,2},{8,12},{10,14},{12,8},{14,10},{16,20},{18,... | collective-permute-start | bytes 196616 | tf_op jit(solution)/shard_map/ppermute | solution.py:362
  15.1 2.5 %collective-permute-start.5 = (bf16[2,2,4,4224]{3,2,1,0:T(4,128)(2,1)S(1)}, bf16[2,2,4,4224]{3,2,1,0:T(4,128)(2,1)S(1)}, u32[]{:S(2)}, u32[]{:S(2)}) collective-permute-start(bf16[2,2,4,4224]{3,2,1,0:T(4,128)(2,1)S(1)} %pad_maximum_fusion), channel_id=1, source_target_pairs={{0,2},{2,0},{4,6},{6,4},{8,10},{10,8},{12,14},{14,12},{16,18},{18,... | collective-permute-start | bytes 405512 | tf_op jit(solution)/shard_map/ppermute | solution.py:362
  15.3 2.3 %collective-permute-start.6 = (bf16[2,2,4,4096]{3,2,1,0:T(4,128)(2,1)S(1)}, bf16[2,2,4,4096]{3,2,1,0:T(4,128)(2,1)S(1)}, u32[]{:S(2)}, u32[]{:S(2)}) collective-permute-start(bf16[2,2,4,4096]{3,2,1,0:T(4,128)(2,1)S(1)} %pad_maximum_fusion.1), channel_id=1, source_target_pairs={{0,2},{2,0},{4,6},{6,4},{8,10},{10,8},{12,14},{14,12},{16,18},{18,... | collective-permute-start | bytes 393224 | tf_op jit(solution)/shard_map/ppermute | solution.py:362
  17.6 16.8 %copy-start.1 = (bf16[4,512]{1,0:T(4,128)(2,1)S(1)}, bf16[4,512]{1,0:T(4,128)(2,1)}, u32[]{:S(2)}) copy-start(bf16[4,512]{1,0:T(4,128)(2,1)} %nk_ref.1) | copy-start | bytes 12292
  17.6 16.7 %copy-start.2 = (bf16[4,512]{1,0:T(4,128)(2,1)S(1)}, bf16[4,512]{1,0:T(4,128)(2,1)}, u32[]{:S(2)}) copy-start(bf16[4,512]{1,0:T(4,128)(2,1)} %nv_ref.1) | copy-start | bytes 12292
  17.7 30.0 %copy-start = (bf16[4096,512]{1,0:T(8,128)(2,1)S(1)}, bf16[4096,512]{1,0:T(8,128)(2,1)}, u32[]{:S(2)}) copy-start(bf16[4096,512]{1,0:T(8,128)(2,1)} %w_ref.1) | copy-start | bytes 12582916
  19.7 1.4 %collective-permute-start.8 = (bf16[16,4224]{1,0:T(8,128)(2,1)S(1)}, bf16[16,4224]{1,0:T(8,128)(2,1)S(1)}, u32[]{:S(2)}, u32[]{:S(2)}) collective-permute-start(bf16[16,4224]{1,0:T(8,128)(2,1)S(1)} %get-tuple-element.53), channel_id=1, source_target_pairs={{0,2},{2,0},{4,6},{6,4},{8,10},{10,8},{12,14},{14,12},{16,18},{18,... | collective-permute-start | bytes 405512 | tf_op jit(solution)/shard_map/ppermute | solution.py:362
  19.8 3.8 %collective-permute-start.7 = (bf16[16,4224]{1,0:T(8,128)(2,1)S(1)}, bf16[16,4224]{1,0:T(8,128)(2,1)S(1)}, u32[]{:S(2)}, u32[]{:S(2)}) collective-permute-start(bf16[16,4224]{1,0:T(8,128)(2,1)S(1)} %get-tuple-element.50), channel_id=1, source_target_pairs={{0,2},{2,0},{4,6},{6,4},{8,10},{10,8},{12,14},{14,12},{16,18},{18,... | collective-permute-start | bytes 405512 | tf_op jit(solution)/shard_map/ppermute | solution.py:362
  21.5 5.0 %collective-permute-start.9 = (bf16[2,4,4224]{2,1,0:T(4,128)(2,1)S(1)}, bf16[2,4,4224]{2,1,0:T(4,128)(2,1)S(1)}, u32[]{:S(2)}, u32[]{:S(2)}) collective-permute-start(bf16[2,4,4224]{2,1,0:T(4,128)(2,1)S(1)} %get-tuple-element.54), channel_id=1, source_target_pairs={{0,4},{2,6},{4,0},{6,2},{8,12},{10,14},{12,8},{14,10},{16,20},{18,... | collective-permute-start | bytes 202760 | tf_op jit(solution)/shard_map/ppermute | solution.py:362
  22.5 7.1 %collective-permute-start.12 = (bf16[2,4,4224]{2,1,0:T(4,128)(2,1)S(1)}, bf16[2,4,4224]{2,1,0:T(4,128)(2,1)S(1)}, u32[]{:S(2)}, u32[]{:S(2)}) collective-permute-start(bf16[2,4,4224]{2,1,0:T(4,128)(2,1)S(1)} %get-tuple-element.58), channel_id=1, source_target_pairs={{0,4},{2,6},{4,0},{6,2},{8,12},{10,14},{12,8},{14,10},{16,20},{18,... | collective-permute-start | bytes 202760 | tf_op jit(solution)/shard_map/ppermute | solution.py:362
  26.7 5.8 %collective-permute-start.10 = (bf16[4,4224]{1,0:T(4,128)(2,1)S(1)}, bf16[4,4224]{1,0:T(4,128)(2,1)S(1)}, u32[]{:S(2)}, u32[]{:S(2)}) collective-permute-start(bf16[4,4224]{1,0:T(4,128)(2,1)S(1)} %get-tuple-element.55), channel_id=1, source_target_pairs={{0,24},{2,26},{4,28},{6,30},{8,16},{10,18},{12,20},{14,22},{16,8},... | collective-permute-start | bytes 101384 | tf_op jit(solution)/shard_map/ppermute | solution.py:362
  29.5 4.8 %collective-permute-start.11 = (bf16[4,4224]{1,0:T(4,128)(2,1)S(1)}, bf16[4,4224]{1,0:T(4,128)(2,1)S(1)}, u32[]{:S(2)}, u32[]{:S(2)}) collective-permute-start(bf16[4,4224]{1,0:T(4,128)(2,1)S(1)} %get-tuple-element.56), channel_id=1, source_target_pairs={{0,16},{2,18},{4,20},{6,22},{8,24},{10,26},{12,28},{14,30},{16,0},... | collective-permute-start | bytes 101384 | tf_op jit(solution)/shard_map/ppermute | solution.py:362
  29.8 4.5 %collective-permute-start.13 = (bf16[4,4224]{1,0:T(4,128)(2,1)S(1)}, bf16[4,4224]{1,0:T(4,128)(2,1)S(1)}, u32[]{:S(2)}, u32[]{:S(2)}) collective-permute-start(bf16[4,4224]{1,0:T(4,128)(2,1)S(1)} %get-tuple-element.59), channel_id=1, source_target_pairs={{0,8},{2,10},{4,12},{6,14},{8,0},{10,2},{12,4},{14,6},{16,24},{18,... | collective-permute-start | bytes 101384 | tf_op jit(solution)/shard_map/ppermute | solution.py:362
  34.9 5.8 %collective-permute-start.14 = (bf16[4,4096]{1,0:T(4,128)(2,1)S(1)}, bf16[4,4096]{1,0:T(4,128)(2,1)S(1)}, u32[]{:S(2)}, u32[]{:S(2)}) collective-permute-start(bf16[4,4096]{1,0:T(4,128)(2,1)S(1)} %finish.1), channel_id=1, source_target_pairs={{0,24},{2,26},{4,28},{6,30},{8,16},{10,18},{12,20},{14,22},{16,8},... | collective-permute-start | bytes 98312 | tf_op jit(solution)/shard_map/ppermute | solution.py:362
  36.9 4.9 %collective-permute-start.18 = (bf16[4,4096]{1,0:T(4,128)(2,1)S(1)}, bf16[4,4096]{1,0:T(4,128)(2,1)S(1)}, u32[]{:S(2)}, u32[]{:S(2)}) collective-permute-start(bf16[4,4096]{1,0:T(4,128)(2,1)S(1)} %finish.1), channel_id=1, source_target_pairs={{0,16},{2,18},{4,20},{6,22},{8,24},{10,26},{12,28},{14,30},{16,0},... | collective-permute-start | bytes 98312 | tf_op jit(solution)/shard_map/ppermute | solution.py:362
  37.5 4.3 %collective-permute-start.17 = (bf16[4,4096]{1,0:T(4,128)(2,1)S(1)}, bf16[4,4096]{1,0:T(4,128)(2,1)S(1)}, u32[]{:S(2)}, u32[]{:S(2)}) collective-permute-start(bf16[4,4096]{1,0:T(4,128)(2,1)S(1)} %finish.1), channel_id=1, source_target_pairs={{0,8},{2,10},{4,12},{6,14},{8,0},{10,2},{12,4},{14,6},{16,24},{18,... | collective-permute-start | bytes 98312 | tf_op jit(solution)/shard_map/ppermute | solution.py:362
  40.7 4.3 %collective-permute-start.15 = (bf16[2,4,4096]{2,1,0:T(4,128)(2,1)S(1)}, bf16[2,4,4096]{2,1,0:T(4,128)(2,1)S(1)}, u32[]{:S(2)}, u32[]{:S(2)}) collective-permute-start(bf16[2,4,4096]{2,1,0:T(4,128)(2,1)S(1)} %get-tuple-element.66), channel_id=1, source_target_pairs={{0,4},{2,6},{4,0},{6,2},{8,12},{10,14},{12,8},{14,10},{16,20},{18,... | collective-permute-start | bytes 196616 | tf_op jit(solution)/shard_map/ppermute | solution.py:362
  41.8 4.3 %collective-permute-start.19 = (bf16[2,4,4096]{2,1,0:T(4,128)(2,1)S(1)}, bf16[2,4,4096]{2,1,0:T(4,128)(2,1)S(1)}, u32[]{:S(2)}, u32[]{:S(2)}) collective-permute-start(bf16[2,4,4096]{2,1,0:T(4,128)(2,1)S(1)} %get-tuple-element.64), channel_id=1, source_target_pairs={{0,4},{2,6},{4,0},{6,2},{8,12},{10,14},{12,8},{14,10},{16,20},{18,... | collective-permute-start | bytes 196616 | tf_op jit(solution)/shard_map/ppermute | solution.py:362
  45.1 1.4 %collective-permute-start.16 = (bf16[2,2,4,4096]{3,2,1,0:T(4,128)(2,1)S(1)}, bf16[2,2,4,4096]{3,2,1,0:T(4,128)(2,1)S(1)}, u32[]{:S(2)}, u32[]{:S(2)}) collective-permute-start(bf16[2,2,4,4096]{3,2,1,0:T(4,128)(2,1)S(1)} %pad_maximum_fusion.2.near_a), channel_id=1, source_target_pairs={{0,2},{2,0},{4,6},{6,4},{8,10},{10,8},{12,14},{14,12},{16,18},{18,... | collective-permute-start | bytes 393224 | tf_op jit(solution)/shard_map/ppermute | solution.py:362
  46.2 1.4 %collective-permute-start.20 = (bf16[2,2,4,4096]{3,2,1,0:T(4,128)(2,1)S(1)}, bf16[2,2,4,4096]{3,2,1,0:T(4,128)(2,1)S(1)}, u32[]{:S(2)}, u32[]{:S(2)}) collective-permute-start(bf16[2,2,4,4096]{3,2,1,0:T(4,128)(2,1)S(1)} %pad_maximum_fusion.3.near_b), channel_id=1, source_target_pairs={{0,2},{2,0},{4,6},{6,4},{8,10},{10,8},{12,14},{14,12},{16,18},{18,... | collective-permute-start | bytes 393224 | tf_op jit(solution)/shard_map/ppermute | solution.py:362
  48.5 4.0 %collective-permute-start.21 = (bf16[32,512]{1,0:T(8,128)(2,1)S(1)}, bf16[32,512]{1,0:T(8,128)(2,1)S(1)}, u32[]{:S(2)}, u32[]{:S(2)}) collective-permute-start(bf16[32,512]{1,0:T(8,128)(2,1)S(1)} %get-tuple-element.62), channel_id=1, source_target_pairs={{0,1},{1,0},{2,3},{3,2},{4,5},{5,4},{6,7},{7,6},{8,9},{9,8},{10,11... | collective-permute-start | bytes 98312 | tf_op jit(solution)/shard_map/ppermute | solution.py:488

commit v3 on v2

--- a/solution.py
+++ b/solution.py
@@ -31,29 +31,36 @@
 
 
 def line_order(requests):
-    return [requests - 1, 0, *range(1, requests - 1)]
+    return list(range(requests))[::-1]
 
 
 def line_kernel(tail_ref, *refs):
     *pieces, out_ref = refs
     width = pieces[0].shape[1]
-    for n, x in enumerate(pieces):
-        out_ref[n, :, :width] = x[...]
-        out_ref[n, :, width:] = tail_ref[...]
+    out_ref[:, :width] = jnp.concatenate([x[...] for x in pieces], axis=0)
+    out_ref[:, width:] = jnp.concatenate([tail_ref[...]] * len(pieces), axis=0)
 
 
 def load_private_kernel(
     q_hbm, par_hbm, cnt_hbm, ck_hbm, cv_hbm,
     q_ref, tail_ref, lim_ref, ck_ref, cv_ref, par_ref, cnt_ref, sems, old_sems,
 ):
+    heads = ck_ref.shape[0]
+    olds = ck_hbm.shape[0]
     copies = [
         pltpu.make_async_copy(src, dst, sems.at[n])
         for n, (src, dst) in enumerate(((q_hbm, q_ref), (par_hbm, par_ref), (cnt_hbm, cnt_ref)))
-    ] + [
-        pltpu.make_async_copy(src.at[o], dst.at[o], old_sems.at[n, o])
-        for n, (src, dst) in enumerate(((ck_hbm, ck_ref), (cv_hbm, cv_ref)))
-        for o in range(ck_ref.shape[0])
     ]
+    for k in range(heads):
+        for n, (src, dst) in enumerate(((ck_hbm, ck_ref), (cv_hbm, cv_ref))):
+            for o in range(olds):
+                copies.append(
+                    pltpu.make_async_copy(
+                        src.at[o, :, pl.ds(k * HD, HD)],
+                        dst.at[k, :, pl.ds(o * HD, HD)],
+                        old_sems.at[n, k, o],
+                    )
+                )
     for x in copies:
         x.start()
     for x in copies[:3]:
@@ -65,7 +72,7 @@
     tail_ref[...] = parent.astype(f32).astype(bf16)
     lane = lax.broadcasted_iota(jnp.int32, lim_ref.shape, 1)
     limit = jnp.zeros(lim_ref.shape, jnp.int32)
-    for o in range(ck_ref.shape[0]):
+    for o in range(olds):
         limit = jnp.where(lane == o, cnt_ref[o] * BLOCK_LEN, limit)
     lim_ref[...] = limit
     for x in copies[3:]:
@@ -73,11 +80,18 @@
 
 
 def load_prompt_kernel(group, pk_hbm, pv_hbm, pk_ref, pv_ref, sems):
+    heads, pairs, _, _ = pk_ref.shape
     mine = lax.axis_index("beam") // group
+    order = line_order(2 * pairs)
     copies = [
-        pltpu.make_async_copy(src.at[mine ^ t], dst.at[at], sems.at[n, at])
+        pltpu.make_async_copy(
+            src.at[mine ^ t, :, pl.ds(k * HD, HD)],
+            dst.at[k, at // 2, :, pl.ds(at % 2 * HD, HD)],
+            sems.at[n, k, at],
+        )
+        for k in range(heads)
         for n, (src, dst) in enumerate(((pk_hbm, pk_ref), (pv_hbm, pv_ref)))
-        for at, t in enumerate(line_order(pk_ref.shape[0]))
+        for at, t in enumerate(order)
     ]
     for x in copies:
         x.start()
@@ -85,29 +99,42 @@
         x.wait()
 
 
-def attend_kernel(qa_ref, qb_ref, pk_ref, pv_ref, lim_ref, ck_ref, cv_ref, *refs):
+def attend_kernel(other, q_ref, pk_ref, pv_ref, lim_ref, ck_ref, cv_ref, *refs):
     *outs, s_ref, p_ref, cs_ref, cp_ref = refs
-    count, half, beams, total = qa_ref.shape
-    requests, length, width = pk_ref.shape
+    count = q_ref.shape[0]
+    pieces = [q_ref.at[r] for r in range(count)]
+    total = q_ref.shape[2]
+    heads = (total - STATS) // (QPK * HD)
+    if other:
+        requests, length, _ = pk_ref.shape
+        olds, span, _ = ck_ref.shape
+    else:
+        _, pairs, length, _ = pk_ref.shape
+        requests = 2 * pairs
+        _, span, olds = ck_ref.shape
+        olds = olds // HD
     pairs = requests // 2
-    heads = width // HD
-    olds, span, _ = ck_ref.shape
+    beams = q_ref.shape[1] // requests
     block = count * beams
     stride = heads * QPK
     rows = QPK * block
-    own_at = line_order(requests).index(0)
-    pieces = [
-        [qa_ref.at[r, n] for n in range(half)] + [qb_ref.at[r, n] for n in range(half)]
-        for r in range(count)
-    ]
-
-    def beside(ref, k, places):
-        return jnp.concatenate([ref[at, :, k * HD : (k + 1) * HD] for at in places], axis=1)
-
     me = lax.axis_index("beam")
-
-    parent = jnp.concatenate([x[own_at][:, total - STATS :].astype(f32) for x in pieces], axis=0)
-    parent = jnp.concatenate([parent] * QPK, axis=0).astype(jnp.int32) - me * olds
+    mine = me // (BEAM_WIDTH // beams)
+    order = line_order(requests)
+
+    def prompt(ref, k, u):
+        if not other:
+            return ref[k, u]
+        both = [ref[mine ^ order[2 * u + n], :, k * HD : (k + 1) * HD] for n in range(2)]
+        return jnp.concatenate(both, axis=1)
+
+    def private(ref, k):
+        if not other:
+            return ref[k]
+        return jnp.concatenate([ref[o, :, k * HD : (k + 1) * HD] for o in range(olds)], axis=1)
+
+    parent = jnp.concatenate([x[:, total - STATS :].astype(f32)[:beams] for x in pieces], axis=0)
+    parent = jnp.concatenate([parent] * QPK, axis=0).astype(jnp.int32) - (me ^ other) * olds
     column = parent[:, :1]
     local = (column >= 0) & (column < olds)
     limit = jnp.zeros((rows, 1), jnp.int32)
@@ -119,15 +146,11 @@
     kept = {}
 
     def scores(k):
+        tiles = [
+            x[:, (k * QPK + i) * HD : (k * QPK + i + 1) * HD] for i in range(QPK) for x in pieces
+        ]
         q = [
-            jnp.concatenate(
-                [
-                    x[t][:, (k * QPK + i) * HD : (k * QPK + i + 1) * HD]
-                    for i in range(QPK)
-                    for x in pieces
-                ],
-                axis=0,
-            )
+            jnp.concatenate([x[t * beams : (t + 1) * beams] for x in tiles], axis=0)
             for t in range(requests)
         ]
         for u in range(pairs):
@@ -138,11 +161,9 @@
                 ],
                 axis=0,
             )
-            s_ref[k, 2 * u * rows : 2 * (u + 1) * rows] = dot(
-                both, beside(pk_ref, k, (2 * u, 2 * u + 1)), 1, 1
-            )
-        chosen = jnp.concatenate([jnp.where(parent == o, q[own_at], blank) for o in range(olds)], axis=1)
-        cs_ref[k] = dot(chosen, beside(ck_ref, k, range(olds)), 1, 1)
+            s_ref[k, 2 * u * rows : 2 * (u + 1) * rows] = dot(both, prompt(pk_ref, k, u), 1, 1)
+        chosen = jnp.concatenate([jnp.where(parent == o, q[-1], blank) for o in range(olds)], axis=1)
+        cs_ref[k] = dot(chosen, private(ck_ref, k), 1, 1)
 
     def weigh(k):
         p, top, den = soft(s_ref[k])
@@ -156,14 +177,9 @@
         tops, dens, ctop, cden = kept.pop(k)
         nums = []
         for u in range(pairs):
-            both = dot(
-                p_ref[k, 2 * u * rows : 2 * (u + 1) * rows],
-                beside(pv_ref, k, (2 * u, 2 * u + 1)),
-                1,
-                0,
-            )
+            both = dot(p_ref[k, 2 * u * rows : 2 * (u + 1) * rows], prompt(pv_ref, k, u), 1, 0)
             nums += [both[:rows, :HD], both[rows:, HD:]]
-        every = dot(cp_ref[k], beside(cv_ref, k, range(olds)), 1, 0)
+        every = dot(cp_ref[k], private(cv_ref, k), 1, 0)
         cnum = every[:, :HD]
         for o in range(1, olds):
             cnum = jnp.where(parent == o, every[:, o * HD : (o + 1) * HD], cnum)
@@ -171,7 +187,7 @@
         for t in range(requests):
             part = slice(t * rows, (t + 1) * rows)
             num, top, den = nums[t], tops[part], dens[part]
-            if t == own_at:
+            if t == requests - 1:
                 both = jnp.where(local, jnp.maximum(top, ctop), top)
                 a = jnp.exp(top - both)
                 e = jnp.where(local, jnp.exp(jnp.where(local, ctop, both) - both), 0.0)
@@ -251,10 +267,8 @@
     store(slice(total - STATS, total), pack_stats(again, count))
 
 
-def core_kernel(kept_ref, came_ref, a_ref, b_ref):
-    half = a_ref.shape[0]
-    outs = {2 * half - 1 - n: ref.at[n % half] for n, ref in enumerate([a_ref] * half + [b_ref] * half)}
-    merge(kept_ref, came_ref, [outs[t] for t in line_order(2 * half)])
+def core_kernel(kept_ref, came_ref, *outs):
+    merge(kept_ref, came_ref, [out.at[n] for out in outs for n in range(out.shape[0])])
 
 
 def plane_kernel(kept_ref, came_ref, *outs):
@@ -296,7 +310,8 @@
     requests, group = rows_ref.shape[:2]
     me, side = lax.axis_index("beam"), lax.axis_index("head")
     mine, spot = me // group, me % group
-    order = [0, requests - 1] + list(range(1, requests - 1))
+    order = line_order(requests)
+    order = order[-1:] + order[:1] + order[-2:0:-1]
     for first, refs in ((0, (near_a, far_a)), (requests // 2, (near_b, far_b))):
         for core, ref in enumerate(refs):
             for x in range(2):
@@ -366,10 +381,11 @@
     length, span = prompt_keys.shape[1], private_keys.shape[1]
     line = jax.ShapeDtypeStruct((rows, total), bf16)
     order = line_order(requests)
-    middle = requests // 2
-    came = {t: swap(queries, t * group) for t in [requests - 1, *range(1, requests - 1)]}
-    prompt = jax.ShapeDtypeStruct(prompt_keys.shape, bf16)
-    private = jax.ShapeDtypeStruct(private_keys.shape, bf16)
+    others = order[:-1]
+    came = [swap(queries, t * group) for t in others]
+    prompt = jax.ShapeDtypeStruct((heads, requests // 2, length, 2 * HD), bf16)
+    private = jax.ShapeDtypeStruct((heads, span, beams * HD), bf16)
+    stored = (swap(private_keys, 1), swap(private_values, 1))
     own, parent_tail, *olds = call(
         load_private_kernel,
         "load_private",
@@ -390,22 +406,14 @@
             pltpu.SMEM((beams,), jnp.int32),
             pltpu.SMEM((beams,), jnp.int32),
             pltpu.SemaphoreType.DMA((3,)),
-            pltpu.SemaphoreType.DMA((2, beams)),
+            pltpu.SemaphoreType.DMA((2, heads, beams)),
         ],
         vmem=10,
-        cost=8 * 2**20,
-    )
-    came[requests - 1], parent_tail = lax.optimization_barrier((came[requests - 1], parent_tail))
-    came[0] = own
-    asked_a = call(
-        line_kernel,
-        "line",
-        jax.ShapeDtypeStruct((middle, beams, total), bf16),
-        parent_tail,
-        *(came[t] for t in order[:middle]),
-    )
-    asked_b = jnp.stack([came[t] for t in order[middle:]])
-    prompt_keys, prompt_values, _ = lax.optimization_barrier((prompt_keys, prompt_values, asked_b))
+        cost=2**26,
+    )
+    *came, parent_tail = lax.optimization_barrier((*came, parent_tail))
+    asked = call(line_kernel, "line", line, parent_tail, *came, own)
+    prompt_keys, prompt_values, _ = lax.optimization_barrier((prompt_keys, prompt_values, asked))
     prompts = call(
         functools.partial(load_prompt_kernel, group),
         "load_prompt",
@@ -413,20 +421,20 @@
         prompt_keys,
         prompt_values,
         far=(0, 1),
-        scratch=[pltpu.SemaphoreType.DMA((2, requests))],
+        scratch=[pltpu.SemaphoreType.DMA((2, heads, requests))],
         vmem=10,
-        cost=4 * 2**20,
+        cost=2**26,
     )
     caches = (*prompts, *olds)
-
-    def attend(asked_a, asked_b, name):
-        many = asked_a.shape[0] * beams * QPK
+    stored = (swap(prompt_keys, 1), swap(prompt_values, 1), swap(olds[0], 1), *stored)
+
+    def attend(asked, name, caches, other=0):
+        many = asked.shape[0] * beams * QPK
         return call(
-            attend_kernel,
+            functools.partial(attend_kernel, other),
             name,
-            (line,) * asked_a.shape[0],
-            asked_a,
-            asked_b,
+            (line,) * asked.shape[0],
+            asked,
             *caches,
             scratch=[
                 pltpu.VMEM((heads, requests * many, length), f32),
@@ -435,28 +443,26 @@
                 pltpu.VMEM((heads, many, span), bf16),
             ],
             vmem=24,
+            cost=2**26,
         )
 
-    other_a, other_b = swap(asked_a, 2), swap(asked_b, 2)
-    (keep0,) = attend(asked_a[None], asked_b[None], "attend_own")
-    other_a, other_b, keep0 = lax.optimization_barrier((other_a, other_b, keep0))
-    far_a = swap(jnp.stack([asked_a, other_a]), 1)
-    far_b = swap(jnp.stack([asked_b, other_b]), 1)
-    (keep2,) = attend(other_a[None], other_b[None], "attend_side")
-    far_a, far_b, keep2 = lax.optimization_barrier((far_a, far_b, keep2))
-    far_own, far_side = attend(far_a, far_b, "attend_far")
+    other = swap(asked, 2)
+    (own_here,) = attend(asked[None], "attend_own", caches)
+    other, own_here = lax.optimization_barrier((other, own_here))
+    (side_here,) = attend(other[None], "attend_side", caches)
+    (side_there,) = attend(other[None], "attend_side_other", stored, 1)
     half = jax.ShapeDtypeStruct((requests // 2, beams, total), bf16)
-    send_a, send_b = call(core_kernel, "side_merge", (half, half), keep2, swap(far_side, 1))
-    keep_a, keep_b = call(core_kernel, "own_merge", (half, half), keep0, swap(far_own, 1))
+    send_a, send_b = call(core_kernel, "side_merge", (half, half), side_here, side_there)
+    asked, _ = lax.optimization_barrier((asked, send_a))
+    (own_there,) = attend(asked[None], "attend_own_other", stored, 1)
+    keep_a, keep_b = call(core_kernel, "own_merge", (half, half), own_here, own_there)
     piece = jax.ShapeDtypeStruct((beams, total), bf16)
     parts = []
     for keep, send in ((keep_a, send_a), (keep_b, send_b)):
         parts += call(
             plane_kernel, "plane_merge", (piece,) * (requests // 2), keep, swap(send, 2)
         )
-    parts = [
-        swap(x, t * group) if t else x for t, x in zip(range(requests - 1, -1, -1), parts)
-    ]
+    parts = [swap(x, t * group) if t else x for t, x in zip(order, parts)]
     attended = call(
         finish_kernel,
         "finish",
@@ -467,9 +473,7 @@
         *parts,
     )
     if sides == 2:
-        line = [attended] + [
-            swap(attended, t * group) for t in [requests - 1, *range(1, requests - 1)]
-        ]
+        line = [attended] + [swap(attended, t * group) for t in others[:1] + others[:0:-1]]
         halves = []
         for pieces in (line[: requests // 2], line[requests // 2 :]):
             near = jnp.stack(pieces)

time: 53.3 us -> 52.7 us (0.989)
  Pallas kernels: 11.9 us -> 13.9 us
  waiting for transfers between devices: 14.7 us -> 13.3 us
  starting transfers between devices: 25.1 us -> 24 us
    pallas_call x12 -> x13, Pallas kernels: 11.9 us -> 13.9 us  [call(): pl.pallas_call(kernel, out_shape=out_shape, in_specs=whole_blocks(len(arg...]
    ppermute x21, waiting for transfers between devices: 12.3 us -> 11 us  [swap(): return lax.ppermute(x, 'beam', [(i, i ^ with_bit) for i in range(devices)])]
    ppermute x21, starting transfers between devices: 23.5 us -> 22.4 us  [swap(): return lax.ppermute(x, 'beam', [(i, i ^ with_bit) for i in range(devices)])]
  transfers between devices with their start and end apart: 22 -> 22, of which waited for: 11 -> 10; matrix products, arithmetic and copies ran while one was open for 1% -> 1% of each run, Pallas kernels for 16% -> 20%
where the time goes in v3:
time: 52.7 us; the launch traced here: 52.5 us
  starting transfers between devices  24 us (46%)
  Pallas kernels  13.9 us (26%)
  waiting for transfers between devices  13.3 us (25%)
  other arithmetic  0.92 us (2%)
    ppermute x21, starting transfers between devices, swap(): return lax.ppermute(x, 'beam', [(i, i ^ with_bit) for i in range(devices)])  22.4 us
    pallas_call x13, Pallas kernels, call(): pl.pallas_call(kernel, out_shape=out_shape, in_specs=whole_blocks(len(arg...  13.9 us
    ppermute x21, waiting for transfers between devices, swap(): return lax.ppermute(x, 'beam', [(i, i ^ with_bit) for i in range(devices)])  11 us
    ppermute x1, waiting for transfers between devices, per_device(): came = lax.ppermute(send, 'head', [(0, 1), (1, 0)])  2.39 us
    ppermute x1, starting transfers between devices, per_device(): came = lax.ppermute(send, 'head', [(0, 1), (1, 0)])  1.59 us
  transfers between devices with their start and end apart: 22, of which 10 were waited for; matrix products, arithmetic and copies ran while one was open for 1% of the time, Pallas kernels for 20%

profile of v3, /device:TPU:0, one launch (start us, length us, event | category | flops | bytes accessed | tf_op | source)
XLA Modules:
  0.0 52.5 jit_solution(6269988384745103339)
XLA Ops:
  0.0 0.5 collective-permute-start.7
  0.5 0.1 collective-permute-start.8
  0.5 5.0 %collective-permute-start = (bf16[4,4096]{1,0:T(4,128)(2,1)}, bf16[4,4096]{1,0:T(4,128)(2,1)S(1)}, u32[]{:S(2)}, u32[]{:S(2)}) collective-permute-start(bf16[4,4096]{1,0:T(4,128)(2,1)} %q_hbm.1), channel_id=1, source_target_pairs={{0,24},{2,26},{4,28},{6,30},{8,16},{10,18},{12,20},{14,22},{16,8},... | collective-permute-start | bytes 98312 | tf_op jit(solution)/shard_map/ppermute | solution.py:377
  5.6 0.0 collective-permute-start.1
  5.6 0.6 %collective-permute-start.2 = (bf16[4,4096]{1,0:T(4,128)(2,1)}, bf16[4,4096]{1,0:T(4,128)(2,1)S(1)}, u32[]{:S(2)}, u32[]{:S(2)}) collective-permute-start(bf16[4,4096]{1,0:T(4,128)(2,1)} %q_hbm.1), channel_id=1, source_target_pairs={{0,8},{2,10},{4,12},{6,14},{8,0},{10,2},{12,4},{14,6},{16,24},{18,... | collective-permute-start | bytes 98312 | tf_op jit(solution)/shard_map/ppermute | solution.py:377
  6.1 2.7 %load_private.1 = (bf16[4,4096]{1,0:T(4,128)(2,1)S(1)}, bf16[4,128]{1,0:T(4,128)(2,1)S(1)}, s32[8,128]{1,0:T(8,128)S(1)}, bf16[4,512,512]{2,1,0:T(8,128)(2,1)S(1)}, bf16[4,512,512]{2,1,0:T(8,128)(2,1)S(1)}) custom-call(bf16[4,4096]{1,0:T(4,128)(2,1)} %q_hbm.1, s32[4]{0:T(128)} %par_hbm.1, s32[4]{0:T(128)} %cnt_hbm.1, bf16[4,512,512]{2,1,0:T(8,128)(2,1)} %ck_hbm.1, ...), custom_call_target="tpu_custom_call" | custom-call | flops 67108864 | bytes 67108864 | tf_op jit(solution)/shard_map/load_private/pallas_call | solution.py:344
  8.8 1.8 %collective-permute-done.1.refs_1_ = bf16[4,4096]{1,0:T(4,128)(2,1)S(1)} collective-permute-done((bf16[4,4096]{1,0:T(4,128)(2,1)}, bf16[4,4096]{1,0:T(4,128)(2,1)S(1)}, u32[]{:S(2)}, u32[]{:S(2)}) %collective-permute-start.1) | collective-permute-done | bytes 32800 | tf_op jit(solution)/shard_map/ppermute | solution.py:377
  10.7 0.1 collective-permute-start.4
  10.7 0.5 collective-permute-start.5
  11.2 1.5 %collective-permute-start.3 = (bf16[16,4224]{1,0:T(8,128)(2,1)S(1)}, bf16[16,4224]{1,0:T(8,128)(2,1)S(1)}, u32[]{:S(2)}, u32[]{:S(2)}) collective-permute-start(bf16[16,4224]{1,0:T(8,128)(2,1)S(1)} %line.1), channel_id=1, source_target_pairs={{0,4},{2,6},{4,0},{6,2},{8,12},{10,14},{12,8},{14,10},{16,20},{18,... | collective-permute-start | bytes 405512 | tf_op jit(solution)/shard_map/ppermute | solution.py:377
  12.7 1.9 %load_prompt.1 = (bf16[4,2,256,256]{3,2,1,0:T(8,128)(2,1)S(1)}, bf16[4,2,256,256]{3,2,1,0:T(8,128)(2,1)S(1)}) custom-call(bf16[4,256,512]{2,1,0:T(8,128)(2,1)} %pk_hbm, bf16[4,256,512]{2,1,0:T(8,128)(2,1)} %pv_hbm), custom_call_target="tpu_custom_call" | custom-call | flops 67108864 | bytes 67108864 | tf_op jit(solution)/shard_map/load_prompt/pallas_call | solution.py:344
  14.6 1.6 %attend_own.1.kept_ref = bf16[16,4224]{1,0:T(8,128)(2,1)S(1)} custom-call(bf16[1,16,4224]{2,1,0:T(8,128)(2,1)S(1)} %bitcast.13, bf16[4,2,256,256]{3,2,1,0:T(8,128)(2,1)S(1)} %get-tuple-element.39.pk_ref, bf16[4,2,256,256]{3,2,1,0:T(8,128)(2,1)S(1)} %get-tuple-element.40.pv_ref, s32[8,128]{1,0:T(8,128)S(1)} %get-tuple-element.41.lim_ref, ...), custom_call_target="tpu_custom_call" | custom-call | flops 67108864 | bytes 67108864 | tf_op jit(solution)/shard_map/attend_own/pallas_call | solution.py:344
  16.3 0.5 %collective-permute-done.3 = bf16[16,4224]{1,0:T(8,128)(2,1)S(1)} collective-permute-done((bf16[16,4224]{1,0:T(8,128)(2,1)S(1)}, bf16[16,4224]{1,0:T(8,128)(2,1)S(1)}, u32[]{:S(2)}, u32[]{:S(2)}) %collective-permute-start.3) | collective-permute-done | bytes 135200 | tf_op jit(solution)/shard_map/ppermute | solution.py:377
  16.8 1.6 %attend_side.1.kept_ref = bf16[16,4224]{1,0:T(8,128)(2,1)S(1)} custom-call(bf16[1,16,4224]{2,1,0:T(8,128)(2,1)S(1)} %bitcast.15, bf16[4,2,256,256]{3,2,1,0:T(8,128)(2,1)S(1)} %get-tuple-element.39.pk_ref, bf16[4,2,256,256]{3,2,1,0:T(8,128)(2,1)S(1)} %get-tuple-element.40.pv_ref, s32[8,128]{1,0:T(8,128)S(1)} %get-tuple-element.41.lim_ref, ...), custom_call_target="tpu_custom_call" | custom-call | flops 67108864 | bytes 67108864 | tf_op jit(solution)/shard_map/attend_side/pallas_call | solution.py:344
  18.5 1.7 %attend_side_other.1.came_ref = bf16[16,4224]{1,0:T(8,128)(2,1)S(1)} custom-call(bf16[1,16,4224]{2,1,0:T(8,128)(2,1)S(1)} %bitcast.16, bf16[4,256,512]{2,1,0:T(8,128)(2,1)S(1)} %collective-permute-done.4.pk_ref, bf16[4,256,512]{2,1,0:T(8,128)(2,1)S(1)} %collective-permute-done.5.pv_ref, s32[8,128]{1,0:T(8,128)S(1)} %collective-permute-done.6.lim_ref, ...), custom_call_target="tpu_custom_call" | custom-call | flops 67108864 | bytes 67108864 | tf_op jit(solution)/shard_map/attend_side_other/pallas_call | solution.py:344
  20.3 0.4 side_merge.1
  20.6 1.6 %collective-permute-start.9 = (bf16[2,4,4224]{2,1,0:T(4,128)(2,1)S(1)}, bf16[2,4,4224]{2,1,0:T(4,128)(2,1)S(1)}, u32[]{:S(2)}, u32[]{:S(2)}) collective-permute-start(bf16[2,4,4224]{2,1,0:T(4,128)(2,1)S(1)} %get-tuple-element.46), channel_id=1, source_target_pairs={{0,4},{2,6},{4,0},{6,2},{8,12},{10,14},{12,8},{14,10},{16,20},{18,... | collective-permute-start | bytes 202760 | tf_op jit(solution)/shard_map/ppermute | solution.py:377
  22.2 0.5 %collective-permute-start.12 = (bf16[2,4,4224]{2,1,0:T(4,128)(2,1)S(1)}, bf16[2,4,4224]{2,1,0:T(4,128)(2,1)S(1)}, u32[]{:S(2)}, u32[]{:S(2)}) collective-permute-start(bf16[2,4,4224]{2,1,0:T(4,128)(2,1)S(1)} %get-tuple-element.52), channel_id=1, source_target_pairs={{0,4},{2,6},{4,0},{6,2},{8,12},{10,14},{12,8},{14,10},{16,20},{18,... | collective-permute-start | bytes 202760 | tf_op jit(solution)/shard_map/ppermute | solution.py:377
  22.7 1.7 %attend_own_other.1.came_ref = bf16[16,4224]{1,0:T(8,128)(2,1)S(1)} custom-call(bf16[1,16,4224]{2,1,0:T(8,128)(2,1)S(1)} %bitcast.14, bf16[4,256,512]{2,1,0:T(8,128)(2,1)S(1)} %collective-permute-done.4.pk_ref, bf16[4,256,512]{2,1,0:T(8,128)(2,1)S(1)} %collective-permute-done.5.pv_ref, s32[8,128]{1,0:T(8,128)S(1)} %collective-permute-done.6.lim_ref, ...), custom_call_target="tpu_custom_call" | custom-call | flops 67108864 | bytes 67108864 | tf_op jit(solution)/shard_map/attend_own_other/pallas_call | solution.py:344
  24.5 0.4 own_merge.1
  24.8 0.7 %collective-permute-done.9.came_ref = bf16[2,4,4224]{2,1,0:T(4,128)(2,1)S(1)} collective-permute-done((bf16[2,4,4224]{2,1,0:T(4,128)(2,1)S(1)}, bf16[2,4,4224]{2,1,0:T(4,128)(2,1)S(1)}, u32[]{:S(2)}, u32[]{:S(2)}) %collective-permute-start.9) | collective-permute-done | bytes 67616 | tf_op jit(solution)/shard_map/ppermute | solution.py:377
  25.5 0.3 plane_merge.2
  25.8 2.1 %collective-permute-start.10 = (bf16[4,4224]{1,0:T(4,128)(2,1)S(1)}, bf16[4,4224]{1,0:T(4,128)(2,1)S(1)}, u32[]{:S(2)}, u32[]{:S(2)}) collective-permute-start(bf16[4,4224]{1,0:T(4,128)(2,1)S(1)} %get-tuple-element.49), channel_id=1, source_target_pairs={{0,24},{2,26},{4,28},{6,30},{8,16},{10,18},{12,20},{14,22},{16,8},... | collective-permute-start | bytes 101384 | tf_op jit(solution)/shard_map/ppermute | solution.py:377
  27.9 0.0 collective-permute-start.11
  28.0 0.3 plane_merge.3
  28.2 2.3 %collective-permute-start.13 = (bf16[4,4224]{1,0:T(4,128)(2,1)S(1)}, bf16[4,4224]{1,0:T(4,128)(2,1)S(1)}, u32[]{:S(2)}, u32[]{:S(2)}) collective-permute-start(bf16[4,4224]{1,0:T(4,128)(2,1)S(1)} %get-tuple-element.53), channel_id=1, source_target_pairs={{0,8},{2,10},{4,12},{6,14},{8,0},{10,2},{12,4},{14,6},{16,24},{18,... | collective-permute-start | bytes 101384 | tf_op jit(solution)/shard_map/ppermute | solution.py:377
  30.6 1.0 %collective-permute-done.10.refs_0_ = bf16[4,4224]{1,0:T(4,128)(2,1)S(1)} collective-permute-done((bf16[4,4224]{1,0:T(4,128)(2,1)S(1)}, bf16[4,4224]{1,0:T(4,128)(2,1)S(1)}, u32[]{:S(2)}, u32[]{:S(2)}) %collective-permute-start.10) | collective-permute-done | bytes 33824 | tf_op jit(solution)/shard_map/ppermute | solution.py:377
  31.6 1.5 %collective-permute-done.11.refs_1_ = bf16[4,4224]{1,0:T(4,128)(2,1)S(1)} collective-permute-done((bf16[4,4224]{1,0:T(4,128)(2,1)S(1)}, bf16[4,4224]{1,0:T(4,128)(2,1)S(1)}, u32[]{:S(2)}, u32[]{:S(2)}) %collective-permute-start.11) | collective-permute-done | bytes 33824 | tf_op jit(solution)/shard_map/ppermute | solution.py:377
  33.1 0.5 finish.1
  33.6 2.1 %collective-permute-start.14 = (bf16[4,4096]{1,0:T(4,128)(2,1)S(1)}, bf16[4,4096]{1,0:T(4,128)(2,1)S(1)}, u32[]{:S(2)}, u32[]{:S(2)}) collective-permute-start(bf16[4,4096]{1,0:T(4,128)(2,1)S(1)} %finish.1), channel_id=1, source_target_pairs={{0,24},{2,26},{4,28},{6,30},{8,16},{10,18},{12,20},{14,22},{16,8},... | collective-permute-start | bytes 98312 | tf_op jit(solution)/shard_map/ppermute | solution.py:377
  35.6 0.9 %collective-permute-start.18 = (bf16[4,4096]{1,0:T(4,128)(2,1)S(1)}, bf16[4,4096]{1,0:T(4,128)(2,1)S(1)}, u32[]{:S(2)}, u32[]{:S(2)}) collective-permute-start(bf16[4,4096]{1,0:T(4,128)(2,1)S(1)} %finish.1), channel_id=1, source_target_pairs={{0,16},{2,18},{4,20},{6,22},{8,24},{10,26},{12,28},{14,30},{16,0},... | collective-permute-start | bytes 98312 | tf_op jit(solution)/shard_map/ppermute | solution.py:377
  36.5 1.5 %collective-permute-start.17 = (bf16[4,4096]{1,0:T(4,128)(2,1)S(1)}, bf16[4,4096]{1,0:T(4,128)(2,1)S(1)}, u32[]{:S(2)}, u32[]{:S(2)}) collective-permute-start(bf16[4,4096]{1,0:T(4,128)(2,1)S(1)} %finish.1), channel_id=1, source_target_pairs={{0,8},{2,10},{4,12},{6,14},{8,0},{10,2},{12,4},{14,6},{16,24},{18,... | collective-permute-start | bytes 98312 | tf_op jit(solution)/shard_map/ppermute | solution.py:377
  38.0 1.3 %collective-permute-done.14 = bf16[4,4096]{1,0:T(4,128)(2,1)S(1)} collective-permute-done((bf16[4,4096]{1,0:T(4,128)(2,1)S(1)}, bf16[4,4096]{1,0:T(4,128)(2,1)S(1)}, u32[]{:S(2)}, u32[]{:S(2)}) %collective-permute-start.14) | collective-permute-done | bytes 32800 | tf_op jit(solution)/shard_map/ppermute | solution.py:377
  39.3 0.1 fusion.1
  39.4 1.7 %collective-permute-start.15 = (bf16[2,4,4096]{2,1,0:T(4,128)(2,1)S(1)}, bf16[2,4,4096]{2,1,0:T(4,128)(2,1)S(1)}, u32[]{:S(2)}, u32[]{:S(2)}) collective-permute-start(bf16[2,4,4096]{2,1,0:T(4,128)(2,1)S(1)} %get-tuple-element.60), channel_id=1, source_target_pairs={{0,4},{2,6},{4,0},{6,2},{8,12},{10,14},{12,8},{14,10},{16,20},{18,... | collective-permute-start | bytes 196616 | tf_op jit(solution)/shard_map/ppermute | solution.py:377
  41.1 0.1 fusion
  41.1 1.4 %collective-permute-start.19 = (bf16[2,4,4096]{2,1,0:T(4,128)(2,1)S(1)}, bf16[2,4,4096]{2,1,0:T(4,128)(2,1)S(1)}, u32[]{:S(2)}, u32[]{:S(2)}) collective-permute-start(bf16[2,4,4096]{2,1,0:T(4,128)(2,1)S(1)} %get-tuple-element.58), channel_id=1, source_target_pairs={{0,4},{2,6},{4,0},{6,2},{8,12},{10,14},{12,8},{14,10},{16,20},{18,... | collective-permute-start | bytes 196616 | tf_op jit(solution)/shard_map/ppermute | solution.py:377
  42.5 1.2 %collective-permute-done.15 = bf16[2,4,4096]{2,1,0:T(4,128)(2,1)S(1)} collective-permute-done((bf16[2,4,4096]{2,1,0:T(4,128)(2,1)S(1)}, bf16[2,4,4096]{2,1,0:T(4,128)(2,1)S(1)}, u32[]{:S(2)}, u32[]{:S(2)}) %collective-permute-start.15) | collective-permute-done | bytes 65568 | tf_op jit(solution)/shard_map/ppermute | solution.py:377
  43.7 0.1 pad_maximum_fusion.near_a
  43.8 0.1 collective-permute-start.16
  43.9 1.6 %collective-permute-done.19 = bf16[2,4,4096]{2,1,0:T(4,128)(2,1)S(1)} collective-permute-done((bf16[2,4,4096]{2,1,0:T(4,128)(2,1)S(1)}, bf16[2,4,4096]{2,1,0:T(4,128)(2,1)S(1)}, u32[]{:S(2)}, u32[]{:S(2)}) %collective-permute-start.19) | collective-permute-done | bytes 65568 | tf_op jit(solution)/shard_map/ppermute | solution.py:377
  45.5 0.1 pad_maximum_fusion.1.near_b
  45.6 0.1 collective-permute-start.20
  45.7 1.3 %collective-permute-done.20.far_b = bf16[2,2,4,4096]{3,2,1,0:T(4,128)(2,1)S(1)} collective-permute-done((bf16[2,2,4,4096]{3,2,1,0:T(4,128)(2,1)S(1)}, bf16[2,2,4,4096]{3,2,1,0:T(4,128)(2,1)S(1)}, u32[]{:S(2)}, u32[]{:S(2)}) %collective-permute-start.20) | collective-permute-done | bytes 131104 | tf_op jit(solution)/shard_map/ppermute | solution.py:377
  47.0 0.9 %project.1 = (f32[32,512]{1,0:T(8,128)S(1)}, bf16[32,512]{1,0:T(8,128)(2,1)S(1)}) custom-call(bf16[2,2,4,4096]{3,2,1,0:T(4,128)(2,1)S(1)} %pad_maximum_fusion.near_a, bf16[2,2,4,4096]{3,2,1,0:T(4,128)(2,1)S(1)} %collective-permute-done.16.far_a, bf16[2,2,4,4096]{3,2,1,0:T(4,128)(2,1)S(1)} %pad_maximum_fusion.1.near_b, ...), custom_call_target="tpu_custom_call" | custom-call | tf_op jit(solution)/shard_map/project/pallas_call | solution.py:344
  47.9 1.6 %collective-permute-start.21 = (bf16[32,512]{1,0:T(8,128)(2,1)S(1)}, bf16[32,512]{1,0:T(8,128)(2,1)S(1)}, u32[]{:S(2)}, u32[]{:S(2)}) collective-permute-start(bf16[32,512]{1,0:T(8,128)(2,1)S(1)} %get-tuple-element.56), channel_id=1, source_target_pairs={{0,1},{1,0},{2,3},{3,2},{4,5},{5,4},{6,7},{7,6},{8,9},{9,8},{10,11... | collective-permute-start | bytes 98312 | tf_op jit(solution)/shard_map/ppermute | solution.py:492
  49.4 2.4 %collective-permute-done.21 = bf16[32,512]{1,0:T(8,128)(2,1)S(1)} collective-permute-done((bf16[32,512]{1,0:T(8,128)(2,1)S(1)}, bf16[32,512]{1,0:T(8,128)(2,1)S(1)}, u32[]{:S(2)}, u32[]{:S(2)}) %collective-permute-start.21) | collective-permute-done | bytes 32800 | tf_op jit(solution)/shard_map/ppermute | solution.py:492
  51.8 0.6 %add_convert_fusion = bf16[32,512]{1,0:T(8,128)(2,1)} fusion(f32[32,512]{1,0:T(8,128)S(1)} %get-tuple-element.55, bf16[32,512]{1,0:T(8,128)(2,1)S(1)} %collective-permute-done.21), kind=kLoop, calls=%fused_computation.4 | loop fusion | flops 49152 | bytes 131072 | tf_op jit(solution)/shard_map/convert_element_type | solution.py:493
  (24 shorter events, 0.1 us)
Async XLA Ops:
  0.0 10.6 %copy-start.3 = (bf16[4,256,512]{2,1,0:T(8,128)(2,1)S(1)}, bf16[4,256,512]{2,1,0:T(8,128)(2,1)}, u32[]{:S(2)}) copy-start(bf16[4,256,512]{2,1,0:T(8,128)(2,1)} %pk_hbm) | copy-start | bytes 3145732
  0.0 10.7 %copy-start.4 = (bf16[4,256,512]{2,1,0:T(8,128)(2,1)S(1)}, bf16[4,256,512]{2,1,0:T(8,128)(2,1)}, u32[]{:S(2)}) copy-start(bf16[4,256,512]{2,1,0:T(8,128)(2,1)} %pv_hbm) | copy-start | bytes 3145732
  0.0 18.5 %collective-permute-start.7 = (bf16[4,512,512]{2,1,0:T(8,128)(2,1)}, bf16[4,512,512]{2,1,0:T(8,128)(2,1)S(1)}, u32[]{:S(2)}, u32[]{:S(2)}) collective-permute-start(bf16[4,512,512]{2,1,0:T(8,128)(2,1)} %ck_hbm.1), channel_id=1, source_target_pairs={{0,2},{2,0},{4,6},{6,4},{8,10},{10,8},{12,14},{14,12},{16,18},{18,... | collective-permute-start | bytes 6291464 | tf_op jit(solution)/shard_map/ppermute | solution.py:377
  0.5 18.0 %collective-permute-start.8 = (bf16[4,512,512]{2,1,0:T(8,128)(2,1)}, bf16[4,512,512]{2,1,0:T(8,128)(2,1)S(1)}, u32[]{:S(2)}, u32[]{:S(2)}) collective-permute-start(bf16[4,512,512]{2,1,0:T(8,128)(2,1)} %cv_hbm.1), channel_id=1, source_target_pairs={{0,2},{2,0},{4,6},{6,4},{8,10},{10,8},{12,14},{14,12},{16,18},{18,... | collective-permute-start | bytes 6291464 | tf_op jit(solution)/shard_map/ppermute | solution.py:377
  0.5 8.3 %collective-permute-start = (bf16[4,4096]{1,0:T(4,128)(2,1)}, bf16[4,4096]{1,0:T(4,128)(2,1)S(1)}, u32[]{:S(2)}, u32[]{:S(2)}) collective-permute-start(bf16[4,4096]{1,0:T(4,128)(2,1)} %q_hbm.1), channel_id=1, source_target_pairs={{0,24},{2,26},{4,28},{6,30},{8,16},{10,18},{12,20},{14,22},{16,8},... | collective-permute-start | bytes 98312 | tf_op jit(solution)/shard_map/ppermute | solution.py:377
  5.6 5.0 %collective-permute-start.1 = (bf16[4,4096]{1,0:T(4,128)(2,1)}, bf16[4,4096]{1,0:T(4,128)(2,1)S(1)}, u32[]{:S(2)}, u32[]{:S(2)}) collective-permute-start(bf16[4,4096]{1,0:T(4,128)(2,1)} %q_hbm.1), channel_id=1, source_target_pairs={{0,16},{2,18},{4,20},{6,22},{8,24},{10,26},{12,28},{14,30},{16,0},... | collective-permute-start | bytes 98312 | tf_op jit(solution)/shard_map/ppermute | solution.py:377
  5.6 5.0 %collective-permute-start.2 = (bf16[4,4096]{1,0:T(4,128)(2,1)}, bf16[4,4096]{1,0:T(4,128)(2,1)S(1)}, u32[]{:S(2)}, u32[]{:S(2)}) collective-permute-start(bf16[4,4096]{1,0:T(4,128)(2,1)} %q_hbm.1), channel_id=1, source_target_pairs={{0,8},{2,10},{4,12},{6,14},{8,0},{10,2},{12,4},{14,6},{16,24},{18,... | collective-permute-start | bytes 98312 | tf_op jit(solution)/shard_map/ppermute | solution.py:377
  10.7 7.8 %collective-permute-start.4 = (bf16[4,256,512]{2,1,0:T(8,128)(2,1)S(1)}, bf16[4,256,512]{2,1,0:T(8,128)(2,1)S(1)}, u32[]{:S(2)}, u32[]{:S(2)}) collective-permute-start(bf16[4,256,512]{2,1,0:T(8,128)(2,1)S(1)} %copy-done.3), channel_id=1, source_target_pairs={{0,2},{2,0},{4,6},{6,4},{8,10},{10,8},{12,14},{14,12},{16,18},{18,... | collective-permute-start | bytes 3145736 | tf_op jit(solution)/shard_map/ppermute | solution.py:377
  10.7 7.7 %collective-permute-start.5 = (bf16[4,256,512]{2,1,0:T(8,128)(2,1)S(1)}, bf16[4,256,512]{2,1,0:T(8,128)(2,1)S(1)}, u32[]{:S(2)}, u32[]{:S(2)}) collective-permute-start(bf16[4,256,512]{2,1,0:T(8,128)(2,1)S(1)} %copy-done.4), channel_id=1, source_target_pairs={{0,2},{2,0},{4,6},{6,4},{8,10},{10,8},{12,14},{14,12},{16,18},{18,... | collective-permute-start | bytes 3145736 | tf_op jit(solution)/shard_map/ppermute | solution.py:377
  11.2 5.6 %collective-permute-start.3 = (bf16[16,4224]{1,0:T(8,128)(2,1)S(1)}, bf16[16,4224]{1,0:T(8,128)(2,1)S(1)}, u32[]{:S(2)}, u32[]{:S(2)}) collective-permute-start(bf16[16,4224]{1,0:T(8,128)(2,1)S(1)} %line.1), channel_id=1, source_target_pairs={{0,4},{2,6},{4,0},{6,2},{8,12},{10,14},{12,8},{14,10},{16,20},{18,... | collective-permute-start | bytes 405512 | tf_op jit(solution)/shard_map/ppermute | solution.py:377
  16.8 1.6 %collective-permute-start.6 = (s32[8,128]{1,0:T(8,128)S(1)}, s32[8,128]{1,0:T(8,128)S(1)}, u32[]{:S(2)}, u32[]{:S(2)}) collective-permute-start(s32[8,128]{1,0:T(8,128)S(1)} %get-tuple-element.41.lim_ref), channel_id=1, source_target_pairs={{0,2},{2,0},{4,6},{6,4},{8,10},{10,8},{12,14},{14,12},{16,18},{18,... | collective-permute-start | bytes 12296 | tf_op jit(solution)/shard_map/ppermute | solution.py:377
  20.6 4.9 %collective-permute-start.9 = (bf16[2,4,4224]{2,1,0:T(4,128)(2,1)S(1)}, bf16[2,4,4224]{2,1,0:T(4,128)(2,1)S(1)}, u32[]{:S(2)}, u32[]{:S(2)}) collective-permute-start(bf16[2,4,4224]{2,1,0:T(4,128)(2,1)S(1)} %get-tuple-element.46), channel_id=1, source_target_pairs={{0,4},{2,6},{4,0},{6,2},{8,12},{10,14},{12,8},{14,10},{16,20},{18,... | collective-permute-start | bytes 202760 | tf_op jit(solution)/shard_map/ppermute | solution.py:377
  22.2 5.8 %collective-permute-start.12 = (bf16[2,4,4224]{2,1,0:T(4,128)(2,1)S(1)}, bf16[2,4,4224]{2,1,0:T(4,128)(2,1)S(1)}, u32[]{:S(2)}, u32[]{:S(2)}) collective-permute-start(bf16[2,4,4224]{2,1,0:T(4,128)(2,1)S(1)} %get-tuple-element.52), channel_id=1, source_target_pairs={{0,4},{2,6},{4,0},{6,2},{8,12},{10,14},{12,8},{14,10},{16,20},{18,... | collective-permute-start | bytes 202760 | tf_op jit(solution)/shard_map/ppermute | solution.py:377
  22.7 10.4 %copy-start.1 = (bf16[4,512]{1,0:T(4,128)(2,1)S(1)}, bf16[4,512]{1,0:T(4,128)(2,1)}, u32[]{:S(2)}) copy-start(bf16[4,512]{1,0:T(4,128)(2,1)} %nk_ref.1) | copy-start | bytes 12292
  22.7 10.4 %copy-start.2 = (bf16[4,512]{1,0:T(4,128)(2,1)S(1)}, bf16[4,512]{1,0:T(4,128)(2,1)}, u32[]{:S(2)}) copy-start(bf16[4,512]{1,0:T(4,128)(2,1)} %nv_ref.1) | copy-start | bytes 12292
  22.7 24.3 %copy-start = (bf16[4096,512]{1,0:T(8,128)(2,1)S(1)}, bf16[4096,512]{1,0:T(8,128)(2,1)}, u32[]{:S(2)}) copy-start(bf16[4096,512]{1,0:T(8,128)(2,1)} %w_ref.1) | copy-start | bytes 12582916
  25.8 5.8 %collective-permute-start.10 = (bf16[4,4224]{1,0:T(4,128)(2,1)S(1)}, bf16[4,4224]{1,0:T(4,128)(2,1)S(1)}, u32[]{:S(2)}, u32[]{:S(2)}) collective-permute-start(bf16[4,4224]{1,0:T(4,128)(2,1)S(1)} %get-tuple-element.49), channel_id=1, source_target_pairs={{0,24},{2,26},{4,28},{6,30},{8,16},{10,18},{12,20},{14,22},{16,8},... | collective-permute-start | bytes 101384 | tf_op jit(solution)/shard_map/ppermute | solution.py:377
  27.9 5.2 %collective-permute-start.11 = (bf16[4,4224]{1,0:T(4,128)(2,1)S(1)}, bf16[4,4224]{1,0:T(4,128)(2,1)S(1)}, u32[]{:S(2)}, u32[]{:S(2)}) collective-permute-start(bf16[4,4224]{1,0:T(4,128)(2,1)S(1)} %get-tuple-element.50), channel_id=1, source_target_pairs={{0,16},{2,18},{4,20},{6,22},{8,24},{10,26},{12,28},{14,30},{16,0},... | collective-permute-start | bytes 101384 | tf_op jit(solution)/shard_map/ppermute | solution.py:377
  28.2 4.8 %collective-permute-start.13 = (bf16[4,4224]{1,0:T(4,128)(2,1)S(1)}, bf16[4,4224]{1,0:T(4,128)(2,1)S(1)}, u32[]{:S(2)}, u32[]{:S(2)}) collective-permute-start(bf16[4,4224]{1,0:T(4,128)(2,1)S(1)} %get-tuple-element.53), channel_id=1, source_target_pairs={{0,8},{2,10},{4,12},{6,14},{8,0},{10,2},{12,4},{14,6},{16,24},{18,... | collective-permute-start | bytes 101384 | tf_op jit(solution)/shard_map/ppermute | solution.py:377
  33.6 5.8 %collective-permute-start.14 = (bf16[4,4096]{1,0:T(4,128)(2,1)S(1)}, bf16[4,4096]{1,0:T(4,128)(2,1)S(1)}, u32[]{:S(2)}, u32[]{:S(2)}) collective-permute-start(bf16[4,4096]{1,0:T(4,128)(2,1)S(1)} %finish.1), channel_id=1, source_target_pairs={{0,24},{2,26},{4,28},{6,30},{8,16},{10,18},{12,20},{14,22},{16,8},... | collective-permute-start | bytes 98312 | tf_op jit(solution)/shard_map/ppermute | solution.py:377
  35.6 5.5 %collective-permute-start.18 = (bf16[4,4096]{1,0:T(4,128)(2,1)S(1)}, bf16[4,4096]{1,0:T(4,128)(2,1)S(1)}, u32[]{:S(2)}, u32[]{:S(2)}) collective-permute-start(bf16[4,4096]{1,0:T(4,128)(2,1)S(1)} %finish.1), channel_id=1, source_target_pairs={{0,16},{2,18},{4,20},{6,22},{8,24},{10,26},{12,28},{14,30},{16,0},... | collective-permute-start | bytes 98312 | tf_op jit(solution)/shard_map/ppermute | solution.py:377
  36.5 4.6 %collective-permute-start.17 = (bf16[4,4096]{1,0:T(4,128)(2,1)S(1)}, bf16[4,4096]{1,0:T(4,128)(2,1)S(1)}, u32[]{:S(2)}, u32[]{:S(2)}) collective-permute-start(bf16[4,4096]{1,0:T(4,128)(2,1)S(1)} %finish.1), channel_id=1, source_target_pairs={{0,8},{2,10},{4,12},{6,14},{8,0},{10,2},{12,4},{14,6},{16,24},{18,... | collective-permute-start | bytes 98312 | tf_op jit(solution)/shard_map/ppermute | solution.py:377
  39.4 4.3 %collective-permute-start.15 = (bf16[2,4,4096]{2,1,0:T(4,128)(2,1)S(1)}, bf16[2,4,4096]{2,1,0:T(4,128)(2,1)S(1)}, u32[]{:S(2)}, u32[]{:S(2)}) collective-permute-start(bf16[2,4,4096]{2,1,0:T(4,128)(2,1)S(1)} %get-tuple-element.60), channel_id=1, source_target_pairs={{0,4},{2,6},{4,0},{6,2},{8,12},{10,14},{12,8},{14,10},{16,20},{18,... | collective-permute-start | bytes 196616 | tf_op jit(solution)/shard_map/ppermute | solution.py:377
  41.1 4.3 %collective-permute-start.19 = (bf16[2,4,4096]{2,1,0:T(4,128)(2,1)S(1)}, bf16[2,4,4096]{2,1,0:T(4,128)(2,1)S(1)}, u32[]{:S(2)}, u32[]{:S(2)}) collective-permute-start(bf16[2,4,4096]{2,1,0:T(4,128)(2,1)S(1)} %get-tuple-element.58), channel_id=1, source_target_pairs={{0,4},{2,6},{4,0},{6,2},{8,12},{10,14},{12,8},{14,10},{16,20},{18,... | collective-permute-start | bytes 196616 | tf_op jit(solution)/shard_map/ppermute | solution.py:377
  43.8 1.8 %collective-permute-start.16 = (bf16[2,2,4,4096]{3,2,1,0:T(4,128)(2,1)S(1)}, bf16[2,2,4,4096]{3,2,1,0:T(4,128)(2,1)S(1)}, u32[]{:S(2)}, u32[]{:S(2)}) collective-permute-start(bf16[2,2,4,4096]{3,2,1,0:T(4,128)(2,1)S(1)} %pad_maximum_fusion.near_a), channel_id=1, source_target_pairs={{0,2},{2,0},{4,6},{6,4},{8,10},{10,8},{12,14},{14,12},{16,18},{18,... | collective-permute-start | bytes 393224 | tf_op jit(solution)/shard_map/ppermute | solution.py:377
  45.6 1.4 %collective-permute-start.20 = (bf16[2,2,4,4096]{3,2,1,0:T(4,128)(2,1)S(1)}, bf16[2,2,4,4096]{3,2,1,0:T(4,128)(2,1)S(1)}, u32[]{:S(2)}, u32[]{:S(2)}) collective-permute-start(bf16[2,2,4,4096]{3,2,1,0:T(4,128)(2,1)S(1)} %pad_maximum_fusion.1.near_b), channel_id=1, source_target_pairs={{0,2},{2,0},{4,6},{6,4},{8,10},{10,8},{12,14},{14,12},{16,18},{18,... | collective-permute-start | bytes 393224 | tf_op jit(solution)/shard_map/ppermute | solution.py:377
  47.9 4.0 %collective-permute-start.21 = (bf16[32,512]{1,0:T(8,128)(2,1)S(1)}, bf16[32,512]{1,0:T(8,128)(2,1)S(1)}, u32[]{:S(2)}, u32[]{:S(2)}) collective-permute-start(bf16[32,512]{1,0:T(8,128)(2,1)S(1)} %get-tuple-element.56), channel_id=1, source_target_pairs={{0,1},{1,0},{2,3},{3,2},{4,5},{5,4},{6,7},{7,6},{8,9},{9,8},{10,11... | collective-permute-start | bytes 98312 | tf_op jit(solution)/shard_map/ppermute | solution.py:492

commit v4 on v3

--- a/solution.py
+++ b/solution.py
@@ -99,56 +99,52 @@
         x.wait()
 
 
-def attend_kernel(other, q_ref, pk_ref, pv_ref, lim_ref, ck_ref, cv_ref, *refs):
-    *outs, s_ref, p_ref, cs_ref, cp_ref = refs
-    count = q_ref.shape[0]
-    pieces = [q_ref.at[r] for r in range(count)]
-    total = q_ref.shape[2]
+def attend_kernel(kinds, q_ref, *refs):
+    total = q_ref.shape[1]
     heads = (total - STATS) // (QPK * HD)
-    if other:
-        requests, length, _ = pk_ref.shape
-        olds, span, _ = ck_ref.shape
-    else:
-        _, pairs, length, _ = pk_ref.shape
-        requests = 2 * pairs
-        _, span, olds = ck_ref.shape
-        olds = olds // HD
+    caches = [refs[5 * n : 5 * n + 5] for n in range(len(kinds))]
+    *outs, s_ref, p_ref, cs_ref, cp_ref = refs[5 * len(kinds) :]
+    requests, span = s_ref.shape[2] // cs_ref.shape[2], cs_ref.shape[3]
     pairs = requests // 2
-    beams = q_ref.shape[1] // requests
-    block = count * beams
+    beams = q_ref.shape[0] // requests
     stride = heads * QPK
-    rows = QPK * block
+    rows = QPK * beams
     me = lax.axis_index("beam")
     mine = me // (BEAM_WIDTH // beams)
     order = line_order(requests)
-
-    def prompt(ref, k, u):
-        if not other:
+    olds = beams
+
+    def prompt(n, ref, k, u):
+        if not kinds[n]:
             return ref[k, u]
-        both = [ref[mine ^ order[2 * u + n], :, k * HD : (k + 1) * HD] for n in range(2)]
+        both = [ref[mine ^ order[2 * u + m], :, k * HD : (k + 1) * HD] for m in range(2)]
         return jnp.concatenate(both, axis=1)
 
-    def private(ref, k):
-        if not other:
+    def private(n, ref, k):
+        if not kinds[n]:
             return ref[k]
         return jnp.concatenate([ref[o, :, k * HD : (k + 1) * HD] for o in range(olds)], axis=1)
 
-    parent = jnp.concatenate([x[:, total - STATS :].astype(f32)[:beams] for x in pieces], axis=0)
-    parent = jnp.concatenate([parent] * QPK, axis=0).astype(jnp.int32) - (me ^ other) * olds
-    column = parent[:, :1]
-    local = (column >= 0) & (column < olds)
-    limit = jnp.zeros((rows, 1), jnp.int32)
-    for o in range(olds):
-        limit = jnp.where(column == o, lim_ref[0:1, o : o + 1], limit)
-    stats = [jnp.zeros((block, STATS), f32) for _ in range(requests)]
-    lane = lax.broadcasted_iota(jnp.int32, (block, STATS), 1) % stride
+    whose = jnp.concatenate([q_ref[:, total - STATS :].astype(f32)[:beams]] * QPK, axis=0)
+    parents, limits, locals_ = [], [], []
+    for kind, (_, _, lim_ref, _, _) in zip(kinds, caches):
+        parent = whose.astype(jnp.int32) - (me ^ kind) * olds
+        column = parent[:, :1]
+        limit = jnp.zeros((rows, 1), jnp.int32)
+        for o in range(olds):
+            known = lim_ref[0:1, o : o + 1]
+            limit = jnp.where(column == o, known, limit)
+        parents.append(parent)
+        limits.append(limit)
+        locals_.append((column >= 0) & (column < olds))
+    stats = [jnp.zeros((beams, STATS), f32) for _ in range(requests)]
+    lane = lax.broadcasted_iota(jnp.int32, (beams, STATS), 1) % stride
     blank = jnp.zeros((rows, HD), bf16)
     kept = {}
 
-    def scores(k):
-        tiles = [
-            x[:, (k * QPK + i) * HD : (k * QPK + i + 1) * HD] for i in range(QPK) for x in pieces
-        ]
+    def scores(n, k):
+        pk_ref, _, _, ck_ref, _ = caches[n]
+        tiles = [q_ref[:, (k * QPK + i) * HD : (k * QPK + i + 1) * HD] for i in range(QPK)]
         q = [
             jnp.concatenate([x[t * beams : (t + 1) * beams] for x in tiles], axis=0)
             for t in range(requests)
@@ -161,64 +157,80 @@
                 ],
                 axis=0,
             )
-            s_ref[k, 2 * u * rows : 2 * (u + 1) * rows] = dot(both, prompt(pk_ref, k, u), 1, 1)
-        chosen = jnp.concatenate([jnp.where(parent == o, q[-1], blank) for o in range(olds)], axis=1)
-        cs_ref[k] = dot(chosen, private(ck_ref, k), 1, 1)
-
-    def weigh(k):
-        p, top, den = soft(s_ref[k])
-        p_ref[k] = p.astype(bf16)
+            s_ref[n, k, 2 * u * rows : 2 * (u + 1) * rows] = dot(both, prompt(n, pk_ref, k, u), 1, 1)
+        chosen = jnp.concatenate(
+            [jnp.where(parents[n] == o, q[-1], blank) for o in range(olds)], axis=1
+        )
+        cs_ref[n, k] = dot(chosen, private(n, ck_ref, k), 1, 1)
+
+    def weigh(n, k):
+        p, top, den = soft(s_ref[n, k])
+        p_ref[n, k] = p.astype(bf16)
         place = lax.broadcasted_iota(jnp.int32, (rows, span), 1)
-        c, ctop, cden = soft(jnp.where(place < limit, cs_ref[k], masked_score))
-        cp_ref[k] = c.astype(bf16)
-        kept[k] = (top, den, ctop, cden)
-
-    def values(k):
-        tops, dens, ctop, cden = kept.pop(k)
-        nums = []
+        c, ctop, cden = soft(jnp.where(place < limits[n], cs_ref[n, k], masked_score))
+        cp_ref[n, k] = c.astype(bf16)
+        kept[n, k] = (top, den, ctop, cden)
+
+    def values(n, k):
+        _, pv_ref, _, _, cv_ref = caches[n]
+        tops, dens, ctop, cden = kept.pop((n, k))
+        found = []
         for u in range(pairs):
-            both = dot(p_ref[k, 2 * u * rows : 2 * (u + 1) * rows], prompt(pv_ref, k, u), 1, 0)
-            nums += [both[:rows, :HD], both[rows:, HD:]]
-        every = dot(cp_ref[k], private(cv_ref, k), 1, 0)
+            both = dot(
+                p_ref[n, k, 2 * u * rows : 2 * (u + 1) * rows], prompt(n, pv_ref, k, u), 1, 0
+            )
+            for m, num in enumerate((both[:rows, :HD], both[rows:, HD:])):
+                part = slice((2 * u + m) * rows, (2 * u + m + 1) * rows)
+                found.append((num, tops[part], dens[part]))
+        every = dot(cp_ref[n, k], private(n, cv_ref, k), 1, 0)
         cnum = every[:, :HD]
         for o in range(1, olds):
-            cnum = jnp.where(parent == o, every[:, o * HD : (o + 1) * HD], cnum)
+            cnum = jnp.where(parents[n] == o, every[:, o * HD : (o + 1) * HD], cnum)
+        num, top, den = found[-1]
+        both = jnp.where(locals_[n], jnp.maximum(top, ctop), top)
+        a = jnp.exp(top - both)
+        e = jnp.where(locals_[n], jnp.exp(jnp.where(locals_[n], ctop, both) - both), 0.0)
+        found[-1] = (a * num + e * cnum, both, a * den + e * cden)
+        return found
+
+    def finish(k):
+        found = [values(n, k) for n in range(len(kinds))]
         done = []
         for t in range(requests):
-            part = slice(t * rows, (t + 1) * rows)
-            num, top, den = nums[t], tops[part], dens[part]
-            if t == requests - 1:
-                both = jnp.where(local, jnp.maximum(top, ctop), top)
-                a = jnp.exp(top - both)
-                e = jnp.where(local, jnp.exp(jnp.where(local, ctop, both) - both), 0.0)
-                num = a * num + e * cnum
-                den = a * den + e * cden
-                top = both
+            num, top, den = found[0][t]
+            for other in found[1:]:
+                num2, top2, den2 = other[t]
+                both = jnp.maximum(top, top2)
+                a, e = jnp.exp(top - both), jnp.exp(top2 - both)
+                num, top, den = a * num + e * num2, both, a * den + e * den2
             done.append(num * (1.0 / den))
             lse = top + jnp.log(den)
             for i in range(QPK):
                 stats[t] = jnp.where(
                     lane == k * QPK + i,
-                    jnp.broadcast_to(
-                        lse[i * block : (i + 1) * block], (block, STATS)
-                    ),
+                    jnp.broadcast_to(lse[i * beams : (i + 1) * beams], (beams, STATS)),
                     stats[t],
                 )
         for i in range(QPK):
-            cols = slice((k * QPK + i) * HD, (k * QPK + i + 1) * HD)
-            for r, out in enumerate(outs):
-                first = i * block + r * beams
-                out[:, cols] = jnp.concatenate(
-                    [x[first : first + beams] for x in done], axis=0
-                ).astype(bf16)
-
-    for stage in (scores, weigh, values):
-        for k in range(heads):
-            stage(k)
-    for r, out in enumerate(outs):
-        out[:, total - STATS :] = pack_stats(
-            jnp.concatenate([x[r * beams : (r + 1) * beams] for x in stats], axis=0), stride
-        )
+            store(
+                slice((k * QPK + i) * HD, (k * QPK + i + 1) * HD),
+                [x[i * beams : (i + 1) * beams] for x in done],
+            )
+
+    def store(cols, pieces):
+        if len(outs) == 1:
+            outs[0][:, cols] = jnp.concatenate(pieces, axis=0).astype(bf16)
+        else:
+            for n, piece in enumerate(pieces):
+                outs[n // pairs][n % pairs, :, cols] = piece.astype(bf16)
+
+    for stage in (scores, weigh):
+        for n in range(len(kinds)):
+            for k in range(heads):
+                stage(n, k)
+    for k in range(heads):
+        finish(k)
+    store(slice(total - STATS, total), [pack_stats(x, stride) for x in stats])
 
 
 def pack_stats(x, stride):
@@ -426,35 +438,37 @@
         cost=2**26,
     )
     caches = (*prompts, *olds)
-    stored = (swap(prompt_keys, 1), swap(prompt_values, 1), swap(olds[0], 1), *stored)
-
-    def attend(asked, name, caches, other=0):
-        many = asked.shape[0] * beams * QPK
+    limits, late_keys, late_values = lax.optimization_barrier(
+        (swap(olds[0], 1), prompt_keys, prompt_values)
+    )
+    stored = (swap(late_keys, 1), swap(late_values, 1), limits, *stored)
+
+    many = beams * QPK
+
+    def attend(asked, name, out_shape, kinds, *caches):
         return call(
-            functools.partial(attend_kernel, other),
+            functools.partial(attend_kernel, kinds),
             name,
-            (line,) * asked.shape[0],
+            out_shape,
             asked,
             *caches,
             scratch=[
-                pltpu.VMEM((heads, requests * many, length), f32),
-                pltpu.VMEM((heads, requests * many, length), bf16),
-                pltpu.VMEM((heads, many, span), f32),
-                pltpu.VMEM((heads, many, span), bf16),
+                pltpu.VMEM((len(kinds), heads, requests * many, length), f32),
+                pltpu.VMEM((len(kinds), heads, requests * many, length), bf16),
+                pltpu.VMEM((len(kinds), heads, many, span), f32),
+                pltpu.VMEM((len(kinds), heads, many, span), bf16),
             ],
             vmem=24,
             cost=2**26,
         )
 
     other = swap(asked, 2)
-    (own_here,) = attend(asked[None], "attend_own", caches)
+    own_here = attend(asked, "attend_own", line, (0,), *caches)
     other, own_here = lax.optimization_barrier((other, own_here))
-    (side_here,) = attend(other[None], "attend_side", caches)
-    (side_there,) = attend(other[None], "attend_side_other", stored, 1)
     half = jax.ShapeDtypeStruct((requests // 2, beams, total), bf16)
-    send_a, send_b = call(core_kernel, "side_merge", (half, half), side_here, side_there)
+    send_a, send_b = attend(other, "attend_side", (half, half), (0, 1), *caches, *stored)
     asked, _ = lax.optimization_barrier((asked, send_a))
-    (own_there,) = attend(asked[None], "attend_own_other", stored, 1)
+    own_there = attend(asked, "attend_own_other", line, (1,), *stored)
     keep_a, keep_b = call(core_kernel, "own_merge", (half, half), own_here, own_there)
     piece = jax.ShapeDtypeStruct((beams, total), bf16)
     parts = []

time: 52.7 us -> 52.3 us (level)
  waiting for transfers between devices: 13.3 us -> 14.3 us
  starting transfers between devices: 24 us -> 23.2 us
    ppermute x21, waiting for transfers between devices: 11 us -> 12 us  [swap(): return lax.ppermute(x, 'beam', [(i, i ^ with_bit) for i in range(devices)])]
    ppermute x21, starting transfers between devices: 22.4 us -> 21.6 us  [swap(): return lax.ppermute(x, 'beam', [(i, i ^ with_bit) for i in range(devices)])]
    pallas_call x13 -> x11, Pallas kernels: 13.9 us -> 13.4 us  [call(): pl.pallas_call(kernel, out_shape=out_shape, in_specs=whole_blocks(len(arg...]
  transfers between devices with their start and end apart: 22 -> 22, of which waited for: 10 -> 10; matrix products, arithmetic and copies ran while one was open for 1% -> 1% of each run, Pallas kernels for 20% -> 17%
where the time goes in v4:
time: 52.3 us; the launch traced here: 52.1 us
  starting transfers between devices  23.2 us (44%)
  waiting for transfers between devices  14.3 us (27%)
  Pallas kernels  13.4 us (26%)
  other arithmetic  0.92 us (2%)
    ppermute x21, starting transfers between devices, swap(): return lax.ppermute(x, 'beam', [(i, i ^ with_bit) for i in range(devices)])  21.6 us
    pallas_call x11, Pallas kernels, call(): pl.pallas_call(kernel, out_shape=out_shape, in_specs=whole_blocks(len(arg...  13.4 us
    ppermute x21, waiting for transfers between devices, swap(): return lax.ppermute(x, 'beam', [(i, i ^ with_bit) for i in range(devices)])  12 us
    ppermute x1, waiting for transfers between devices, per_device(): came = lax.ppermute(send, 'head', [(0, 1), (1, 0)])  2.39 us
    ppermute x1, starting transfers between devices, per_device(): came = lax.ppermute(send, 'head', [(0, 1), (1, 0)])  1.59 us
  transfers between devices with their start and end apart: 22, of which 10 were waited for; matrix products, arithmetic and copies ran while one was open for 1% of the time, Pallas kernels for 17%

profile of v4, /device:TPU:0, one launch (start us, length us, event | category | flops | bytes accessed | tf_op | source)
XLA Modules:
  0.0 52.1 jit_solution(13902801508821788619)
XLA Ops:
  0.0 0.5 collective-permute-start.7
  0.5 0.1 collective-permute-start.8
  0.5 5.0 %collective-permute-start = (bf16[4,4096]{1,0:T(4,128)(2,1)}, bf16[4,4096]{1,0:T(4,128)(2,1)S(1)}, u32[]{:S(2)}, u32[]{:S(2)}) collective-permute-start(bf16[4,4096]{1,0:T(4,128)(2,1)} %q_hbm.1), channel_id=1, source_target_pairs={{0,24},{2,26},{4,28},{6,30},{8,16},{10,18},{12,20},{14,22},{16,8},... | collective-permute-start | bytes 98312 | tf_op jit(solution)/shard_map/ppermute | solution.py:389
  5.6 0.6 %collective-permute-start.2 = (bf16[4,4096]{1,0:T(4,128)(2,1)}, bf16[4,4096]{1,0:T(4,128)(2,1)S(1)}, u32[]{:S(2)}, u32[]{:S(2)}) collective-permute-start(bf16[4,4096]{1,0:T(4,128)(2,1)} %q_hbm.1), channel_id=1, source_target_pairs={{0,8},{2,10},{4,12},{6,14},{8,0},{10,2},{12,4},{14,6},{16,24},{18,... | collective-permute-start | bytes 98312 | tf_op jit(solution)/shard_map/ppermute | solution.py:389
  6.1 2.7 %load_private.1 = (bf16[4,4096]{1,0:T(4,128)(2,1)S(1)}, bf16[4,128]{1,0:T(4,128)(2,1)S(1)}, s32[8,128]{1,0:T(8,128)S(1)}, bf16[4,512,512]{2,1,0:T(8,128)(2,1)S(1)}, bf16[4,512,512]{2,1,0:T(8,128)(2,1)S(1)}) custom-call(bf16[4,4096]{1,0:T(4,128)(2,1)} %q_hbm.1, s32[4]{0:T(128)} %par_hbm.1, s32[4]{0:T(128)} %cnt_hbm.1, bf16[4,512,512]{2,1,0:T(8,128)(2,1)} %ck_hbm.1, ...), custom_call_target="tpu_custom_call" | custom-call | flops 67108864 | bytes 67108864 | tf_op jit(solution)/shard_map/load_private/pallas_call | solution.py:356
  8.8 0.1 collective-permute-start.4
  8.9 1.7 %collective-permute-done.1.refs_1_ = bf16[4,4096]{1,0:T(4,128)(2,1)S(1)} collective-permute-done((bf16[4,4096]{1,0:T(4,128)(2,1)}, bf16[4,4096]{1,0:T(4,128)(2,1)S(1)}, u32[]{:S(2)}, u32[]{:S(2)}) %collective-permute-start.1) | collective-permute-done | bytes 32800 | tf_op jit(solution)/shard_map/ppermute | solution.py:389
  10.6 0.0 collective-permute-done.4.refs_7_.refs_2_
  10.7 0.1 collective-permute-start.5
  10.8 0.5 collective-permute-start.6
  11.2 1.5 %collective-permute-start.3 = (bf16[16,4224]{1,0:T(8,128)(2,1)S(1)}, bf16[16,4224]{1,0:T(8,128)(2,1)S(1)}, u32[]{:S(2)}, u32[]{:S(2)}) collective-permute-start(bf16[16,4224]{1,0:T(8,128)(2,1)S(1)} %line.1.q_ref), channel_id=1, source_target_pairs={{0,4},{2,6},{4,0},{6,2},{8,12},{10,14},{12,8},{14,10},{16,20},{18,... | collective-permute-start | bytes 405512 | tf_op jit(solution)/shard_map/ppermute | solution.py:389
  12.7 1.9 %load_prompt.1 = (bf16[4,2,256,256]{3,2,1,0:T(8,128)(2,1)S(1)}, bf16[4,2,256,256]{3,2,1,0:T(8,128)(2,1)S(1)}) custom-call(bf16[4,256,512]{2,1,0:T(8,128)(2,1)} %pk_hbm, bf16[4,256,512]{2,1,0:T(8,128)(2,1)} %pv_hbm), custom_call_target="tpu_custom_call" | custom-call | flops 67108864 | bytes 67108864 | tf_op jit(solution)/shard_map/load_prompt/pallas_call | solution.py:356
  14.6 1.6 %attend_own.1.kept_ref = bf16[16,4224]{1,0:T(8,128)(2,1)S(1)} custom-call(bf16[16,4224]{1,0:T(8,128)(2,1)S(1)} %line.1.q_ref, bf16[4,2,256,256]{3,2,1,0:T(8,128)(2,1)S(1)} %get-tuple-element.42.refs_0_, bf16[4,2,256,256]{3,2,1,0:T(8,128)(2,1)S(1)} %get-tuple-element.43.refs_1_, s32[8,128]{1,0:T(8,128)S(1)} %get-tuple-element.44.refs_2_, ...), custom_call_target="tpu_custom_call" | custom-call | flops 67108864 | bytes 67108864 | tf_op jit(solution)/shard_map/attend_own/pallas_call | solution.py:356
  16.3 0.5 %collective-permute-done.3.q_ref = bf16[16,4224]{1,0:T(8,128)(2,1)S(1)} collective-permute-done((bf16[16,4224]{1,0:T(8,128)(2,1)S(1)}, bf16[16,4224]{1,0:T(8,128)(2,1)S(1)}, u32[]{:S(2)}, u32[]{:S(2)}) %collective-permute-start.3) | collective-permute-done | bytes 135200 | tf_op jit(solution)/shard_map/ppermute | solution.py:389
  16.8 0.0 collective-permute-done.5.refs_5_.refs_0_
  16.8 3.3 %attend_side.1 = (bf16[2,4,4224]{2,1,0:T(4,128)(2,1)S(1)}, bf16[2,4,4224]{2,1,0:T(4,128)(2,1)S(1)}) custom-call(bf16[16,4224]{1,0:T(8,128)(2,1)S(1)} %collective-permute-done.3.q_ref, bf16[4,2,256,256]{3,2,1,0:T(8,128)(2,1)S(1)} %get-tuple-element.42.refs_0_, bf16[4,2,256,256]{3,2,1,0:T(8,128)(2,1)S(1)} %get-tuple-element.43.refs_1_, ...), custom_call_target="tpu_custom_call" | custom-call | flops 67108864 | bytes 67108864 | tf_op jit(solution)/shard_map/attend_side/pallas_call | solution.py:356
  20.1 1.6 %collective-permute-start.9 = (bf16[2,4,4224]{2,1,0:T(4,128)(2,1)S(1)}, bf16[2,4,4224]{2,1,0:T(4,128)(2,1)S(1)}, u32[]{:S(2)}, u32[]{:S(2)}) collective-permute-start(bf16[2,4,4224]{2,1,0:T(4,128)(2,1)S(1)} %get-tuple-element.52), channel_id=1, source_target_pairs={{0,4},{2,6},{4,0},{6,2},{8,12},{10,14},{12,8},{14,10},{16,20},{18,... | collective-permute-start | bytes 202760 | tf_op jit(solution)/shard_map/ppermute | solution.py:389
  21.7 0.5 %collective-permute-start.12 = (bf16[2,4,4224]{2,1,0:T(4,128)(2,1)S(1)}, bf16[2,4,4224]{2,1,0:T(4,128)(2,1)S(1)}, u32[]{:S(2)}, u32[]{:S(2)}) collective-permute-start(bf16[2,4,4224]{2,1,0:T(4,128)(2,1)S(1)} %get-tuple-element.58), channel_id=1, source_target_pairs={{0,4},{2,6},{4,0},{6,2},{8,12},{10,14},{12,8},{14,10},{16,20},{18,... | collective-permute-start | bytes 202760 | tf_op jit(solution)/shard_map/ppermute | solution.py:389
  22.2 1.7 %attend_own_other.1.came_ref = bf16[16,4224]{1,0:T(8,128)(2,1)S(1)} custom-call(bf16[16,4224]{1,0:T(8,128)(2,1)S(1)} %line.1.q_ref, bf16[4,256,512]{2,1,0:T(8,128)(2,1)S(1)} %collective-permute-done.5.refs_5_.refs_0_, bf16[4,256,512]{2,1,0:T(8,128)(2,1)S(1)} %collective-permute-done.6.refs_6_.refs_1_, s32[8,128]{1,0:T(8,128)S(1)} %collective-permute-done.4.refs_7_.refs_2_, ...), custom_call_target="tpu_custom_call" | custom-call | flops 67108864 | bytes 67108864 | tf_op jit(solution)/shard_map/attend_own_other/pallas_call | solution.py:356
  23.9 0.4 own_merge.1
  24.3 0.4 collective-permute-done.9.came_ref
  24.7 0.3 plane_merge.2
  25.0 3.4 %collective-permute-start.10 = (bf16[4,4224]{1,0:T(4,128)(2,1)S(1)}, bf16[4,4224]{1,0:T(4,128)(2,1)S(1)}, u32[]{:S(2)}, u32[]{:S(2)}) collective-permute-start(bf16[4,4224]{1,0:T(4,128)(2,1)S(1)} %get-tuple-element.55), channel_id=1, source_target_pairs={{0,24},{2,26},{4,28},{6,30},{8,16},{10,18},{12,20},{14,22},{16,8},... | collective-permute-start | bytes 101384 | tf_op jit(solution)/shard_map/ppermute | solution.py:389
  28.4 0.3 plane_merge.3
  28.6 1.1 %collective-permute-start.13 = (bf16[4,4224]{1,0:T(4,128)(2,1)S(1)}, bf16[4,4224]{1,0:T(4,128)(2,1)S(1)}, u32[]{:S(2)}, u32[]{:S(2)}) collective-permute-start(bf16[4,4224]{1,0:T(4,128)(2,1)S(1)} %get-tuple-element.59), channel_id=1, source_target_pairs={{0,8},{2,10},{4,12},{6,14},{8,0},{10,2},{12,4},{14,6},{16,24},{18,... | collective-permute-start | bytes 101384 | tf_op jit(solution)/shard_map/ppermute | solution.py:389
  29.8 1.0 %collective-permute-done.10.refs_0_ = bf16[4,4224]{1,0:T(4,128)(2,1)S(1)} collective-permute-done((bf16[4,4224]{1,0:T(4,128)(2,1)S(1)}, bf16[4,4224]{1,0:T(4,128)(2,1)S(1)}, u32[]{:S(2)}, u32[]{:S(2)}) %collective-permute-start.10) | collective-permute-done | bytes 33824 | tf_op jit(solution)/shard_map/ppermute | solution.py:389
  30.8 2.4 %collective-permute-done.11.refs_1_ = bf16[4,4224]{1,0:T(4,128)(2,1)S(1)} collective-permute-done((bf16[4,4224]{1,0:T(4,128)(2,1)S(1)}, bf16[4,4224]{1,0:T(4,128)(2,1)S(1)}, u32[]{:S(2)}, u32[]{:S(2)}) %collective-permute-start.11) | collective-permute-done | bytes 33824 | tf_op jit(solution)/shard_map/ppermute | solution.py:389
  33.2 0.5 finish.1
  33.7 1.9 %collective-permute-start.14 = (bf16[4,4096]{1,0:T(4,128)(2,1)S(1)}, bf16[4,4096]{1,0:T(4,128)(2,1)S(1)}, u32[]{:S(2)}, u32[]{:S(2)}) collective-permute-start(bf16[4,4096]{1,0:T(4,128)(2,1)S(1)} %finish.1), channel_id=1, source_target_pairs={{0,24},{2,26},{4,28},{6,30},{8,16},{10,18},{12,20},{14,22},{16,8},... | collective-permute-start | bytes 98312 | tf_op jit(solution)/shard_map/ppermute | solution.py:389
  35.5 0.7 %collective-permute-start.18 = (bf16[4,4096]{1,0:T(4,128)(2,1)S(1)}, bf16[4,4096]{1,0:T(4,128)(2,1)S(1)}, u32[]{:S(2)}, u32[]{:S(2)}) collective-permute-start(bf16[4,4096]{1,0:T(4,128)(2,1)S(1)} %finish.1), channel_id=1, source_target_pairs={{0,16},{2,18},{4,20},{6,22},{8,24},{10,26},{12,28},{14,30},{16,0},... | collective-permute-start | bytes 98312 | tf_op jit(solution)/shard_map/ppermute | solution.py:389
  36.2 1.9 %collective-permute-start.17 = (bf16[4,4096]{1,0:T(4,128)(2,1)S(1)}, bf16[4,4096]{1,0:T(4,128)(2,1)S(1)}, u32[]{:S(2)}, u32[]{:S(2)}) collective-permute-start(bf16[4,4096]{1,0:T(4,128)(2,1)S(1)} %finish.1), channel_id=1, source_target_pairs={{0,8},{2,10},{4,12},{6,14},{8,0},{10,2},{12,4},{14,6},{16,24},{18,... | collective-permute-start | bytes 98312 | tf_op jit(solution)/shard_map/ppermute | solution.py:389
  38.1 1.3 %collective-permute-done.14 = bf16[4,4096]{1,0:T(4,128)(2,1)S(1)} collective-permute-done((bf16[4,4096]{1,0:T(4,128)(2,1)S(1)}, bf16[4,4096]{1,0:T(4,128)(2,1)S(1)}, u32[]{:S(2)}, u32[]{:S(2)}) %collective-permute-start.14) | collective-permute-done | bytes 32800 | tf_op jit(solution)/shard_map/ppermute | solution.py:389
  39.4 0.1 fusion.1
  39.5 1.3 %collective-permute-start.15 = (bf16[2,4,4096]{2,1,0:T(4,128)(2,1)S(1)}, bf16[2,4,4096]{2,1,0:T(4,128)(2,1)S(1)}, u32[]{:S(2)}, u32[]{:S(2)}) collective-permute-start(bf16[2,4,4096]{2,1,0:T(4,128)(2,1)S(1)} %get-tuple-element.66), channel_id=1, source_target_pairs={{0,4},{2,6},{4,0},{6,2},{8,12},{10,14},{12,8},{14,10},{16,20},{18,... | collective-permute-start | bytes 196616 | tf_op jit(solution)/shard_map/ppermute | solution.py:389
  40.8 0.1 fusion
  40.8 0.9 %collective-permute-start.19 = (bf16[2,4,4096]{2,1,0:T(4,128)(2,1)S(1)}, bf16[2,4,4096]{2,1,0:T(4,128)(2,1)S(1)}, u32[]{:S(2)}, u32[]{:S(2)}) collective-permute-start(bf16[2,4,4096]{2,1,0:T(4,128)(2,1)S(1)} %get-tuple-element.64), channel_id=1, source_target_pairs={{0,4},{2,6},{4,0},{6,2},{8,12},{10,14},{12,8},{14,10},{16,20},{18,... | collective-permute-start | bytes 196616 | tf_op jit(solution)/shard_map/ppermute | solution.py:389
  41.8 2.1 %collective-permute-done.15 = bf16[2,4,4096]{2,1,0:T(4,128)(2,1)S(1)} collective-permute-done((bf16[2,4,4096]{2,1,0:T(4,128)(2,1)S(1)}, bf16[2,4,4096]{2,1,0:T(4,128)(2,1)S(1)}, u32[]{:S(2)}, u32[]{:S(2)}) %collective-permute-start.15) | collective-permute-done | bytes 65568 | tf_op jit(solution)/shard_map/ppermute | solution.py:389
  43.8 0.1 pad_maximum_fusion.near_a
  43.9 0.1 collective-permute-start.16
  44.0 1.1 %collective-permute-done.19 = bf16[2,4,4096]{2,1,0:T(4,128)(2,1)S(1)} collective-permute-done((bf16[2,4,4096]{2,1,0:T(4,128)(2,1)S(1)}, bf16[2,4,4096]{2,1,0:T(4,128)(2,1)S(1)}, u32[]{:S(2)}, u32[]{:S(2)}) %collective-permute-start.19) | collective-permute-done | bytes 65568 | tf_op jit(solution)/shard_map/ppermute | solution.py:389
  45.2 0.1 pad_maximum_fusion.1.near_b
  45.2 0.1 collective-permute-start.20
  45.3 0.0 collective-permute-done.16.far_a
  45.3 1.3 %collective-permute-done.20.far_b = bf16[2,2,4,4096]{3,2,1,0:T(4,128)(2,1)S(1)} collective-permute-done((bf16[2,2,4,4096]{3,2,1,0:T(4,128)(2,1)S(1)}, bf16[2,2,4,4096]{3,2,1,0:T(4,128)(2,1)S(1)}, u32[]{:S(2)}, u32[]{:S(2)}) %collective-permute-start.20) | collective-permute-done | bytes 131104 | tf_op jit(solution)/shard_map/ppermute | solution.py:389
  46.7 0.9 %project.1 = (f32[32,512]{1,0:T(8,128)S(1)}, bf16[32,512]{1,0:T(8,128)(2,1)S(1)}) custom-call(bf16[2,2,4,4096]{3,2,1,0:T(4,128)(2,1)S(1)} %pad_maximum_fusion.near_a, bf16[2,2,4,4096]{3,2,1,0:T(4,128)(2,1)S(1)} %collective-permute-done.16.far_a, bf16[2,2,4,4096]{3,2,1,0:T(4,128)(2,1)S(1)} %pad_maximum_fusion.1.near_b, ...), custom_call_target="tpu_custom_call" | custom-call | tf_op jit(solution)/shard_map/project/pallas_call | solution.py:356
  47.5 1.6 %collective-permute-start.21 = (bf16[32,512]{1,0:T(8,128)(2,1)S(1)}, bf16[32,512]{1,0:T(8,128)(2,1)S(1)}, u32[]{:S(2)}, u32[]{:S(2)}) collective-permute-start(bf16[32,512]{1,0:T(8,128)(2,1)S(1)} %get-tuple-element.62), channel_id=1, source_target_pairs={{0,1},{1,0},{2,3},{3,2},{4,5},{5,4},{6,7},{7,6},{8,9},{9,8},{10,11... | collective-permute-start | bytes 98312 | tf_op jit(solution)/shard_map/ppermute | solution.py:506
  49.1 2.4 %collective-permute-done.21 = bf16[32,512]{1,0:T(8,128)(2,1)S(1)} collective-permute-done((bf16[32,512]{1,0:T(8,128)(2,1)S(1)}, bf16[32,512]{1,0:T(8,128)(2,1)S(1)}, u32[]{:S(2)}, u32[]{:S(2)}) %collective-permute-start.21) | collective-permute-done | bytes 32800 | tf_op jit(solution)/shard_map/ppermute | solution.py:506
  51.5 0.6 %add_convert_fusion = bf16[32,512]{1,0:T(8,128)(2,1)} fusion(f32[32,512]{1,0:T(8,128)S(1)} %get-tuple-element.61, bf16[32,512]{1,0:T(8,128)(2,1)S(1)} %collective-permute-done.21), kind=kLoop, calls=%fused_computation.4 | loop fusion | flops 49152 | bytes 131072 | tf_op jit(solution)/shard_map/convert_element_type | solution.py:507
  (22 shorter events, 0.1 us)
Async XLA Ops:
  0.0 10.7 %copy-start.3 = (bf16[4,256,512]{2,1,0:T(8,128)(2,1)S(1)}, bf16[4,256,512]{2,1,0:T(8,128)(2,1)}, u32[]{:S(2)}) copy-start(bf16[4,256,512]{2,1,0:T(8,128)(2,1)} %pk_hbm) | copy-start | bytes 3145732
  0.0 10.7 %copy-start.4 = (bf16[4,256,512]{2,1,0:T(8,128)(2,1)S(1)}, bf16[4,256,512]{2,1,0:T(8,128)(2,1)}, u32[]{:S(2)}) copy-start(bf16[4,256,512]{2,1,0:T(8,128)(2,1)} %pv_hbm) | copy-start | bytes 3145732
  0.0 16.8 %collective-permute-start.7 = (bf16[4,512,512]{2,1,0:T(8,128)(2,1)}, bf16[4,512,512]{2,1,0:T(8,128)(2,1)S(1)}, u32[]{:S(2)}, u32[]{:S(2)}) collective-permute-start(bf16[4,512,512]{2,1,0:T(8,128)(2,1)} %ck_hbm.1), channel_id=1, source_target_pairs={{0,2},{2,0},{4,6},{6,4},{8,10},{10,8},{12,14},{14,12},{16,18},{18,... | collective-permute-start | bytes 6291464 | tf_op jit(solution)/shard_map/ppermute | solution.py:389
  0.5 16.4 %collective-permute-start.8 = (bf16[4,512,512]{2,1,0:T(8,128)(2,1)}, bf16[4,512,512]{2,1,0:T(8,128)(2,1)S(1)}, u32[]{:S(2)}, u32[]{:S(2)}) collective-permute-start(bf16[4,512,512]{2,1,0:T(8,128)(2,1)} %cv_hbm.1), channel_id=1, source_target_pairs={{0,2},{2,0},{4,6},{6,4},{8,10},{10,8},{12,14},{14,12},{16,18},{18,... | collective-permute-start | bytes 6291464 | tf_op jit(solution)/shard_map/ppermute | solution.py:389
  0.5 8.3 %collective-permute-start = (bf16[4,4096]{1,0:T(4,128)(2,1)}, bf16[4,4096]{1,0:T(4,128)(2,1)S(1)}, u32[]{:S(2)}, u32[]{:S(2)}) collective-permute-start(bf16[4,4096]{1,0:T(4,128)(2,1)} %q_hbm.1), channel_id=1, source_target_pairs={{0,24},{2,26},{4,28},{6,30},{8,16},{10,18},{12,20},{14,22},{16,8},... | collective-permute-start | bytes 98312 | tf_op jit(solution)/shard_map/ppermute | solution.py:389
  5.6 5.0 %collective-permute-start.1 = (bf16[4,4096]{1,0:T(4,128)(2,1)}, bf16[4,4096]{1,0:T(4,128)(2,1)S(1)}, u32[]{:S(2)}, u32[]{:S(2)}) collective-permute-start(bf16[4,4096]{1,0:T(4,128)(2,1)} %q_hbm.1), channel_id=1, source_target_pairs={{0,16},{2,18},{4,20},{6,22},{8,24},{10,26},{12,28},{14,30},{16,0},... | collective-permute-start | bytes 98312 | tf_op jit(solution)/shard_map/ppermute | solution.py:389
  5.6 5.0 %collective-permute-start.2 = (bf16[4,4096]{1,0:T(4,128)(2,1)}, bf16[4,4096]{1,0:T(4,128)(2,1)S(1)}, u32[]{:S(2)}, u32[]{:S(2)}) collective-permute-start(bf16[4,4096]{1,0:T(4,128)(2,1)} %q_hbm.1), channel_id=1, source_target_pairs={{0,8},{2,10},{4,12},{6,14},{8,0},{10,2},{12,4},{14,6},{16,24},{18,... | collective-permute-start | bytes 98312 | tf_op jit(solution)/shard_map/ppermute | solution.py:389
  8.8 1.8 %collective-permute-start.4 = (s32[8,128]{1,0:T(8,128)S(1)}, s32[8,128]{1,0:T(8,128)S(1)}, u32[]{:S(2)}, u32[]{:S(2)}) collective-permute-start(s32[8,128]{1,0:T(8,128)S(1)} %get-tuple-element.44.refs_2_), channel_id=1, source_target_pairs={{0,2},{2,0},{4,6},{6,4},{8,10},{10,8},{12,14},{14,12},{16,18},{18,... | collective-permute-start | bytes 12296 | tf_op jit(solution)/shard_map/ppermute | solution.py:389
  10.7 6.2 %collective-permute-start.5 = (bf16[4,256,512]{2,1,0:T(8,128)(2,1)S(1)}, bf16[4,256,512]{2,1,0:T(8,128)(2,1)S(1)}, u32[]{:S(2)}, u32[]{:S(2)}) collective-permute-start(bf16[4,256,512]{2,1,0:T(8,128)(2,1)S(1)} %copy-done.3), channel_id=1, source_target_pairs={{0,2},{2,0},{4,6},{6,4},{8,10},{10,8},{12,14},{14,12},{16,18},{18,... | collective-permute-start | bytes 3145736 | tf_op jit(solution)/shard_map/ppermute | solution.py:389
  10.8 6.1 %collective-permute-start.6 = (bf16[4,256,512]{2,1,0:T(8,128)(2,1)S(1)}, bf16[4,256,512]{2,1,0:T(8,128)(2,1)S(1)}, u32[]{:S(2)}, u32[]{:S(2)}) collective-permute-start(bf16[4,256,512]{2,1,0:T(8,128)(2,1)S(1)} %copy-done.4), channel_id=1, source_target_pairs={{0,2},{2,0},{4,6},{6,4},{8,10},{10,8},{12,14},{14,12},{16,18},{18,... | collective-permute-start | bytes 3145736 | tf_op jit(solution)/shard_map/ppermute | solution.py:389
  11.2 5.6 %collective-permute-start.3 = (bf16[16,4224]{1,0:T(8,128)(2,1)S(1)}, bf16[16,4224]{1,0:T(8,128)(2,1)S(1)}, u32[]{:S(2)}, u32[]{:S(2)}) collective-permute-start(bf16[16,4224]{1,0:T(8,128)(2,1)S(1)} %line.1.q_ref), channel_id=1, source_target_pairs={{0,4},{2,6},{4,0},{6,2},{8,12},{10,14},{12,8},{14,10},{16,20},{18,... | collective-permute-start | bytes 405512 | tf_op jit(solution)/shard_map/ppermute | solution.py:389
  20.1 4.6 %collective-permute-start.9 = (bf16[2,4,4224]{2,1,0:T(4,128)(2,1)S(1)}, bf16[2,4,4224]{2,1,0:T(4,128)(2,1)S(1)}, u32[]{:S(2)}, u32[]{:S(2)}) collective-permute-start(bf16[2,4,4224]{2,1,0:T(4,128)(2,1)S(1)} %get-tuple-element.52), channel_id=1, source_target_pairs={{0,4},{2,6},{4,0},{6,2},{8,12},{10,14},{12,8},{14,10},{16,20},{18,... | collective-permute-start | bytes 202760 | tf_op jit(solution)/shard_map/ppermute | solution.py:389
  21.7 11.5 %copy-start.1 = (bf16[4,512]{1,0:T(4,128)(2,1)S(1)}, bf16[4,512]{1,0:T(4,128)(2,1)}, u32[]{:S(2)}) copy-start(bf16[4,512]{1,0:T(4,128)(2,1)} %nk_ref.1) | copy-start | bytes 12292
  21.7 11.5 %copy-start.2 = (bf16[4,512]{1,0:T(4,128)(2,1)S(1)}, bf16[4,512]{1,0:T(4,128)(2,1)}, u32[]{:S(2)}) copy-start(bf16[4,512]{1,0:T(4,128)(2,1)} %nv_ref.1) | copy-start | bytes 12292
  21.7 6.7 %collective-permute-start.12 = (bf16[2,4,4224]{2,1,0:T(4,128)(2,1)S(1)}, bf16[2,4,4224]{2,1,0:T(4,128)(2,1)S(1)}, u32[]{:S(2)}, u32[]{:S(2)}) collective-permute-start(bf16[2,4,4224]{2,1,0:T(4,128)(2,1)S(1)} %get-tuple-element.58), channel_id=1, source_target_pairs={{0,4},{2,6},{4,0},{6,2},{8,12},{10,14},{12,8},{14,10},{16,20},{18,... | collective-permute-start | bytes 202760 | tf_op jit(solution)/shard_map/ppermute | solution.py:389
  22.2 24.4 %copy-start = (bf16[4096,512]{1,0:T(8,128)(2,1)S(1)}, bf16[4096,512]{1,0:T(8,128)(2,1)}, u32[]{:S(2)}) copy-start(bf16[4096,512]{1,0:T(8,128)(2,1)} %w_ref.1) | copy-start | bytes 12582916
  25.0 5.8 %collective-permute-start.10 = (bf16[4,4224]{1,0:T(4,128)(2,1)S(1)}, bf16[4,4224]{1,0:T(4,128)(2,1)S(1)}, u32[]{:S(2)}, u32[]{:S(2)}) collective-permute-start(bf16[4,4224]{1,0:T(4,128)(2,1)S(1)} %get-tuple-element.55), channel_id=1, source_target_pairs={{0,24},{2,26},{4,28},{6,30},{8,16},{10,18},{12,20},{14,22},{16,8},... | collective-permute-start | bytes 101384 | tf_op jit(solution)/shard_map/ppermute | solution.py:389
  28.4 4.8 %collective-permute-start.11 = (bf16[4,4224]{1,0:T(4,128)(2,1)S(1)}, bf16[4,4224]{1,0:T(4,128)(2,1)S(1)}, u32[]{:S(2)}, u32[]{:S(2)}) collective-permute-start(bf16[4,4224]{1,0:T(4,128)(2,1)S(1)} %get-tuple-element.56), channel_id=1, source_target_pairs={{0,16},{2,18},{4,20},{6,22},{8,24},{10,26},{12,28},{14,30},{16,0},... | collective-permute-start | bytes 101384 | tf_op jit(solution)/shard_map/ppermute | solution.py:389
  28.6 4.5 %collective-permute-start.13 = (bf16[4,4224]{1,0:T(4,128)(2,1)S(1)}, bf16[4,4224]{1,0:T(4,128)(2,1)S(1)}, u32[]{:S(2)}, u32[]{:S(2)}) collective-permute-start(bf16[4,4224]{1,0:T(4,128)(2,1)S(1)} %get-tuple-element.59), channel_id=1, source_target_pairs={{0,8},{2,10},{4,12},{6,14},{8,0},{10,2},{12,4},{14,6},{16,24},{18,... | collective-permute-start | bytes 101384 | tf_op jit(solution)/shard_map/ppermute | solution.py:389
  33.7 5.8 %collective-permute-start.14 = (bf16[4,4096]{1,0:T(4,128)(2,1)S(1)}, bf16[4,4096]{1,0:T(4,128)(2,1)S(1)}, u32[]{:S(2)}, u32[]{:S(2)}) collective-permute-start(bf16[4,4096]{1,0:T(4,128)(2,1)S(1)} %finish.1), channel_id=1, source_target_pairs={{0,24},{2,26},{4,28},{6,30},{8,16},{10,18},{12,20},{14,22},{16,8},... | collective-permute-start | bytes 98312 | tf_op jit(solution)/shard_map/ppermute | solution.py:389
  35.5 5.2 %collective-permute-start.18 = (bf16[4,4096]{1,0:T(4,128)(2,1)S(1)}, bf16[4,4096]{1,0:T(4,128)(2,1)S(1)}, u32[]{:S(2)}, u32[]{:S(2)}) collective-permute-start(bf16[4,4096]{1,0:T(4,128)(2,1)S(1)} %finish.1), channel_id=1, source_target_pairs={{0,16},{2,18},{4,20},{6,22},{8,24},{10,26},{12,28},{14,30},{16,0},... | collective-permute-start | bytes 98312 | tf_op jit(solution)/shard_map/ppermute | solution.py:389
  36.2 4.6 %collective-permute-start.17 = (bf16[4,4096]{1,0:T(4,128)(2,1)S(1)}, bf16[4,4096]{1,0:T(4,128)(2,1)S(1)}, u32[]{:S(2)}, u32[]{:S(2)}) collective-permute-start(bf16[4,4096]{1,0:T(4,128)(2,1)S(1)} %finish.1), channel_id=1, source_target_pairs={{0,8},{2,10},{4,12},{6,14},{8,0},{10,2},{12,4},{14,6},{16,24},{18,... | collective-permute-start | bytes 98312 | tf_op jit(solution)/shard_map/ppermute | solution.py:389
  39.5 4.3 %collective-permute-start.15 = (bf16[2,4,4096]{2,1,0:T(4,128)(2,1)S(1)}, bf16[2,4,4096]{2,1,0:T(4,128)(2,1)S(1)}, u32[]{:S(2)}, u32[]{:S(2)}) collective-permute-start(bf16[2,4,4096]{2,1,0:T(4,128)(2,1)S(1)} %get-tuple-element.66), channel_id=1, source_target_pairs={{0,4},{2,6},{4,0},{6,2},{8,12},{10,14},{12,8},{14,10},{16,20},{18,... | collective-permute-start | bytes 196616 | tf_op jit(solution)/shard_map/ppermute | solution.py:389
  40.8 4.3 %collective-permute-start.19 = (bf16[2,4,4096]{2,1,0:T(4,128)(2,1)S(1)}, bf16[2,4,4096]{2,1,0:T(4,128)(2,1)S(1)}, u32[]{:S(2)}, u32[]{:S(2)}) collective-permute-start(bf16[2,4,4096]{2,1,0:T(4,128)(2,1)S(1)} %get-tuple-element.64), channel_id=1, source_target_pairs={{0,4},{2,6},{4,0},{6,2},{8,12},{10,14},{12,8},{14,10},{16,20},{18,... | collective-permute-start | bytes 196616 | tf_op jit(solution)/shard_map/ppermute | solution.py:389
  43.9 1.4 %collective-permute-start.16 = (bf16[2,2,4,4096]{3,2,1,0:T(4,128)(2,1)S(1)}, bf16[2,2,4,4096]{3,2,1,0:T(4,128)(2,1)S(1)}, u32[]{:S(2)}, u32[]{:S(2)}) collective-permute-start(bf16[2,2,4,4096]{3,2,1,0:T(4,128)(2,1)S(1)} %pad_maximum_fusion.near_a), channel_id=1, source_target_pairs={{0,2},{2,0},{4,6},{6,4},{8,10},{10,8},{12,14},{14,12},{16,18},{18,... | collective-permute-start | bytes 393224 | tf_op jit(solution)/shard_map/ppermute | solution.py:389
  45.2 1.4 %collective-permute-start.20 = (bf16[2,2,4,4096]{3,2,1,0:T(4,128)(2,1)S(1)}, bf16[2,2,4,4096]{3,2,1,0:T(4,128)(2,1)S(1)}, u32[]{:S(2)}, u32[]{:S(2)}) collective-permute-start(bf16[2,2,4,4096]{3,2,1,0:T(4,128)(2,1)S(1)} %pad_maximum_fusion.1.near_b), channel_id=1, source_target_pairs={{0,2},{2,0},{4,6},{6,4},{8,10},{10,8},{12,14},{14,12},{16,18},{18,... | collective-permute-start | bytes 393224 | tf_op jit(solution)/shard_map/ppermute | solution.py:389
  47.5 4.0 %collective-permute-start.21 = (bf16[32,512]{1,0:T(8,128)(2,1)S(1)}, bf16[32,512]{1,0:T(8,128)(2,1)S(1)}, u32[]{:S(2)}, u32[]{:S(2)}) collective-permute-start(bf16[32,512]{1,0:T(8,128)(2,1)S(1)} %get-tuple-element.62), channel_id=1, source_target_pairs={{0,1},{1,0},{2,3},{3,2},{4,5},{5,4},{6,7},{7,6},{8,9},{9,8},{10,11... | collective-permute-start | bytes 98312 | tf_op jit(solution)/shard_map/ppermute | solution.py:506

commit v5 on v4

--- a/solution.py
+++ b/solution.py
@@ -45,22 +45,15 @@
     q_hbm, par_hbm, cnt_hbm, ck_hbm, cv_hbm,
     q_ref, tail_ref, lim_ref, ck_ref, cv_ref, par_ref, cnt_ref, sems, old_sems,
 ):
-    heads = ck_ref.shape[0]
     olds = ck_hbm.shape[0]
     copies = [
         pltpu.make_async_copy(src, dst, sems.at[n])
         for n, (src, dst) in enumerate(((q_hbm, q_ref), (par_hbm, par_ref), (cnt_hbm, cnt_ref)))
+    ] + [
+        pltpu.make_async_copy(src.at[o], dst.at[o], old_sems.at[n, o])
+        for n, (src, dst) in enumerate(((ck_hbm, ck_ref), (cv_hbm, cv_ref)))
+        for o in range(olds)
     ]
-    for k in range(heads):
-        for n, (src, dst) in enumerate(((ck_hbm, ck_ref), (cv_hbm, cv_ref))):
-            for o in range(olds):
-                copies.append(
-                    pltpu.make_async_copy(
-                        src.at[o, :, pl.ds(k * HD, HD)],
-                        dst.at[k, :, pl.ds(o * HD, HD)],
-                        old_sems.at[n, k, o],
-                    )
-                )
     for x in copies:
         x.start()
     for x in copies[:3]:
@@ -79,19 +72,11 @@
         x.wait()
 
 
-def load_prompt_kernel(group, pk_hbm, pv_hbm, pk_ref, pv_ref, sems):
-    heads, pairs, _, _ = pk_ref.shape
-    mine = lax.axis_index("beam") // group
-    order = line_order(2 * pairs)
+def load_prompt_kernel(pk_hbm, pv_hbm, pk_ref, pv_ref, sems):
     copies = [
-        pltpu.make_async_copy(
-            src.at[mine ^ t, :, pl.ds(k * HD, HD)],
-            dst.at[k, at // 2, :, pl.ds(at % 2 * HD, HD)],
-            sems.at[n, k, at],
-        )
-        for k in range(heads)
+        pltpu.make_async_copy(src.at[r], dst.at[r], sems.at[n, r])
         for n, (src, dst) in enumerate(((pk_hbm, pk_ref), (pv_hbm, pv_ref)))
-        for at, t in enumerate(order)
+        for r in range(pk_ref.shape[0])
     ]
     for x in copies:
         x.start()
@@ -114,15 +99,11 @@
     order = line_order(requests)
     olds = beams
 
-    def prompt(n, ref, k, u):
-        if not kinds[n]:
-            return ref[k, u]
+    def prompt(ref, k, u):
         both = [ref[mine ^ order[2 * u + m], :, k * HD : (k + 1) * HD] for m in range(2)]
         return jnp.concatenate(both, axis=1)
 
-    def private(n, ref, k):
-        if not kinds[n]:
-            return ref[k]
+    def private(ref, k):
         return jnp.concatenate([ref[o, :, k * HD : (k + 1) * HD] for o in range(olds)], axis=1)
 
     whose = jnp.concatenate([q_ref[:, total - STATS :].astype(f32)[:beams]] * QPK, axis=0)
@@ -157,11 +138,11 @@
                 ],
                 axis=0,
             )
-            s_ref[n, k, 2 * u * rows : 2 * (u + 1) * rows] = dot(both, prompt(n, pk_ref, k, u), 1, 1)
+            s_ref[n, k, 2 * u * rows : 2 * (u + 1) * rows] = dot(both, prompt(pk_ref, k, u), 1, 1)
         chosen = jnp.concatenate(
             [jnp.where(parents[n] == o, q[-1], blank) for o in range(olds)], axis=1
         )
-        cs_ref[n, k] = dot(chosen, private(n, ck_ref, k), 1, 1)
+        cs_ref[n, k] = dot(chosen, private(ck_ref, k), 1, 1)
 
     def weigh(n, k):
         p, top, den = soft(s_ref[n, k])
@@ -177,12 +158,12 @@
         found = []
         for u in range(pairs):
             both = dot(
-                p_ref[n, k, 2 * u * rows : 2 * (u + 1) * rows], prompt(n, pv_ref, k, u), 1, 0
+                p_ref[n, k, 2 * u * rows : 2 * (u + 1) * rows], prompt(pv_ref, k, u), 1, 0
             )
             for m, num in enumerate((both[:rows, :HD], both[rows:, HD:])):
                 part = slice((2 * u + m) * rows, (2 * u + m + 1) * rows)
                 found.append((num, tops[part], dens[part]))
-        every = dot(cp_ref[n, k], private(n, cv_ref, k), 1, 0)
+        every = dot(cp_ref[n, k], private(cv_ref, k), 1, 0)
         cnum = every[:, :HD]
         for o in range(1, olds):
             cnum = jnp.where(parents[n] == o, every[:, o * HD : (o + 1) * HD], cnum)
@@ -395,8 +376,8 @@
     order = line_order(requests)
     others = order[:-1]
     came = [swap(queries, t * group) for t in others]
-    prompt = jax.ShapeDtypeStruct((heads, requests // 2, length, 2 * HD), bf16)
-    private = jax.ShapeDtypeStruct((heads, span, beams * HD), bf16)
+    prompt = jax.ShapeDtypeStruct(prompt_keys.shape, bf16)
+    private = jax.ShapeDtypeStruct(private_keys.shape, bf16)
     stored = (swap(private_keys, 1), swap(private_values, 1))
     own, parent_tail, *olds = call(
         load_private_kernel,
@@ -418,7 +399,7 @@
             pltpu.SMEM((beams,), jnp.int32),
             pltpu.SMEM((beams,), jnp.int32),
             pltpu.SemaphoreType.DMA((3,)),
-            pltpu.SemaphoreType.DMA((2, heads, beams)),
+            pltpu.SemaphoreType.DMA((2, beams)),
         ],
         vmem=10,
         cost=2**26,
@@ -427,13 +408,13 @@
     asked = call(line_kernel, "line", line, parent_tail, *came, own)
     prompt_keys, prompt_values, _ = lax.optimization_barrier((prompt_keys, prompt_values, asked))
     prompts = call(
-        functools.partial(load_prompt_kernel, group),
+        load_prompt_kernel,
         "load_prompt",
         (prompt, prompt),
         prompt_keys,
         prompt_values,
         far=(0, 1),
-        scratch=[pltpu.SemaphoreType.DMA((2, heads, requests))],
+        scratch=[pltpu.SemaphoreType.DMA((2, requests))],
         vmem=10,
         cost=2**26,
     )

time: 52.3 us -> 52 us (level)
  transfers between devices with their start and end apart: 22 -> 22, of which waited for: 10 -> 10; matrix products, arithmetic and copies ran while one was open for 1% -> 1% of each run, Pallas kernels for 17% -> 16%
where the time goes in v5:
time: 52 us; the launch traced here: 51.9 us
  starting transfers between devices  23.3 us (45%)
  waiting for transfers between devices  14.5 us (28%)
  Pallas kernels  13 us (25%)
  other arithmetic  0.92 us (2%)
    ppermute x21, starting transfers between devices, swap(): return lax.ppermute(x, 'beam', [(i, i ^ with_bit) for i in range(devices)])  21.7 us
    pallas_call x11, Pallas kernels, call(): pl.pallas_call(kernel, out_shape=out_shape, in_specs=whole_blocks(len(arg...  13 us
    ppermute x21, waiting for transfers between devices, swap(): return lax.ppermute(x, 'beam', [(i, i ^ with_bit) for i in range(devices)])  12.1 us
    ppermute x1, waiting for transfers between devices, per_device(): came = lax.ppermute(send, 'head', [(0, 1), (1, 0)])  2.39 us
    ppermute x1, starting transfers between devices, per_device(): came = lax.ppermute(send, 'head', [(0, 1), (1, 0)])  1.59 us
  transfers between devices with their start and end apart: 22, of which 10 were waited for; matrix products, arithmetic and copies ran while one was open for 1% of the time, Pallas kernels for 16%

profile of v5, /device:TPU:0, one launch (start us, length us, event | category | flops | bytes accessed | tf_op | source)
XLA Modules:
  0.0 51.9 jit_solution(7651427062512478732)
XLA Ops:
  0.0 0.5 collective-permute-start.7
  0.5 0.1 collective-permute-start.8
  0.5 5.0 %collective-permute-start = (bf16[4,4096]{1,0:T(4,128)(2,1)}, bf16[4,4096]{1,0:T(4,128)(2,1)S(1)}, u32[]{:S(2)}, u32[]{:S(2)}) collective-permute-start(bf16[4,4096]{1,0:T(4,128)(2,1)} %q_hbm.1), channel_id=1, source_target_pairs={{0,24},{2,26},{4,28},{6,30},{8,16},{10,18},{12,20},{14,22},{16,8},... | collective-permute-start | bytes 98312 | tf_op jit(solution)/shard_map/ppermute | solution.py:370
  5.6 0.0 collective-permute-start.1
  5.6 0.6 %collective-permute-start.2 = (bf16[4,4096]{1,0:T(4,128)(2,1)}, bf16[4,4096]{1,0:T(4,128)(2,1)S(1)}, u32[]{:S(2)}, u32[]{:S(2)}) collective-permute-start(bf16[4,4096]{1,0:T(4,128)(2,1)} %q_hbm.1), channel_id=1, source_target_pairs={{0,8},{2,10},{4,12},{6,14},{8,0},{10,2},{12,4},{14,6},{16,24},{18,... | collective-permute-start | bytes 98312 | tf_op jit(solution)/shard_map/ppermute | solution.py:370
  6.1 2.3 %load_private.1 = (bf16[4,4096]{1,0:T(4,128)(2,1)S(1)}, bf16[4,128]{1,0:T(4,128)(2,1)S(1)}, s32[8,128]{1,0:T(8,128)S(1)}, bf16[4,512,512]{2,1,0:T(8,128)(2,1)S(1)}, bf16[4,512,512]{2,1,0:T(8,128)(2,1)S(1)}) custom-call(bf16[4,4096]{1,0:T(4,128)(2,1)} %q_hbm.1, s32[4]{0:T(128)} %par_hbm.1, s32[4]{0:T(128)} %cnt_hbm.1, bf16[4,512,512]{2,1,0:T(8,128)(2,1)} %ck_hbm.1, ...), custom_call_target="tpu_custom_call" | custom-call | flops 67108864 | bytes 67108864 | tf_op jit(solution)/shard_map/load_private/pallas_call | solution.py:337
  8.4 0.1 collective-permute-start.4
  8.5 2.1 %collective-permute-done.1.refs_1_ = bf16[4,4096]{1,0:T(4,128)(2,1)S(1)} collective-permute-done((bf16[4,4096]{1,0:T(4,128)(2,1)}, bf16[4,4096]{1,0:T(4,128)(2,1)S(1)}, u32[]{:S(2)}, u32[]{:S(2)}) %collective-permute-start.1) | collective-permute-done | bytes 32800 | tf_op jit(solution)/shard_map/ppermute | solution.py:370
  10.6 0.0 collective-permute-done.2.refs_2_
  10.7 0.1 collective-permute-start.5
  10.8 0.5 collective-permute-start.6
  11.2 1.5 %collective-permute-start.3 = (bf16[16,4224]{1,0:T(8,128)(2,1)S(1)}, bf16[16,4224]{1,0:T(8,128)(2,1)S(1)}, u32[]{:S(2)}, u32[]{:S(2)}) collective-permute-start(bf16[16,4224]{1,0:T(8,128)(2,1)S(1)} %line.1.q_ref), channel_id=1, source_target_pairs={{0,4},{2,6},{4,0},{6,2},{8,12},{10,14},{12,8},{14,10},{16,20},{18,... | collective-permute-start | bytes 405512 | tf_op jit(solution)/shard_map/ppermute | solution.py:370
  12.7 1.6 %load_prompt.1 = (bf16[4,256,512]{2,1,0:T(8,128)(2,1)S(1)}, bf16[4,256,512]{2,1,0:T(8,128)(2,1)S(1)}) custom-call(bf16[4,256,512]{2,1,0:T(8,128)(2,1)} %pk_hbm, bf16[4,256,512]{2,1,0:T(8,128)(2,1)} %pv_hbm), custom_call_target="tpu_custom_call" | custom-call | flops 67108864 | bytes 67108864 | tf_op jit(solution)/shard_map/load_prompt/pallas_call | solution.py:337
  14.3 1.7 %attend_own.1.kept_ref = bf16[16,4224]{1,0:T(8,128)(2,1)S(1)} custom-call(bf16[16,4224]{1,0:T(8,128)(2,1)S(1)} %line.1.q_ref, bf16[4,256,512]{2,1,0:T(8,128)(2,1)S(1)} %get-tuple-element.42.refs_0_, bf16[4,256,512]{2,1,0:T(8,128)(2,1)S(1)} %get-tuple-element.43.refs_1_, s32[8,128]{1,0:T(8,128)S(1)} %get-tuple-element.44.refs_2_, ...), custom_call_target="tpu_custom_call" | custom-call | flops 67108864 | bytes 67108864 | tf_op jit(solution)/shard_map/attend_own/pallas_call | solution.py:337
  16.1 0.8 %collective-permute-done.3.q_ref = bf16[16,4224]{1,0:T(8,128)(2,1)S(1)} collective-permute-done((bf16[16,4224]{1,0:T(8,128)(2,1)S(1)}, bf16[16,4224]{1,0:T(8,128)(2,1)S(1)}, u32[]{:S(2)}, u32[]{:S(2)}) %collective-permute-start.3) | collective-permute-done | bytes 135200 | tf_op jit(solution)/shard_map/ppermute | solution.py:370
  16.8 3.4 %attend_side.1 = (bf16[2,4,4224]{2,1,0:T(4,128)(2,1)S(1)}, bf16[2,4,4224]{2,1,0:T(4,128)(2,1)S(1)}) custom-call(bf16[16,4224]{1,0:T(8,128)(2,1)S(1)} %collective-permute-done.3.q_ref, bf16[4,256,512]{2,1,0:T(8,128)(2,1)S(1)} %get-tuple-element.42.refs_0_, bf16[4,256,512]{2,1,0:T(8,128)(2,1)S(1)} %get-tuple-element.43.refs_1_, ...), custom_call_target="tpu_custom_call" | custom-call | flops 67108864 | bytes 67108864 | tf_op jit(solution)/shard_map/attend_side/pallas_call | solution.py:337
  20.3 1.6 %collective-permute-start.9 = (bf16[2,4,4224]{2,1,0:T(4,128)(2,1)S(1)}, bf16[2,4,4224]{2,1,0:T(4,128)(2,1)S(1)}, u32[]{:S(2)}, u32[]{:S(2)}) collective-permute-start(bf16[2,4,4224]{2,1,0:T(4,128)(2,1)S(1)} %get-tuple-element.52), channel_id=1, source_target_pairs={{0,4},{2,6},{4,0},{6,2},{8,12},{10,14},{12,8},{14,10},{16,20},{18,... | collective-permute-start | bytes 202760 | tf_op jit(solution)/shard_map/ppermute | solution.py:370
  21.8 0.5 %collective-permute-start.12 = (bf16[2,4,4224]{2,1,0:T(4,128)(2,1)S(1)}, bf16[2,4,4224]{2,1,0:T(4,128)(2,1)S(1)}, u32[]{:S(2)}, u32[]{:S(2)}) collective-permute-start(bf16[2,4,4224]{2,1,0:T(4,128)(2,1)S(1)} %get-tuple-element.58), channel_id=1, source_target_pairs={{0,4},{2,6},{4,0},{6,2},{8,12},{10,14},{12,8},{14,10},{16,20},{18,... | collective-permute-start | bytes 202760 | tf_op jit(solution)/shard_map/ppermute | solution.py:370
  22.4 1.7 %attend_own_other.1.came_ref = bf16[16,4224]{1,0:T(8,128)(2,1)S(1)} custom-call(bf16[16,4224]{1,0:T(8,128)(2,1)S(1)} %line.1.q_ref, bf16[4,256,512]{2,1,0:T(8,128)(2,1)S(1)} %collective-permute-done.5.refs_5_.refs_0_, bf16[4,256,512]{2,1,0:T(8,128)(2,1)S(1)} %collective-permute-done.6.refs_6_.refs_1_, s32[8,128]{1,0:T(8,128)S(1)} %collective-permute-done.4.refs_7_.refs_2_, ...), custom_call_target="tpu_custom_call" | custom-call | flops 67108864 | bytes 67108864 | tf_op jit(solution)/shard_map/attend_own_other/pallas_call | solution.py:337
  24.1 0.4 own_merge.1
  24.4 0.4 collective-permute-done.9.came_ref
  24.8 0.3 plane_merge.2
  25.1 3.0 %collective-permute-start.10 = (bf16[4,4224]{1,0:T(4,128)(2,1)S(1)}, bf16[4,4224]{1,0:T(4,128)(2,1)S(1)}, u32[]{:S(2)}, u32[]{:S(2)}) collective-permute-start(bf16[4,4224]{1,0:T(4,128)(2,1)S(1)} %get-tuple-element.55), channel_id=1, source_target_pairs={{0,24},{2,26},{4,28},{6,30},{8,16},{10,18},{12,20},{14,22},{16,8},... | collective-permute-start | bytes 101384 | tf_op jit(solution)/shard_map/ppermute | solution.py:370
  28.1 0.3 plane_merge.3
  28.4 1.5 %collective-permute-start.13 = (bf16[4,4224]{1,0:T(4,128)(2,1)S(1)}, bf16[4,4224]{1,0:T(4,128)(2,1)S(1)}, u32[]{:S(2)}, u32[]{:S(2)}) collective-permute-start(bf16[4,4224]{1,0:T(4,128)(2,1)S(1)} %get-tuple-element.59), channel_id=1, source_target_pairs={{0,8},{2,10},{4,12},{6,14},{8,0},{10,2},{12,4},{14,6},{16,24},{18,... | collective-permute-start | bytes 101384 | tf_op jit(solution)/shard_map/ppermute | solution.py:370
  29.9 1.0 %collective-permute-done.10.refs_0_ = bf16[4,4224]{1,0:T(4,128)(2,1)S(1)} collective-permute-done((bf16[4,4224]{1,0:T(4,128)(2,1)S(1)}, bf16[4,4224]{1,0:T(4,128)(2,1)S(1)}, u32[]{:S(2)}, u32[]{:S(2)}) %collective-permute-start.10) | collective-permute-done | bytes 33824 | tf_op jit(solution)/shard_map/ppermute | solution.py:370
  30.9 2.0 %collective-permute-done.11.refs_1_ = bf16[4,4224]{1,0:T(4,128)(2,1)S(1)} collective-permute-done((bf16[4,4224]{1,0:T(4,128)(2,1)S(1)}, bf16[4,4224]{1,0:T(4,128)(2,1)S(1)}, u32[]{:S(2)}, u32[]{:S(2)}) %collective-permute-start.11) | collective-permute-done | bytes 33824 | tf_op jit(solution)/shard_map/ppermute | solution.py:370
  32.9 0.5 finish.1
  33.4 2.0 %collective-permute-start.14 = (bf16[4,4096]{1,0:T(4,128)(2,1)S(1)}, bf16[4,4096]{1,0:T(4,128)(2,1)S(1)}, u32[]{:S(2)}, u32[]{:S(2)}) collective-permute-start(bf16[4,4096]{1,0:T(4,128)(2,1)S(1)} %finish.1), channel_id=1, source_target_pairs={{0,24},{2,26},{4,28},{6,30},{8,16},{10,18},{12,20},{14,22},{16,8},... | collective-permute-start | bytes 98312 | tf_op jit(solution)/shard_map/ppermute | solution.py:370
  35.5 0.5 collective-permute-start.18
  36.0 1.9 %collective-permute-start.17 = (bf16[4,4096]{1,0:T(4,128)(2,1)S(1)}, bf16[4,4096]{1,0:T(4,128)(2,1)S(1)}, u32[]{:S(2)}, u32[]{:S(2)}) collective-permute-start(bf16[4,4096]{1,0:T(4,128)(2,1)S(1)} %finish.1), channel_id=1, source_target_pairs={{0,8},{2,10},{4,12},{6,14},{8,0},{10,2},{12,4},{14,6},{16,24},{18,... | collective-permute-start | bytes 98312 | tf_op jit(solution)/shard_map/ppermute | solution.py:370
  37.9 1.3 %collective-permute-done.14 = bf16[4,4096]{1,0:T(4,128)(2,1)S(1)} collective-permute-done((bf16[4,4096]{1,0:T(4,128)(2,1)S(1)}, bf16[4,4096]{1,0:T(4,128)(2,1)S(1)}, u32[]{:S(2)}, u32[]{:S(2)}) %collective-permute-start.14) | collective-permute-done | bytes 32800 | tf_op jit(solution)/shard_map/ppermute | solution.py:370
  39.2 0.1 fusion.1
  39.2 1.2 %collective-permute-start.15 = (bf16[2,4,4096]{2,1,0:T(4,128)(2,1)S(1)}, bf16[2,4,4096]{2,1,0:T(4,128)(2,1)S(1)}, u32[]{:S(2)}, u32[]{:S(2)}) collective-permute-start(bf16[2,4,4096]{2,1,0:T(4,128)(2,1)S(1)} %get-tuple-element.66), channel_id=1, source_target_pairs={{0,4},{2,6},{4,0},{6,2},{8,12},{10,14},{12,8},{14,10},{16,20},{18,... | collective-permute-start | bytes 196616 | tf_op jit(solution)/shard_map/ppermute | solution.py:370
  40.5 0.1 fusion
  40.6 1.0 %collective-permute-start.19 = (bf16[2,4,4096]{2,1,0:T(4,128)(2,1)S(1)}, bf16[2,4,4096]{2,1,0:T(4,128)(2,1)S(1)}, u32[]{:S(2)}, u32[]{:S(2)}) collective-permute-start(bf16[2,4,4096]{2,1,0:T(4,128)(2,1)S(1)} %get-tuple-element.64), channel_id=1, source_target_pairs={{0,4},{2,6},{4,0},{6,2},{8,12},{10,14},{12,8},{14,10},{16,20},{18,... | collective-permute-start | bytes 196616 | tf_op jit(solution)/shard_map/ppermute | solution.py:370
  41.6 2.0 %collective-permute-done.15 = bf16[2,4,4096]{2,1,0:T(4,128)(2,1)S(1)} collective-permute-done((bf16[2,4,4096]{2,1,0:T(4,128)(2,1)S(1)}, bf16[2,4,4096]{2,1,0:T(4,128)(2,1)S(1)}, u32[]{:S(2)}, u32[]{:S(2)}) %collective-permute-start.15) | collective-permute-done | bytes 65568 | tf_op jit(solution)/shard_map/ppermute | solution.py:370
  43.6 0.1 pad_maximum_fusion.near_a
  43.7 0.1 collective-permute-start.16
  43.8 1.1 %collective-permute-done.19 = bf16[2,4,4096]{2,1,0:T(4,128)(2,1)S(1)} collective-permute-done((bf16[2,4,4096]{2,1,0:T(4,128)(2,1)S(1)}, bf16[2,4,4096]{2,1,0:T(4,128)(2,1)S(1)}, u32[]{:S(2)}, u32[]{:S(2)}) %collective-permute-start.19) | collective-permute-done | bytes 65568 | tf_op jit(solution)/shard_map/ppermute | solution.py:370
  44.9 0.1 pad_maximum_fusion.1.near_b
  45.0 0.1 collective-permute-start.20
  45.1 0.0 collective-permute-done.16.far_a
  45.1 1.3 %collective-permute-done.20.far_b = bf16[2,2,4,4096]{3,2,1,0:T(4,128)(2,1)S(1)} collective-permute-done((bf16[2,2,4,4096]{3,2,1,0:T(4,128)(2,1)S(1)}, bf16[2,2,4,4096]{3,2,1,0:T(4,128)(2,1)S(1)}, u32[]{:S(2)}, u32[]{:S(2)}) %collective-permute-start.20) | collective-permute-done | bytes 131104 | tf_op jit(solution)/shard_map/ppermute | solution.py:370
  46.4 0.9 %project.1 = (f32[32,512]{1,0:T(8,128)S(1)}, bf16[32,512]{1,0:T(8,128)(2,1)S(1)}) custom-call(bf16[2,2,4,4096]{3,2,1,0:T(4,128)(2,1)S(1)} %pad_maximum_fusion.near_a, bf16[2,2,4,4096]{3,2,1,0:T(4,128)(2,1)S(1)} %collective-permute-done.16.far_a, bf16[2,2,4,4096]{3,2,1,0:T(4,128)(2,1)S(1)} %pad_maximum_fusion.1.near_b, ...), custom_call_target="tpu_custom_call" | custom-call | tf_op jit(solution)/shard_map/project/pallas_call | solution.py:337
  47.3 1.6 %collective-permute-start.21 = (bf16[32,512]{1,0:T(8,128)(2,1)S(1)}, bf16[32,512]{1,0:T(8,128)(2,1)S(1)}, u32[]{:S(2)}, u32[]{:S(2)}) collective-permute-start(bf16[32,512]{1,0:T(8,128)(2,1)S(1)} %get-tuple-element.62), channel_id=1, source_target_pairs={{0,1},{1,0},{2,3},{3,2},{4,5},{5,4},{6,7},{7,6},{8,9},{9,8},{10,11... | collective-permute-start | bytes 98312 | tf_op jit(solution)/shard_map/ppermute | solution.py:487
  48.9 2.4 %collective-permute-done.21 = bf16[32,512]{1,0:T(8,128)(2,1)S(1)} collective-permute-done((bf16[32,512]{1,0:T(8,128)(2,1)S(1)}, bf16[32,512]{1,0:T(8,128)(2,1)S(1)}, u32[]{:S(2)}, u32[]{:S(2)}) %collective-permute-start.21) | collective-permute-done | bytes 32800 | tf_op jit(solution)/shard_map/ppermute | solution.py:487
  51.3 0.6 %add_convert_fusion = bf16[32,512]{1,0:T(8,128)(2,1)} fusion(f32[32,512]{1,0:T(8,128)S(1)} %get-tuple-element.61, bf16[32,512]{1,0:T(8,128)(2,1)S(1)} %collective-permute-done.21), kind=kLoop, calls=%fused_computation.4 | loop fusion | flops 49152 | bytes 131072 | tf_op jit(solution)/shard_map/convert_element_type | solution.py:488
  (22 shorter events, 0.1 us)
Async XLA Ops:
  0.0 10.7 %copy-start.3 = (bf16[4,256,512]{2,1,0:T(8,128)(2,1)S(1)}, bf16[4,256,512]{2,1,0:T(8,128)(2,1)}, u32[]{:S(2)}) copy-start(bf16[4,256,512]{2,1,0:T(8,128)(2,1)} %pk_hbm) | copy-start | bytes 3145732
  0.0 10.7 %copy-start.4 = (bf16[4,256,512]{2,1,0:T(8,128)(2,1)S(1)}, bf16[4,256,512]{2,1,0:T(8,128)(2,1)}, u32[]{:S(2)}) copy-start(bf16[4,256,512]{2,1,0:T(8,128)(2,1)} %pv_hbm) | copy-start | bytes 3145732
  0.0 16.8 %collective-permute-start.7 = (bf16[4,512,512]{2,1,0:T(8,128)(2,1)}, bf16[4,512,512]{2,1,0:T(8,128)(2,1)S(1)}, u32[]{:S(2)}, u32[]{:S(2)}) collective-permute-start(bf16[4,512,512]{2,1,0:T(8,128)(2,1)} %ck_hbm.1), channel_id=1, source_target_pairs={{0,2},{2,0},{4,6},{6,4},{8,10},{10,8},{12,14},{14,12},{16,18},{18,... | collective-permute-start | bytes 6291464 | tf_op jit(solution)/shard_map/ppermute | solution.py:370
  0.5 16.4 %collective-permute-start.8 = (bf16[4,512,512]{2,1,0:T(8,128)(2,1)}, bf16[4,512,512]{2,1,0:T(8,128)(2,1)S(1)}, u32[]{:S(2)}, u32[]{:S(2)}) collective-permute-start(bf16[4,512,512]{2,1,0:T(8,128)(2,1)} %cv_hbm.1), channel_id=1, source_target_pairs={{0,2},{2,0},{4,6},{6,4},{8,10},{10,8},{12,14},{14,12},{16,18},{18,... | collective-permute-start | bytes 6291464 | tf_op jit(solution)/shard_map/ppermute | solution.py:370
  0.5 7.9 %collective-permute-start = (bf16[4,4096]{1,0:T(4,128)(2,1)}, bf16[4,4096]{1,0:T(4,128)(2,1)S(1)}, u32[]{:S(2)}, u32[]{:S(2)}) collective-permute-start(bf16[4,4096]{1,0:T(4,128)(2,1)} %q_hbm.1), channel_id=1, source_target_pairs={{0,24},{2,26},{4,28},{6,30},{8,16},{10,18},{12,20},{14,22},{16,8},... | collective-permute-start | bytes 98312 | tf_op jit(solution)/shard_map/ppermute | solution.py:370
  5.6 5.0 %collective-permute-start.1 = (bf16[4,4096]{1,0:T(4,128)(2,1)}, bf16[4,4096]{1,0:T(4,128)(2,1)S(1)}, u32[]{:S(2)}, u32[]{:S(2)}) collective-permute-start(bf16[4,4096]{1,0:T(4,128)(2,1)} %q_hbm.1), channel_id=1, source_target_pairs={{0,16},{2,18},{4,20},{6,22},{8,24},{10,26},{12,28},{14,30},{16,0},... | collective-permute-start | bytes 98312 | tf_op jit(solution)/shard_map/ppermute | solution.py:370
  5.6 5.0 %collective-permute-start.2 = (bf16[4,4096]{1,0:T(4,128)(2,1)}, bf16[4,4096]{1,0:T(4,128)(2,1)S(1)}, u32[]{:S(2)}, u32[]{:S(2)}) collective-permute-start(bf16[4,4096]{1,0:T(4,128)(2,1)} %q_hbm.1), channel_id=1, source_target_pairs={{0,8},{2,10},{4,12},{6,14},{8,0},{10,2},{12,4},{14,6},{16,24},{18,... | collective-permute-start | bytes 98312 | tf_op jit(solution)/shard_map/ppermute | solution.py:370
  8.4 2.2 %collective-permute-start.4 = (s32[8,128]{1,0:T(8,128)S(1)}, s32[8,128]{1,0:T(8,128)S(1)}, u32[]{:S(2)}, u32[]{:S(2)}) collective-permute-start(s32[8,128]{1,0:T(8,128)S(1)} %get-tuple-element.44.refs_2_), channel_id=1, source_target_pairs={{0,2},{2,0},{4,6},{6,4},{8,10},{10,8},{12,14},{14,12},{16,18},{18,... | collective-permute-start | bytes 12296 | tf_op jit(solution)/shard_map/ppermute | solution.py:370
  10.7 6.2 %collective-permute-start.5 = (bf16[4,256,512]{2,1,0:T(8,128)(2,1)S(1)}, bf16[4,256,512]{2,1,0:T(8,128)(2,1)S(1)}, u32[]{:S(2)}, u32[]{:S(2)}) collective-permute-start(bf16[4,256,512]{2,1,0:T(8,128)(2,1)S(1)} %copy-done.3), channel_id=1, source_target_pairs={{0,2},{2,0},{4,6},{6,4},{8,10},{10,8},{12,14},{14,12},{16,18},{18,... | collective-permute-start | bytes 3145736 | tf_op jit(solution)/shard_map/ppermute | solution.py:370
  10.8 6.1 %collective-permute-start.6 = (bf16[4,256,512]{2,1,0:T(8,128)(2,1)S(1)}, bf16[4,256,512]{2,1,0:T(8,128)(2,1)S(1)}, u32[]{:S(2)}, u32[]{:S(2)}) collective-permute-start(bf16[4,256,512]{2,1,0:T(8,128)(2,1)S(1)} %copy-done.4), channel_id=1, source_target_pairs={{0,2},{2,0},{4,6},{6,4},{8,10},{10,8},{12,14},{14,12},{16,18},{18,... | collective-permute-start | bytes 3145736 | tf_op jit(solution)/shard_map/ppermute | solution.py:370
  11.2 5.6 %collective-permute-start.3 = (bf16[16,4224]{1,0:T(8,128)(2,1)S(1)}, bf16[16,4224]{1,0:T(8,128)(2,1)S(1)}, u32[]{:S(2)}, u32[]{:S(2)}) collective-permute-start(bf16[16,4224]{1,0:T(8,128)(2,1)S(1)} %line.1.q_ref), channel_id=1, source_target_pairs={{0,4},{2,6},{4,0},{6,2},{8,12},{10,14},{12,8},{14,10},{16,20},{18,... | collective-permute-start | bytes 405512 | tf_op jit(solution)/shard_map/ppermute | solution.py:370
  20.3 4.6 %collective-permute-start.9 = (bf16[2,4,4224]{2,1,0:T(4,128)(2,1)S(1)}, bf16[2,4,4224]{2,1,0:T(4,128)(2,1)S(1)}, u32[]{:S(2)}, u32[]{:S(2)}) collective-permute-start(bf16[2,4,4224]{2,1,0:T(4,128)(2,1)S(1)} %get-tuple-element.52), channel_id=1, source_target_pairs={{0,4},{2,6},{4,0},{6,2},{8,12},{10,14},{12,8},{14,10},{16,20},{18,... | collective-permute-start | bytes 202760 | tf_op jit(solution)/shard_map/ppermute | solution.py:370
  21.8 11.1 %copy-start.1 = (bf16[4,512]{1,0:T(4,128)(2,1)S(1)}, bf16[4,512]{1,0:T(4,128)(2,1)}, u32[]{:S(2)}) copy-start(bf16[4,512]{1,0:T(4,128)(2,1)} %nk_ref.1) | copy-start | bytes 12292
  21.8 11.1 %copy-start.2 = (bf16[4,512]{1,0:T(4,128)(2,1)S(1)}, bf16[4,512]{1,0:T(4,128)(2,1)}, u32[]{:S(2)}) copy-start(bf16[4,512]{1,0:T(4,128)(2,1)} %nv_ref.1) | copy-start | bytes 12292
  21.8 6.3 %collective-permute-start.12 = (bf16[2,4,4224]{2,1,0:T(4,128)(2,1)S(1)}, bf16[2,4,4224]{2,1,0:T(4,128)(2,1)S(1)}, u32[]{:S(2)}, u32[]{:S(2)}) collective-permute-start(bf16[2,4,4224]{2,1,0:T(4,128)(2,1)S(1)} %get-tuple-element.58), channel_id=1, source_target_pairs={{0,4},{2,6},{4,0},{6,2},{8,12},{10,14},{12,8},{14,10},{16,20},{18,... | collective-permute-start | bytes 202760 | tf_op jit(solution)/shard_map/ppermute | solution.py:370
  22.4 24.0 %copy-start = (bf16[4096,512]{1,0:T(8,128)(2,1)S(1)}, bf16[4096,512]{1,0:T(8,128)(2,1)}, u32[]{:S(2)}) copy-start(bf16[4096,512]{1,0:T(8,128)(2,1)} %w_ref.1) | copy-start | bytes 12582916
  25.1 5.8 %collective-permute-start.10 = (bf16[4,4224]{1,0:T(4,128)(2,1)S(1)}, bf16[4,4224]{1,0:T(4,128)(2,1)S(1)}, u32[]{:S(2)}, u32[]{:S(2)}) collective-permute-start(bf16[4,4224]{1,0:T(4,128)(2,1)S(1)} %get-tuple-element.55), channel_id=1, source_target_pairs={{0,24},{2,26},{4,28},{6,30},{8,16},{10,18},{12,20},{14,22},{16,8},... | collective-permute-start | bytes 101384 | tf_op jit(solution)/shard_map/ppermute | solution.py:370
  28.1 4.8 %collective-permute-start.11 = (bf16[4,4224]{1,0:T(4,128)(2,1)S(1)}, bf16[4,4224]{1,0:T(4,128)(2,1)S(1)}, u32[]{:S(2)}, u32[]{:S(2)}) collective-permute-start(bf16[4,4224]{1,0:T(4,128)(2,1)S(1)} %get-tuple-element.56), channel_id=1, source_target_pairs={{0,16},{2,18},{4,20},{6,22},{8,24},{10,26},{12,28},{14,30},{16,0},... | collective-permute-start | bytes 101384 | tf_op jit(solution)/shard_map/ppermute | solution.py:370
  28.4 4.5 %collective-permute-start.13 = (bf16[4,4224]{1,0:T(4,128)(2,1)S(1)}, bf16[4,4224]{1,0:T(4,128)(2,1)S(1)}, u32[]{:S(2)}, u32[]{:S(2)}) collective-permute-start(bf16[4,4224]{1,0:T(4,128)(2,1)S(1)} %get-tuple-element.59), channel_id=1, source_target_pairs={{0,8},{2,10},{4,12},{6,14},{8,0},{10,2},{12,4},{14,6},{16,24},{18,... | collective-permute-start | bytes 101384 | tf_op jit(solution)/shard_map/ppermute | solution.py:370
  33.4 5.8 %collective-permute-start.14 = (bf16[4,4096]{1,0:T(4,128)(2,1)S(1)}, bf16[4,4096]{1,0:T(4,128)(2,1)S(1)}, u32[]{:S(2)}, u32[]{:S(2)}) collective-permute-start(bf16[4,4096]{1,0:T(4,128)(2,1)S(1)} %finish.1), channel_id=1, source_target_pairs={{0,24},{2,26},{4,28},{6,30},{8,16},{10,18},{12,20},{14,22},{16,8},... | collective-permute-start | bytes 98312 | tf_op jit(solution)/shard_map/ppermute | solution.py:370
  35.5 5.0 %collective-permute-start.18 = (bf16[4,4096]{1,0:T(4,128)(2,1)S(1)}, bf16[4,4096]{1,0:T(4,128)(2,1)S(1)}, u32[]{:S(2)}, u32[]{:S(2)}) collective-permute-start(bf16[4,4096]{1,0:T(4,128)(2,1)S(1)} %finish.1), channel_id=1, source_target_pairs={{0,16},{2,18},{4,20},{6,22},{8,24},{10,26},{12,28},{14,30},{16,0},... | collective-permute-start | bytes 98312 | tf_op jit(solution)/shard_map/ppermute | solution.py:370
  36.0 4.5 %collective-permute-start.17 = (bf16[4,4096]{1,0:T(4,128)(2,1)S(1)}, bf16[4,4096]{1,0:T(4,128)(2,1)S(1)}, u32[]{:S(2)}, u32[]{:S(2)}) collective-permute-start(bf16[4,4096]{1,0:T(4,128)(2,1)S(1)} %finish.1), channel_id=1, source_target_pairs={{0,8},{2,10},{4,12},{6,14},{8,0},{10,2},{12,4},{14,6},{16,24},{18,... | collective-permute-start | bytes 98312 | tf_op jit(solution)/shard_map/ppermute | solution.py:370
  39.2 4.3 %collective-permute-start.15 = (bf16[2,4,4096]{2,1,0:T(4,128)(2,1)S(1)}, bf16[2,4,4096]{2,1,0:T(4,128)(2,1)S(1)}, u32[]{:S(2)}, u32[]{:S(2)}) collective-permute-start(bf16[2,4,4096]{2,1,0:T(4,128)(2,1)S(1)} %get-tuple-element.66), channel_id=1, source_target_pairs={{0,4},{2,6},{4,0},{6,2},{8,12},{10,14},{12,8},{14,10},{16,20},{18,... | collective-permute-start | bytes 196616 | tf_op jit(solution)/shard_map/ppermute | solution.py:370
  40.6 4.3 %collective-permute-start.19 = (bf16[2,4,4096]{2,1,0:T(4,128)(2,1)S(1)}, bf16[2,4,4096]{2,1,0:T(4,128)(2,1)S(1)}, u32[]{:S(2)}, u32[]{:S(2)}) collective-permute-start(bf16[2,4,4096]{2,1,0:T(4,128)(2,1)S(1)} %get-tuple-element.64), channel_id=1, source_target_pairs={{0,4},{2,6},{4,0},{6,2},{8,12},{10,14},{12,8},{14,10},{16,20},{18,... | collective-permute-start | bytes 196616 | tf_op jit(solution)/shard_map/ppermute | solution.py:370
  43.7 1.4 %collective-permute-start.16 = (bf16[2,2,4,4096]{3,2,1,0:T(4,128)(2,1)S(1)}, bf16[2,2,4,4096]{3,2,1,0:T(4,128)(2,1)S(1)}, u32[]{:S(2)}, u32[]{:S(2)}) collective-permute-start(bf16[2,2,4,4096]{3,2,1,0:T(4,128)(2,1)S(1)} %pad_maximum_fusion.near_a), channel_id=1, source_target_pairs={{0,2},{2,0},{4,6},{6,4},{8,10},{10,8},{12,14},{14,12},{16,18},{18,... | collective-permute-start | bytes 393224 | tf_op jit(solution)/shard_map/ppermute | solution.py:370
  45.0 1.4 %collective-permute-start.20 = (bf16[2,2,4,4096]{3,2,1,0:T(4,128)(2,1)S(1)}, bf16[2,2,4,4096]{3,2,1,0:T(4,128)(2,1)S(1)}, u32[]{:S(2)}, u32[]{:S(2)}) collective-permute-start(bf16[2,2,4,4096]{3,2,1,0:T(4,128)(2,1)S(1)} %pad_maximum_fusion.1.near_b), channel_id=1, source_target_pairs={{0,2},{2,0},{4,6},{6,4},{8,10},{10,8},{12,14},{14,12},{16,18},{18,... | collective-permute-start | bytes 393224 | tf_op jit(solution)/shard_map/ppermute | solution.py:370
  47.3 4.0 %collective-permute-start.21 = (bf16[32,512]{1,0:T(8,128)(2,1)S(1)}, bf16[32,512]{1,0:T(8,128)(2,1)S(1)}, u32[]{:S(2)}, u32[]{:S(2)}) collective-permute-start(bf16[32,512]{1,0:T(8,128)(2,1)S(1)} %get-tuple-element.62), channel_id=1, source_target_pairs={{0,1},{1,0},{2,3},{3,2},{4,5},{5,4},{6,7},{7,6},{8,9},{9,8},{10,11... | collective-permute-start | bytes 98312 | tf_op jit(solution)/shard_map/ppermute | solution.py:487

commit v6 on v5

--- a/solution.py
+++ b/solution.py
@@ -212,6 +212,28 @@
     for k in range(heads):
         finish(k)
     store(slice(total - STATS, total), [pack_stats(x, stride) for x in stats])
+
+
+def side_kernel(q_ref, own_ref, *refs):
+    caches, (a_ref, b_ref, early_ref), scratch = refs[:10], refs[10:13], refs[13:]
+    attend_kernel((0, 1), q_ref, *caches, a_ref, b_ref, *scratch)
+
+    @pl.when(lax.axis_index("beam") % 2 == 1)
+    def _():
+        attend_kernel((1,), own_ref, *caches[5:], early_ref, *scratch)
+
+
+def late_kernel(q_ref, early_ref, *refs):
+    out_ref = refs[5]
+    core = lax.axis_index("beam") % 2
+
+    @pl.when(core == 0)
+    def _():
+        attend_kernel((1,), q_ref, *refs)
+
+    @pl.when(core == 1)
+    def _():
+        out_ref[...] = early_ref[...]
 
 
 def pack_stats(x, stride):
@@ -426,30 +448,32 @@
 
     many = beams * QPK
 
-    def attend(asked, name, out_shape, kinds, *caches):
+    def attend(kernel, name, out_shape, kinds, *args):
         return call(
-            functools.partial(attend_kernel, kinds),
+            kernel,
             name,
             out_shape,
-            asked,
-            *caches,
+            *args,
             scratch=[
-                pltpu.VMEM((len(kinds), heads, requests * many, length), f32),
-                pltpu.VMEM((len(kinds), heads, requests * many, length), bf16),
-                pltpu.VMEM((len(kinds), heads, many, span), f32),
-                pltpu.VMEM((len(kinds), heads, many, span), bf16),
+                pltpu.VMEM((kinds, heads, requests * many, length), f32),
+                pltpu.VMEM((kinds, heads, requests * many, length), bf16),
+                pltpu.VMEM((kinds, heads, many, span), f32),
+                pltpu.VMEM((kinds, heads, many, span), bf16),
             ],
             vmem=24,
             cost=2**26,
         )
 
     other = swap(asked, 2)
-    own_here = attend(asked, "attend_own", line, (0,), *caches)
+    own_kernel = functools.partial(attend_kernel, (0,))
+    own_here = attend(own_kernel, "attend_own", line, 1, asked, *caches)
     other, own_here = lax.optimization_barrier((other, own_here))
     half = jax.ShapeDtypeStruct((requests // 2, beams, total), bf16)
-    send_a, send_b = attend(other, "attend_side", (half, half), (0, 1), *caches, *stored)
+    send_a, send_b, early = attend(
+        side_kernel, "attend_side", (half, half, line), 2, other, asked, *caches, *stored
+    )
     asked, _ = lax.optimization_barrier((asked, send_a))
-    own_there = attend(asked, "attend_own_other", line, (1,), *stored)
+    own_there = attend(late_kernel, "attend_late", line, 1, asked, early, *stored)
     keep_a, keep_b = call(core_kernel, "own_merge", (half, half), own_here, own_there)
     piece = jax.ShapeDtypeStruct((beams, total), bf16)
     parts = []

time: 52 us -> 52.7 us (1.013)
  no operation moved by 1% of the time
where the time goes in v6:
time: 52.7 us; the launch traced here: 52.5 us
  starting transfers between devices  23.6 us (45%)
  waiting for transfers between devices  14.9 us (28%)
  Pallas kernels  12.9 us (24%)
  other arithmetic  0.92 us (2%)
    ppermute x21, starting transfers between devices, swap(): return lax.ppermute(x, 'beam', [(i, i ^ with_bit) for i in range(devices)])  22 us
    pallas_call x11, Pallas kernels, call(): pl.pallas_call(kernel, out_shape=out_shape, in_specs=whole_blocks(len(arg...  12.9 us
    ppermute x21, waiting for transfers between devices, swap(): return lax.ppermute(x, 'beam', [(i, i ^ with_bit) for i in range(devices)])  12.6 us
    ppermute x1, waiting for transfers between devices, per_device(): came = lax.ppermute(send, 'head', [(0, 1), (1, 0)])  2.38 us
    ppermute x1, starting transfers between devices, per_device(): came = lax.ppermute(send, 'head', [(0, 1), (1, 0)])  1.6 us
  transfers between devices with their start and end apart: 22, of which 10 were waited for; matrix products, arithmetic and copies ran while one was open for 1% of the time, Pallas kernels for 16%

profile of v6, /device:TPU:0, one launch (start us, length us, event | category | flops | bytes accessed | tf_op | source)
XLA Modules:
  0.0 52.5 jit_solution(16219103303401440627)
XLA Ops:
  0.0 0.5 collective-permute-start.7
  0.5 0.1 collective-permute-start.8
  0.5 5.0 %collective-permute-start = (bf16[4,4096]{1,0:T(4,128)(2,1)}, bf16[4,4096]{1,0:T(4,128)(2,1)S(1)}, u32[]{:S(2)}, u32[]{:S(2)}) collective-permute-start(bf16[4,4096]{1,0:T(4,128)(2,1)} %q_hbm.1), channel_id=1, source_target_pairs={{0,24},{2,26},{4,28},{6,30},{8,16},{10,18},{12,20},{14,22},{16,8},... | collective-permute-start | bytes 98312 | tf_op jit(solution)/shard_map/ppermute | solution.py:392
  5.6 0.6 %collective-permute-start.2 = (bf16[4,4096]{1,0:T(4,128)(2,1)}, bf16[4,4096]{1,0:T(4,128)(2,1)S(1)}, u32[]{:S(2)}, u32[]{:S(2)}) collective-permute-start(bf16[4,4096]{1,0:T(4,128)(2,1)} %q_hbm.1), channel_id=1, source_target_pairs={{0,8},{2,10},{4,12},{6,14},{8,0},{10,2},{12,4},{14,6},{16,24},{18,... | collective-permute-start | bytes 98312 | tf_op jit(solution)/shard_map/ppermute | solution.py:392
  6.1 2.3 %load_private.1 = (bf16[4,4096]{1,0:T(4,128)(2,1)S(1)}, bf16[4,128]{1,0:T(4,128)(2,1)S(1)}, s32[8,128]{1,0:T(8,128)S(1)}, bf16[4,512,512]{2,1,0:T(8,128)(2,1)S(1)}, bf16[4,512,512]{2,1,0:T(8,128)(2,1)S(1)}) custom-call(bf16[4,4096]{1,0:T(4,128)(2,1)} %q_hbm.1, s32[4]{0:T(128)} %par_hbm.1, s32[4]{0:T(128)} %cnt_hbm.1, bf16[4,512,512]{2,1,0:T(8,128)(2,1)} %ck_hbm.1, ...), custom_call_target="tpu_custom_call" | custom-call | flops 67108864 | bytes 67108864 | tf_op jit(solution)/shard_map/load_private/pallas_call | solution.py:359
  8.4 0.1 collective-permute-start.4
  8.5 2.1 %collective-permute-done.1.refs_1_ = bf16[4,4096]{1,0:T(4,128)(2,1)S(1)} collective-permute-done((bf16[4,4096]{1,0:T(4,128)(2,1)}, bf16[4,4096]{1,0:T(4,128)(2,1)S(1)}, u32[]{:S(2)}, u32[]{:S(2)}) %collective-permute-start.1) | collective-permute-done | bytes 32800 | tf_op jit(solution)/shard_map/ppermute | solution.py:392
  10.6 0.0 collective-permute-done.2.refs_2_
  10.6 0.0 collective-permute-done.4.refs_7_.refs_2_
  10.7 0.1 collective-permute-start.5
  10.8 0.5 collective-permute-start.6
  11.2 1.5 %collective-permute-start.3 = (bf16[16,4224]{1,0:T(8,128)(2,1)S(1)}, bf16[16,4224]{1,0:T(8,128)(2,1)S(1)}, u32[]{:S(2)}, u32[]{:S(2)}) collective-permute-start(bf16[16,4224]{1,0:T(8,128)(2,1)S(1)} %line.1.q_ref.own_ref), channel_id=1, source_target_pairs={{0,4},{2,6},{4,0},{6,2},{8,12},{10,14},{12,8},{14,10},{16,20},{18,... | collective-permute-start | bytes 405512 | tf_op jit(solution)/shard_map/ppermute | solution.py:392
  12.7 1.6 %load_prompt.1 = (bf16[4,256,512]{2,1,0:T(8,128)(2,1)S(1)}, bf16[4,256,512]{2,1,0:T(8,128)(2,1)S(1)}) custom-call(bf16[4,256,512]{2,1,0:T(8,128)(2,1)} %pk_hbm, bf16[4,256,512]{2,1,0:T(8,128)(2,1)} %pv_hbm), custom_call_target="tpu_custom_call" | custom-call | flops 67108864 | bytes 67108864 | tf_op jit(solution)/shard_map/load_prompt/pallas_call | solution.py:359
  14.3 1.7 %attend_own.1.kept_ref = bf16[16,4224]{1,0:T(8,128)(2,1)S(1)} custom-call(bf16[16,4224]{1,0:T(8,128)(2,1)S(1)} %line.1.q_ref.own_ref, bf16[4,256,512]{2,1,0:T(8,128)(2,1)S(1)} %get-tuple-element.43.refs_0_, bf16[4,256,512]{2,1,0:T(8,128)(2,1)S(1)} %get-tuple-element.44.refs_1_, s32[8,128]{1,0:T(8,128)S(1)} %get-tuple-element.45.refs_2_, ...), custom_call_target="tpu_custom_call" | custom-call | flops 67108864 | bytes 67108864 | tf_op jit(solution)/shard_map/attend_own/pallas_call | solution.py:359
  16.0 0.8 %collective-permute-done.3.q_ref = bf16[16,4224]{1,0:T(8,128)(2,1)S(1)} collective-permute-done((bf16[16,4224]{1,0:T(8,128)(2,1)S(1)}, bf16[16,4224]{1,0:T(8,128)(2,1)S(1)}, u32[]{:S(2)}, u32[]{:S(2)}) %collective-permute-start.3) | collective-permute-done | bytes 135200 | tf_op jit(solution)/shard_map/ppermute | solution.py:392
  16.8 0.0 collective-permute-done.8.refs_9_.refs_4_
  16.8 3.4 %attend_side.1 = (bf16[2,4,4224]{2,1,0:T(4,128)(2,1)S(1)}, bf16[2,4,4224]{2,1,0:T(4,128)(2,1)S(1)}, bf16[16,4224]{1,0:T(8,128)(2,1)S(1)}) custom-call(bf16[16,4224]{1,0:T(8,128)(2,1)S(1)} %collective-permute-done.3.q_ref, bf16[16,4224]{1,0:T(8,128)(2,1)S(1)} %line.1.q_ref.own_ref, bf16[4,256,512]{2,1,0:T(8,128)(2,1)S(1)} %get-tuple-element.43.refs_0_, ...), custom_call_target="tpu_custom_call" | custom-call | flops 67108864 | bytes 67108864 | tf_op jit(solution)/shard_map/attend_side/pallas_call | solution.py:359
  20.2 1.6 %collective-permute-start.9 = (bf16[2,4,4224]{2,1,0:T(4,128)(2,1)S(1)}, bf16[2,4,4224]{2,1,0:T(4,128)(2,1)S(1)}, u32[]{:S(2)}, u32[]{:S(2)}) collective-permute-start(bf16[2,4,4224]{2,1,0:T(4,128)(2,1)S(1)} %get-tuple-element.53), channel_id=1, source_target_pairs={{0,4},{2,6},{4,0},{6,2},{8,12},{10,14},{12,8},{14,10},{16,20},{18,... | collective-permute-start | bytes 202760 | tf_op jit(solution)/shard_map/ppermute | solution.py:392
  21.8 0.5 %collective-permute-start.12 = (bf16[2,4,4224]{2,1,0:T(4,128)(2,1)S(1)}, bf16[2,4,4224]{2,1,0:T(4,128)(2,1)S(1)}, u32[]{:S(2)}, u32[]{:S(2)}) collective-permute-start(bf16[2,4,4224]{2,1,0:T(4,128)(2,1)S(1)} %get-tuple-element.60), channel_id=1, source_target_pairs={{0,4},{2,6},{4,0},{6,2},{8,12},{10,14},{12,8},{14,10},{16,20},{18,... | collective-permute-start | bytes 202760 | tf_op jit(solution)/shard_map/ppermute | solution.py:392
  22.3 1.7 %attend_late.1.came_ref = bf16[16,4224]{1,0:T(8,128)(2,1)S(1)} custom-call(bf16[16,4224]{1,0:T(8,128)(2,1)S(1)} %line.1.q_ref.own_ref, bf16[16,4224]{1,0:T(8,128)(2,1)S(1)} %get-tuple-element.55.early_ref, bf16[4,256,512]{2,1,0:T(8,128)(2,1)S(1)} %collective-permute-done.5.refs_5_.refs_0_, bf16[4,256,512]{2,1,0:T(8,128)(2,1)S(1)} %collective-permute-done.6.refs_6_.refs_1_, ...), custom_call_target="tpu_custom_call" | custom-call | flops 67108864 | bytes 67108864 | tf_op jit(solution)/shard_map/attend_late/pallas_call | solution.py:359
  24.0 0.4 own_merge.1
  24.3 0.9 %collective-permute-done.9.came_ref = bf16[2,4,4224]{2,1,0:T(4,128)(2,1)S(1)} collective-permute-done((bf16[2,4,4224]{2,1,0:T(4,128)(2,1)S(1)}, bf16[2,4,4224]{2,1,0:T(4,128)(2,1)S(1)}, u32[]{:S(2)}, u32[]{:S(2)}) %collective-permute-start.9) | collective-permute-done | bytes 67616 | tf_op jit(solution)/shard_map/ppermute | solution.py:392
  25.3 0.3 plane_merge.2
  25.6 2.9 %collective-permute-start.10 = (bf16[4,4224]{1,0:T(4,128)(2,1)S(1)}, bf16[4,4224]{1,0:T(4,128)(2,1)S(1)}, u32[]{:S(2)}, u32[]{:S(2)}) collective-permute-start(bf16[4,4224]{1,0:T(4,128)(2,1)S(1)} %get-tuple-element.57), channel_id=1, source_target_pairs={{0,24},{2,26},{4,28},{6,30},{8,16},{10,18},{12,20},{14,22},{16,8},... | collective-permute-start | bytes 101384 | tf_op jit(solution)/shard_map/ppermute | solution.py:392
  28.4 0.3 plane_merge.3
  28.7 1.6 %collective-permute-start.13 = (bf16[4,4224]{1,0:T(4,128)(2,1)S(1)}, bf16[4,4224]{1,0:T(4,128)(2,1)S(1)}, u32[]{:S(2)}, u32[]{:S(2)}) collective-permute-start(bf16[4,4224]{1,0:T(4,128)(2,1)S(1)} %get-tuple-element.61), channel_id=1, source_target_pairs={{0,8},{2,10},{4,12},{6,14},{8,0},{10,2},{12,4},{14,6},{16,24},{18,... | collective-permute-start | bytes 101384 | tf_op jit(solution)/shard_map/ppermute | solution.py:392
  30.4 1.3 %collective-permute-done.10.refs_0_ = bf16[4,4224]{1,0:T(4,128)(2,1)S(1)} collective-permute-done((bf16[4,4224]{1,0:T(4,128)(2,1)S(1)}, bf16[4,4224]{1,0:T(4,128)(2,1)S(1)}, u32[]{:S(2)}, u32[]{:S(2)}) %collective-permute-start.10) | collective-permute-done | bytes 33824 | tf_op jit(solution)/shard_map/ppermute | solution.py:392
  31.7 1.6 %collective-permute-done.11.refs_1_ = bf16[4,4224]{1,0:T(4,128)(2,1)S(1)} collective-permute-done((bf16[4,4224]{1,0:T(4,128)(2,1)S(1)}, bf16[4,4224]{1,0:T(4,128)(2,1)S(1)}, u32[]{:S(2)}, u32[]{:S(2)}) %collective-permute-start.11) | collective-permute-done | bytes 33824 | tf_op jit(solution)/shard_map/ppermute | solution.py:392
  33.3 0.5 finish.1
  33.8 1.9 %collective-permute-start.14 = (bf16[4,4096]{1,0:T(4,128)(2,1)S(1)}, bf16[4,4096]{1,0:T(4,128)(2,1)S(1)}, u32[]{:S(2)}, u32[]{:S(2)}) collective-permute-start(bf16[4,4096]{1,0:T(4,128)(2,1)S(1)} %finish.1), channel_id=1, source_target_pairs={{0,24},{2,26},{4,28},{6,30},{8,16},{10,18},{12,20},{14,22},{16,8},... | collective-permute-start | bytes 98312 | tf_op jit(solution)/shard_map/ppermute | solution.py:392
  35.7 0.6 %collective-permute-start.18 = (bf16[4,4096]{1,0:T(4,128)(2,1)S(1)}, bf16[4,4096]{1,0:T(4,128)(2,1)S(1)}, u32[]{:S(2)}, u32[]{:S(2)}) collective-permute-start(bf16[4,4096]{1,0:T(4,128)(2,1)S(1)} %finish.1), channel_id=1, source_target_pairs={{0,16},{2,18},{4,20},{6,22},{8,24},{10,26},{12,28},{14,30},{16,0},... | collective-permute-start | bytes 98312 | tf_op jit(solution)/shard_map/ppermute | solution.py:392
  36.3 1.9 %collective-permute-start.17 = (bf16[4,4096]{1,0:T(4,128)(2,1)S(1)}, bf16[4,4096]{1,0:T(4,128)(2,1)S(1)}, u32[]{:S(2)}, u32[]{:S(2)}) collective-permute-start(bf16[4,4096]{1,0:T(4,128)(2,1)S(1)} %finish.1), channel_id=1, source_target_pairs={{0,8},{2,10},{4,12},{6,14},{8,0},{10,2},{12,4},{14,6},{16,24},{18,... | collective-permute-start | bytes 98312 | tf_op jit(solution)/shard_map/ppermute | solution.py:392
  38.2 1.3 %collective-permute-done.14 = bf16[4,4096]{1,0:T(4,128)(2,1)S(1)} collective-permute-done((bf16[4,4096]{1,0:T(4,128)(2,1)S(1)}, bf16[4,4096]{1,0:T(4,128)(2,1)S(1)}, u32[]{:S(2)}, u32[]{:S(2)}) %collective-permute-start.14) | collective-permute-done | bytes 32800 | tf_op jit(solution)/shard_map/ppermute | solution.py:392
  39.5 0.1 fusion.1
  39.6 1.6 %collective-permute-start.15 = (bf16[2,4,4096]{2,1,0:T(4,128)(2,1)S(1)}, bf16[2,4,4096]{2,1,0:T(4,128)(2,1)S(1)}, u32[]{:S(2)}, u32[]{:S(2)}) collective-permute-start(bf16[2,4,4096]{2,1,0:T(4,128)(2,1)S(1)} %get-tuple-element.68), channel_id=1, source_target_pairs={{0,4},{2,6},{4,0},{6,2},{8,12},{10,14},{12,8},{14,10},{16,20},{18,... | collective-permute-start | bytes 196616 | tf_op jit(solution)/shard_map/ppermute | solution.py:392
  41.1 0.1 fusion
  41.2 1.0 %collective-permute-start.19 = (bf16[2,4,4096]{2,1,0:T(4,128)(2,1)S(1)}, bf16[2,4,4096]{2,1,0:T(4,128)(2,1)S(1)}, u32[]{:S(2)}, u32[]{:S(2)}) collective-permute-start(bf16[2,4,4096]{2,1,0:T(4,128)(2,1)S(1)} %get-tuple-element.66), channel_id=1, source_target_pairs={{0,4},{2,6},{4,0},{6,2},{8,12},{10,14},{12,8},{14,10},{16,20},{18,... | collective-permute-start | bytes 196616 | tf_op jit(solution)/shard_map/ppermute | solution.py:392
  42.2 1.7 %collective-permute-done.15 = bf16[2,4,4096]{2,1,0:T(4,128)(2,1)S(1)} collective-permute-done((bf16[2,4,4096]{2,1,0:T(4,128)(2,1)S(1)}, bf16[2,4,4096]{2,1,0:T(4,128)(2,1)S(1)}, u32[]{:S(2)}, u32[]{:S(2)}) %collective-permute-start.15) | collective-permute-done | bytes 65568 | tf_op jit(solution)/shard_map/ppermute | solution.py:392
  43.9 0.1 pad_maximum_fusion.near_a
  44.0 0.1 collective-permute-start.16
  44.1 1.4 %collective-permute-done.19 = bf16[2,4,4096]{2,1,0:T(4,128)(2,1)S(1)} collective-permute-done((bf16[2,4,4096]{2,1,0:T(4,128)(2,1)S(1)}, bf16[2,4,4096]{2,1,0:T(4,128)(2,1)S(1)}, u32[]{:S(2)}, u32[]{:S(2)}) %collective-permute-start.19) | collective-permute-done | bytes 65568 | tf_op jit(solution)/shard_map/ppermute | solution.py:392
  45.5 0.1 pad_maximum_fusion.1.near_b
  45.6 0.1 collective-permute-start.20
  45.7 1.3 %collective-permute-done.20.far_b = bf16[2,2,4,4096]{3,2,1,0:T(4,128)(2,1)S(1)} collective-permute-done((bf16[2,2,4,4096]{3,2,1,0:T(4,128)(2,1)S(1)}, bf16[2,2,4,4096]{3,2,1,0:T(4,128)(2,1)S(1)}, u32[]{:S(2)}, u32[]{:S(2)}) %collective-permute-start.20) | collective-permute-done | bytes 131104 | tf_op jit(solution)/shard_map/ppermute | solution.py:392
  47.0 0.9 %project.1 = (f32[32,512]{1,0:T(8,128)S(1)}, bf16[32,512]{1,0:T(8,128)(2,1)S(1)}) custom-call(bf16[2,2,4,4096]{3,2,1,0:T(4,128)(2,1)S(1)} %pad_maximum_fusion.near_a, bf16[2,2,4,4096]{3,2,1,0:T(4,128)(2,1)S(1)} %collective-permute-done.16.far_a, bf16[2,2,4,4096]{3,2,1,0:T(4,128)(2,1)S(1)} %pad_maximum_fusion.1.near_b, ...), custom_call_target="tpu_custom_call" | custom-call | tf_op jit(solution)/shard_map/project/pallas_call | solution.py:359
  47.9 1.6 %collective-permute-start.21 = (bf16[32,512]{1,0:T(8,128)(2,1)S(1)}, bf16[32,512]{1,0:T(8,128)(2,1)S(1)}, u32[]{:S(2)}, u32[]{:S(2)}) collective-permute-start(bf16[32,512]{1,0:T(8,128)(2,1)S(1)} %get-tuple-element.64), channel_id=1, source_target_pairs={{0,1},{1,0},{2,3},{3,2},{4,5},{5,4},{6,7},{7,6},{8,9},{9,8},{10,11... | collective-permute-start | bytes 98312 | tf_op jit(solution)/shard_map/ppermute | solution.py:511
  49.5 2.4 %collective-permute-done.21 = bf16[32,512]{1,0:T(8,128)(2,1)S(1)} collective-permute-done((bf16[32,512]{1,0:T(8,128)(2,1)S(1)}, bf16[32,512]{1,0:T(8,128)(2,1)S(1)}, u32[]{:S(2)}, u32[]{:S(2)}) %collective-permute-start.21) | collective-permute-done | bytes 32800 | tf_op jit(solution)/shard_map/ppermute | solution.py:511
  51.9 0.6 %add_convert_fusion = bf16[32,512]{1,0:T(8,128)(2,1)} fusion(f32[32,512]{1,0:T(8,128)S(1)} %get-tuple-element.63, bf16[32,512]{1,0:T(8,128)(2,1)S(1)} %collective-permute-done.21), kind=kLoop, calls=%fused_computation.4 | loop fusion | flops 49152 | bytes 131072 | tf_op jit(solution)/shard_map/convert_element_type | solution.py:512
  (22 shorter events, 0.1 us)
Async XLA Ops:
  0.0 10.7 %copy-start.3 = (bf16[4,256,512]{2,1,0:T(8,128)(2,1)S(1)}, bf16[4,256,512]{2,1,0:T(8,128)(2,1)}, u32[]{:S(2)}) copy-start(bf16[4,256,512]{2,1,0:T(8,128)(2,1)} %pk_hbm) | copy-start | bytes 3145732
  0.0 10.7 %copy-start.4 = (bf16[4,256,512]{2,1,0:T(8,128)(2,1)S(1)}, bf16[4,256,512]{2,1,0:T(8,128)(2,1)}, u32[]{:S(2)}) copy-start(bf16[4,256,512]{2,1,0:T(8,128)(2,1)} %pv_hbm) | copy-start | bytes 3145732
  0.0 16.8 %collective-permute-start.7 = (bf16[4,512,512]{2,1,0:T(8,128)(2,1)}, bf16[4,512,512]{2,1,0:T(8,128)(2,1)S(1)}, u32[]{:S(2)}, u32[]{:S(2)}) collective-permute-start(bf16[4,512,512]{2,1,0:T(8,128)(2,1)} %ck_hbm.1), channel_id=1, source_target_pairs={{0,2},{2,0},{4,6},{6,4},{8,10},{10,8},{12,14},{14,12},{16,18},{18,... | collective-permute-start | bytes 6291464 | tf_op jit(solution)/shard_map/ppermute | solution.py:392
  0.5 16.4 %collective-permute-start.8 = (bf16[4,512,512]{2,1,0:T(8,128)(2,1)}, bf16[4,512,512]{2,1,0:T(8,128)(2,1)S(1)}, u32[]{:S(2)}, u32[]{:S(2)}) collective-permute-start(bf16[4,512,512]{2,1,0:T(8,128)(2,1)} %cv_hbm.1), channel_id=1, source_target_pairs={{0,2},{2,0},{4,6},{6,4},{8,10},{10,8},{12,14},{14,12},{16,18},{18,... | collective-permute-start | bytes 6291464 | tf_op jit(solution)/shard_map/ppermute | solution.py:392
  0.5 7.9 %collective-permute-start = (bf16[4,4096]{1,0:T(4,128)(2,1)}, bf16[4,4096]{1,0:T(4,128)(2,1)S(1)}, u32[]{:S(2)}, u32[]{:S(2)}) collective-permute-start(bf16[4,4096]{1,0:T(4,128)(2,1)} %q_hbm.1), channel_id=1, source_target_pairs={{0,24},{2,26},{4,28},{6,30},{8,16},{10,18},{12,20},{14,22},{16,8},... | collective-permute-start | bytes 98312 | tf_op jit(solution)/shard_map/ppermute | solution.py:392
  5.6 5.0 %collective-permute-start.1 = (bf16[4,4096]{1,0:T(4,128)(2,1)}, bf16[4,4096]{1,0:T(4,128)(2,1)S(1)}, u32[]{:S(2)}, u32[]{:S(2)}) collective-permute-start(bf16[4,4096]{1,0:T(4,128)(2,1)} %q_hbm.1), channel_id=1, source_target_pairs={{0,16},{2,18},{4,20},{6,22},{8,24},{10,26},{12,28},{14,30},{16,0},... | collective-permute-start | bytes 98312 | tf_op jit(solution)/shard_map/ppermute | solution.py:392
  5.6 5.0 %collective-permute-start.2 = (bf16[4,4096]{1,0:T(4,128)(2,1)}, bf16[4,4096]{1,0:T(4,128)(2,1)S(1)}, u32[]{:S(2)}, u32[]{:S(2)}) collective-permute-start(bf16[4,4096]{1,0:T(4,128)(2,1)} %q_hbm.1), channel_id=1, source_target_pairs={{0,8},{2,10},{4,12},{6,14},{8,0},{10,2},{12,4},{14,6},{16,24},{18,... | collective-permute-start | bytes 98312 | tf_op jit(solution)/shard_map/ppermute | solution.py:392
  8.4 2.2 %collective-permute-start.4 = (s32[8,128]{1,0:T(8,128)S(1)}, s32[8,128]{1,0:T(8,128)S(1)}, u32[]{:S(2)}, u32[]{:S(2)}) collective-permute-start(s32[8,128]{1,0:T(8,128)S(1)} %get-tuple-element.45.refs_2_), channel_id=1, source_target_pairs={{0,2},{2,0},{4,6},{6,4},{8,10},{10,8},{12,14},{14,12},{16,18},{18,... | collective-permute-start | bytes 12296 | tf_op jit(solution)/shard_map/ppermute | solution.py:392
  10.7 6.2 %collective-permute-start.5 = (bf16[4,256,512]{2,1,0:T(8,128)(2,1)S(1)}, bf16[4,256,512]{2,1,0:T(8,128)(2,1)S(1)}, u32[]{:S(2)}, u32[]{:S(2)}) collective-permute-start(bf16[4,256,512]{2,1,0:T(8,128)(2,1)S(1)} %copy-done.3), channel_id=1, source_target_pairs={{0,2},{2,0},{4,6},{6,4},{8,10},{10,8},{12,14},{14,12},{16,18},{18,... | collective-permute-start | bytes 3145736 | tf_op jit(solution)/shard_map/ppermute | solution.py:392
  10.8 6.1 %collective-permute-start.6 = (bf16[4,256,512]{2,1,0:T(8,128)(2,1)S(1)}, bf16[4,256,512]{2,1,0:T(8,128)(2,1)S(1)}, u32[]{:S(2)}, u32[]{:S(2)}) collective-permute-start(bf16[4,256,512]{2,1,0:T(8,128)(2,1)S(1)} %copy-done.4), channel_id=1, source_target_pairs={{0,2},{2,0},{4,6},{6,4},{8,10},{10,8},{12,14},{14,12},{16,18},{18,... | collective-permute-start | bytes 3145736 | tf_op jit(solution)/shard_map/ppermute | solution.py:392
  11.2 5.6 %collective-permute-start.3 = (bf16[16,4224]{1,0:T(8,128)(2,1)S(1)}, bf16[16,4224]{1,0:T(8,128)(2,1)S(1)}, u32[]{:S(2)}, u32[]{:S(2)}) collective-permute-start(bf16[16,4224]{1,0:T(8,128)(2,1)S(1)} %line.1.q_ref.own_ref), channel_id=1, source_target_pairs={{0,4},{2,6},{4,0},{6,2},{8,12},{10,14},{12,8},{14,10},{16,20},{18,... | collective-permute-start | bytes 405512 | tf_op jit(solution)/shard_map/ppermute | solution.py:392
  20.2 5.1 %collective-permute-start.9 = (bf16[2,4,4224]{2,1,0:T(4,128)(2,1)S(1)}, bf16[2,4,4224]{2,1,0:T(4,128)(2,1)S(1)}, u32[]{:S(2)}, u32[]{:S(2)}) collective-permute-start(bf16[2,4,4224]{2,1,0:T(4,128)(2,1)S(1)} %get-tuple-element.53), channel_id=1, source_target_pairs={{0,4},{2,6},{4,0},{6,2},{8,12},{10,14},{12,8},{14,10},{16,20},{18,... | collective-permute-start | bytes 202760 | tf_op jit(solution)/shard_map/ppermute | solution.py:392
  21.8 6.7 %collective-permute-start.12 = (bf16[2,4,4224]{2,1,0:T(4,128)(2,1)S(1)}, bf16[2,4,4224]{2,1,0:T(4,128)(2,1)S(1)}, u32[]{:S(2)}, u32[]{:S(2)}) collective-permute-start(bf16[2,4,4224]{2,1,0:T(4,128)(2,1)S(1)} %get-tuple-element.60), channel_id=1, source_target_pairs={{0,4},{2,6},{4,0},{6,2},{8,12},{10,14},{12,8},{14,10},{16,20},{18,... | collective-permute-start | bytes 202760 | tf_op jit(solution)/shard_map/ppermute | solution.py:392
  22.3 11.0 %copy-start.1 = (bf16[4,512]{1,0:T(4,128)(2,1)S(1)}, bf16[4,512]{1,0:T(4,128)(2,1)}, u32[]{:S(2)}) copy-start(bf16[4,512]{1,0:T(4,128)(2,1)} %nk_ref.1) | copy-start | bytes 12292
  22.3 11.0 %copy-start.2 = (bf16[4,512]{1,0:T(4,128)(2,1)S(1)}, bf16[4,512]{1,0:T(4,128)(2,1)}, u32[]{:S(2)}) copy-start(bf16[4,512]{1,0:T(4,128)(2,1)} %nv_ref.1) | copy-start | bytes 12292
  22.3 24.7 %copy-start = (bf16[4096,512]{1,0:T(8,128)(2,1)S(1)}, bf16[4096,512]{1,0:T(8,128)(2,1)}, u32[]{:S(2)}) copy-start(bf16[4096,512]{1,0:T(8,128)(2,1)} %w_ref.1) | copy-start | bytes 12582916
  25.6 6.1 %collective-permute-start.10 = (bf16[4,4224]{1,0:T(4,128)(2,1)S(1)}, bf16[4,4224]{1,0:T(4,128)(2,1)S(1)}, u32[]{:S(2)}, u32[]{:S(2)}) collective-permute-start(bf16[4,4224]{1,0:T(4,128)(2,1)S(1)} %get-tuple-element.57), channel_id=1, source_target_pairs={{0,24},{2,26},{4,28},{6,30},{8,16},{10,18},{12,20},{14,22},{16,8},... | collective-permute-start | bytes 101384 | tf_op jit(solution)/shard_map/ppermute | solution.py:392
  28.4 4.8 %collective-permute-start.11 = (bf16[4,4224]{1,0:T(4,128)(2,1)S(1)}, bf16[4,4224]{1,0:T(4,128)(2,1)S(1)}, u32[]{:S(2)}, u32[]{:S(2)}) collective-permute-start(bf16[4,4224]{1,0:T(4,128)(2,1)S(1)} %get-tuple-element.58), channel_id=1, source_target_pairs={{0,16},{2,18},{4,20},{6,22},{8,24},{10,26},{12,28},{14,30},{16,0},... | collective-permute-start | bytes 101384 | tf_op jit(solution)/shard_map/ppermute | solution.py:392
  28.7 4.5 %collective-permute-start.13 = (bf16[4,4224]{1,0:T(4,128)(2,1)S(1)}, bf16[4,4224]{1,0:T(4,128)(2,1)S(1)}, u32[]{:S(2)}, u32[]{:S(2)}) collective-permute-start(bf16[4,4224]{1,0:T(4,128)(2,1)S(1)} %get-tuple-element.61), channel_id=1, source_target_pairs={{0,8},{2,10},{4,12},{6,14},{8,0},{10,2},{12,4},{14,6},{16,24},{18,... | collective-permute-start | bytes 101384 | tf_op jit(solution)/shard_map/ppermute | solution.py:392
  33.8 5.8 %collective-permute-start.14 = (bf16[4,4096]{1,0:T(4,128)(2,1)S(1)}, bf16[4,4096]{1,0:T(4,128)(2,1)S(1)}, u32[]{:S(2)}, u32[]{:S(2)}) collective-permute-start(bf16[4,4096]{1,0:T(4,128)(2,1)S(1)} %finish.1), channel_id=1, source_target_pairs={{0,24},{2,26},{4,28},{6,30},{8,16},{10,18},{12,20},{14,22},{16,8},... | collective-permute-start | bytes 98312 | tf_op jit(solution)/shard_map/ppermute | solution.py:392
  35.7 5.5 %collective-permute-start.18 = (bf16[4,4096]{1,0:T(4,128)(2,1)S(1)}, bf16[4,4096]{1,0:T(4,128)(2,1)S(1)}, u32[]{:S(2)}, u32[]{:S(2)}) collective-permute-start(bf16[4,4096]{1,0:T(4,128)(2,1)S(1)} %finish.1), channel_id=1, source_target_pairs={{0,16},{2,18},{4,20},{6,22},{8,24},{10,26},{12,28},{14,30},{16,0},... | collective-permute-start | bytes 98312 | tf_op jit(solution)/shard_map/ppermute | solution.py:392
  36.3 4.8 %collective-permute-start.17 = (bf16[4,4096]{1,0:T(4,128)(2,1)S(1)}, bf16[4,4096]{1,0:T(4,128)(2,1)S(1)}, u32[]{:S(2)}, u32[]{:S(2)}) collective-permute-start(bf16[4,4096]{1,0:T(4,128)(2,1)S(1)} %finish.1), channel_id=1, source_target_pairs={{0,8},{2,10},{4,12},{6,14},{8,0},{10,2},{12,4},{14,6},{16,24},{18,... | collective-permute-start | bytes 98312 | tf_op jit(solution)/shard_map/ppermute | solution.py:392
  39.6 4.3 %collective-permute-start.15 = (bf16[2,4,4096]{2,1,0:T(4,128)(2,1)S(1)}, bf16[2,4,4096]{2,1,0:T(4,128)(2,1)S(1)}, u32[]{:S(2)}, u32[]{:S(2)}) collective-permute-start(bf16[2,4,4096]{2,1,0:T(4,128)(2,1)S(1)} %get-tuple-element.68), channel_id=1, source_target_pairs={{0,4},{2,6},{4,0},{6,2},{8,12},{10,14},{12,8},{14,10},{16,20},{18,... | collective-permute-start | bytes 196616 | tf_op jit(solution)/shard_map/ppermute | solution.py:392
  41.2 4.3 %collective-permute-start.19 = (bf16[2,4,4096]{2,1,0:T(4,128)(2,1)S(1)}, bf16[2,4,4096]{2,1,0:T(4,128)(2,1)S(1)}, u32[]{:S(2)}, u32[]{:S(2)}) collective-permute-start(bf16[2,4,4096]{2,1,0:T(4,128)(2,1)S(1)} %get-tuple-element.66), channel_id=1, source_target_pairs={{0,4},{2,6},{4,0},{6,2},{8,12},{10,14},{12,8},{14,10},{16,20},{18,... | collective-permute-start | bytes 196616 | tf_op jit(solution)/shard_map/ppermute | solution.py:392
  44.0 1.7 %collective-permute-start.16 = (bf16[2,2,4,4096]{3,2,1,0:T(4,128)(2,1)S(1)}, bf16[2,2,4,4096]{3,2,1,0:T(4,128)(2,1)S(1)}, u32[]{:S(2)}, u32[]{:S(2)}) collective-permute-start(bf16[2,2,4,4096]{3,2,1,0:T(4,128)(2,1)S(1)} %pad_maximum_fusion.near_a), channel_id=1, source_target_pairs={{0,2},{2,0},{4,6},{6,4},{8,10},{10,8},{12,14},{14,12},{16,18},{18,... | collective-permute-start | bytes 393224 | tf_op jit(solution)/shard_map/ppermute | solution.py:392
  45.6 1.4 %collective-permute-start.20 = (bf16[2,2,4,4096]{3,2,1,0:T(4,128)(2,1)S(1)}, bf16[2,2,4,4096]{3,2,1,0:T(4,128)(2,1)S(1)}, u32[]{:S(2)}, u32[]{:S(2)}) collective-permute-start(bf16[2,2,4,4096]{3,2,1,0:T(4,128)(2,1)S(1)} %pad_maximum_fusion.1.near_b), channel_id=1, source_target_pairs={{0,2},{2,0},{4,6},{6,4},{8,10},{10,8},{12,14},{14,12},{16,18},{18,... | collective-permute-start | bytes 393224 | tf_op jit(solution)/shard_map/ppermute | solution.py:392
  47.9 4.0 %collective-permute-start.21 = (bf16[32,512]{1,0:T(8,128)(2,1)S(1)}, bf16[32,512]{1,0:T(8,128)(2,1)S(1)}, u32[]{:S(2)}, u32[]{:S(2)}) collective-permute-start(bf16[32,512]{1,0:T(8,128)(2,1)S(1)} %get-tuple-element.64), channel_id=1, source_target_pairs={{0,1},{1,0},{2,3},{3,2},{4,5},{5,4},{6,7},{7,6},{8,9},{9,8},{10,11... | collective-permute-start | bytes 98312 | tf_op jit(solution)/shard_map/ppermute | solution.py:511

commit v7 on v5

--- a/solution.py
+++ b/solution.py
@@ -37,6 +37,7 @@
 def line_kernel(tail_ref, *refs):
     *pieces, out_ref = refs
     width = pieces[0].shape[1]
+    pieces = pieces[:1] + pieces[-2:0:-1] + pieces[-1:]
     out_ref[:, :width] = jnp.concatenate([x[...] for x in pieces], axis=0)
     out_ref[:, width:] = jnp.concatenate([tail_ref[...]] * len(pieces), axis=0)
 
@@ -84,11 +85,13 @@
         x.wait()
 
 
-def attend_kernel(kinds, q_ref, *refs):
+def attend_kernel(kinds, prompts, privates, q_ref, *refs):
     total = q_ref.shape[1]
     heads = (total - STATS) // (QPK * HD)
     caches = [refs[5 * n : 5 * n + 5] for n in range(len(kinds))]
     *outs, s_ref, p_ref, cs_ref, cp_ref = refs[5 * len(kinds) :]
+    if not prompts:
+        base_ref, *outs = outs
     requests, span = s_ref.shape[2] // cs_ref.shape[2], cs_ref.shape[3]
     pairs = requests // 2
     beams = q_ref.shape[0] // requests
@@ -130,7 +133,7 @@
             jnp.concatenate([x[t * beams : (t + 1) * beams] for x in tiles], axis=0)
             for t in range(requests)
         ]
-        for u in range(pairs):
+        for u in range(pairs if prompts else 0):
             both = jnp.concatenate(
                 [
                     jnp.concatenate([q[2 * u], blank], axis=1),
@@ -139,14 +142,21 @@
                 axis=0,
             )
             s_ref[n, k, 2 * u * rows : 2 * (u + 1) * rows] = dot(both, prompt(pk_ref, k, u), 1, 1)
+        if not privates:
+            return
         chosen = jnp.concatenate(
             [jnp.where(parents[n] == o, q[-1], blank) for o in range(olds)], axis=1
         )
         cs_ref[n, k] = dot(chosen, private(ck_ref, k), 1, 1)
 
     def weigh(n, k):
-        p, top, den = soft(s_ref[n, k])
-        p_ref[n, k] = p.astype(bf16)
+        top = den = ctop = cden = None
+        if prompts:
+            p, top, den = soft(s_ref[n, k])
+            p_ref[n, k] = p.astype(bf16)
+        if not privates:
+            kept[n, k] = (top, den, ctop, cden)
+            return
         place = lax.broadcasted_iota(jnp.int32, (rows, span), 1)
         c, ctop, cden = soft(jnp.where(place < limits[n], cs_ref[n, k], masked_score))
         cp_ref[n, k] = c.astype(bf16)
@@ -156,17 +166,22 @@
         _, pv_ref, _, _, cv_ref = caches[n]
         tops, dens, ctop, cden = kept.pop((n, k))
         found = []
-        for u in range(pairs):
+        for u in range(pairs if prompts else 0):
             both = dot(
                 p_ref[n, k, 2 * u * rows : 2 * (u + 1) * rows], prompt(pv_ref, k, u), 1, 0
             )
             for m, num in enumerate((both[:rows, :HD], both[rows:, HD:])):
                 part = slice((2 * u + m) * rows, (2 * u + m + 1) * rows)
                 found.append((num, tops[part], dens[part]))
+        if not privates:
+            return found
         every = dot(cp_ref[n, k], private(cv_ref, k), 1, 0)
         cnum = every[:, :HD]
         for o in range(1, olds):
             cnum = jnp.where(parents[n] == o, every[:, o * HD : (o + 1) * HD], cnum)
+        if not prompts:
+            cden = jnp.where(locals_[n], cden, 0.0)
+            return [(jnp.where(locals_[n], cnum, 0.0), jnp.where(locals_[n], ctop, masked_score), cden)]
         num, top, den = found[-1]
         both = jnp.where(locals_[n], jnp.maximum(top, ctop), top)
         a = jnp.exp(top - both)
@@ -178,9 +193,24 @@
         found = [values(n, k) for n in range(len(kinds))]
         done = []
         for t in range(requests):
-            num, top, den = found[0][t]
-            for other in found[1:]:
-                num2, top2, den2 = other[t]
+            if not prompts and t < requests - 1:
+                continue
+            at = t if prompts else 0
+            if prompts:
+                num, top, den = found[0][t]
+                others = found[1:]
+            else:
+                cols = [
+                    slice((k * QPK + i) * HD, (k * QPK + i + 1) * HD) for i in range(QPK)
+                ]
+                num = jnp.concatenate([base_ref[pairs - 1, :, c] for c in cols], axis=0).astype(f32)
+                top = jnp.concatenate(
+                    [base_lse[:, k * QPK + i : k * QPK + i + 1] for i in range(QPK)], axis=0
+                )
+                den = jnp.ones_like(top)
+                others = found
+            for other in others:
+                num2, top2, den2 = other[at]
                 both = jnp.maximum(top, top2)
                 a, e = jnp.exp(top - both), jnp.exp(top2 - both)
                 num, top, den = a * num + e * num2, both, a * den + e * den2
@@ -193,25 +223,30 @@
                     stats[t],
                 )
         for i in range(QPK):
-            store(
-                slice((k * QPK + i) * HD, (k * QPK + i + 1) * HD),
-                [x[i * beams : (i + 1) * beams] for x in done],
-            )
+            cols = slice((k * QPK + i) * HD, (k * QPK + i + 1) * HD)
+            if prompts:
+                store(cols, [x[i * beams : (i + 1) * beams] for x in done])
+            else:
+                outs[0][pairs - 1, :, cols] = done[0][i * beams : (i + 1) * beams].astype(bf16)
 
     def store(cols, pieces):
-        if len(outs) == 1:
-            outs[0][:, cols] = jnp.concatenate(pieces, axis=0).astype(bf16)
-        else:
-            for n, piece in enumerate(pieces):
-                outs[n // pairs][n % pairs, :, cols] = piece.astype(bf16)
-
+        for n, piece in enumerate(pieces):
+            outs[n // pairs][n % pairs, :, cols] = piece.astype(bf16)
+
+    if not prompts:
+        base_lse = read_stats(base_ref[pairs - 1, :, total - STATS :], stride)
+        for n in range(pairs - 1):
+            outs[0][n] = base_ref[n]
     for stage in (scores, weigh):
         for n in range(len(kinds)):
             for k in range(heads):
                 stage(n, k)
     for k in range(heads):
         finish(k)
-    store(slice(total - STATS, total), [pack_stats(x, stride) for x in stats])
+    if prompts:
+        store(slice(total - STATS, total), [pack_stats(x, stride) for x in stats])
+    else:
+        outs[0][pairs - 1, :, total - STATS :] = pack_stats(stats[-1], stride)
 
 
 def pack_stats(x, stride):
@@ -226,49 +261,37 @@
     return x + pltpu.roll(x, STATS - stride, 1) + pltpu.roll(x, STATS - 2 * stride, 1)
 
 
-def merge(a, b, outs):
-    total = a.shape[1]
-    count = (total - STATS) // HD
-    size = a.shape[0] // len(outs)
+def plane_kernel(*refs):
+    count, beams, total = refs[0].shape
+    parts, outs = refs[:-count], refs[-count:]
+    parts = [jnp.concatenate([x[n] for n in range(count)], axis=0) for x in parts]
+    heads = (total - STATS) // HD
 
     def store(cols, value):
         for n, out in enumerate(outs):
-            out[:, cols] = value[n * size : (n + 1) * size]
-
-    la, lb = read_stats(a[:, total - STATS :], count), read_stats(b[:, total - STATS :], count)
-    top = jnp.maximum(la, lb)
-    wa, wb = jnp.exp(la - top), jnp.exp(lb - top)
-    den = wa + wb
-    wa = wa * (1.0 / den)
-    wb = wb * (1.0 / den)
-    for h in range(count):
+            out[:, cols] = value[n * beams : (n + 1) * beams]
+
+    lses = [read_stats(x[:, total - STATS :], heads) for x in parts]
+    top = functools.reduce(jnp.maximum, lses)
+    ws = [jnp.exp(x - top) for x in lses]
+    den = functools.reduce(jnp.add, ws)
+    inv = 1.0 / den
+    ws = [w * inv for w in ws]
+    for h in range(heads):
         cols = slice(h * HD, (h + 1) * HD)
-        store(
-            cols,
-            (
-                wa[:, h : h + 1] * a[:, cols].astype(f32)
-                + wb[:, h : h + 1] * b[:, cols].astype(f32)
-            ).astype(bf16),
-        )
+        acc = None
+        for w, x in zip(ws, parts):
+            one = w[:, h : h + 1] * x[:, cols].astype(f32)
+            acc = one if acc is None else acc + one
+        store(cols, acc.astype(bf16))
     lse = top + jnp.log(den)
     lane = lax.broadcasted_iota(jnp.int32, lse.shape, 1)
     again = jnp.where(
-        lane < count,
+        lane < heads,
         lse,
-        jnp.where(lane < 2 * count, pltpu.roll(lse, count, 1), pltpu.roll(lse, 2 * count, 1)),
-    )
-    store(slice(total - STATS, total), pack_stats(again, count))
-
-
-def core_kernel(kept_ref, came_ref, *outs):
-    merge(kept_ref, came_ref, [out.at[n] for out in outs for n in range(out.shape[0])])
-
-
-def plane_kernel(kept_ref, came_ref, *outs):
-    kept, came = (
-        jnp.concatenate([x[n] for n in range(len(outs))], axis=0) for x in (kept_ref, came_ref)
-    )
-    merge(kept, came, outs)
+        jnp.where(lane < 2 * heads, pltpu.roll(lse, heads, 1), pltpu.roll(lse, 2 * heads, 1)),
+    )
+    store(slice(total - STATS, total), pack_stats(again, heads))
 
 
 def finish_kernel(q_ref, nk_ref, nv_ref, *refs):
@@ -375,7 +398,7 @@
     line = jax.ShapeDtypeStruct((rows, total), bf16)
     order = line_order(requests)
     others = order[:-1]
-    came = [swap(queries, t * group) for t in others]
+    came = [swap(queries, t * group) for t in others[:1] + others[:0:-1]]
     prompt = jax.ShapeDtypeStruct(prompt_keys.shape, bf16)
     private = jax.ShapeDtypeStruct(private_keys.shape, bf16)
     stored = (swap(private_keys, 1), swap(private_values, 1))
@@ -426,11 +449,12 @@
 
     many = beams * QPK
 
-    def attend(asked, name, out_shape, kinds, *caches):
+    def attend(name, kinds, prompts, privates, asked, *caches):
+        both = (half, half) if prompts else half
         return call(
-            functools.partial(attend_kernel, kinds),
+            functools.partial(attend_kernel, kinds, prompts, privates),
             name,
-            out_shape,
+            both,
             asked,
             *caches,
             scratch=[
@@ -443,20 +467,22 @@
             cost=2**26,
         )
 
+    half = jax.ShapeDtypeStruct((requests // 2, beams, total), bf16)
     other = swap(asked, 2)
-    own_here = attend(asked, "attend_own", line, (0,), *caches)
-    other, own_here = lax.optimization_barrier((other, own_here))
-    half = jax.ShapeDtypeStruct((requests // 2, beams, total), bf16)
-    send_a, send_b = attend(other, "attend_side", (half, half), (0, 1), *caches, *stored)
-    asked, _ = lax.optimization_barrier((asked, send_a))
-    own_there = attend(asked, "attend_own_other", line, (1,), *stored)
-    keep_a, keep_b = call(core_kernel, "own_merge", (half, half), own_here, own_there)
+    here_a, here_b = attend("attend_own", (0,), True, True, asked, *caches)
+    other, here_a, here_b = lax.optimization_barrier((other, here_a, here_b))
+    send_a, send_b = attend("side_prompt", (0, 1), True, False, other, *caches, *stored)
+    asked, send_a = lax.optimization_barrier((asked, send_a))
+    there_a, there_b = attend("own_prompt", (1,), True, False, asked, *stored)
+    send_b, there_a = lax.optimization_barrier((send_b, there_a))
+    send_b = attend("side_private", (0, 1), False, True, other, *caches, *stored, send_b)
     piece = jax.ShapeDtypeStruct((beams, total), bf16)
-    parts = []
-    for keep, send in ((keep_a, send_a), (keep_b, send_b)):
-        parts += call(
-            plane_kernel, "plane_merge", (piece,) * (requests // 2), keep, swap(send, 2)
-        )
+    few = (piece,) * (requests // 2)
+    came_a, came_b = swap(send_a, 2), swap(send_b, 2)
+    parts = call(plane_kernel, "plane_merge", few, here_a, there_a, came_a)
+    there_b, *parts = lax.optimization_barrier((there_b, *parts))
+    there_b = attend("own_private", (1,), False, True, asked, *stored, there_b)
+    parts = [*parts, *call(plane_kernel, "plane_merge", few, here_b, there_b, came_b)]
     parts = [swap(x, t * group) if t else x for t, x in zip(order, parts)]
     attended = call(
         finish_kernel,

time: 52 us -> 51.8 us (level)
  waiting for transfers between devices: 14.5 us -> 13 us
  starting transfers between devices: 23.3 us -> 24.2 us
    ppermute x21, waiting for transfers between devices: 12.1 us -> 10.6 us  [swap(): return lax.ppermute(x, 'beam', [(i, i ^ with_bit) for i in range(devices)])]
    ppermute x21, starting transfers between devices: 21.7 us -> 22.6 us  [swap(): return lax.ppermute(x, 'beam', [(i, i ^ with_bit) for i in range(devices)])]
    pallas_call x11 -> x12, Pallas kernels: 13 us -> 13.3 us  [call(): pl.pallas_call(kernel, out_shape=out_shape, in_specs=whole_blocks(len(arg...]
  transfers between devices with their start and end apart: 22 -> 22, of which waited for: 10 -> 9; matrix products, arithmetic and copies ran while one was open for 1% -> 1% of each run, Pallas kernels for 16% -> 20%
where the time goes in v7:
time: 51.8 us; the launch traced here: 51.6 us
  starting transfers between devices  24.2 us (47%)
  Pallas kernels  13.3 us (26%)
  waiting for transfers between devices  13 us (25%)
  other arithmetic  0.92 us (2%)
    ppermute x21, starting transfers between devices, swap(): return lax.ppermute(x, 'beam', [(i, i ^ with_bit) for i in range(devices)])  22.6 us
    pallas_call x12, Pallas kernels, call(): pl.pallas_call(kernel, out_shape=out_shape, in_specs=whole_blocks(len(arg...  13.3 us
    ppermute x21, waiting for transfers between devices, swap(): return lax.ppermute(x, 'beam', [(i, i ^ with_bit) for i in range(devices)])  10.6 us
    ppermute x1, waiting for transfers between devices, per_device(): came = lax.ppermute(send, 'head', [(0, 1), (1, 0)])  2.39 us
    ppermute x1, starting transfers between devices, per_device(): came = lax.ppermute(send, 'head', [(0, 1), (1, 0)])  1.59 us
  transfers between devices with their start and end apart: 22, of which 9 were waited for; matrix products, arithmetic and copies ran while one was open for 1% of the time, Pallas kernels for 20%

profile of v7, /device:TPU:0, one launch (start us, length us, event | category | flops | bytes accessed | tf_op | source)
XLA Modules:
  0.0 51.6 jit_solution(17145275578336978793)
XLA Ops:
  0.0 0.5 collective-permute-start.7
  0.5 0.1 collective-permute-start.8
  0.5 5.0 %collective-permute-start = (bf16[4,4096]{1,0:T(4,128)(2,1)}, bf16[4,4096]{1,0:T(4,128)(2,1)S(1)}, u32[]{:S(2)}, u32[]{:S(2)}) collective-permute-start(bf16[4,4096]{1,0:T(4,128)(2,1)} %q_hbm.1), channel_id=1, source_target_pairs={{0,24},{2,26},{4,28},{6,30},{8,16},{10,18},{12,20},{14,22},{16,8},... | collective-permute-start | bytes 98312 | tf_op jit(solution)/shard_map/ppermute | solution.py:393
  5.6 0.6 %collective-permute-start.1 = (bf16[4,4096]{1,0:T(4,128)(2,1)}, bf16[4,4096]{1,0:T(4,128)(2,1)S(1)}, u32[]{:S(2)}, u32[]{:S(2)}) collective-permute-start(bf16[4,4096]{1,0:T(4,128)(2,1)} %q_hbm.1), channel_id=1, source_target_pairs={{0,8},{2,10},{4,12},{6,14},{8,0},{10,2},{12,4},{14,6},{16,24},{18,... | collective-permute-start | bytes 98312 | tf_op jit(solution)/shard_map/ppermute | solution.py:393
  6.1 2.3 %load_private.1 = (bf16[4,4096]{1,0:T(4,128)(2,1)S(1)}, bf16[4,128]{1,0:T(4,128)(2,1)S(1)}, s32[8,128]{1,0:T(8,128)S(1)}, bf16[4,512,512]{2,1,0:T(8,128)(2,1)S(1)}, bf16[4,512,512]{2,1,0:T(8,128)(2,1)S(1)}) custom-call(bf16[4,4096]{1,0:T(4,128)(2,1)} %q_hbm.1, s32[4]{0:T(128)} %par_hbm.1, s32[4]{0:T(128)} %cnt_hbm.1, bf16[4,512,512]{2,1,0:T(8,128)(2,1)} %ck_hbm.1, ...), custom_call_target="tpu_custom_call" | custom-call | flops 67108864 | bytes 67108864 | tf_op jit(solution)/shard_map/load_private/pallas_call | solution.py:360
  8.4 0.0 collective-permute-done.refs_0_
  8.4 0.1 collective-permute-start.4
  8.5 2.1 %collective-permute-done.2.refs_2_ = bf16[4,4096]{1,0:T(4,128)(2,1)S(1)} collective-permute-done((bf16[4,4096]{1,0:T(4,128)(2,1)}, bf16[4,4096]{1,0:T(4,128)(2,1)S(1)}, u32[]{:S(2)}, u32[]{:S(2)}) %collective-permute-start.2) | collective-permute-done | bytes 32800 | tf_op jit(solution)/shard_map/ppermute | solution.py:393
  10.7 0.1 collective-permute-start.5
  10.8 0.5 collective-permute-start.6
  11.2 1.5 %collective-permute-start.3 = (bf16[16,4224]{1,0:T(8,128)(2,1)S(1)}, bf16[16,4224]{1,0:T(8,128)(2,1)S(1)}, u32[]{:S(2)}, u32[]{:S(2)}) collective-permute-start(bf16[16,4224]{1,0:T(8,128)(2,1)S(1)} %line.1.q_ref), channel_id=1, source_target_pairs={{0,4},{2,6},{4,0},{6,2},{8,12},{10,14},{12,8},{14,10},{16,20},{18,... | collective-permute-start | bytes 405512 | tf_op jit(solution)/shard_map/ppermute | solution.py:393
  12.7 1.6 %load_prompt.1 = (bf16[4,256,512]{2,1,0:T(8,128)(2,1)S(1)}, bf16[4,256,512]{2,1,0:T(8,128)(2,1)S(1)}) custom-call(bf16[4,256,512]{2,1,0:T(8,128)(2,1)} %pk_hbm, bf16[4,256,512]{2,1,0:T(8,128)(2,1)} %pv_hbm), custom_call_target="tpu_custom_call" | custom-call | flops 67108864 | bytes 67108864 | tf_op jit(solution)/shard_map/load_prompt/pallas_call | solution.py:360
  14.3 1.7 %attend_own.1 = (bf16[2,4,4224]{2,1,0:T(4,128)(2,1)S(1)}, bf16[2,4,4224]{2,1,0:T(4,128)(2,1)S(1)}) custom-call(bf16[16,4224]{1,0:T(8,128)(2,1)S(1)} %line.1.q_ref, bf16[4,256,512]{2,1,0:T(8,128)(2,1)S(1)} %get-tuple-element.51.refs_0_, bf16[4,256,512]{2,1,0:T(8,128)(2,1)S(1)} %get-tuple-element.52.refs_1_, s32[8,128]{1,0:T(8,128)S(1)} %get-tuple-element.53.refs_2_, ...), custom_call_target="tpu_custom_call" | custom-call | flops 67108864 | bytes 67108864 | tf_op jit(solution)/shard_map/attend_own/pallas_call | solution.py:360
  16.0 0.8 %collective-permute-done.3.q_ref = bf16[16,4224]{1,0:T(8,128)(2,1)S(1)} collective-permute-done((bf16[16,4224]{1,0:T(8,128)(2,1)S(1)}, bf16[16,4224]{1,0:T(8,128)(2,1)S(1)}, u32[]{:S(2)}, u32[]{:S(2)}) %collective-permute-start.3) | collective-permute-done | bytes 135200 | tf_op jit(solution)/shard_map/ppermute | solution.py:393
  16.8 1.4 %side_prompt.1 = (bf16[2,4,4224]{2,1,0:T(4,128)(2,1)S(1)}, bf16[2,4,4224]{2,1,0:T(4,128)(2,1)S(1)}) custom-call(bf16[16,4224]{1,0:T(8,128)(2,1)S(1)} %collective-permute-done.3.q_ref, bf16[4,256,512]{2,1,0:T(8,128)(2,1)S(1)} %get-tuple-element.51.refs_0_, bf16[4,256,512]{2,1,0:T(8,128)(2,1)S(1)} %get-tuple-element.52.refs_1_, ...), custom_call_target="tpu_custom_call" | custom-call | flops 67108864 | bytes 67108864 | tf_op jit(solution)/shard_map/side_prompt/pallas_call | solution.py:360
  18.3 1.6 %collective-permute-start.9 = (bf16[2,4,4224]{2,1,0:T(4,128)(2,1)S(1)}, bf16[2,4,4224]{2,1,0:T(4,128)(2,1)S(1)}, u32[]{:S(2)}, u32[]{:S(2)}) collective-permute-start(bf16[2,4,4224]{2,1,0:T(4,128)(2,1)S(1)} %get-tuple-element.69), channel_id=1, source_target_pairs={{0,4},{2,6},{4,0},{6,2},{8,12},{10,14},{12,8},{14,10},{16,20},{18,... | collective-permute-start | bytes 202760 | tf_op jit(solution)/shard_map/ppermute | solution.py:393
  19.8 0.7 %own_prompt.1 = (bf16[2,4,4224]{2,1,0:T(4,128)(2,1)S(1)}, bf16[2,4,4224]{2,1,0:T(4,128)(2,1)S(1)}) custom-call(bf16[16,4224]{1,0:T(8,128)(2,1)S(1)} %line.1.q_ref, bf16[4,256,512]{2,1,0:T(8,128)(2,1)S(1)} %collective-permute-done.5.refs_5_.refs_0_, bf16[4,256,512]{2,1,0:T(8,128)(2,1)S(1)} %collective-permute-done.6.refs_6_.refs_1_, ...), custom_call_target="tpu_custom_call" | custom-call | flops 67108864 | bytes 67108864 | tf_op jit(solution)/shard_map/own_prompt/pallas_call | solution.py:360
  20.5 2.4 %side_private.1 = bf16[2,4,4224]{2,1,0:T(4,128)(2,1)S(1)} custom-call(bf16[16,4224]{1,0:T(8,128)(2,1)S(1)} %collective-permute-done.3.q_ref, bf16[4,256,512]{2,1,0:T(8,128)(2,1)S(1)} %get-tuple-element.51.refs_0_, bf16[4,256,512]{2,1,0:T(8,128)(2,1)S(1)} %get-tuple-element.52.refs_1_, s32[8,128]{1,0:T(8,128)S(1)} %get-tuple-element.53.refs_2_, ...), custom_call_target="tpu_custom_call" | custom-call | flops 67108864 | bytes 67108864 | tf_op jit(solution)/shard_map/side_private/pallas_call | solution.py:360
  22.9 0.6 %collective-permute-start.12 = (bf16[2,4,4224]{2,1,0:T(4,128)(2,1)S(1)}, bf16[2,4,4224]{2,1,0:T(4,128)(2,1)S(1)}, u32[]{:S(2)}, u32[]{:S(2)}) collective-permute-start(bf16[2,4,4224]{2,1,0:T(4,128)(2,1)S(1)} %side_private.1), channel_id=1, source_target_pairs={{0,4},{2,6},{4,0},{6,2},{8,12},{10,14},{12,8},{14,10},{16,20},{18,... | collective-permute-start | bytes 202760 | tf_op jit(solution)/shard_map/ppermute | solution.py:393
  23.5 0.3 plane_merge.2
  23.8 0.0 copy-start.1
  23.8 0.0 copy-start.2
  23.9 2.9 %collective-permute-start.10 = (bf16[4,4224]{1,0:T(4,128)(2,1)S(1)}, bf16[4,4224]{1,0:T(4,128)(2,1)S(1)}, u32[]{:S(2)}, u32[]{:S(2)}) collective-permute-start(bf16[4,4224]{1,0:T(4,128)(2,1)S(1)} %get-tuple-element.72), channel_id=1, source_target_pairs={{0,24},{2,26},{4,28},{6,30},{8,16},{10,18},{12,20},{14,22},{16,8},... | collective-permute-start | bytes 101384 | tf_op jit(solution)/shard_map/ppermute | solution.py:393
  26.7 1.3 %own_private.1.refs_1_ = bf16[2,4,4224]{2,1,0:T(4,128)(2,1)S(1)} custom-call(bf16[16,4224]{1,0:T(8,128)(2,1)S(1)} %line.1.q_ref, bf16[4,256,512]{2,1,0:T(8,128)(2,1)S(1)} %collective-permute-done.5.refs_5_.refs_0_, bf16[4,256,512]{2,1,0:T(8,128)(2,1)S(1)} %collective-permute-done.6.refs_6_.refs_1_, s32[8,128]{1,0:T(8,128)S(1)} %collective-permute-done.4.refs_7_.refs_2_, ...), custom_call_target="tpu_custom_call" | custom-call | flops 67108864 | bytes 67108864 | tf_op jit(solution)/shard_map/own_private/pallas_call | solution.py:360
  28.0 0.3 plane_merge.3
  28.4 1.6 %collective-permute-start.13 = (bf16[4,4224]{1,0:T(4,128)(2,1)S(1)}, bf16[4,4224]{1,0:T(4,128)(2,1)S(1)}, u32[]{:S(2)}, u32[]{:S(2)}) collective-permute-start(bf16[4,4224]{1,0:T(4,128)(2,1)S(1)} %get-tuple-element.77), channel_id=1, source_target_pairs={{0,8},{2,10},{4,12},{6,14},{8,0},{10,2},{12,4},{14,6},{16,24},{18,... | collective-permute-start | bytes 101384 | tf_op jit(solution)/shard_map/ppermute | solution.py:393
  30.0 1.6 %collective-permute-done.11.refs_1_ = bf16[4,4224]{1,0:T(4,128)(2,1)S(1)} collective-permute-done((bf16[4,4224]{1,0:T(4,128)(2,1)S(1)}, bf16[4,4224]{1,0:T(4,128)(2,1)S(1)}, u32[]{:S(2)}, u32[]{:S(2)}) %collective-permute-start.11) | collective-permute-done | bytes 33824 | tf_op jit(solution)/shard_map/ppermute | solution.py:393
  31.6 0.8 %collective-permute-done.13.refs_2_ = bf16[4,4224]{1,0:T(4,128)(2,1)S(1)} collective-permute-done((bf16[4,4224]{1,0:T(4,128)(2,1)S(1)}, bf16[4,4224]{1,0:T(4,128)(2,1)S(1)}, u32[]{:S(2)}, u32[]{:S(2)}) %collective-permute-start.13) | collective-permute-done | bytes 33824 | tf_op jit(solution)/shard_map/ppermute | solution.py:393
  32.4 0.5 finish.1
  32.8 2.4 %collective-permute-start.14 = (bf16[4,4096]{1,0:T(4,128)(2,1)S(1)}, bf16[4,4096]{1,0:T(4,128)(2,1)S(1)}, u32[]{:S(2)}, u32[]{:S(2)}) collective-permute-start(bf16[4,4096]{1,0:T(4,128)(2,1)S(1)} %finish.1), channel_id=1, source_target_pairs={{0,24},{2,26},{4,28},{6,30},{8,16},{10,18},{12,20},{14,22},{16,8},... | collective-permute-start | bytes 98312 | tf_op jit(solution)/shard_map/ppermute | solution.py:393
  35.3 0.7 %collective-permute-start.18 = (bf16[4,4096]{1,0:T(4,128)(2,1)S(1)}, bf16[4,4096]{1,0:T(4,128)(2,1)S(1)}, u32[]{:S(2)}, u32[]{:S(2)}) collective-permute-start(bf16[4,4096]{1,0:T(4,128)(2,1)S(1)} %finish.1), channel_id=1, source_target_pairs={{0,16},{2,18},{4,20},{6,22},{8,24},{10,26},{12,28},{14,30},{16,0},... | collective-permute-start | bytes 98312 | tf_op jit(solution)/shard_map/ppermute | solution.py:393
  35.9 1.4 %collective-permute-start.17 = (bf16[4,4096]{1,0:T(4,128)(2,1)S(1)}, bf16[4,4096]{1,0:T(4,128)(2,1)S(1)}, u32[]{:S(2)}, u32[]{:S(2)}) collective-permute-start(bf16[4,4096]{1,0:T(4,128)(2,1)S(1)} %finish.1), channel_id=1, source_target_pairs={{0,8},{2,10},{4,12},{6,14},{8,0},{10,2},{12,4},{14,6},{16,24},{18,... | collective-permute-start | bytes 98312 | tf_op jit(solution)/shard_map/ppermute | solution.py:393
  37.3 1.3 %collective-permute-done.14 = bf16[4,4096]{1,0:T(4,128)(2,1)S(1)} collective-permute-done((bf16[4,4096]{1,0:T(4,128)(2,1)S(1)}, bf16[4,4096]{1,0:T(4,128)(2,1)S(1)}, u32[]{:S(2)}, u32[]{:S(2)}) %collective-permute-start.14) | collective-permute-done | bytes 32800 | tf_op jit(solution)/shard_map/ppermute | solution.py:393
  38.6 0.1 fusion.1
  38.7 1.6 %collective-permute-start.15 = (bf16[2,4,4096]{2,1,0:T(4,128)(2,1)S(1)}, bf16[2,4,4096]{2,1,0:T(4,128)(2,1)S(1)}, u32[]{:S(2)}, u32[]{:S(2)}) collective-permute-start(bf16[2,4,4096]{2,1,0:T(4,128)(2,1)S(1)} %get-tuple-element.84), channel_id=1, source_target_pairs={{0,4},{2,6},{4,0},{6,2},{8,12},{10,14},{12,8},{14,10},{16,20},{18,... | collective-permute-start | bytes 196616 | tf_op jit(solution)/shard_map/ppermute | solution.py:393
  40.2 0.1 fusion
  40.3 1.5 %collective-permute-start.19 = (bf16[2,4,4096]{2,1,0:T(4,128)(2,1)S(1)}, bf16[2,4,4096]{2,1,0:T(4,128)(2,1)S(1)}, u32[]{:S(2)}, u32[]{:S(2)}) collective-permute-start(bf16[2,4,4096]{2,1,0:T(4,128)(2,1)S(1)} %get-tuple-element.82), channel_id=1, source_target_pairs={{0,4},{2,6},{4,0},{6,2},{8,12},{10,14},{12,8},{14,10},{16,20},{18,... | collective-permute-start | bytes 196616 | tf_op jit(solution)/shard_map/ppermute | solution.py:393
  41.8 1.2 %collective-permute-done.15 = bf16[2,4,4096]{2,1,0:T(4,128)(2,1)S(1)} collective-permute-done((bf16[2,4,4096]{2,1,0:T(4,128)(2,1)S(1)}, bf16[2,4,4096]{2,1,0:T(4,128)(2,1)S(1)}, u32[]{:S(2)}, u32[]{:S(2)}) %collective-permute-start.15) | collective-permute-done | bytes 65568 | tf_op jit(solution)/shard_map/ppermute | solution.py:393
  43.0 0.1 pad_maximum_fusion.near_a
  43.1 0.1 collective-permute-start.16
  43.2 1.4 %collective-permute-done.19 = bf16[2,4,4096]{2,1,0:T(4,128)(2,1)S(1)} collective-permute-done((bf16[2,4,4096]{2,1,0:T(4,128)(2,1)S(1)}, bf16[2,4,4096]{2,1,0:T(4,128)(2,1)S(1)}, u32[]{:S(2)}, u32[]{:S(2)}) %collective-permute-start.19) | collective-permute-done | bytes 65568 | tf_op jit(solution)/shard_map/ppermute | solution.py:393
  44.6 0.1 pad_maximum_fusion.1.near_b
  44.7 0.1 collective-permute-start.20
  44.8 1.3 %collective-permute-done.20.far_b = bf16[2,2,4,4096]{3,2,1,0:T(4,128)(2,1)S(1)} collective-permute-done((bf16[2,2,4,4096]{3,2,1,0:T(4,128)(2,1)S(1)}, bf16[2,2,4,4096]{3,2,1,0:T(4,128)(2,1)S(1)}, u32[]{:S(2)}, u32[]{:S(2)}) %collective-permute-start.20) | collective-permute-done | bytes 131104 | tf_op jit(solution)/shard_map/ppermute | solution.py:393
  46.1 0.9 %project.1 = (f32[32,512]{1,0:T(8,128)S(1)}, bf16[32,512]{1,0:T(8,128)(2,1)S(1)}) custom-call(bf16[2,2,4,4096]{3,2,1,0:T(4,128)(2,1)S(1)} %pad_maximum_fusion.near_a, bf16[2,2,4,4096]{3,2,1,0:T(4,128)(2,1)S(1)} %collective-permute-done.16.far_a, bf16[2,2,4,4096]{3,2,1,0:T(4,128)(2,1)S(1)} %pad_maximum_fusion.1.near_b, ...), custom_call_target="tpu_custom_call" | custom-call | tf_op jit(solution)/shard_map/project/pallas_call | solution.py:360
  47.0 1.6 %collective-permute-start.21 = (bf16[32,512]{1,0:T(8,128)(2,1)S(1)}, bf16[32,512]{1,0:T(8,128)(2,1)S(1)}, u32[]{:S(2)}, u32[]{:S(2)}) collective-permute-start(bf16[32,512]{1,0:T(8,128)(2,1)S(1)} %get-tuple-element.80), channel_id=1, source_target_pairs={{0,1},{1,0},{2,3},{3,2},{4,5},{5,4},{6,7},{7,6},{8,9},{9,8},{10,11... | collective-permute-start | bytes 98312 | tf_op jit(solution)/shard_map/ppermute | solution.py:513
  48.6 2.4 %collective-permute-done.21 = bf16[32,512]{1,0:T(8,128)(2,1)S(1)} collective-permute-done((bf16[32,512]{1,0:T(8,128)(2,1)S(1)}, bf16[32,512]{1,0:T(8,128)(2,1)S(1)}, u32[]{:S(2)}, u32[]{:S(2)}) %collective-permute-start.21) | collective-permute-done | bytes 32800 | tf_op jit(solution)/shard_map/ppermute | solution.py:513
  51.0 0.6 %add_convert_fusion = bf16[32,512]{1,0:T(8,128)(2,1)} fusion(f32[32,512]{1,0:T(8,128)S(1)} %get-tuple-element.79, bf16[32,512]{1,0:T(8,128)(2,1)S(1)} %collective-permute-done.21), kind=kLoop, calls=%fused_computation.4 | loop fusion | flops 49152 | bytes 131072 | tf_op jit(solution)/shard_map/convert_element_type | solution.py:514
  (23 shorter events, 0.1 us)
Async XLA Ops:
  0.0 10.7 %copy-start.4 = (bf16[4,256,512]{2,1,0:T(8,128)(2,1)S(1)}, bf16[4,256,512]{2,1,0:T(8,128)(2,1)}, u32[]{:S(2)}) copy-start(bf16[4,256,512]{2,1,0:T(8,128)(2,1)} %pv_hbm) | copy-start | bytes 3145732
  0.0 10.7 %copy-start.3 = (bf16[4,256,512]{2,1,0:T(8,128)(2,1)S(1)}, bf16[4,256,512]{2,1,0:T(8,128)(2,1)}, u32[]{:S(2)}) copy-start(bf16[4,256,512]{2,1,0:T(8,128)(2,1)} %pk_hbm) | copy-start | bytes 3145732
  0.0 16.8 %collective-permute-start.7 = (bf16[4,512,512]{2,1,0:T(8,128)(2,1)}, bf16[4,512,512]{2,1,0:T(8,128)(2,1)S(1)}, u32[]{:S(2)}, u32[]{:S(2)}) collective-permute-start(bf16[4,512,512]{2,1,0:T(8,128)(2,1)} %ck_hbm.1), channel_id=1, source_target_pairs={{0,2},{2,0},{4,6},{6,4},{8,10},{10,8},{12,14},{14,12},{16,18},{18,... | collective-permute-start | bytes 6291464 | tf_op jit(solution)/shard_map/ppermute | solution.py:393
  0.5 16.4 %collective-permute-start.8 = (bf16[4,512,512]{2,1,0:T(8,128)(2,1)}, bf16[4,512,512]{2,1,0:T(8,128)(2,1)S(1)}, u32[]{:S(2)}, u32[]{:S(2)}) collective-permute-start(bf16[4,512,512]{2,1,0:T(8,128)(2,1)} %cv_hbm.1), channel_id=1, source_target_pairs={{0,2},{2,0},{4,6},{6,4},{8,10},{10,8},{12,14},{14,12},{16,18},{18,... | collective-permute-start | bytes 6291464 | tf_op jit(solution)/shard_map/ppermute | solution.py:393
  0.5 7.9 %collective-permute-start = (bf16[4,4096]{1,0:T(4,128)(2,1)}, bf16[4,4096]{1,0:T(4,128)(2,1)S(1)}, u32[]{:S(2)}, u32[]{:S(2)}) collective-permute-start(bf16[4,4096]{1,0:T(4,128)(2,1)} %q_hbm.1), channel_id=1, source_target_pairs={{0,24},{2,26},{4,28},{6,30},{8,16},{10,18},{12,20},{14,22},{16,8},... | collective-permute-start | bytes 98312 | tf_op jit(solution)/shard_map/ppermute | solution.py:393
  5.6 5.0 %collective-permute-start.2 = (bf16[4,4096]{1,0:T(4,128)(2,1)}, bf16[4,4096]{1,0:T(4,128)(2,1)S(1)}, u32[]{:S(2)}, u32[]{:S(2)}) collective-permute-start(bf16[4,4096]{1,0:T(4,128)(2,1)} %q_hbm.1), channel_id=1, source_target_pairs={{0,16},{2,18},{4,20},{6,22},{8,24},{10,26},{12,28},{14,30},{16,0},... | collective-permute-start | bytes 98312 | tf_op jit(solution)/shard_map/ppermute | solution.py:393
  5.6 5.0 %collective-permute-start.1 = (bf16[4,4096]{1,0:T(4,128)(2,1)}, bf16[4,4096]{1,0:T(4,128)(2,1)S(1)}, u32[]{:S(2)}, u32[]{:S(2)}) collective-permute-start(bf16[4,4096]{1,0:T(4,128)(2,1)} %q_hbm.1), channel_id=1, source_target_pairs={{0,8},{2,10},{4,12},{6,14},{8,0},{10,2},{12,4},{14,6},{16,24},{18,... | collective-permute-start | bytes 98312 | tf_op jit(solution)/shard_map/ppermute | solution.py:393
  8.4 2.2 %collective-permute-start.4 = (s32[8,128]{1,0:T(8,128)S(1)}, s32[8,128]{1,0:T(8,128)S(1)}, u32[]{:S(2)}, u32[]{:S(2)}) collective-permute-start(s32[8,128]{1,0:T(8,128)S(1)} %get-tuple-element.53.refs_2_), channel_id=1, source_target_pairs={{0,2},{2,0},{4,6},{6,4},{8,10},{10,8},{12,14},{14,12},{16,18},{18,... | collective-permute-start | bytes 12296 | tf_op jit(solution)/shard_map/ppermute | solution.py:393
  10.7 6.2 %collective-permute-start.5 = (bf16[4,256,512]{2,1,0:T(8,128)(2,1)S(1)}, bf16[4,256,512]{2,1,0:T(8,128)(2,1)S(1)}, u32[]{:S(2)}, u32[]{:S(2)}) collective-permute-start(bf16[4,256,512]{2,1,0:T(8,128)(2,1)S(1)} %copy-done.3), channel_id=1, source_target_pairs={{0,2},{2,0},{4,6},{6,4},{8,10},{10,8},{12,14},{14,12},{16,18},{18,... | collective-permute-start | bytes 3145736 | tf_op jit(solution)/shard_map/ppermute | solution.py:393
  10.8 6.1 %collective-permute-start.6 = (bf16[4,256,512]{2,1,0:T(8,128)(2,1)S(1)}, bf16[4,256,512]{2,1,0:T(8,128)(2,1)S(1)}, u32[]{:S(2)}, u32[]{:S(2)}) collective-permute-start(bf16[4,256,512]{2,1,0:T(8,128)(2,1)S(1)} %copy-done.4), channel_id=1, source_target_pairs={{0,2},{2,0},{4,6},{6,4},{8,10},{10,8},{12,14},{14,12},{16,18},{18,... | collective-permute-start | bytes 3145736 | tf_op jit(solution)/shard_map/ppermute | solution.py:393
  11.2 5.6 %collective-permute-start.3 = (bf16[16,4224]{1,0:T(8,128)(2,1)S(1)}, bf16[16,4224]{1,0:T(8,128)(2,1)S(1)}, u32[]{:S(2)}, u32[]{:S(2)}) collective-permute-start(bf16[16,4224]{1,0:T(8,128)(2,1)S(1)} %line.1.q_ref), channel_id=1, source_target_pairs={{0,4},{2,6},{4,0},{6,2},{8,12},{10,14},{12,8},{14,10},{16,20},{18,... | collective-permute-start | bytes 405512 | tf_op jit(solution)/shard_map/ppermute | solution.py:393
  18.3 5.2 %collective-permute-start.9 = (bf16[2,4,4224]{2,1,0:T(4,128)(2,1)S(1)}, bf16[2,4,4224]{2,1,0:T(4,128)(2,1)S(1)}, u32[]{:S(2)}, u32[]{:S(2)}) collective-permute-start(bf16[2,4,4224]{2,1,0:T(4,128)(2,1)S(1)} %get-tuple-element.69), channel_id=1, source_target_pairs={{0,4},{2,6},{4,0},{6,2},{8,12},{10,14},{12,8},{14,10},{16,20},{18,... | collective-permute-start | bytes 202760 | tf_op jit(solution)/shard_map/ppermute | solution.py:393
  22.9 5.1 %collective-permute-start.12 = (bf16[2,4,4224]{2,1,0:T(4,128)(2,1)S(1)}, bf16[2,4,4224]{2,1,0:T(4,128)(2,1)S(1)}, u32[]{:S(2)}, u32[]{:S(2)}) collective-permute-start(bf16[2,4,4224]{2,1,0:T(4,128)(2,1)S(1)} %side_private.1), channel_id=1, source_target_pairs={{0,4},{2,6},{4,0},{6,2},{8,12},{10,14},{12,8},{14,10},{16,20},{18,... | collective-permute-start | bytes 202760 | tf_op jit(solution)/shard_map/ppermute | solution.py:393
  23.8 8.5 %copy-start.1 = (bf16[4,512]{1,0:T(4,128)(2,1)S(1)}, bf16[4,512]{1,0:T(4,128)(2,1)}, u32[]{:S(2)}) copy-start(bf16[4,512]{1,0:T(4,128)(2,1)} %nk_ref.1) | copy-start | bytes 12292
  23.8 8.5 %copy-start.2 = (bf16[4,512]{1,0:T(4,128)(2,1)S(1)}, bf16[4,512]{1,0:T(4,128)(2,1)}, u32[]{:S(2)}) copy-start(bf16[4,512]{1,0:T(4,128)(2,1)} %nv_ref.1) | copy-start | bytes 12292
  23.9 6.1 %collective-permute-start.10 = (bf16[4,4224]{1,0:T(4,128)(2,1)S(1)}, bf16[4,4224]{1,0:T(4,128)(2,1)S(1)}, u32[]{:S(2)}, u32[]{:S(2)}) collective-permute-start(bf16[4,4224]{1,0:T(4,128)(2,1)S(1)} %get-tuple-element.72), channel_id=1, source_target_pairs={{0,24},{2,26},{4,28},{6,30},{8,16},{10,18},{12,20},{14,22},{16,8},... | collective-permute-start | bytes 101384 | tf_op jit(solution)/shard_map/ppermute | solution.py:393
  26.7 4.8 %collective-permute-start.11 = (bf16[4,4224]{1,0:T(4,128)(2,1)S(1)}, bf16[4,4224]{1,0:T(4,128)(2,1)S(1)}, u32[]{:S(2)}, u32[]{:S(2)}) collective-permute-start(bf16[4,4224]{1,0:T(4,128)(2,1)S(1)} %get-tuple-element.73), channel_id=1, source_target_pairs={{0,16},{2,18},{4,20},{6,22},{8,24},{10,26},{12,28},{14,30},{16,0},... | collective-permute-start | bytes 101384 | tf_op jit(solution)/shard_map/ppermute | solution.py:393
  26.7 19.4 %copy-start = (bf16[4096,512]{1,0:T(8,128)(2,1)S(1)}, bf16[4096,512]{1,0:T(8,128)(2,1)}, u32[]{:S(2)}) copy-start(bf16[4096,512]{1,0:T(8,128)(2,1)} %w_ref.1) | copy-start | bytes 12582916
  28.4 4.0 %collective-permute-start.13 = (bf16[4,4224]{1,0:T(4,128)(2,1)S(1)}, bf16[4,4224]{1,0:T(4,128)(2,1)S(1)}, u32[]{:S(2)}, u32[]{:S(2)}) collective-permute-start(bf16[4,4224]{1,0:T(4,128)(2,1)S(1)} %get-tuple-element.77), channel_id=1, source_target_pairs={{0,8},{2,10},{4,12},{6,14},{8,0},{10,2},{12,4},{14,6},{16,24},{18,... | collective-permute-start | bytes 101384 | tf_op jit(solution)/shard_map/ppermute | solution.py:393
  32.8 5.8 %collective-permute-start.14 = (bf16[4,4096]{1,0:T(4,128)(2,1)S(1)}, bf16[4,4096]{1,0:T(4,128)(2,1)S(1)}, u32[]{:S(2)}, u32[]{:S(2)}) collective-permute-start(bf16[4,4096]{1,0:T(4,128)(2,1)S(1)} %finish.1), channel_id=1, source_target_pairs={{0,24},{2,26},{4,28},{6,30},{8,16},{10,18},{12,20},{14,22},{16,8},... | collective-permute-start | bytes 98312 | tf_op jit(solution)/shard_map/ppermute | solution.py:393
  35.3 5.0 %collective-permute-start.18 = (bf16[4,4096]{1,0:T(4,128)(2,1)S(1)}, bf16[4,4096]{1,0:T(4,128)(2,1)S(1)}, u32[]{:S(2)}, u32[]{:S(2)}) collective-permute-start(bf16[4,4096]{1,0:T(4,128)(2,1)S(1)} %finish.1), channel_id=1, source_target_pairs={{0,16},{2,18},{4,20},{6,22},{8,24},{10,26},{12,28},{14,30},{16,0},... | collective-permute-start | bytes 98312 | tf_op jit(solution)/shard_map/ppermute | solution.py:393
  35.9 4.3 %collective-permute-start.17 = (bf16[4,4096]{1,0:T(4,128)(2,1)S(1)}, bf16[4,4096]{1,0:T(4,128)(2,1)S(1)}, u32[]{:S(2)}, u32[]{:S(2)}) collective-permute-start(bf16[4,4096]{1,0:T(4,128)(2,1)S(1)} %finish.1), channel_id=1, source_target_pairs={{0,8},{2,10},{4,12},{6,14},{8,0},{10,2},{12,4},{14,6},{16,24},{18,... | collective-permute-start | bytes 98312 | tf_op jit(solution)/shard_map/ppermute | solution.py:393
  38.7 4.3 %collective-permute-start.15 = (bf16[2,4,4096]{2,1,0:T(4,128)(2,1)S(1)}, bf16[2,4,4096]{2,1,0:T(4,128)(2,1)S(1)}, u32[]{:S(2)}, u32[]{:S(2)}) collective-permute-start(bf16[2,4,4096]{2,1,0:T(4,128)(2,1)S(1)} %get-tuple-element.84), channel_id=1, source_target_pairs={{0,4},{2,6},{4,0},{6,2},{8,12},{10,14},{12,8},{14,10},{16,20},{18,... | collective-permute-start | bytes 196616 | tf_op jit(solution)/shard_map/ppermute | solution.py:393
  40.3 4.3 %collective-permute-start.19 = (bf16[2,4,4096]{2,1,0:T(4,128)(2,1)S(1)}, bf16[2,4,4096]{2,1,0:T(4,128)(2,1)S(1)}, u32[]{:S(2)}, u32[]{:S(2)}) collective-permute-start(bf16[2,4,4096]{2,1,0:T(4,128)(2,1)S(1)} %get-tuple-element.82), channel_id=1, source_target_pairs={{0,4},{2,6},{4,0},{6,2},{8,12},{10,14},{12,8},{14,10},{16,20},{18,... | collective-permute-start | bytes 196616 | tf_op jit(solution)/shard_map/ppermute | solution.py:393
  43.1 1.7 %collective-permute-start.16 = (bf16[2,2,4,4096]{3,2,1,0:T(4,128)(2,1)S(1)}, bf16[2,2,4,4096]{3,2,1,0:T(4,128)(2,1)S(1)}, u32[]{:S(2)}, u32[]{:S(2)}) collective-permute-start(bf16[2,2,4,4096]{3,2,1,0:T(4,128)(2,1)S(1)} %pad_maximum_fusion.near_a), channel_id=1, source_target_pairs={{0,2},{2,0},{4,6},{6,4},{8,10},{10,8},{12,14},{14,12},{16,18},{18,... | collective-permute-start | bytes 393224 | tf_op jit(solution)/shard_map/ppermute | solution.py:393
  44.7 1.4 %collective-permute-start.20 = (bf16[2,2,4,4096]{3,2,1,0:T(4,128)(2,1)S(1)}, bf16[2,2,4,4096]{3,2,1,0:T(4,128)(2,1)S(1)}, u32[]{:S(2)}, u32[]{:S(2)}) collective-permute-start(bf16[2,2,4,4096]{3,2,1,0:T(4,128)(2,1)S(1)} %pad_maximum_fusion.1.near_b), channel_id=1, source_target_pairs={{0,2},{2,0},{4,6},{6,4},{8,10},{10,8},{12,14},{14,12},{16,18},{18,... | collective-permute-start | bytes 393224 | tf_op jit(solution)/shard_map/ppermute | solution.py:393
  47.0 4.0 %collective-permute-start.21 = (bf16[32,512]{1,0:T(8,128)(2,1)S(1)}, bf16[32,512]{1,0:T(8,128)(2,1)S(1)}, u32[]{:S(2)}, u32[]{:S(2)}) collective-permute-start(bf16[32,512]{1,0:T(8,128)(2,1)S(1)} %get-tuple-element.80), channel_id=1, source_target_pairs={{0,1},{1,0},{2,3},{3,2},{4,5},{5,4},{6,7},{7,6},{8,9},{9,8},{10,11... | collective-permute-start | bytes 98312 | tf_op jit(solution)/shard_map/ppermute | solution.py:513

commit v8 on v7

--- a/solution.py
+++ b/solution.py
@@ -470,6 +470,7 @@
     half = jax.ShapeDtypeStruct((requests // 2, beams, total), bf16)
     other = swap(asked, 2)
     here_a, here_b = attend("attend_own", (0,), True, True, asked, *caches)
+    here_b = attend("own_private", (1,), False, True, asked, *stored, here_b)
     other, here_a, here_b = lax.optimization_barrier((other, here_a, here_b))
     send_a, send_b = attend("side_prompt", (0, 1), True, False, other, *caches, *stored)
     asked, send_a = lax.optimization_barrier((asked, send_a))
@@ -480,8 +481,7 @@
     few = (piece,) * (requests // 2)
     came_a, came_b = swap(send_a, 2), swap(send_b, 2)
     parts = call(plane_kernel, "plane_merge", few, here_a, there_a, came_a)
-    there_b, *parts = lax.optimization_barrier((there_b, *parts))
-    there_b = attend("own_private", (1,), False, True, asked, *stored, there_b)
+    here_b, *parts = lax.optimization_barrier((here_b, *parts))
     parts = [*parts, *call(plane_kernel, "plane_merge", few, here_b, there_b, came_b)]
     parts = [swap(x, t * group) if t else x for t, x in zip(order, parts)]
     attended = call(

time: 51.8 us -> 51.7 us (level)
  starting transfers between devices: 24.2 us -> 23.2 us
  waiting for transfers between devices: 13 us -> 13.8 us
    ppermute x21, starting transfers between devices: 22.6 us -> 21.6 us  [swap(): return lax.ppermute(x, 'beam', [(i, i ^ with_bit) for i in range(devices)])]
    ppermute x21, waiting for transfers between devices: 10.6 us -> 11.4 us  [swap(): return lax.ppermute(x, 'beam', [(i, i ^ with_bit) for i in range(devices)])]
  transfers between devices with their start and end apart: 22 -> 22, of which waited for: 9 -> 10; matrix products, arithmetic and copies ran while one was open for 1% -> 1% of each run, Pallas kernels for 20% -> 19%
where the time goes in v8:
time: 51.7 us; the launch traced here: 51.5 us
  starting transfers between devices  23.2 us (45%)
  waiting for transfers between devices  13.8 us (27%)
  Pallas kernels  13.3 us (26%)
  other arithmetic  0.92 us (2%)
    ppermute x21, starting transfers between devices, swap(): return lax.ppermute(x, 'beam', [(i, i ^ with_bit) for i in range(devices)])  21.6 us
    pallas_call x12, Pallas kernels, call(): pl.pallas_call(kernel, out_shape=out_shape, in_specs=whole_blocks(len(arg...  13.3 us
    ppermute x21, waiting for transfers between devices, swap(): return lax.ppermute(x, 'beam', [(i, i ^ with_bit) for i in range(devices)])  11.4 us
    ppermute x1, waiting for transfers between devices, per_device(): came = lax.ppermute(send, 'head', [(0, 1), (1, 0)])  2.39 us
    ppermute x1, starting transfers between devices, per_device(): came = lax.ppermute(send, 'head', [(0, 1), (1, 0)])  1.59 us
  transfers between devices with their start and end apart: 22, of which 10 were waited for; matrix products, arithmetic and copies ran while one was open for 1% of the time, Pallas kernels for 19%

profile of v8, /device:TPU:0, one launch (start us, length us, event | category | flops | bytes accessed | tf_op | source)
XLA Modules:
  0.0 51.5 jit_solution(5887798821804841288)
XLA Ops:
  0.0 0.5 collective-permute-start.7
  0.5 0.1 collective-permute-start.8
  0.5 5.0 %collective-permute-start = (bf16[4,4096]{1,0:T(4,128)(2,1)}, bf16[4,4096]{1,0:T(4,128)(2,1)S(1)}, u32[]{:S(2)}, u32[]{:S(2)}) collective-permute-start(bf16[4,4096]{1,0:T(4,128)(2,1)} %q_hbm.1), channel_id=1, source_target_pairs={{0,24},{2,26},{4,28},{6,30},{8,16},{10,18},{12,20},{14,22},{16,8},... | collective-permute-start | bytes 98312 | tf_op jit(solution)/shard_map/ppermute | solution.py:393
  5.6 0.6 %collective-permute-start.1 = (bf16[4,4096]{1,0:T(4,128)(2,1)}, bf16[4,4096]{1,0:T(4,128)(2,1)S(1)}, u32[]{:S(2)}, u32[]{:S(2)}) collective-permute-start(bf16[4,4096]{1,0:T(4,128)(2,1)} %q_hbm.1), channel_id=1, source_target_pairs={{0,8},{2,10},{4,12},{6,14},{8,0},{10,2},{12,4},{14,6},{16,24},{18,... | collective-permute-start | bytes 98312 | tf_op jit(solution)/shard_map/ppermute | solution.py:393
  6.1 2.3 %load_private.1 = (bf16[4,4096]{1,0:T(4,128)(2,1)S(1)}, bf16[4,128]{1,0:T(4,128)(2,1)S(1)}, s32[8,128]{1,0:T(8,128)S(1)}, bf16[4,512,512]{2,1,0:T(8,128)(2,1)S(1)}, bf16[4,512,512]{2,1,0:T(8,128)(2,1)S(1)}) custom-call(bf16[4,4096]{1,0:T(4,128)(2,1)} %q_hbm.1, s32[4]{0:T(128)} %par_hbm.1, s32[4]{0:T(128)} %cnt_hbm.1, bf16[4,512,512]{2,1,0:T(8,128)(2,1)} %ck_hbm.1, ...), custom_call_target="tpu_custom_call" | custom-call | flops 67108864 | bytes 67108864 | tf_op jit(solution)/shard_map/load_private/pallas_call | solution.py:360
  8.4 0.1 collective-permute-start.4
  8.5 2.1 %collective-permute-done.2.refs_2_ = bf16[4,4096]{1,0:T(4,128)(2,1)S(1)} collective-permute-done((bf16[4,4096]{1,0:T(4,128)(2,1)}, bf16[4,4096]{1,0:T(4,128)(2,1)S(1)}, u32[]{:S(2)}, u32[]{:S(2)}) %collective-permute-start.2) | collective-permute-done | bytes 32800 | tf_op jit(solution)/shard_map/ppermute | solution.py:393
  10.7 0.1 collective-permute-start.5
  10.8 0.5 collective-permute-start.6
  11.2 1.5 %collective-permute-start.3 = (bf16[16,4224]{1,0:T(8,128)(2,1)S(1)}, bf16[16,4224]{1,0:T(8,128)(2,1)S(1)}, u32[]{:S(2)}, u32[]{:S(2)}) collective-permute-start(bf16[16,4224]{1,0:T(8,128)(2,1)S(1)} %line.1.q_ref), channel_id=1, source_target_pairs={{0,4},{2,6},{4,0},{6,2},{8,12},{10,14},{12,8},{14,10},{16,20},{18,... | collective-permute-start | bytes 405512 | tf_op jit(solution)/shard_map/ppermute | solution.py:393
  12.7 1.6 %load_prompt.1 = (bf16[4,256,512]{2,1,0:T(8,128)(2,1)S(1)}, bf16[4,256,512]{2,1,0:T(8,128)(2,1)S(1)}) custom-call(bf16[4,256,512]{2,1,0:T(8,128)(2,1)} %pk_hbm, bf16[4,256,512]{2,1,0:T(8,128)(2,1)} %pv_hbm), custom_call_target="tpu_custom_call" | custom-call | flops 67108864 | bytes 67108864 | tf_op jit(solution)/shard_map/load_prompt/pallas_call | solution.py:360
  14.3 1.7 %attend_own.1 = (bf16[2,4,4224]{2,1,0:T(4,128)(2,1)S(1)}, bf16[2,4,4224]{2,1,0:T(4,128)(2,1)S(1)}) custom-call(bf16[16,4224]{1,0:T(8,128)(2,1)S(1)} %line.1.q_ref, bf16[4,256,512]{2,1,0:T(8,128)(2,1)S(1)} %get-tuple-element.51.refs_0_, bf16[4,256,512]{2,1,0:T(8,128)(2,1)S(1)} %get-tuple-element.52.refs_1_, s32[8,128]{1,0:T(8,128)S(1)} %get-tuple-element.53.refs_2_, ...), custom_call_target="tpu_custom_call" | custom-call | flops 67108864 | bytes 67108864 | tf_op jit(solution)/shard_map/attend_own/pallas_call | solution.py:360
  16.1 1.3 %own_private.1.refs_0_ = bf16[2,4,4224]{2,1,0:T(4,128)(2,1)S(1)} custom-call(bf16[16,4224]{1,0:T(8,128)(2,1)S(1)} %line.1.q_ref, bf16[4,256,512]{2,1,0:T(8,128)(2,1)S(1)} %collective-permute-done.5.refs_0_.refs_5_, bf16[4,256,512]{2,1,0:T(8,128)(2,1)S(1)} %collective-permute-done.6.refs_1_.refs_6_, s32[8,128]{1,0:T(8,128)S(1)} %collective-permute-done.4.refs_2_.refs_7_, ...), custom_call_target="tpu_custom_call" | custom-call | flops 67108864 | bytes 67108864 | tf_op jit(solution)/shard_map/own_private/pallas_call | solution.py:360
  17.3 1.4 %side_prompt.1 = (bf16[2,4,4224]{2,1,0:T(4,128)(2,1)S(1)}, bf16[2,4,4224]{2,1,0:T(4,128)(2,1)S(1)}) custom-call(bf16[16,4224]{1,0:T(8,128)(2,1)S(1)} %collective-permute-done.3.q_ref, bf16[4,256,512]{2,1,0:T(8,128)(2,1)S(1)} %get-tuple-element.51.refs_0_, bf16[4,256,512]{2,1,0:T(8,128)(2,1)S(1)} %get-tuple-element.52.refs_1_, ...), custom_call_target="tpu_custom_call" | custom-call | flops 67108864 | bytes 67108864 | tf_op jit(solution)/shard_map/side_prompt/pallas_call | solution.py:360
  18.8 0.7 %own_prompt.1 = (bf16[2,4,4224]{2,1,0:T(4,128)(2,1)S(1)}, bf16[2,4,4224]{2,1,0:T(4,128)(2,1)S(1)}) custom-call(bf16[16,4224]{1,0:T(8,128)(2,1)S(1)} %line.1.q_ref, bf16[4,256,512]{2,1,0:T(8,128)(2,1)S(1)} %collective-permute-done.5.refs_0_.refs_5_, bf16[4,256,512]{2,1,0:T(8,128)(2,1)S(1)} %collective-permute-done.6.refs_1_.refs_6_, ...), custom_call_target="tpu_custom_call" | custom-call | flops 67108864 | bytes 67108864 | tf_op jit(solution)/shard_map/own_prompt/pallas_call | solution.py:360
  19.5 0.0 copy-start.1
  19.5 0.0 copy-start.2
  19.5 1.0 %collective-permute-start.9 = (bf16[2,4,4224]{2,1,0:T(4,128)(2,1)S(1)}, bf16[2,4,4224]{2,1,0:T(4,128)(2,1)S(1)}, u32[]{:S(2)}, u32[]{:S(2)}) collective-permute-start(bf16[2,4,4224]{2,1,0:T(4,128)(2,1)S(1)} %get-tuple-element.69), channel_id=1, source_target_pairs={{0,4},{2,6},{4,0},{6,2},{8,12},{10,14},{12,8},{14,10},{16,20},{18,... | collective-permute-start | bytes 202760 | tf_op jit(solution)/shard_map/ppermute | solution.py:393
  20.5 2.4 %side_private.1 = bf16[2,4,4224]{2,1,0:T(4,128)(2,1)S(1)} custom-call(bf16[16,4224]{1,0:T(8,128)(2,1)S(1)} %collective-permute-done.3.q_ref, bf16[4,256,512]{2,1,0:T(8,128)(2,1)S(1)} %get-tuple-element.51.refs_0_, bf16[4,256,512]{2,1,0:T(8,128)(2,1)S(1)} %get-tuple-element.52.refs_1_, s32[8,128]{1,0:T(8,128)S(1)} %get-tuple-element.53.refs_2_, ...), custom_call_target="tpu_custom_call" | custom-call | flops 67108864 | bytes 67108864 | tf_op jit(solution)/shard_map/side_private/pallas_call | solution.py:360
  22.9 1.1 %collective-permute-start.12 = (bf16[2,4,4224]{2,1,0:T(4,128)(2,1)S(1)}, bf16[2,4,4224]{2,1,0:T(4,128)(2,1)S(1)}, u32[]{:S(2)}, u32[]{:S(2)}) collective-permute-start(bf16[2,4,4224]{2,1,0:T(4,128)(2,1)S(1)} %side_private.1), channel_id=1, source_target_pairs={{0,4},{2,6},{4,0},{6,2},{8,12},{10,14},{12,8},{14,10},{16,20},{18,... | collective-permute-start | bytes 202760 | tf_op jit(solution)/shard_map/ppermute | solution.py:393
  24.1 0.3 plane_merge.2
  24.4 2.8 %collective-permute-start.10 = (bf16[4,4224]{1,0:T(4,128)(2,1)S(1)}, bf16[4,4224]{1,0:T(4,128)(2,1)S(1)}, u32[]{:S(2)}, u32[]{:S(2)}) collective-permute-start(bf16[4,4224]{1,0:T(4,128)(2,1)S(1)} %get-tuple-element.72), channel_id=1, source_target_pairs={{0,24},{2,26},{4,28},{6,30},{8,16},{10,18},{12,20},{14,22},{16,8},... | collective-permute-start | bytes 101384 | tf_op jit(solution)/shard_map/ppermute | solution.py:393
  27.2 0.1 collective-permute-done.12.refs_2_
  27.3 0.3 plane_merge.3
  27.6 1.6 %collective-permute-start.13 = (bf16[4,4224]{1,0:T(4,128)(2,1)S(1)}, bf16[4,4224]{1,0:T(4,128)(2,1)S(1)}, u32[]{:S(2)}, u32[]{:S(2)}) collective-permute-start(bf16[4,4224]{1,0:T(4,128)(2,1)S(1)} %get-tuple-element.77), channel_id=1, source_target_pairs={{0,8},{2,10},{4,12},{6,14},{8,0},{10,2},{12,4},{14,6},{16,24},{18,... | collective-permute-start | bytes 101384 | tf_op jit(solution)/shard_map/ppermute | solution.py:393
  29.2 1.0 %collective-permute-done.10.refs_0_ = bf16[4,4224]{1,0:T(4,128)(2,1)S(1)} collective-permute-done((bf16[4,4224]{1,0:T(4,128)(2,1)S(1)}, bf16[4,4224]{1,0:T(4,128)(2,1)S(1)}, u32[]{:S(2)}, u32[]{:S(2)}) %collective-permute-start.10) | collective-permute-done | bytes 33824 | tf_op jit(solution)/shard_map/ppermute | solution.py:393
  30.3 1.7 %collective-permute-done.11.refs_1_ = bf16[4,4224]{1,0:T(4,128)(2,1)S(1)} collective-permute-done((bf16[4,4224]{1,0:T(4,128)(2,1)S(1)}, bf16[4,4224]{1,0:T(4,128)(2,1)S(1)}, u32[]{:S(2)}, u32[]{:S(2)}) %collective-permute-start.11) | collective-permute-done | bytes 33824 | tf_op jit(solution)/shard_map/ppermute | solution.py:393
  32.0 0.5 finish.1
  32.5 2.5 %collective-permute-start.14 = (bf16[4,4096]{1,0:T(4,128)(2,1)S(1)}, bf16[4,4096]{1,0:T(4,128)(2,1)S(1)}, u32[]{:S(2)}, u32[]{:S(2)}) collective-permute-start(bf16[4,4096]{1,0:T(4,128)(2,1)S(1)} %finish.1), channel_id=1, source_target_pairs={{0,24},{2,26},{4,28},{6,30},{8,16},{10,18},{12,20},{14,22},{16,8},... | collective-permute-start | bytes 98312 | tf_op jit(solution)/shard_map/ppermute | solution.py:393
  34.9 0.2 collective-permute-start.18
  35.2 1.8 %collective-permute-start.17 = (bf16[4,4096]{1,0:T(4,128)(2,1)S(1)}, bf16[4,4096]{1,0:T(4,128)(2,1)S(1)}, u32[]{:S(2)}, u32[]{:S(2)}) collective-permute-start(bf16[4,4096]{1,0:T(4,128)(2,1)S(1)} %finish.1), channel_id=1, source_target_pairs={{0,8},{2,10},{4,12},{6,14},{8,0},{10,2},{12,4},{14,6},{16,24},{18,... | collective-permute-start | bytes 98312 | tf_op jit(solution)/shard_map/ppermute | solution.py:393
  36.9 1.3 %collective-permute-done.14 = bf16[4,4096]{1,0:T(4,128)(2,1)S(1)} collective-permute-done((bf16[4,4096]{1,0:T(4,128)(2,1)S(1)}, bf16[4,4096]{1,0:T(4,128)(2,1)S(1)}, u32[]{:S(2)}, u32[]{:S(2)}) %collective-permute-start.14) | collective-permute-done | bytes 32800 | tf_op jit(solution)/shard_map/ppermute | solution.py:393
  38.3 0.1 fusion.1
  38.3 1.1 %collective-permute-start.15 = (bf16[2,4,4096]{2,1,0:T(4,128)(2,1)S(1)}, bf16[2,4,4096]{2,1,0:T(4,128)(2,1)S(1)}, u32[]{:S(2)}, u32[]{:S(2)}) collective-permute-start(bf16[2,4,4096]{2,1,0:T(4,128)(2,1)S(1)} %get-tuple-element.84), channel_id=1, source_target_pairs={{0,4},{2,6},{4,0},{6,2},{8,12},{10,14},{12,8},{14,10},{16,20},{18,... | collective-permute-start | bytes 196616 | tf_op jit(solution)/shard_map/ppermute | solution.py:393
  39.4 0.7 %collective-permute-done.18 = bf16[4,4096]{1,0:T(4,128)(2,1)S(1)} collective-permute-done((bf16[4,4096]{1,0:T(4,128)(2,1)S(1)}, bf16[4,4096]{1,0:T(4,128)(2,1)S(1)}, u32[]{:S(2)}, u32[]{:S(2)}) %collective-permute-start.18) | collective-permute-done | bytes 32800 | tf_op jit(solution)/shard_map/ppermute | solution.py:393
  40.1 0.1 fusion
  40.2 1.1 %collective-permute-start.19 = (bf16[2,4,4096]{2,1,0:T(4,128)(2,1)S(1)}, bf16[2,4,4096]{2,1,0:T(4,128)(2,1)S(1)}, u32[]{:S(2)}, u32[]{:S(2)}) collective-permute-start(bf16[2,4,4096]{2,1,0:T(4,128)(2,1)S(1)} %get-tuple-element.82), channel_id=1, source_target_pairs={{0,4},{2,6},{4,0},{6,2},{8,12},{10,14},{12,8},{14,10},{16,20},{18,... | collective-permute-start | bytes 196616 | tf_op jit(solution)/shard_map/ppermute | solution.py:393
  41.2 1.4 %collective-permute-done.15 = bf16[2,4,4096]{2,1,0:T(4,128)(2,1)S(1)} collective-permute-done((bf16[2,4,4096]{2,1,0:T(4,128)(2,1)S(1)}, bf16[2,4,4096]{2,1,0:T(4,128)(2,1)S(1)}, u32[]{:S(2)}, u32[]{:S(2)}) %collective-permute-start.15) | collective-permute-done | bytes 65568 | tf_op jit(solution)/shard_map/ppermute | solution.py:393
  42.7 0.1 pad_maximum_fusion.near_a
  42.8 0.1 collective-permute-start.16
  42.8 1.7 %collective-permute-done.19 = bf16[2,4,4096]{2,1,0:T(4,128)(2,1)S(1)} collective-permute-done((bf16[2,4,4096]{2,1,0:T(4,128)(2,1)S(1)}, bf16[2,4,4096]{2,1,0:T(4,128)(2,1)S(1)}, u32[]{:S(2)}, u32[]{:S(2)}) %collective-permute-start.19) | collective-permute-done | bytes 65568 | tf_op jit(solution)/shard_map/ppermute | solution.py:393
  44.5 0.1 pad_maximum_fusion.1.near_b
  44.6 0.1 collective-permute-start.20
  44.7 1.3 %collective-permute-done.20.far_b = bf16[2,2,4,4096]{3,2,1,0:T(4,128)(2,1)S(1)} collective-permute-done((bf16[2,2,4,4096]{3,2,1,0:T(4,128)(2,1)S(1)}, bf16[2,2,4,4096]{3,2,1,0:T(4,128)(2,1)S(1)}, u32[]{:S(2)}, u32[]{:S(2)}) %collective-permute-start.20) | collective-permute-done | bytes 131104 | tf_op jit(solution)/shard_map/ppermute | solution.py:393
  46.0 0.9 %project.1 = (f32[32,512]{1,0:T(8,128)S(1)}, bf16[32,512]{1,0:T(8,128)(2,1)S(1)}) custom-call(bf16[2,2,4,4096]{3,2,1,0:T(4,128)(2,1)S(1)} %pad_maximum_fusion.near_a, bf16[2,2,4,4096]{3,2,1,0:T(4,128)(2,1)S(1)} %collective-permute-done.16.far_a, bf16[2,2,4,4096]{3,2,1,0:T(4,128)(2,1)S(1)} %pad_maximum_fusion.1.near_b, ...), custom_call_target="tpu_custom_call" | custom-call | tf_op jit(solution)/shard_map/project/pallas_call | solution.py:360
  46.9 1.6 %collective-permute-start.21 = (bf16[32,512]{1,0:T(8,128)(2,1)S(1)}, bf16[32,512]{1,0:T(8,128)(2,1)S(1)}, u32[]{:S(2)}, u32[]{:S(2)}) collective-permute-start(bf16[32,512]{1,0:T(8,128)(2,1)S(1)} %get-tuple-element.80), channel_id=1, source_target_pairs={{0,1},{1,0},{2,3},{3,2},{4,5},{5,4},{6,7},{7,6},{8,9},{9,8},{10,11... | collective-permute-start | bytes 98312 | tf_op jit(solution)/shard_map/ppermute | solution.py:513
  48.5 2.4 %collective-permute-done.21 = bf16[32,512]{1,0:T(8,128)(2,1)S(1)} collective-permute-done((bf16[32,512]{1,0:T(8,128)(2,1)S(1)}, bf16[32,512]{1,0:T(8,128)(2,1)S(1)}, u32[]{:S(2)}, u32[]{:S(2)}) %collective-permute-start.21) | collective-permute-done | bytes 32800 | tf_op jit(solution)/shard_map/ppermute | solution.py:513
  50.9 0.6 %add_convert_fusion = bf16[32,512]{1,0:T(8,128)(2,1)} fusion(f32[32,512]{1,0:T(8,128)S(1)} %get-tuple-element.79, bf16[32,512]{1,0:T(8,128)(2,1)S(1)} %collective-permute-done.21), kind=kLoop, calls=%fused_computation.4 | loop fusion | flops 49152 | bytes 131072 | tf_op jit(solution)/shard_map/convert_element_type | solution.py:514
  (23 shorter events, 0.1 us)
Async XLA Ops:
  0.0 10.7 %copy-start.4 = (bf16[4,256,512]{2,1,0:T(8,128)(2,1)S(1)}, bf16[4,256,512]{2,1,0:T(8,128)(2,1)}, u32[]{:S(2)}) copy-start(bf16[4,256,512]{2,1,0:T(8,128)(2,1)} %pv_hbm) | copy-start | bytes 3145732
  0.0 10.7 %copy-start.3 = (bf16[4,256,512]{2,1,0:T(8,128)(2,1)S(1)}, bf16[4,256,512]{2,1,0:T(8,128)(2,1)}, u32[]{:S(2)}) copy-start(bf16[4,256,512]{2,1,0:T(8,128)(2,1)} %pk_hbm) | copy-start | bytes 3145732
  0.0 16.0 %collective-permute-start.7 = (bf16[4,512,512]{2,1,0:T(8,128)(2,1)}, bf16[4,512,512]{2,1,0:T(8,128)(2,1)S(1)}, u32[]{:S(2)}, u32[]{:S(2)}) collective-permute-start(bf16[4,512,512]{2,1,0:T(8,128)(2,1)} %ck_hbm.1), channel_id=1, source_target_pairs={{0,2},{2,0},{4,6},{6,4},{8,10},{10,8},{12,14},{14,12},{16,18},{18,... | collective-permute-start | bytes 6291464 | tf_op jit(solution)/shard_map/ppermute | solution.py:393
  0.5 15.6 %collective-permute-start.8 = (bf16[4,512,512]{2,1,0:T(8,128)(2,1)}, bf16[4,512,512]{2,1,0:T(8,128)(2,1)S(1)}, u32[]{:S(2)}, u32[]{:S(2)}) collective-permute-start(bf16[4,512,512]{2,1,0:T(8,128)(2,1)} %cv_hbm.1), channel_id=1, source_target_pairs={{0,2},{2,0},{4,6},{6,4},{8,10},{10,8},{12,14},{14,12},{16,18},{18,... | collective-permute-start | bytes 6291464 | tf_op jit(solution)/shard_map/ppermute | solution.py:393
  0.5 7.9 %collective-permute-start = (bf16[4,4096]{1,0:T(4,128)(2,1)}, bf16[4,4096]{1,0:T(4,128)(2,1)S(1)}, u32[]{:S(2)}, u32[]{:S(2)}) collective-permute-start(bf16[4,4096]{1,0:T(4,128)(2,1)} %q_hbm.1), channel_id=1, source_target_pairs={{0,24},{2,26},{4,28},{6,30},{8,16},{10,18},{12,20},{14,22},{16,8},... | collective-permute-start | bytes 98312 | tf_op jit(solution)/shard_map/ppermute | solution.py:393
  5.6 5.0 %collective-permute-start.2 = (bf16[4,4096]{1,0:T(4,128)(2,1)}, bf16[4,4096]{1,0:T(4,128)(2,1)S(1)}, u32[]{:S(2)}, u32[]{:S(2)}) collective-permute-start(bf16[4,4096]{1,0:T(4,128)(2,1)} %q_hbm.1), channel_id=1, source_target_pairs={{0,16},{2,18},{4,20},{6,22},{8,24},{10,26},{12,28},{14,30},{16,0},... | collective-permute-start | bytes 98312 | tf_op jit(solution)/shard_map/ppermute | solution.py:393
  5.6 5.0 %collective-permute-start.1 = (bf16[4,4096]{1,0:T(4,128)(2,1)}, bf16[4,4096]{1,0:T(4,128)(2,1)S(1)}, u32[]{:S(2)}, u32[]{:S(2)}) collective-permute-start(bf16[4,4096]{1,0:T(4,128)(2,1)} %q_hbm.1), channel_id=1, source_target_pairs={{0,8},{2,10},{4,12},{6,14},{8,0},{10,2},{12,4},{14,6},{16,24},{18,... | collective-permute-start | bytes 98312 | tf_op jit(solution)/shard_map/ppermute | solution.py:393
  8.4 2.2 %collective-permute-start.4 = (s32[8,128]{1,0:T(8,128)S(1)}, s32[8,128]{1,0:T(8,128)S(1)}, u32[]{:S(2)}, u32[]{:S(2)}) collective-permute-start(s32[8,128]{1,0:T(8,128)S(1)} %get-tuple-element.53.refs_2_), channel_id=1, source_target_pairs={{0,2},{2,0},{4,6},{6,4},{8,10},{10,8},{12,14},{14,12},{16,18},{18,... | collective-permute-start | bytes 12296 | tf_op jit(solution)/shard_map/ppermute | solution.py:393
  10.7 5.4 %collective-permute-start.5 = (bf16[4,256,512]{2,1,0:T(8,128)(2,1)S(1)}, bf16[4,256,512]{2,1,0:T(8,128)(2,1)S(1)}, u32[]{:S(2)}, u32[]{:S(2)}) collective-permute-start(bf16[4,256,512]{2,1,0:T(8,128)(2,1)S(1)} %copy-done.3), channel_id=1, source_target_pairs={{0,2},{2,0},{4,6},{6,4},{8,10},{10,8},{12,14},{14,12},{16,18},{18,... | collective-permute-start | bytes 3145736 | tf_op jit(solution)/shard_map/ppermute | solution.py:393
  10.8 5.3 %collective-permute-start.6 = (bf16[4,256,512]{2,1,0:T(8,128)(2,1)S(1)}, bf16[4,256,512]{2,1,0:T(8,128)(2,1)S(1)}, u32[]{:S(2)}, u32[]{:S(2)}) collective-permute-start(bf16[4,256,512]{2,1,0:T(8,128)(2,1)S(1)} %copy-done.4), channel_id=1, source_target_pairs={{0,2},{2,0},{4,6},{6,4},{8,10},{10,8},{12,14},{14,12},{16,18},{18,... | collective-permute-start | bytes 3145736 | tf_op jit(solution)/shard_map/ppermute | solution.py:393
  11.2 6.1 %collective-permute-start.3 = (bf16[16,4224]{1,0:T(8,128)(2,1)S(1)}, bf16[16,4224]{1,0:T(8,128)(2,1)S(1)}, u32[]{:S(2)}, u32[]{:S(2)}) collective-permute-start(bf16[16,4224]{1,0:T(8,128)(2,1)S(1)} %line.1.q_ref), channel_id=1, source_target_pairs={{0,4},{2,6},{4,0},{6,2},{8,12},{10,14},{12,8},{14,10},{16,20},{18,... | collective-permute-start | bytes 405512 | tf_op jit(solution)/shard_map/ppermute | solution.py:393
  19.5 12.5 %copy-start.1 = (bf16[4,512]{1,0:T(4,128)(2,1)S(1)}, bf16[4,512]{1,0:T(4,128)(2,1)}, u32[]{:S(2)}) copy-start(bf16[4,512]{1,0:T(4,128)(2,1)} %nk_ref.1) | copy-start | bytes 12292
  19.5 12.5 %copy-start.2 = (bf16[4,512]{1,0:T(4,128)(2,1)S(1)}, bf16[4,512]{1,0:T(4,128)(2,1)}, u32[]{:S(2)}) copy-start(bf16[4,512]{1,0:T(4,128)(2,1)} %nv_ref.1) | copy-start | bytes 12292
  19.5 4.5 %collective-permute-start.9 = (bf16[2,4,4224]{2,1,0:T(4,128)(2,1)S(1)}, bf16[2,4,4224]{2,1,0:T(4,128)(2,1)S(1)}, u32[]{:S(2)}, u32[]{:S(2)}) collective-permute-start(bf16[2,4,4224]{2,1,0:T(4,128)(2,1)S(1)} %get-tuple-element.69), channel_id=1, source_target_pairs={{0,4},{2,6},{4,0},{6,2},{8,12},{10,14},{12,8},{14,10},{16,20},{18,... | collective-permute-start | bytes 202760 | tf_op jit(solution)/shard_map/ppermute | solution.py:393
  20.5 25.5 %copy-start = (bf16[4096,512]{1,0:T(8,128)(2,1)S(1)}, bf16[4096,512]{1,0:T(8,128)(2,1)}, u32[]{:S(2)}) copy-start(bf16[4096,512]{1,0:T(8,128)(2,1)} %w_ref.1) | copy-start | bytes 12582916
  22.9 4.4 %collective-permute-start.12 = (bf16[2,4,4224]{2,1,0:T(4,128)(2,1)S(1)}, bf16[2,4,4224]{2,1,0:T(4,128)(2,1)S(1)}, u32[]{:S(2)}, u32[]{:S(2)}) collective-permute-start(bf16[2,4,4224]{2,1,0:T(4,128)(2,1)S(1)} %side_private.1), channel_id=1, source_target_pairs={{0,4},{2,6},{4,0},{6,2},{8,12},{10,14},{12,8},{14,10},{16,20},{18,... | collective-permute-start | bytes 202760 | tf_op jit(solution)/shard_map/ppermute | solution.py:393
  24.4 5.9 %collective-permute-start.10 = (bf16[4,4224]{1,0:T(4,128)(2,1)S(1)}, bf16[4,4224]{1,0:T(4,128)(2,1)S(1)}, u32[]{:S(2)}, u32[]{:S(2)}) collective-permute-start(bf16[4,4224]{1,0:T(4,128)(2,1)S(1)} %get-tuple-element.72), channel_id=1, source_target_pairs={{0,24},{2,26},{4,28},{6,30},{8,16},{10,18},{12,20},{14,22},{16,8},... | collective-permute-start | bytes 101384 | tf_op jit(solution)/shard_map/ppermute | solution.py:393
  27.2 4.8 %collective-permute-start.11 = (bf16[4,4224]{1,0:T(4,128)(2,1)S(1)}, bf16[4,4224]{1,0:T(4,128)(2,1)S(1)}, u32[]{:S(2)}, u32[]{:S(2)}) collective-permute-start(bf16[4,4224]{1,0:T(4,128)(2,1)S(1)} %get-tuple-element.73), channel_id=1, source_target_pairs={{0,16},{2,18},{4,20},{6,22},{8,24},{10,26},{12,28},{14,30},{16,0},... | collective-permute-start | bytes 101384 | tf_op jit(solution)/shard_map/ppermute | solution.py:393
  27.6 4.4 %collective-permute-start.13 = (bf16[4,4224]{1,0:T(4,128)(2,1)S(1)}, bf16[4,4224]{1,0:T(4,128)(2,1)S(1)}, u32[]{:S(2)}, u32[]{:S(2)}) collective-permute-start(bf16[4,4224]{1,0:T(4,128)(2,1)S(1)} %get-tuple-element.77), channel_id=1, source_target_pairs={{0,8},{2,10},{4,12},{6,14},{8,0},{10,2},{12,4},{14,6},{16,24},{18,... | collective-permute-start | bytes 101384 | tf_op jit(solution)/shard_map/ppermute | solution.py:393
  32.5 5.8 %collective-permute-start.14 = (bf16[4,4096]{1,0:T(4,128)(2,1)S(1)}, bf16[4,4096]{1,0:T(4,128)(2,1)S(1)}, u32[]{:S(2)}, u32[]{:S(2)}) collective-permute-start(bf16[4,4096]{1,0:T(4,128)(2,1)S(1)} %finish.1), channel_id=1, source_target_pairs={{0,24},{2,26},{4,28},{6,30},{8,16},{10,18},{12,20},{14,22},{16,8},... | collective-permute-start | bytes 98312 | tf_op jit(solution)/shard_map/ppermute | solution.py:393
  34.9 5.2 %collective-permute-start.18 = (bf16[4,4096]{1,0:T(4,128)(2,1)S(1)}, bf16[4,4096]{1,0:T(4,128)(2,1)S(1)}, u32[]{:S(2)}, u32[]{:S(2)}) collective-permute-start(bf16[4,4096]{1,0:T(4,128)(2,1)S(1)} %finish.1), channel_id=1, source_target_pairs={{0,16},{2,18},{4,20},{6,22},{8,24},{10,26},{12,28},{14,30},{16,0},... | collective-permute-start | bytes 98312 | tf_op jit(solution)/shard_map/ppermute | solution.py:393
  35.2 4.9 %collective-permute-start.17 = (bf16[4,4096]{1,0:T(4,128)(2,1)S(1)}, bf16[4,4096]{1,0:T(4,128)(2,1)S(1)}, u32[]{:S(2)}, u32[]{:S(2)}) collective-permute-start(bf16[4,4096]{1,0:T(4,128)(2,1)S(1)} %finish.1), channel_id=1, source_target_pairs={{0,8},{2,10},{4,12},{6,14},{8,0},{10,2},{12,4},{14,6},{16,24},{18,... | collective-permute-start | bytes 98312 | tf_op jit(solution)/shard_map/ppermute | solution.py:393
  38.3 4.3 %collective-permute-start.15 = (bf16[2,4,4096]{2,1,0:T(4,128)(2,1)S(1)}, bf16[2,4,4096]{2,1,0:T(4,128)(2,1)S(1)}, u32[]{:S(2)}, u32[]{:S(2)}) collective-permute-start(bf16[2,4,4096]{2,1,0:T(4,128)(2,1)S(1)} %get-tuple-element.84), channel_id=1, source_target_pairs={{0,4},{2,6},{4,0},{6,2},{8,12},{10,14},{12,8},{14,10},{16,20},{18,... | collective-permute-start | bytes 196616 | tf_op jit(solution)/shard_map/ppermute | solution.py:393
  40.2 4.3 %collective-permute-start.19 = (bf16[2,4,4096]{2,1,0:T(4,128)(2,1)S(1)}, bf16[2,4,4096]{2,1,0:T(4,128)(2,1)S(1)}, u32[]{:S(2)}, u32[]{:S(2)}) collective-permute-start(bf16[2,4,4096]{2,1,0:T(4,128)(2,1)S(1)} %get-tuple-element.82), channel_id=1, source_target_pairs={{0,4},{2,6},{4,0},{6,2},{8,12},{10,14},{12,8},{14,10},{16,20},{18,... | collective-permute-start | bytes 196616 | tf_op jit(solution)/shard_map/ppermute | solution.py:393
  42.8 1.9 %collective-permute-start.16 = (bf16[2,2,4,4096]{3,2,1,0:T(4,128)(2,1)S(1)}, bf16[2,2,4,4096]{3,2,1,0:T(4,128)(2,1)S(1)}, u32[]{:S(2)}, u32[]{:S(2)}) collective-permute-start(bf16[2,2,4,4096]{3,2,1,0:T(4,128)(2,1)S(1)} %pad_maximum_fusion.near_a), channel_id=1, source_target_pairs={{0,2},{2,0},{4,6},{6,4},{8,10},{10,8},{12,14},{14,12},{16,18},{18,... | collective-permute-start | bytes 393224 | tf_op jit(solution)/shard_map/ppermute | solution.py:393
  44.6 1.4 %collective-permute-start.20 = (bf16[2,2,4,4096]{3,2,1,0:T(4,128)(2,1)S(1)}, bf16[2,2,4,4096]{3,2,1,0:T(4,128)(2,1)S(1)}, u32[]{:S(2)}, u32[]{:S(2)}) collective-permute-start(bf16[2,2,4,4096]{3,2,1,0:T(4,128)(2,1)S(1)} %pad_maximum_fusion.1.near_b), channel_id=1, source_target_pairs={{0,2},{2,0},{4,6},{6,4},{8,10},{10,8},{12,14},{14,12},{16,18},{18,... | collective-permute-start | bytes 393224 | tf_op jit(solution)/shard_map/ppermute | solution.py:393
  46.9 4.0 %collective-permute-start.21 = (bf16[32,512]{1,0:T(8,128)(2,1)S(1)}, bf16[32,512]{1,0:T(8,128)(2,1)S(1)}, u32[]{:S(2)}, u32[]{:S(2)}) collective-permute-start(bf16[32,512]{1,0:T(8,128)(2,1)S(1)} %get-tuple-element.80), channel_id=1, source_target_pairs={{0,1},{1,0},{2,3},{3,2},{4,5},{5,4},{6,7},{7,6},{8,9},{9,8},{10,11... | collective-permute-start | bytes 98312 | tf_op jit(solution)/shard_map/ppermute | solution.py:513

commit v9 on v7

--- a/solution.py
+++ b/solution.py
@@ -470,11 +470,9 @@
     half = jax.ShapeDtypeStruct((requests // 2, beams, total), bf16)
     other = swap(asked, 2)
     here_a, here_b = attend("attend_own", (0,), True, True, asked, *caches)
-    other, here_a, here_b = lax.optimization_barrier((other, here_a, here_b))
+    there_a, there_b = attend("own_prompt", (1,), True, False, asked, *stored)
+    other, here_a, there_a = lax.optimization_barrier((other, here_a, there_a))
     send_a, send_b = attend("side_prompt", (0, 1), True, False, other, *caches, *stored)
-    asked, send_a = lax.optimization_barrier((asked, send_a))
-    there_a, there_b = attend("own_prompt", (1,), True, False, asked, *stored)
-    send_b, there_a = lax.optimization_barrier((send_b, there_a))
     send_b = attend("side_private", (0, 1), False, True, other, *caches, *stored, send_b)
     piece = jax.ShapeDtypeStruct((beams, total), bf16)
     few = (piece,) * (requests // 2)

time: 51.8 us -> 51 us (0.985)
  waiting for transfers between devices: 13 us -> 12.2 us
    ppermute x21, waiting for transfers between devices: 10.6 us -> 9.85 us  [swap(): return lax.ppermute(x, 'beam', [(i, i ^ with_bit) for i in range(devices)])]
  transfers between devices with their start and end apart: 22 -> 22, of which waited for: 9 -> 8; matrix products, arithmetic and copies ran while one was open for 1% -> 1% of each run, Pallas kernels for 20% -> 21%
where the time goes in v9:
time: 51 us; the launch traced here: 50.9 us
  starting transfers between devices  24.1 us (47%)
  Pallas kernels  13.3 us (26%)
  waiting for transfers between devices  12.2 us (24%)
  other arithmetic  0.92 us (2%)
    ppermute x21, starting transfers between devices, swap(): return lax.ppermute(x, 'beam', [(i, i ^ with_bit) for i in range(devices)])  22.6 us
    pallas_call x12, Pallas kernels, call(): pl.pallas_call(kernel, out_shape=out_shape, in_specs=whole_blocks(len(arg...  13.3 us
    ppermute x21, waiting for transfers between devices, swap(): return lax.ppermute(x, 'beam', [(i, i ^ with_bit) for i in range(devices)])  9.85 us
    ppermute x1, waiting for transfers between devices, per_device(): came = lax.ppermute(send, 'head', [(0, 1), (1, 0)])  2.39 us
    ppermute x1, starting transfers between devices, per_device(): came = lax.ppermute(send, 'head', [(0, 1), (1, 0)])  1.59 us
  transfers between devices with their start and end apart: 22, of which 8 were waited for; matrix products, arithmetic and copies ran while one was open for 1% of the time, Pallas kernels for 21%

profile of v9, /device:TPU:0, one launch (start us, length us, event | category | flops | bytes accessed | tf_op | source)
XLA Modules:
  0.0 50.9 jit_solution(13298933603866645599)
XLA Ops:
  0.0 0.5 collective-permute-start.6
  0.5 0.1 collective-permute-start.7
  0.5 5.0 %collective-permute-start = (bf16[4,4096]{1,0:T(4,128)(2,1)}, bf16[4,4096]{1,0:T(4,128)(2,1)S(1)}, u32[]{:S(2)}, u32[]{:S(2)}) collective-permute-start(bf16[4,4096]{1,0:T(4,128)(2,1)} %q_hbm.1), channel_id=1, source_target_pairs={{0,24},{2,26},{4,28},{6,30},{8,16},{10,18},{12,20},{14,22},{16,8},... | collective-permute-start | bytes 98312 | tf_op jit(solution)/shard_map/ppermute | solution.py:393
  5.6 0.6 %collective-permute-start.1 = (bf16[4,4096]{1,0:T(4,128)(2,1)}, bf16[4,4096]{1,0:T(4,128)(2,1)S(1)}, u32[]{:S(2)}, u32[]{:S(2)}) collective-permute-start(bf16[4,4096]{1,0:T(4,128)(2,1)} %q_hbm.1), channel_id=1, source_target_pairs={{0,8},{2,10},{4,12},{6,14},{8,0},{10,2},{12,4},{14,6},{16,24},{18,... | collective-permute-start | bytes 98312 | tf_op jit(solution)/shard_map/ppermute | solution.py:393
  6.1 2.3 %load_private.1 = (bf16[4,4096]{1,0:T(4,128)(2,1)S(1)}, bf16[4,128]{1,0:T(4,128)(2,1)S(1)}, s32[8,128]{1,0:T(8,128)S(1)}, bf16[4,512,512]{2,1,0:T(8,128)(2,1)S(1)}, bf16[4,512,512]{2,1,0:T(8,128)(2,1)S(1)}) custom-call(bf16[4,4096]{1,0:T(4,128)(2,1)} %q_hbm.1, s32[4]{0:T(128)} %par_hbm.1, s32[4]{0:T(128)} %cnt_hbm.1, bf16[4,512,512]{2,1,0:T(8,128)(2,1)} %ck_hbm.1, ...), custom_call_target="tpu_custom_call" | custom-call | flops 67108864 | bytes 67108864 | tf_op jit(solution)/shard_map/load_private/pallas_call | solution.py:360
  8.4 0.0 collective-permute-done.refs_0_
  8.4 0.1 collective-permute-start.3
  8.5 2.1 %collective-permute-done.2.refs_2_ = bf16[4,4096]{1,0:T(4,128)(2,1)S(1)} collective-permute-done((bf16[4,4096]{1,0:T(4,128)(2,1)}, bf16[4,4096]{1,0:T(4,128)(2,1)S(1)}, u32[]{:S(2)}, u32[]{:S(2)}) %collective-permute-start.2) | collective-permute-done | bytes 32800 | tf_op jit(solution)/shard_map/ppermute | solution.py:393
  10.7 0.1 collective-permute-start.4
  10.8 0.5 collective-permute-start.5
  11.2 1.5 %collective-permute-start.8 = (bf16[16,4224]{1,0:T(8,128)(2,1)S(1)}, bf16[16,4224]{1,0:T(8,128)(2,1)S(1)}, u32[]{:S(2)}, u32[]{:S(2)}) collective-permute-start(bf16[16,4224]{1,0:T(8,128)(2,1)S(1)} %line.1.q_ref), channel_id=1, source_target_pairs={{0,4},{2,6},{4,0},{6,2},{8,12},{10,14},{12,8},{14,10},{16,20},{18,... | collective-permute-start | bytes 405512 | tf_op jit(solution)/shard_map/ppermute | solution.py:393
  12.7 1.6 %load_prompt.1 = (bf16[4,256,512]{2,1,0:T(8,128)(2,1)S(1)}, bf16[4,256,512]{2,1,0:T(8,128)(2,1)S(1)}) custom-call(bf16[4,256,512]{2,1,0:T(8,128)(2,1)} %pk_hbm, bf16[4,256,512]{2,1,0:T(8,128)(2,1)} %pv_hbm), custom_call_target="tpu_custom_call" | custom-call | flops 67108864 | bytes 67108864 | tf_op jit(solution)/shard_map/load_prompt/pallas_call | solution.py:360
  14.3 1.7 %attend_own.1 = (bf16[2,4,4224]{2,1,0:T(4,128)(2,1)S(1)}, bf16[2,4,4224]{2,1,0:T(4,128)(2,1)S(1)}) custom-call(bf16[16,4224]{1,0:T(8,128)(2,1)S(1)} %line.1.q_ref, bf16[4,256,512]{2,1,0:T(8,128)(2,1)S(1)} %get-tuple-element.52.refs_0_, bf16[4,256,512]{2,1,0:T(8,128)(2,1)S(1)} %get-tuple-element.53.refs_1_, s32[8,128]{1,0:T(8,128)S(1)} %get-tuple-element.45.refs_2_, ...), custom_call_target="tpu_custom_call" | custom-call | flops 67108864 | bytes 67108864 | tf_op jit(solution)/shard_map/attend_own/pallas_call | solution.py:360
  16.1 0.7 %own_prompt.1 = (bf16[2,4,4224]{2,1,0:T(4,128)(2,1)S(1)}, bf16[2,4,4224]{2,1,0:T(4,128)(2,1)S(1)}) custom-call(bf16[16,4224]{1,0:T(8,128)(2,1)S(1)} %line.1.q_ref, bf16[4,256,512]{2,1,0:T(8,128)(2,1)S(1)} %collective-permute-done.4.refs_0_.refs_5_, bf16[4,256,512]{2,1,0:T(8,128)(2,1)S(1)} %collective-permute-done.5.refs_1_.refs_6_, ...), custom_call_target="tpu_custom_call" | custom-call | flops 67108864 | bytes 67108864 | tf_op jit(solution)/shard_map/own_prompt/pallas_call | solution.py:360
  16.8 0.0 collective-permute-done.8.q_ref
  16.8 1.4 %side_prompt.1 = (bf16[2,4,4224]{2,1,0:T(4,128)(2,1)S(1)}, bf16[2,4,4224]{2,1,0:T(4,128)(2,1)S(1)}) custom-call(bf16[16,4224]{1,0:T(8,128)(2,1)S(1)} %collective-permute-done.8.q_ref, bf16[4,256,512]{2,1,0:T(8,128)(2,1)S(1)} %get-tuple-element.52.refs_0_, bf16[4,256,512]{2,1,0:T(8,128)(2,1)S(1)} %get-tuple-element.53.refs_1_, ...), custom_call_target="tpu_custom_call" | custom-call | flops 67108864 | bytes 67108864 | tf_op jit(solution)/shard_map/side_prompt/pallas_call | solution.py:360
  18.2 1.6 %collective-permute-start.9 = (bf16[2,4,4224]{2,1,0:T(4,128)(2,1)S(1)}, bf16[2,4,4224]{2,1,0:T(4,128)(2,1)S(1)}, u32[]{:S(2)}, u32[]{:S(2)}) collective-permute-start(bf16[2,4,4224]{2,1,0:T(4,128)(2,1)S(1)} %get-tuple-element.61), channel_id=1, source_target_pairs={{0,4},{2,6},{4,0},{6,2},{8,12},{10,14},{12,8},{14,10},{16,20},{18,... | collective-permute-start | bytes 202760 | tf_op jit(solution)/shard_map/ppermute | solution.py:393
  19.8 2.4 %side_private.1 = bf16[2,4,4224]{2,1,0:T(4,128)(2,1)S(1)} custom-call(bf16[16,4224]{1,0:T(8,128)(2,1)S(1)} %collective-permute-done.8.q_ref, bf16[4,256,512]{2,1,0:T(8,128)(2,1)S(1)} %get-tuple-element.52.refs_0_, bf16[4,256,512]{2,1,0:T(8,128)(2,1)S(1)} %get-tuple-element.53.refs_1_, s32[8,128]{1,0:T(8,128)S(1)} %get-tuple-element.45.refs_2_, ...), custom_call_target="tpu_custom_call" | custom-call | flops 67108864 | bytes 67108864 | tf_op jit(solution)/shard_map/side_private/pallas_call | solution.py:360
  22.1 0.6 %collective-permute-start.12 = (bf16[2,4,4224]{2,1,0:T(4,128)(2,1)S(1)}, bf16[2,4,4224]{2,1,0:T(4,128)(2,1)S(1)}, u32[]{:S(2)}, u32[]{:S(2)}) collective-permute-start(bf16[2,4,4224]{2,1,0:T(4,128)(2,1)S(1)} %side_private.1), channel_id=1, source_target_pairs={{0,4},{2,6},{4,0},{6,2},{8,12},{10,14},{12,8},{14,10},{16,20},{18,... | collective-permute-start | bytes 202760 | tf_op jit(solution)/shard_map/ppermute | solution.py:393
  22.8 0.3 plane_merge.2
  23.1 0.0 copy-start.1
  23.1 0.0 copy-start.2
  23.1 2.9 %collective-permute-start.10 = (bf16[4,4224]{1,0:T(4,128)(2,1)S(1)}, bf16[4,4224]{1,0:T(4,128)(2,1)S(1)}, u32[]{:S(2)}, u32[]{:S(2)}) collective-permute-start(bf16[4,4224]{1,0:T(4,128)(2,1)S(1)} %get-tuple-element.64), channel_id=1, source_target_pairs={{0,24},{2,26},{4,28},{6,30},{8,16},{10,18},{12,20},{14,22},{16,8},... | collective-permute-start | bytes 101384 | tf_op jit(solution)/shard_map/ppermute | solution.py:393
  26.0 1.3 %own_private.1.refs_1_ = bf16[2,4,4224]{2,1,0:T(4,128)(2,1)S(1)} custom-call(bf16[16,4224]{1,0:T(8,128)(2,1)S(1)} %line.1.q_ref, bf16[4,256,512]{2,1,0:T(8,128)(2,1)S(1)} %collective-permute-done.4.refs_0_.refs_5_, bf16[4,256,512]{2,1,0:T(8,128)(2,1)S(1)} %collective-permute-done.5.refs_1_.refs_6_, s32[8,128]{1,0:T(8,128)S(1)} %collective-permute-done.3.refs_2_.refs_7_, ...), custom_call_target="tpu_custom_call" | custom-call | flops 67108864 | bytes 67108864 | tf_op jit(solution)/shard_map/own_private/pallas_call | solution.py:360
  27.3 0.3 plane_merge.3
  27.6 1.6 %collective-permute-start.13 = (bf16[4,4224]{1,0:T(4,128)(2,1)S(1)}, bf16[4,4224]{1,0:T(4,128)(2,1)S(1)}, u32[]{:S(2)}, u32[]{:S(2)}) collective-permute-start(bf16[4,4224]{1,0:T(4,128)(2,1)S(1)} %get-tuple-element.69), channel_id=1, source_target_pairs={{0,8},{2,10},{4,12},{6,14},{8,0},{10,2},{12,4},{14,6},{16,24},{18,... | collective-permute-start | bytes 101384 | tf_op jit(solution)/shard_map/ppermute | solution.py:393
  29.2 1.6 %collective-permute-done.11.refs_1_ = bf16[4,4224]{1,0:T(4,128)(2,1)S(1)} collective-permute-done((bf16[4,4224]{1,0:T(4,128)(2,1)S(1)}, bf16[4,4224]{1,0:T(4,128)(2,1)S(1)}, u32[]{:S(2)}, u32[]{:S(2)}) %collective-permute-start.11) | collective-permute-done | bytes 33824 | tf_op jit(solution)/shard_map/ppermute | solution.py:393
  30.8 0.8 %collective-permute-done.13.refs_2_ = bf16[4,4224]{1,0:T(4,128)(2,1)S(1)} collective-permute-done((bf16[4,4224]{1,0:T(4,128)(2,1)S(1)}, bf16[4,4224]{1,0:T(4,128)(2,1)S(1)}, u32[]{:S(2)}, u32[]{:S(2)}) %collective-permute-start.13) | collective-permute-done | bytes 33824 | tf_op jit(solution)/shard_map/ppermute | solution.py:393
  31.6 0.5 finish.1
  32.1 2.4 %collective-permute-start.14 = (bf16[4,4096]{1,0:T(4,128)(2,1)S(1)}, bf16[4,4096]{1,0:T(4,128)(2,1)S(1)}, u32[]{:S(2)}, u32[]{:S(2)}) collective-permute-start(bf16[4,4096]{1,0:T(4,128)(2,1)S(1)} %finish.1), channel_id=1, source_target_pairs={{0,24},{2,26},{4,28},{6,30},{8,16},{10,18},{12,20},{14,22},{16,8},... | collective-permute-start | bytes 98312 | tf_op jit(solution)/shard_map/ppermute | solution.py:393
  34.5 0.7 %collective-permute-start.18 = (bf16[4,4096]{1,0:T(4,128)(2,1)S(1)}, bf16[4,4096]{1,0:T(4,128)(2,1)S(1)}, u32[]{:S(2)}, u32[]{:S(2)}) collective-permute-start(bf16[4,4096]{1,0:T(4,128)(2,1)S(1)} %finish.1), channel_id=1, source_target_pairs={{0,16},{2,18},{4,20},{6,22},{8,24},{10,26},{12,28},{14,30},{16,0},... | collective-permute-start | bytes 98312 | tf_op jit(solution)/shard_map/ppermute | solution.py:393
  35.2 1.4 %collective-permute-start.17 = (bf16[4,4096]{1,0:T(4,128)(2,1)S(1)}, bf16[4,4096]{1,0:T(4,128)(2,1)S(1)}, u32[]{:S(2)}, u32[]{:S(2)}) collective-permute-start(bf16[4,4096]{1,0:T(4,128)(2,1)S(1)} %finish.1), channel_id=1, source_target_pairs={{0,8},{2,10},{4,12},{6,14},{8,0},{10,2},{12,4},{14,6},{16,24},{18,... | collective-permute-start | bytes 98312 | tf_op jit(solution)/shard_map/ppermute | solution.py:393
  36.5 1.4 %collective-permute-done.14 = bf16[4,4096]{1,0:T(4,128)(2,1)S(1)} collective-permute-done((bf16[4,4096]{1,0:T(4,128)(2,1)S(1)}, bf16[4,4096]{1,0:T(4,128)(2,1)S(1)}, u32[]{:S(2)}, u32[]{:S(2)}) %collective-permute-start.14) | collective-permute-done | bytes 32800 | tf_op jit(solution)/shard_map/ppermute | solution.py:393
  37.9 0.1 fusion.1
  37.9 1.5 %collective-permute-start.15 = (bf16[2,4,4096]{2,1,0:T(4,128)(2,1)S(1)}, bf16[2,4,4096]{2,1,0:T(4,128)(2,1)S(1)}, u32[]{:S(2)}, u32[]{:S(2)}) collective-permute-start(bf16[2,4,4096]{2,1,0:T(4,128)(2,1)S(1)} %get-tuple-element.76), channel_id=1, source_target_pairs={{0,4},{2,6},{4,0},{6,2},{8,12},{10,14},{12,8},{14,10},{16,20},{18,... | collective-permute-start | bytes 196616 | tf_op jit(solution)/shard_map/ppermute | solution.py:393
  39.5 0.1 fusion
  39.5 1.5 %collective-permute-start.19 = (bf16[2,4,4096]{2,1,0:T(4,128)(2,1)S(1)}, bf16[2,4,4096]{2,1,0:T(4,128)(2,1)S(1)}, u32[]{:S(2)}, u32[]{:S(2)}) collective-permute-start(bf16[2,4,4096]{2,1,0:T(4,128)(2,1)S(1)} %get-tuple-element.74), channel_id=1, source_target_pairs={{0,4},{2,6},{4,0},{6,2},{8,12},{10,14},{12,8},{14,10},{16,20},{18,... | collective-permute-start | bytes 196616 | tf_op jit(solution)/shard_map/ppermute | solution.py:393
  41.1 1.2 %collective-permute-done.15 = bf16[2,4,4096]{2,1,0:T(4,128)(2,1)S(1)} collective-permute-done((bf16[2,4,4096]{2,1,0:T(4,128)(2,1)S(1)}, bf16[2,4,4096]{2,1,0:T(4,128)(2,1)S(1)}, u32[]{:S(2)}, u32[]{:S(2)}) %collective-permute-start.15) | collective-permute-done | bytes 65568 | tf_op jit(solution)/shard_map/ppermute | solution.py:393
  42.3 0.1 pad_maximum_fusion.near_a
  42.4 0.1 collective-permute-start.16
  42.5 1.4 %collective-permute-done.19 = bf16[2,4,4096]{2,1,0:T(4,128)(2,1)S(1)} collective-permute-done((bf16[2,4,4096]{2,1,0:T(4,128)(2,1)S(1)}, bf16[2,4,4096]{2,1,0:T(4,128)(2,1)S(1)}, u32[]{:S(2)}, u32[]{:S(2)}) %collective-permute-start.19) | collective-permute-done | bytes 65568 | tf_op jit(solution)/shard_map/ppermute | solution.py:393
  43.9 0.1 pad_maximum_fusion.1.near_b
  44.0 0.1 collective-permute-start.20
  44.1 1.3 %collective-permute-done.20.far_b = bf16[2,2,4,4096]{3,2,1,0:T(4,128)(2,1)S(1)} collective-permute-done((bf16[2,2,4,4096]{3,2,1,0:T(4,128)(2,1)S(1)}, bf16[2,2,4,4096]{3,2,1,0:T(4,128)(2,1)S(1)}, u32[]{:S(2)}, u32[]{:S(2)}) %collective-permute-start.20) | collective-permute-done | bytes 131104 | tf_op jit(solution)/shard_map/ppermute | solution.py:393
  45.4 0.9 %project.1 = (f32[32,512]{1,0:T(8,128)S(1)}, bf16[32,512]{1,0:T(8,128)(2,1)S(1)}) custom-call(bf16[2,2,4,4096]{3,2,1,0:T(4,128)(2,1)S(1)} %pad_maximum_fusion.near_a, bf16[2,2,4,4096]{3,2,1,0:T(4,128)(2,1)S(1)} %collective-permute-done.16.far_a, bf16[2,2,4,4096]{3,2,1,0:T(4,128)(2,1)S(1)} %pad_maximum_fusion.1.near_b, ...), custom_call_target="tpu_custom_call" | custom-call | tf_op jit(solution)/shard_map/project/pallas_call | solution.py:360
  46.3 1.6 %collective-permute-start.21 = (bf16[32,512]{1,0:T(8,128)(2,1)S(1)}, bf16[32,512]{1,0:T(8,128)(2,1)S(1)}, u32[]{:S(2)}, u32[]{:S(2)}) collective-permute-start(bf16[32,512]{1,0:T(8,128)(2,1)S(1)} %get-tuple-element.72), channel_id=1, source_target_pairs={{0,1},{1,0},{2,3},{3,2},{4,5},{5,4},{6,7},{7,6},{8,9},{9,8},{10,11... | collective-permute-start | bytes 98312 | tf_op jit(solution)/shard_map/ppermute | solution.py:511
  47.9 2.4 %collective-permute-done.21 = bf16[32,512]{1,0:T(8,128)(2,1)S(1)} collective-permute-done((bf16[32,512]{1,0:T(8,128)(2,1)S(1)}, bf16[32,512]{1,0:T(8,128)(2,1)S(1)}, u32[]{:S(2)}, u32[]{:S(2)}) %collective-permute-start.21) | collective-permute-done | bytes 32800 | tf_op jit(solution)/shard_map/ppermute | solution.py:511
  50.3 0.6 %add_convert_fusion = bf16[32,512]{1,0:T(8,128)(2,1)} fusion(f32[32,512]{1,0:T(8,128)S(1)} %get-tuple-element.71, bf16[32,512]{1,0:T(8,128)(2,1)S(1)} %collective-permute-done.21), kind=kLoop, calls=%fused_computation.4 | loop fusion | flops 49152 | bytes 131072 | tf_op jit(solution)/shard_map/convert_element_type | solution.py:512
  (23 shorter events, 0.1 us)
Async XLA Ops:
  0.0 10.7 %copy-start.4 = (bf16[4,256,512]{2,1,0:T(8,128)(2,1)S(1)}, bf16[4,256,512]{2,1,0:T(8,128)(2,1)}, u32[]{:S(2)}) copy-start(bf16[4,256,512]{2,1,0:T(8,128)(2,1)} %pv_hbm) | copy-start | bytes 3145732
  0.0 10.7 %copy-start.3 = (bf16[4,256,512]{2,1,0:T(8,128)(2,1)S(1)}, bf16[4,256,512]{2,1,0:T(8,128)(2,1)}, u32[]{:S(2)}) copy-start(bf16[4,256,512]{2,1,0:T(8,128)(2,1)} %pk_hbm) | copy-start | bytes 3145732
  0.0 16.0 %collective-permute-start.6 = (bf16[4,512,512]{2,1,0:T(8,128)(2,1)}, bf16[4,512,512]{2,1,0:T(8,128)(2,1)S(1)}, u32[]{:S(2)}, u32[]{:S(2)}) collective-permute-start(bf16[4,512,512]{2,1,0:T(8,128)(2,1)} %ck_hbm.1), channel_id=1, source_target_pairs={{0,2},{2,0},{4,6},{6,4},{8,10},{10,8},{12,14},{14,12},{16,18},{18,... | collective-permute-start | bytes 6291464 | tf_op jit(solution)/shard_map/ppermute | solution.py:393
  0.5 15.6 %collective-permute-start.7 = (bf16[4,512,512]{2,1,0:T(8,128)(2,1)}, bf16[4,512,512]{2,1,0:T(8,128)(2,1)S(1)}, u32[]{:S(2)}, u32[]{:S(2)}) collective-permute-start(bf16[4,512,512]{2,1,0:T(8,128)(2,1)} %cv_hbm.1), channel_id=1, source_target_pairs={{0,2},{2,0},{4,6},{6,4},{8,10},{10,8},{12,14},{14,12},{16,18},{18,... | collective-permute-start | bytes 6291464 | tf_op jit(solution)/shard_map/ppermute | solution.py:393
  0.5 7.9 %collective-permute-start = (bf16[4,4096]{1,0:T(4,128)(2,1)}, bf16[4,4096]{1,0:T(4,128)(2,1)S(1)}, u32[]{:S(2)}, u32[]{:S(2)}) collective-permute-start(bf16[4,4096]{1,0:T(4,128)(2,1)} %q_hbm.1), channel_id=1, source_target_pairs={{0,24},{2,26},{4,28},{6,30},{8,16},{10,18},{12,20},{14,22},{16,8},... | collective-permute-start | bytes 98312 | tf_op jit(solution)/shard_map/ppermute | solution.py:393
  5.6 5.0 %collective-permute-start.2 = (bf16[4,4096]{1,0:T(4,128)(2,1)}, bf16[4,4096]{1,0:T(4,128)(2,1)S(1)}, u32[]{:S(2)}, u32[]{:S(2)}) collective-permute-start(bf16[4,4096]{1,0:T(4,128)(2,1)} %q_hbm.1), channel_id=1, source_target_pairs={{0,16},{2,18},{4,20},{6,22},{8,24},{10,26},{12,28},{14,30},{16,0},... | collective-permute-start | bytes 98312 | tf_op jit(solution)/shard_map/ppermute | solution.py:393
  5.6 5.0 %collective-permute-start.1 = (bf16[4,4096]{1,0:T(4,128)(2,1)}, bf16[4,4096]{1,0:T(4,128)(2,1)S(1)}, u32[]{:S(2)}, u32[]{:S(2)}) collective-permute-start(bf16[4,4096]{1,0:T(4,128)(2,1)} %q_hbm.1), channel_id=1, source_target_pairs={{0,8},{2,10},{4,12},{6,14},{8,0},{10,2},{12,4},{14,6},{16,24},{18,... | collective-permute-start | bytes 98312 | tf_op jit(solution)/shard_map/ppermute | solution.py:393
  8.4 2.2 %collective-permute-start.3 = (s32[8,128]{1,0:T(8,128)S(1)}, s32[8,128]{1,0:T(8,128)S(1)}, u32[]{:S(2)}, u32[]{:S(2)}) collective-permute-start(s32[8,128]{1,0:T(8,128)S(1)} %get-tuple-element.45.refs_2_), channel_id=1, source_target_pairs={{0,2},{2,0},{4,6},{6,4},{8,10},{10,8},{12,14},{14,12},{16,18},{18,... | collective-permute-start | bytes 12296 | tf_op jit(solution)/shard_map/ppermute | solution.py:393
  10.7 5.4 %collective-permute-start.4 = (bf16[4,256,512]{2,1,0:T(8,128)(2,1)S(1)}, bf16[4,256,512]{2,1,0:T(8,128)(2,1)S(1)}, u32[]{:S(2)}, u32[]{:S(2)}) collective-permute-start(bf16[4,256,512]{2,1,0:T(8,128)(2,1)S(1)} %copy-done.3), channel_id=1, source_target_pairs={{0,2},{2,0},{4,6},{6,4},{8,10},{10,8},{12,14},{14,12},{16,18},{18,... | collective-permute-start | bytes 3145736 | tf_op jit(solution)/shard_map/ppermute | solution.py:393
  10.8 5.3 %collective-permute-start.5 = (bf16[4,256,512]{2,1,0:T(8,128)(2,1)S(1)}, bf16[4,256,512]{2,1,0:T(8,128)(2,1)S(1)}, u32[]{:S(2)}, u32[]{:S(2)}) collective-permute-start(bf16[4,256,512]{2,1,0:T(8,128)(2,1)S(1)} %copy-done.4), channel_id=1, source_target_pairs={{0,2},{2,0},{4,6},{6,4},{8,10},{10,8},{12,14},{14,12},{16,18},{18,... | collective-permute-start | bytes 3145736 | tf_op jit(solution)/shard_map/ppermute | solution.py:393
  11.2 5.6 %collective-permute-start.8 = (bf16[16,4224]{1,0:T(8,128)(2,1)S(1)}, bf16[16,4224]{1,0:T(8,128)(2,1)S(1)}, u32[]{:S(2)}, u32[]{:S(2)}) collective-permute-start(bf16[16,4224]{1,0:T(8,128)(2,1)S(1)} %line.1.q_ref), channel_id=1, source_target_pairs={{0,4},{2,6},{4,0},{6,2},{8,12},{10,14},{12,8},{14,10},{16,20},{18,... | collective-permute-start | bytes 405512 | tf_op jit(solution)/shard_map/ppermute | solution.py:393
  18.2 4.5 %collective-permute-start.9 = (bf16[2,4,4224]{2,1,0:T(4,128)(2,1)S(1)}, bf16[2,4,4224]{2,1,0:T(4,128)(2,1)S(1)}, u32[]{:S(2)}, u32[]{:S(2)}) collective-permute-start(bf16[2,4,4224]{2,1,0:T(4,128)(2,1)S(1)} %get-tuple-element.61), channel_id=1, source_target_pairs={{0,4},{2,6},{4,0},{6,2},{8,12},{10,14},{12,8},{14,10},{16,20},{18,... | collective-permute-start | bytes 202760 | tf_op jit(solution)/shard_map/ppermute | solution.py:393
  22.1 5.1 %collective-permute-start.12 = (bf16[2,4,4224]{2,1,0:T(4,128)(2,1)S(1)}, bf16[2,4,4224]{2,1,0:T(4,128)(2,1)S(1)}, u32[]{:S(2)}, u32[]{:S(2)}) collective-permute-start(bf16[2,4,4224]{2,1,0:T(4,128)(2,1)S(1)} %side_private.1), channel_id=1, source_target_pairs={{0,4},{2,6},{4,0},{6,2},{8,12},{10,14},{12,8},{14,10},{16,20},{18,... | collective-permute-start | bytes 202760 | tf_op jit(solution)/shard_map/ppermute | solution.py:393
  23.1 8.5 %copy-start.1 = (bf16[4,512]{1,0:T(4,128)(2,1)S(1)}, bf16[4,512]{1,0:T(4,128)(2,1)}, u32[]{:S(2)}) copy-start(bf16[4,512]{1,0:T(4,128)(2,1)} %nk_ref.1) | copy-start | bytes 12292
  23.1 8.5 %copy-start.2 = (bf16[4,512]{1,0:T(4,128)(2,1)S(1)}, bf16[4,512]{1,0:T(4,128)(2,1)}, u32[]{:S(2)}) copy-start(bf16[4,512]{1,0:T(4,128)(2,1)} %nv_ref.1) | copy-start | bytes 12292
  23.1 6.1 %collective-permute-start.10 = (bf16[4,4224]{1,0:T(4,128)(2,1)S(1)}, bf16[4,4224]{1,0:T(4,128)(2,1)S(1)}, u32[]{:S(2)}, u32[]{:S(2)}) collective-permute-start(bf16[4,4224]{1,0:T(4,128)(2,1)S(1)} %get-tuple-element.64), channel_id=1, source_target_pairs={{0,24},{2,26},{4,28},{6,30},{8,16},{10,18},{12,20},{14,22},{16,8},... | collective-permute-start | bytes 101384 | tf_op jit(solution)/shard_map/ppermute | solution.py:393
  26.0 4.8 %collective-permute-start.11 = (bf16[4,4224]{1,0:T(4,128)(2,1)S(1)}, bf16[4,4224]{1,0:T(4,128)(2,1)S(1)}, u32[]{:S(2)}, u32[]{:S(2)}) collective-permute-start(bf16[4,4224]{1,0:T(4,128)(2,1)S(1)} %get-tuple-element.65), channel_id=1, source_target_pairs={{0,16},{2,18},{4,20},{6,22},{8,24},{10,26},{12,28},{14,30},{16,0},... | collective-permute-start | bytes 101384 | tf_op jit(solution)/shard_map/ppermute | solution.py:393
  26.0 19.4 %copy-start = (bf16[4096,512]{1,0:T(8,128)(2,1)S(1)}, bf16[4096,512]{1,0:T(8,128)(2,1)}, u32[]{:S(2)}) copy-start(bf16[4096,512]{1,0:T(8,128)(2,1)} %w_ref.1) | copy-start | bytes 12582916
  27.6 4.0 %collective-permute-start.13 = (bf16[4,4224]{1,0:T(4,128)(2,1)S(1)}, bf16[4,4224]{1,0:T(4,128)(2,1)S(1)}, u32[]{:S(2)}, u32[]{:S(2)}) collective-permute-start(bf16[4,4224]{1,0:T(4,128)(2,1)S(1)} %get-tuple-element.69), channel_id=1, source_target_pairs={{0,8},{2,10},{4,12},{6,14},{8,0},{10,2},{12,4},{14,6},{16,24},{18,... | collective-permute-start | bytes 101384 | tf_op jit(solution)/shard_map/ppermute | solution.py:393
  32.1 5.8 %collective-permute-start.14 = (bf16[4,4096]{1,0:T(4,128)(2,1)S(1)}, bf16[4,4096]{1,0:T(4,128)(2,1)S(1)}, u32[]{:S(2)}, u32[]{:S(2)}) collective-permute-start(bf16[4,4096]{1,0:T(4,128)(2,1)S(1)} %finish.1), channel_id=1, source_target_pairs={{0,24},{2,26},{4,28},{6,30},{8,16},{10,18},{12,20},{14,22},{16,8},... | collective-permute-start | bytes 98312 | tf_op jit(solution)/shard_map/ppermute | solution.py:393
  34.5 5.0 %collective-permute-start.18 = (bf16[4,4096]{1,0:T(4,128)(2,1)S(1)}, bf16[4,4096]{1,0:T(4,128)(2,1)S(1)}, u32[]{:S(2)}, u32[]{:S(2)}) collective-permute-start(bf16[4,4096]{1,0:T(4,128)(2,1)S(1)} %finish.1), channel_id=1, source_target_pairs={{0,16},{2,18},{4,20},{6,22},{8,24},{10,26},{12,28},{14,30},{16,0},... | collective-permute-start | bytes 98312 | tf_op jit(solution)/shard_map/ppermute | solution.py:393
  35.2 4.3 %collective-permute-start.17 = (bf16[4,4096]{1,0:T(4,128)(2,1)S(1)}, bf16[4,4096]{1,0:T(4,128)(2,1)S(1)}, u32[]{:S(2)}, u32[]{:S(2)}) collective-permute-start(bf16[4,4096]{1,0:T(4,128)(2,1)S(1)} %finish.1), channel_id=1, source_target_pairs={{0,8},{2,10},{4,12},{6,14},{8,0},{10,2},{12,4},{14,6},{16,24},{18,... | collective-permute-start | bytes 98312 | tf_op jit(solution)/shard_map/ppermute | solution.py:393
  37.9 4.3 %collective-permute-start.15 = (bf16[2,4,4096]{2,1,0:T(4,128)(2,1)S(1)}, bf16[2,4,4096]{2,1,0:T(4,128)(2,1)S(1)}, u32[]{:S(2)}, u32[]{:S(2)}) collective-permute-start(bf16[2,4,4096]{2,1,0:T(4,128)(2,1)S(1)} %get-tuple-element.76), channel_id=1, source_target_pairs={{0,4},{2,6},{4,0},{6,2},{8,12},{10,14},{12,8},{14,10},{16,20},{18,... | collective-permute-start | bytes 196616 | tf_op jit(solution)/shard_map/ppermute | solution.py:393
  39.5 4.3 %collective-permute-start.19 = (bf16[2,4,4096]{2,1,0:T(4,128)(2,1)S(1)}, bf16[2,4,4096]{2,1,0:T(4,128)(2,1)S(1)}, u32[]{:S(2)}, u32[]{:S(2)}) collective-permute-start(bf16[2,4,4096]{2,1,0:T(4,128)(2,1)S(1)} %get-tuple-element.74), channel_id=1, source_target_pairs={{0,4},{2,6},{4,0},{6,2},{8,12},{10,14},{12,8},{14,10},{16,20},{18,... | collective-permute-start | bytes 196616 | tf_op jit(solution)/shard_map/ppermute | solution.py:393
  42.4 1.7 %collective-permute-start.16 = (bf16[2,2,4,4096]{3,2,1,0:T(4,128)(2,1)S(1)}, bf16[2,2,4,4096]{3,2,1,0:T(4,128)(2,1)S(1)}, u32[]{:S(2)}, u32[]{:S(2)}) collective-permute-start(bf16[2,2,4,4096]{3,2,1,0:T(4,128)(2,1)S(1)} %pad_maximum_fusion.near_a), channel_id=1, source_target_pairs={{0,2},{2,0},{4,6},{6,4},{8,10},{10,8},{12,14},{14,12},{16,18},{18,... | collective-permute-start | bytes 393224 | tf_op jit(solution)/shard_map/ppermute | solution.py:393
  44.0 1.4 %collective-permute-start.20 = (bf16[2,2,4,4096]{3,2,1,0:T(4,128)(2,1)S(1)}, bf16[2,2,4,4096]{3,2,1,0:T(4,128)(2,1)S(1)}, u32[]{:S(2)}, u32[]{:S(2)}) collective-permute-start(bf16[2,2,4,4096]{3,2,1,0:T(4,128)(2,1)S(1)} %pad_maximum_fusion.1.near_b), channel_id=1, source_target_pairs={{0,2},{2,0},{4,6},{6,4},{8,10},{10,8},{12,14},{14,12},{16,18},{18,... | collective-permute-start | bytes 393224 | tf_op jit(solution)/shard_map/ppermute | solution.py:393
  46.3 4.0 %collective-permute-start.21 = (bf16[32,512]{1,0:T(8,128)(2,1)S(1)}, bf16[32,512]{1,0:T(8,128)(2,1)S(1)}, u32[]{:S(2)}, u32[]{:S(2)}) collective-permute-start(bf16[32,512]{1,0:T(8,128)(2,1)S(1)} %get-tuple-element.72), channel_id=1, source_target_pairs={{0,1},{1,0},{2,3},{3,2},{4,5},{5,4},{6,7},{7,6},{8,9},{9,8},{10,11... | collective-permute-start | bytes 98312 | tf_op jit(solution)/shard_map/ppermute | solution.py:511

commit v10 on v9

--- a/solution.py
+++ b/solution.py
@@ -261,10 +261,11 @@
     return x + pltpu.roll(x, STATS - stride, 1) + pltpu.roll(x, STATS - 2 * stride, 1)
 
 
-def plane_kernel(*refs):
-    count, beams, total = refs[0].shape
+def plane_kernel(first, last, *refs):
+    _, beams, total = refs[0].shape
+    count = last - first
     parts, outs = refs[:-count], refs[-count:]
-    parts = [jnp.concatenate([x[n] for n in range(count)], axis=0) for x in parts]
+    parts = [jnp.concatenate([x[n] for n in range(first, last)], axis=0) for x in parts]
     heads = (total - STATS) // HD
 
     def store(cols, value):
@@ -475,12 +476,20 @@
     send_a, send_b = attend("side_prompt", (0, 1), True, False, other, *caches, *stored)
     send_b = attend("side_private", (0, 1), False, True, other, *caches, *stored, send_b)
     piece = jax.ShapeDtypeStruct((beams, total), bf16)
-    few = (piece,) * (requests // 2)
+    half_count = requests // 2
+
+    def plane_merge(first, last, *partials):
+        kernel = functools.partial(plane_kernel, first, last)
+        return call(kernel, "plane_merge", (piece,) * (last - first), *partials)
+
     came_a, came_b = swap(send_a, 2), swap(send_b, 2)
-    parts = call(plane_kernel, "plane_merge", few, here_a, there_a, came_a)
-    there_b, *parts = lax.optimization_barrier((there_b, *parts))
+    far_parts = plane_merge(0, half_count, here_a, there_a, came_a)
+    here_b, *far_parts = lax.optimization_barrier((here_b, *far_parts))
+    near_parts = plane_merge(0, half_count - 1, here_b, there_b, came_b)
+    there_b, *near_parts = lax.optimization_barrier((there_b, *near_parts))
     there_b = attend("own_private", (1,), False, True, asked, *stored, there_b)
-    parts = [*parts, *call(plane_kernel, "plane_merge", few, here_b, there_b, came_b)]
+    own_parts = plane_merge(half_count - 1, half_count, here_b, there_b, came_b)
+    parts = [*far_parts, *near_parts, *own_parts]
     parts = [swap(x, t * group) if t else x for t, x in zip(order, parts)]
     attended = call(
         finish_kernel,

time: 51 us -> 50.6 us (level)
  starting transfers between devices: 24.1 us -> 22.5 us
  waiting for transfers between devices: 12.2 us -> 13.1 us
    ppermute x21, starting transfers between devices: 22.6 us -> 20.9 us  [swap(): return lax.ppermute(x, 'beam', [(i, i ^ with_bit) for i in range(devices)])]
    ppermute x21, waiting for transfers between devices: 9.85 us -> 10.7 us  [swap(): return lax.ppermute(x, 'beam', [(i, i ^ with_bit) for i in range(devices)])]
    pallas_call x12 -> x13, Pallas kernels: 13.3 us -> 13.6 us  [call(): pl.pallas_call(kernel, out_shape=out_shape, in_specs=whole_blocks(len(arg...]
  transfers between devices with their start and end apart: 22 -> 22, of which waited for: 8 -> 10; matrix products, arithmetic and copies ran while one was open for 1% -> 1% of each run, Pallas kernels for 21% -> 22%
where the time goes in v10:
time: 50.6 us; the launch traced here: 50.4 us
  starting transfers between devices  22.5 us (44%)
  Pallas kernels  13.6 us (27%)
  waiting for transfers between devices  13.1 us (26%)
  other arithmetic  0.92 us (2%)
    ppermute x21, starting transfers between devices, swap(): return lax.ppermute(x, 'beam', [(i, i ^ with_bit) for i in range(devices)])  20.9 us
    pallas_call x13, Pallas kernels, call(): pl.pallas_call(kernel, out_shape=out_shape, in_specs=whole_blocks(len(arg...  13.6 us
    ppermute x21, waiting for transfers between devices, swap(): return lax.ppermute(x, 'beam', [(i, i ^ with_bit) for i in range(devices)])  10.7 us
    ppermute x1, waiting for transfers between devices, per_device(): came = lax.ppermute(send, 'head', [(0, 1), (1, 0)])  2.39 us
    ppermute x1, starting transfers between devices, per_device(): came = lax.ppermute(send, 'head', [(0, 1), (1, 0)])  1.59 us
  transfers between devices with their start and end apart: 22, of which 10 were waited for; matrix products, arithmetic and copies ran while one was open for 1% of the time, Pallas kernels for 22%

profile of v10, /device:TPU:0, one launch (start us, length us, event | category | flops | bytes accessed | tf_op | source)
XLA Modules:
  0.0 50.4 jit_solution(10386908619259237968)
XLA Ops:
  0.0 0.5 collective-permute-start.7
  0.5 0.1 collective-permute-start.8
  0.5 5.0 %collective-permute-start = (bf16[4,4096]{1,0:T(4,128)(2,1)}, bf16[4,4096]{1,0:T(4,128)(2,1)S(1)}, u32[]{:S(2)}, u32[]{:S(2)}) collective-permute-start(bf16[4,4096]{1,0:T(4,128)(2,1)} %q_hbm.1), channel_id=1, source_target_pairs={{0,24},{2,26},{4,28},{6,30},{8,16},{10,18},{12,20},{14,22},{16,8},... | collective-permute-start | bytes 98312 | tf_op jit(solution)/shard_map/ppermute | solution.py:394
  5.6 0.6 %collective-permute-start.1 = (bf16[4,4096]{1,0:T(4,128)(2,1)}, bf16[4,4096]{1,0:T(4,128)(2,1)S(1)}, u32[]{:S(2)}, u32[]{:S(2)}) collective-permute-start(bf16[4,4096]{1,0:T(4,128)(2,1)} %q_hbm.1), channel_id=1, source_target_pairs={{0,8},{2,10},{4,12},{6,14},{8,0},{10,2},{12,4},{14,6},{16,24},{18,... | collective-permute-start | bytes 98312 | tf_op jit(solution)/shard_map/ppermute | solution.py:394
  6.1 2.3 %load_private.1 = (bf16[4,4096]{1,0:T(4,128)(2,1)S(1)}, bf16[4,128]{1,0:T(4,128)(2,1)S(1)}, s32[8,128]{1,0:T(8,128)S(1)}, bf16[4,512,512]{2,1,0:T(8,128)(2,1)S(1)}, bf16[4,512,512]{2,1,0:T(8,128)(2,1)S(1)}) custom-call(bf16[4,4096]{1,0:T(4,128)(2,1)} %q_hbm.1, s32[4]{0:T(128)} %par_hbm.1, s32[4]{0:T(128)} %cnt_hbm.1, bf16[4,512,512]{2,1,0:T(8,128)(2,1)} %ck_hbm.1, ...), custom_call_target="tpu_custom_call" | custom-call | flops 67108864 | bytes 67108864 | tf_op jit(solution)/shard_map/load_private/pallas_call | solution.py:361
  8.4 0.1 collective-permute-start.4
  8.5 2.1 %collective-permute-done.2.refs_2_ = bf16[4,4096]{1,0:T(4,128)(2,1)S(1)} collective-permute-done((bf16[4,4096]{1,0:T(4,128)(2,1)}, bf16[4,4096]{1,0:T(4,128)(2,1)S(1)}, u32[]{:S(2)}, u32[]{:S(2)}) %collective-permute-start.2) | collective-permute-done | bytes 32800 | tf_op jit(solution)/shard_map/ppermute | solution.py:394
  10.7 0.1 collective-permute-start.5
  10.8 0.5 collective-permute-start.6
  11.2 1.5 %collective-permute-start.3 = (bf16[16,4224]{1,0:T(8,128)(2,1)S(1)}, bf16[16,4224]{1,0:T(8,128)(2,1)S(1)}, u32[]{:S(2)}, u32[]{:S(2)}) collective-permute-start(bf16[16,4224]{1,0:T(8,128)(2,1)S(1)} %line.1.q_ref), channel_id=1, source_target_pairs={{0,4},{2,6},{4,0},{6,2},{8,12},{10,14},{12,8},{14,10},{16,20},{18,... | collective-permute-start | bytes 405512 | tf_op jit(solution)/shard_map/ppermute | solution.py:394
  12.7 1.6 %load_prompt.1 = (bf16[4,256,512]{2,1,0:T(8,128)(2,1)S(1)}, bf16[4,256,512]{2,1,0:T(8,128)(2,1)S(1)}) custom-call(bf16[4,256,512]{2,1,0:T(8,128)(2,1)} %pk_hbm, bf16[4,256,512]{2,1,0:T(8,128)(2,1)} %pv_hbm), custom_call_target="tpu_custom_call" | custom-call | flops 67108864 | bytes 67108864 | tf_op jit(solution)/shard_map/load_prompt/pallas_call | solution.py:361
  14.3 1.7 %attend_own.1 = (bf16[2,4,4224]{2,1,0:T(4,128)(2,1)S(1)}, bf16[2,4,4224]{2,1,0:T(4,128)(2,1)S(1)}) custom-call(bf16[16,4224]{1,0:T(8,128)(2,1)S(1)} %line.1.q_ref, bf16[4,256,512]{2,1,0:T(8,128)(2,1)S(1)} %get-tuple-element.47.refs_0_, bf16[4,256,512]{2,1,0:T(8,128)(2,1)S(1)} %get-tuple-element.48.refs_1_, s32[8,128]{1,0:T(8,128)S(1)} %get-tuple-element.49.refs_2_, ...), custom_call_target="tpu_custom_call" | custom-call | flops 67108864 | bytes 67108864 | tf_op jit(solution)/shard_map/attend_own/pallas_call | solution.py:361
  16.1 0.7 %own_prompt.1 = (bf16[2,4,4224]{2,1,0:T(4,128)(2,1)S(1)}, bf16[2,4,4224]{2,1,0:T(4,128)(2,1)S(1)}) custom-call(bf16[16,4224]{1,0:T(8,128)(2,1)S(1)} %line.1.q_ref, bf16[4,256,512]{2,1,0:T(8,128)(2,1)S(1)} %collective-permute-done.5.refs_0_.refs_5_, bf16[4,256,512]{2,1,0:T(8,128)(2,1)S(1)} %collective-permute-done.6.refs_1_.refs_6_, ...), custom_call_target="tpu_custom_call" | custom-call | flops 67108864 | bytes 67108864 | tf_op jit(solution)/shard_map/own_prompt/pallas_call | solution.py:361
  16.8 0.0 collective-permute-done.3.q_ref
  16.8 1.4 %side_prompt.1 = (bf16[2,4,4224]{2,1,0:T(4,128)(2,1)S(1)}, bf16[2,4,4224]{2,1,0:T(4,128)(2,1)S(1)}) custom-call(bf16[16,4224]{1,0:T(8,128)(2,1)S(1)} %collective-permute-done.3.q_ref, bf16[4,256,512]{2,1,0:T(8,128)(2,1)S(1)} %get-tuple-element.47.refs_0_, bf16[4,256,512]{2,1,0:T(8,128)(2,1)S(1)} %get-tuple-element.48.refs_1_, ...), custom_call_target="tpu_custom_call" | custom-call | flops 67108864 | bytes 67108864 | tf_op jit(solution)/shard_map/side_prompt/pallas_call | solution.py:361
  18.2 1.6 %collective-permute-start.9 = (bf16[2,4,4224]{2,1,0:T(4,128)(2,1)S(1)}, bf16[2,4,4224]{2,1,0:T(4,128)(2,1)S(1)}, u32[]{:S(2)}, u32[]{:S(2)}) collective-permute-start(bf16[2,4,4224]{2,1,0:T(4,128)(2,1)S(1)} %get-tuple-element.61), channel_id=1, source_target_pairs={{0,4},{2,6},{4,0},{6,2},{8,12},{10,14},{12,8},{14,10},{16,20},{18,... | collective-permute-start | bytes 202760 | tf_op jit(solution)/shard_map/ppermute | solution.py:394
  19.8 2.4 %side_private.1 = bf16[2,4,4224]{2,1,0:T(4,128)(2,1)S(1)} custom-call(bf16[16,4224]{1,0:T(8,128)(2,1)S(1)} %collective-permute-done.3.q_ref, bf16[4,256,512]{2,1,0:T(8,128)(2,1)S(1)} %get-tuple-element.47.refs_0_, bf16[4,256,512]{2,1,0:T(8,128)(2,1)S(1)} %get-tuple-element.48.refs_1_, s32[8,128]{1,0:T(8,128)S(1)} %get-tuple-element.49.refs_2_, ...), custom_call_target="tpu_custom_call" | custom-call | flops 67108864 | bytes 67108864 | tf_op jit(solution)/shard_map/side_private/pallas_call | solution.py:361
  22.1 0.6 %collective-permute-start.12 = (bf16[2,4,4224]{2,1,0:T(4,128)(2,1)S(1)}, bf16[2,4,4224]{2,1,0:T(4,128)(2,1)S(1)}, u32[]{:S(2)}, u32[]{:S(2)}) collective-permute-start(bf16[2,4,4224]{2,1,0:T(4,128)(2,1)S(1)} %side_private.1), channel_id=1, source_target_pairs={{0,4},{2,6},{4,0},{6,2},{8,12},{10,14},{12,8},{14,10},{16,20},{18,... | collective-permute-start | bytes 202760 | tf_op jit(solution)/shard_map/ppermute | solution.py:394
  22.8 0.3 plane_merge.3
  23.1 2.9 %collective-permute-start.10 = (bf16[4,4224]{1,0:T(4,128)(2,1)S(1)}, bf16[4,4224]{1,0:T(4,128)(2,1)S(1)}, u32[]{:S(2)}, u32[]{:S(2)}) collective-permute-start(bf16[4,4224]{1,0:T(4,128)(2,1)S(1)} %get-tuple-element.64), channel_id=1, source_target_pairs={{0,24},{2,26},{4,28},{6,30},{8,16},{10,18},{12,20},{14,22},{16,8},... | collective-permute-start | bytes 101384 | tf_op jit(solution)/shard_map/ppermute | solution.py:394
  26.0 0.5 %collective-permute-done.12.refs_2_ = bf16[2,4,4224]{2,1,0:T(4,128)(2,1)S(1)} collective-permute-done((bf16[2,4,4224]{2,1,0:T(4,128)(2,1)S(1)}, bf16[2,4,4224]{2,1,0:T(4,128)(2,1)S(1)}, u32[]{:S(2)}, u32[]{:S(2)}) %collective-permute-start.12) | collective-permute-done | bytes 67616 | tf_op jit(solution)/shard_map/ppermute | solution.py:394
  26.5 0.3 plane_merge.4
  26.8 0.0 copy-start.1
  26.8 1.1 %collective-permute-start.13 = (bf16[4,4224]{1,0:T(4,128)(2,1)S(1)}, bf16[4,4224]{1,0:T(4,128)(2,1)S(1)}, u32[]{:S(2)}, u32[]{:S(2)}) collective-permute-start(bf16[4,4224]{1,0:T(4,128)(2,1)S(1)} %plane_merge.4), channel_id=1, source_target_pairs={{0,8},{2,10},{4,12},{6,14},{8,0},{10,2},{12,4},{14,6},{16,24},{18,... | collective-permute-start | bytes 101384 | tf_op jit(solution)/shard_map/ppermute | solution.py:394
  28.0 1.3 %own_private.1.refs_1_ = bf16[2,4,4224]{2,1,0:T(4,128)(2,1)S(1)} custom-call(bf16[16,4224]{1,0:T(8,128)(2,1)S(1)} %line.1.q_ref, bf16[4,256,512]{2,1,0:T(8,128)(2,1)S(1)} %collective-permute-done.5.refs_0_.refs_5_, bf16[4,256,512]{2,1,0:T(8,128)(2,1)S(1)} %collective-permute-done.6.refs_1_.refs_6_, s32[8,128]{1,0:T(8,128)S(1)} %collective-permute-done.4.refs_2_.refs_7_, ...), custom_call_target="tpu_custom_call" | custom-call | flops 67108864 | bytes 67108864 | tf_op jit(solution)/shard_map/own_private/pallas_call | solution.py:361
  29.2 0.3 plane_merge.5.refs_3_
  29.6 1.2 %collective-permute-done.11.refs_1_ = bf16[4,4224]{1,0:T(4,128)(2,1)S(1)} collective-permute-done((bf16[4,4224]{1,0:T(4,128)(2,1)S(1)}, bf16[4,4224]{1,0:T(4,128)(2,1)S(1)}, u32[]{:S(2)}, u32[]{:S(2)}) %collective-permute-start.11) | collective-permute-done | bytes 33824 | tf_op jit(solution)/shard_map/ppermute | solution.py:394
  30.8 0.3 collective-permute-done.13.refs_2_
  31.2 0.5 finish.1
  31.6 2.6 %collective-permute-start.14 = (bf16[4,4096]{1,0:T(4,128)(2,1)S(1)}, bf16[4,4096]{1,0:T(4,128)(2,1)S(1)}, u32[]{:S(2)}, u32[]{:S(2)}) collective-permute-start(bf16[4,4096]{1,0:T(4,128)(2,1)S(1)} %finish.1), channel_id=1, source_target_pairs={{0,24},{2,26},{4,28},{6,30},{8,16},{10,18},{12,20},{14,22},{16,8},... | collective-permute-start | bytes 98312 | tf_op jit(solution)/shard_map/ppermute | solution.py:394
  34.2 1.9 %collective-permute-start.17 = (bf16[4,4096]{1,0:T(4,128)(2,1)S(1)}, bf16[4,4096]{1,0:T(4,128)(2,1)S(1)}, u32[]{:S(2)}, u32[]{:S(2)}) collective-permute-start(bf16[4,4096]{1,0:T(4,128)(2,1)S(1)} %finish.1), channel_id=1, source_target_pairs={{0,8},{2,10},{4,12},{6,14},{8,0},{10,2},{12,4},{14,6},{16,24},{18,... | collective-permute-start | bytes 98312 | tf_op jit(solution)/shard_map/ppermute | solution.py:394
  36.1 1.3 %collective-permute-done.14 = bf16[4,4096]{1,0:T(4,128)(2,1)S(1)} collective-permute-done((bf16[4,4096]{1,0:T(4,128)(2,1)S(1)}, bf16[4,4096]{1,0:T(4,128)(2,1)S(1)}, u32[]{:S(2)}, u32[]{:S(2)}) %collective-permute-start.14) | collective-permute-done | bytes 32800 | tf_op jit(solution)/shard_map/ppermute | solution.py:394
  37.4 0.1 fusion.1
  37.5 1.2 %collective-permute-start.15 = (bf16[2,4,4096]{2,1,0:T(4,128)(2,1)S(1)}, bf16[2,4,4096]{2,1,0:T(4,128)(2,1)S(1)}, u32[]{:S(2)}, u32[]{:S(2)}) collective-permute-start(bf16[2,4,4096]{2,1,0:T(4,128)(2,1)S(1)} %get-tuple-element.76), channel_id=1, source_target_pairs={{0,4},{2,6},{4,0},{6,2},{8,12},{10,14},{12,8},{14,10},{16,20},{18,... | collective-permute-start | bytes 196616 | tf_op jit(solution)/shard_map/ppermute | solution.py:394
  38.7 0.3 collective-permute-done.18
  39.0 0.1 fusion
  39.1 0.7 %collective-permute-start.19 = (bf16[2,4,4096]{2,1,0:T(4,128)(2,1)S(1)}, bf16[2,4,4096]{2,1,0:T(4,128)(2,1)S(1)}, u32[]{:S(2)}, u32[]{:S(2)}) collective-permute-start(bf16[2,4,4096]{2,1,0:T(4,128)(2,1)S(1)} %get-tuple-element.74), channel_id=1, source_target_pairs={{0,4},{2,6},{4,0},{6,2},{8,12},{10,14},{12,8},{14,10},{16,20},{18,... | collective-permute-start | bytes 196616 | tf_op jit(solution)/shard_map/ppermute | solution.py:394
  39.8 2.0 %collective-permute-done.15 = bf16[2,4,4096]{2,1,0:T(4,128)(2,1)S(1)} collective-permute-done((bf16[2,4,4096]{2,1,0:T(4,128)(2,1)S(1)}, bf16[2,4,4096]{2,1,0:T(4,128)(2,1)S(1)}, u32[]{:S(2)}, u32[]{:S(2)}) %collective-permute-start.15) | collective-permute-done | bytes 65568 | tf_op jit(solution)/shard_map/ppermute | solution.py:394
  41.8 0.1 pad_maximum_fusion.near_a
  41.9 0.1 collective-permute-start.16
  42.0 1.4 %collective-permute-done.19 = bf16[2,4,4096]{2,1,0:T(4,128)(2,1)S(1)} collective-permute-done((bf16[2,4,4096]{2,1,0:T(4,128)(2,1)S(1)}, bf16[2,4,4096]{2,1,0:T(4,128)(2,1)S(1)}, u32[]{:S(2)}, u32[]{:S(2)}) %collective-permute-start.19) | collective-permute-done | bytes 65568 | tf_op jit(solution)/shard_map/ppermute | solution.py:394
  43.4 0.1 pad_maximum_fusion.1.near_b
  43.5 0.1 collective-permute-start.20
  43.6 1.3 %collective-permute-done.20.far_b = bf16[2,2,4,4096]{3,2,1,0:T(4,128)(2,1)S(1)} collective-permute-done((bf16[2,2,4,4096]{3,2,1,0:T(4,128)(2,1)S(1)}, bf16[2,2,4,4096]{3,2,1,0:T(4,128)(2,1)S(1)}, u32[]{:S(2)}, u32[]{:S(2)}) %collective-permute-start.20) | collective-permute-done | bytes 131104 | tf_op jit(solution)/shard_map/ppermute | solution.py:394
  44.9 0.9 %project.1 = (f32[32,512]{1,0:T(8,128)S(1)}, bf16[32,512]{1,0:T(8,128)(2,1)S(1)}) custom-call(bf16[2,2,4,4096]{3,2,1,0:T(4,128)(2,1)S(1)} %pad_maximum_fusion.near_a, bf16[2,2,4,4096]{3,2,1,0:T(4,128)(2,1)S(1)} %collective-permute-done.16.far_a, bf16[2,2,4,4096]{3,2,1,0:T(4,128)(2,1)S(1)} %pad_maximum_fusion.1.near_b, ...), custom_call_target="tpu_custom_call" | custom-call | tf_op jit(solution)/shard_map/project/pallas_call | solution.py:361
  45.8 1.6 %collective-permute-start.21 = (bf16[32,512]{1,0:T(8,128)(2,1)S(1)}, bf16[32,512]{1,0:T(8,128)(2,1)S(1)}, u32[]{:S(2)}, u32[]{:S(2)}) collective-permute-start(bf16[32,512]{1,0:T(8,128)(2,1)S(1)} %get-tuple-element.72), channel_id=1, source_target_pairs={{0,1},{1,0},{2,3},{3,2},{4,5},{5,4},{6,7},{7,6},{8,9},{9,8},{10,11... | collective-permute-start | bytes 98312 | tf_op jit(solution)/shard_map/ppermute | solution.py:520
  47.4 2.4 %collective-permute-done.21 = bf16[32,512]{1,0:T(8,128)(2,1)S(1)} collective-permute-done((bf16[32,512]{1,0:T(8,128)(2,1)S(1)}, bf16[32,512]{1,0:T(8,128)(2,1)S(1)}, u32[]{:S(2)}, u32[]{:S(2)}) %collective-permute-start.21) | collective-permute-done | bytes 32800 | tf_op jit(solution)/shard_map/ppermute | solution.py:520
  49.8 0.6 %add_convert_fusion = bf16[32,512]{1,0:T(8,128)(2,1)} fusion(f32[32,512]{1,0:T(8,128)S(1)} %get-tuple-element.71, bf16[32,512]{1,0:T(8,128)(2,1)S(1)} %collective-permute-done.21), kind=kLoop, calls=%fused_computation.4 | loop fusion | flops 49152 | bytes 131072 | tf_op jit(solution)/shard_map/convert_element_type | solution.py:521
  (24 shorter events, 0.1 us)
Async XLA Ops:
  0.0 10.7 %copy-start.4 = (bf16[4,256,512]{2,1,0:T(8,128)(2,1)S(1)}, bf16[4,256,512]{2,1,0:T(8,128)(2,1)}, u32[]{:S(2)}) copy-start(bf16[4,256,512]{2,1,0:T(8,128)(2,1)} %pv_hbm) | copy-start | bytes 3145732
  0.0 10.7 %copy-start.3 = (bf16[4,256,512]{2,1,0:T(8,128)(2,1)S(1)}, bf16[4,256,512]{2,1,0:T(8,128)(2,1)}, u32[]{:S(2)}) copy-start(bf16[4,256,512]{2,1,0:T(8,128)(2,1)} %pk_hbm) | copy-start | bytes 3145732
  0.0 16.0 %collective-permute-start.7 = (bf16[4,512,512]{2,1,0:T(8,128)(2,1)}, bf16[4,512,512]{2,1,0:T(8,128)(2,1)S(1)}, u32[]{:S(2)}, u32[]{:S(2)}) collective-permute-start(bf16[4,512,512]{2,1,0:T(8,128)(2,1)} %ck_hbm.1), channel_id=1, source_target_pairs={{0,2},{2,0},{4,6},{6,4},{8,10},{10,8},{12,14},{14,12},{16,18},{18,... | collective-permute-start | bytes 6291464 | tf_op jit(solution)/shard_map/ppermute | solution.py:394
  0.5 15.6 %collective-permute-start.8 = (bf16[4,512,512]{2,1,0:T(8,128)(2,1)}, bf16[4,512,512]{2,1,0:T(8,128)(2,1)S(1)}, u32[]{:S(2)}, u32[]{:S(2)}) collective-permute-start(bf16[4,512,512]{2,1,0:T(8,128)(2,1)} %cv_hbm.1), channel_id=1, source_target_pairs={{0,2},{2,0},{4,6},{6,4},{8,10},{10,8},{12,14},{14,12},{16,18},{18,... | collective-permute-start | bytes 6291464 | tf_op jit(solution)/shard_map/ppermute | solution.py:394
  0.5 7.9 %collective-permute-start = (bf16[4,4096]{1,0:T(4,128)(2,1)}, bf16[4,4096]{1,0:T(4,128)(2,1)S(1)}, u32[]{:S(2)}, u32[]{:S(2)}) collective-permute-start(bf16[4,4096]{1,0:T(4,128)(2,1)} %q_hbm.1), channel_id=1, source_target_pairs={{0,24},{2,26},{4,28},{6,30},{8,16},{10,18},{12,20},{14,22},{16,8},... | collective-permute-start | bytes 98312 | tf_op jit(solution)/shard_map/ppermute | solution.py:394
  5.6 5.0 %collective-permute-start.2 = (bf16[4,4096]{1,0:T(4,128)(2,1)}, bf16[4,4096]{1,0:T(4,128)(2,1)S(1)}, u32[]{:S(2)}, u32[]{:S(2)}) collective-permute-start(bf16[4,4096]{1,0:T(4,128)(2,1)} %q_hbm.1), channel_id=1, source_target_pairs={{0,16},{2,18},{4,20},{6,22},{8,24},{10,26},{12,28},{14,30},{16,0},... | collective-permute-start | bytes 98312 | tf_op jit(solution)/shard_map/ppermute | solution.py:394
  5.6 5.0 %collective-permute-start.1 = (bf16[4,4096]{1,0:T(4,128)(2,1)}, bf16[4,4096]{1,0:T(4,128)(2,1)S(1)}, u32[]{:S(2)}, u32[]{:S(2)}) collective-permute-start(bf16[4,4096]{1,0:T(4,128)(2,1)} %q_hbm.1), channel_id=1, source_target_pairs={{0,8},{2,10},{4,12},{6,14},{8,0},{10,2},{12,4},{14,6},{16,24},{18,... | collective-permute-start | bytes 98312 | tf_op jit(solution)/shard_map/ppermute | solution.py:394
  8.4 2.2 %collective-permute-start.4 = (s32[8,128]{1,0:T(8,128)S(1)}, s32[8,128]{1,0:T(8,128)S(1)}, u32[]{:S(2)}, u32[]{:S(2)}) collective-permute-start(s32[8,128]{1,0:T(8,128)S(1)} %get-tuple-element.49.refs_2_), channel_id=1, source_target_pairs={{0,2},{2,0},{4,6},{6,4},{8,10},{10,8},{12,14},{14,12},{16,18},{18,... | collective-permute-start | bytes 12296 | tf_op jit(solution)/shard_map/ppermute | solution.py:394
  10.7 5.4 %collective-permute-start.5 = (bf16[4,256,512]{2,1,0:T(8,128)(2,1)S(1)}, bf16[4,256,512]{2,1,0:T(8,128)(2,1)S(1)}, u32[]{:S(2)}, u32[]{:S(2)}) collective-permute-start(bf16[4,256,512]{2,1,0:T(8,128)(2,1)S(1)} %copy-done.3), channel_id=1, source_target_pairs={{0,2},{2,0},{4,6},{6,4},{8,10},{10,8},{12,14},{14,12},{16,18},{18,... | collective-permute-start | bytes 3145736 | tf_op jit(solution)/shard_map/ppermute | solution.py:394
  10.8 5.3 %collective-permute-start.6 = (bf16[4,256,512]{2,1,0:T(8,128)(2,1)S(1)}, bf16[4,256,512]{2,1,0:T(8,128)(2,1)S(1)}, u32[]{:S(2)}, u32[]{:S(2)}) collective-permute-start(bf16[4,256,512]{2,1,0:T(8,128)(2,1)S(1)} %copy-done.4), channel_id=1, source_target_pairs={{0,2},{2,0},{4,6},{6,4},{8,10},{10,8},{12,14},{14,12},{16,18},{18,... | collective-permute-start | bytes 3145736 | tf_op jit(solution)/shard_map/ppermute | solution.py:394
  11.2 5.6 %collective-permute-start.3 = (bf16[16,4224]{1,0:T(8,128)(2,1)S(1)}, bf16[16,4224]{1,0:T(8,128)(2,1)S(1)}, u32[]{:S(2)}, u32[]{:S(2)}) collective-permute-start(bf16[16,4224]{1,0:T(8,128)(2,1)S(1)} %line.1.q_ref), channel_id=1, source_target_pairs={{0,4},{2,6},{4,0},{6,2},{8,12},{10,14},{12,8},{14,10},{16,20},{18,... | collective-permute-start | bytes 405512 | tf_op jit(solution)/shard_map/ppermute | solution.py:394
  18.2 4.5 %collective-permute-start.9 = (bf16[2,4,4224]{2,1,0:T(4,128)(2,1)S(1)}, bf16[2,4,4224]{2,1,0:T(4,128)(2,1)S(1)}, u32[]{:S(2)}, u32[]{:S(2)}) collective-permute-start(bf16[2,4,4224]{2,1,0:T(4,128)(2,1)S(1)} %get-tuple-element.61), channel_id=1, source_target_pairs={{0,4},{2,6},{4,0},{6,2},{8,12},{10,14},{12,8},{14,10},{16,20},{18,... | collective-permute-start | bytes 202760 | tf_op jit(solution)/shard_map/ppermute | solution.py:394
  22.1 4.4 %collective-permute-start.12 = (bf16[2,4,4224]{2,1,0:T(4,128)(2,1)S(1)}, bf16[2,4,4224]{2,1,0:T(4,128)(2,1)S(1)}, u32[]{:S(2)}, u32[]{:S(2)}) collective-permute-start(bf16[2,4,4224]{2,1,0:T(4,128)(2,1)S(1)} %side_private.1), channel_id=1, source_target_pairs={{0,4},{2,6},{4,0},{6,2},{8,12},{10,14},{12,8},{14,10},{16,20},{18,... | collective-permute-start | bytes 202760 | tf_op jit(solution)/shard_map/ppermute | solution.py:394
  23.1 6.5 %collective-permute-start.10 = (bf16[4,4224]{1,0:T(4,128)(2,1)S(1)}, bf16[4,4224]{1,0:T(4,128)(2,1)S(1)}, u32[]{:S(2)}, u32[]{:S(2)}) collective-permute-start(bf16[4,4224]{1,0:T(4,128)(2,1)S(1)} %get-tuple-element.64), channel_id=1, source_target_pairs={{0,24},{2,26},{4,28},{6,30},{8,16},{10,18},{12,20},{14,22},{16,8},... | collective-permute-start | bytes 101384 | tf_op jit(solution)/shard_map/ppermute | solution.py:394
  26.0 4.9 %collective-permute-start.11 = (bf16[4,4224]{1,0:T(4,128)(2,1)S(1)}, bf16[4,4224]{1,0:T(4,128)(2,1)S(1)}, u32[]{:S(2)}, u32[]{:S(2)}) collective-permute-start(bf16[4,4224]{1,0:T(4,128)(2,1)S(1)} %get-tuple-element.65), channel_id=1, source_target_pairs={{0,16},{2,18},{4,20},{6,22},{8,24},{10,26},{12,28},{14,30},{16,0},... | collective-permute-start | bytes 101384 | tf_op jit(solution)/shard_map/ppermute | solution.py:394
  26.8 4.3 %copy-start.1 = (bf16[4,512]{1,0:T(4,128)(2,1)S(1)}, bf16[4,512]{1,0:T(4,128)(2,1)}, u32[]{:S(2)}) copy-start(bf16[4,512]{1,0:T(4,128)(2,1)} %nk_ref.1) | copy-start | bytes 12292
  26.8 4.3 %copy-start.2 = (bf16[4,512]{1,0:T(4,128)(2,1)S(1)}, bf16[4,512]{1,0:T(4,128)(2,1)}, u32[]{:S(2)}) copy-start(bf16[4,512]{1,0:T(4,128)(2,1)} %nv_ref.1) | copy-start | bytes 12292
  26.8 4.3 %collective-permute-start.13 = (bf16[4,4224]{1,0:T(4,128)(2,1)S(1)}, bf16[4,4224]{1,0:T(4,128)(2,1)S(1)}, u32[]{:S(2)}, u32[]{:S(2)}) collective-permute-start(bf16[4,4224]{1,0:T(4,128)(2,1)S(1)} %plane_merge.4), channel_id=1, source_target_pairs={{0,8},{2,10},{4,12},{6,14},{8,0},{10,2},{12,4},{14,6},{16,24},{18,... | collective-permute-start | bytes 101384 | tf_op jit(solution)/shard_map/ppermute | solution.py:394
  28.0 17.0 %copy-start = (bf16[4096,512]{1,0:T(8,128)(2,1)S(1)}, bf16[4096,512]{1,0:T(8,128)(2,1)}, u32[]{:S(2)}) copy-start(bf16[4096,512]{1,0:T(8,128)(2,1)} %w_ref.1) | copy-start | bytes 12582916
  31.6 5.8 %collective-permute-start.14 = (bf16[4,4096]{1,0:T(4,128)(2,1)S(1)}, bf16[4,4096]{1,0:T(4,128)(2,1)S(1)}, u32[]{:S(2)}, u32[]{:S(2)}) collective-permute-start(bf16[4,4096]{1,0:T(4,128)(2,1)S(1)} %finish.1), channel_id=1, source_target_pairs={{0,24},{2,26},{4,28},{6,30},{8,16},{10,18},{12,20},{14,22},{16,8},... | collective-permute-start | bytes 98312 | tf_op jit(solution)/shard_map/ppermute | solution.py:394
  34.2 4.8 %collective-permute-start.18 = (bf16[4,4096]{1,0:T(4,128)(2,1)S(1)}, bf16[4,4096]{1,0:T(4,128)(2,1)S(1)}, u32[]{:S(2)}, u32[]{:S(2)}) collective-permute-start(bf16[4,4096]{1,0:T(4,128)(2,1)S(1)} %finish.1), channel_id=1, source_target_pairs={{0,16},{2,18},{4,20},{6,22},{8,24},{10,26},{12,28},{14,30},{16,0},... | collective-permute-start | bytes 98312 | tf_op jit(solution)/shard_map/ppermute | solution.py:394
  34.2 4.8 %collective-permute-start.17 = (bf16[4,4096]{1,0:T(4,128)(2,1)S(1)}, bf16[4,4096]{1,0:T(4,128)(2,1)S(1)}, u32[]{:S(2)}, u32[]{:S(2)}) collective-permute-start(bf16[4,4096]{1,0:T(4,128)(2,1)S(1)} %finish.1), channel_id=1, source_target_pairs={{0,8},{2,10},{4,12},{6,14},{8,0},{10,2},{12,4},{14,6},{16,24},{18,... | collective-permute-start | bytes 98312 | tf_op jit(solution)/shard_map/ppermute | solution.py:394
  37.5 4.3 %collective-permute-start.15 = (bf16[2,4,4096]{2,1,0:T(4,128)(2,1)S(1)}, bf16[2,4,4096]{2,1,0:T(4,128)(2,1)S(1)}, u32[]{:S(2)}, u32[]{:S(2)}) collective-permute-start(bf16[2,4,4096]{2,1,0:T(4,128)(2,1)S(1)} %get-tuple-element.76), channel_id=1, source_target_pairs={{0,4},{2,6},{4,0},{6,2},{8,12},{10,14},{12,8},{14,10},{16,20},{18,... | collective-permute-start | bytes 196616 | tf_op jit(solution)/shard_map/ppermute | solution.py:394
  39.1 4.3 %collective-permute-start.19 = (bf16[2,4,4096]{2,1,0:T(4,128)(2,1)S(1)}, bf16[2,4,4096]{2,1,0:T(4,128)(2,1)S(1)}, u32[]{:S(2)}, u32[]{:S(2)}) collective-permute-start(bf16[2,4,4096]{2,1,0:T(4,128)(2,1)S(1)} %get-tuple-element.74), channel_id=1, source_target_pairs={{0,4},{2,6},{4,0},{6,2},{8,12},{10,14},{12,8},{14,10},{16,20},{18,... | collective-permute-start | bytes 196616 | tf_op jit(solution)/shard_map/ppermute | solution.py:394
  41.9 1.7 %collective-permute-start.16 = (bf16[2,2,4,4096]{3,2,1,0:T(4,128)(2,1)S(1)}, bf16[2,2,4,4096]{3,2,1,0:T(4,128)(2,1)S(1)}, u32[]{:S(2)}, u32[]{:S(2)}) collective-permute-start(bf16[2,2,4,4096]{3,2,1,0:T(4,128)(2,1)S(1)} %pad_maximum_fusion.near_a), channel_id=1, source_target_pairs={{0,2},{2,0},{4,6},{6,4},{8,10},{10,8},{12,14},{14,12},{16,18},{18,... | collective-permute-start | bytes 393224 | tf_op jit(solution)/shard_map/ppermute | solution.py:394
  43.5 1.4 %collective-permute-start.20 = (bf16[2,2,4,4096]{3,2,1,0:T(4,128)(2,1)S(1)}, bf16[2,2,4,4096]{3,2,1,0:T(4,128)(2,1)S(1)}, u32[]{:S(2)}, u32[]{:S(2)}) collective-permute-start(bf16[2,2,4,4096]{3,2,1,0:T(4,128)(2,1)S(1)} %pad_maximum_fusion.1.near_b), channel_id=1, source_target_pairs={{0,2},{2,0},{4,6},{6,4},{8,10},{10,8},{12,14},{14,12},{16,18},{18,... | collective-permute-start | bytes 393224 | tf_op jit(solution)/shard_map/ppermute | solution.py:394
  45.8 4.0 %collective-permute-start.21 = (bf16[32,512]{1,0:T(8,128)(2,1)S(1)}, bf16[32,512]{1,0:T(8,128)(2,1)S(1)}, u32[]{:S(2)}, u32[]{:S(2)}) collective-permute-start(bf16[32,512]{1,0:T(8,128)(2,1)S(1)} %get-tuple-element.72), channel_id=1, source_target_pairs={{0,1},{1,0},{2,3},{3,2},{4,5},{5,4},{6,7},{7,6},{8,9},{9,8},{10,11... | collective-permute-start | bytes 98312 | tf_op jit(solution)/shard_map/ppermute | solution.py:520
